TPU v7x, 32 devices: a whole 2x2x4 slice. The times are simulated.
32 devices in a mesh: dp: 4 (over z), seq: 8 (over y, x, core).
Axes of the slice: x: 2, y: 2, z: 4, core: 2. Of those that a mesh axis runs over, the one named last changes fastest.
Arguments:
- hidden_in: bfloat16 [4, 1024, 2048], P('dp', 'seq'), may hold values from -6 to 6
- segment_ids: int32 [4, 1024], P('dp', 'seq'), may hold values from 0 to 7, as said below
- position_ids: int32 [4, 1024], P('dp', 'seq'), may hold values from 0 to 1023, as said below
- w_qkv: bfloat16 [2048, 6144], P(('dp', 'seq')), may hold values from -0.125 to 0.125
- w_out: bfloat16 [2048, 2048], P(('dp', 'seq')), may hold values from -0.125 to 0.125
- w_up: bfloat16 [2048, 8192], P(None, ('dp', 'seq')), may hold values from -0.125 to 0.125
- w_down: bfloat16 [8192, 2048], P(('dp', 'seq')), may hold values from -0.0625 to 0.0625
- gain_attn: bfloat16 [2048], P(('dp', 'seq')), may hold values from 0.25 to 1.75
- gain_attn_sub: bfloat16 [2048], P(('dp', 'seq')), may hold values from 0.25 to 1.75
- gain_ffn: bfloat16 [2048], P(('dp', 'seq')), may hold values from 0.25 to 1.75
- gain_ffn_sub: bfloat16 [8192], P(('dp', 'seq')), may hold values from 0.25 to 1.75
- ema_qkv: float32 [2048, 6144], P(('dp', 'seq')), may hold values from -0.125 to 0.125
- ema_out: float32 [2048, 2048], P(('dp', 'seq')), may hold values from -0.125 to 0.125
- ema_up: float32 [2048, 8192], P(None, ('dp', 'seq')), may hold values from -0.125 to 0.125
- ema_down: float32 [8192, 2048], P(('dp', 'seq')), may hold values from -0.0625 to 0.0625
- ema_gain_attn: float32 [2048], P(('dp', 'seq')), may hold values from 0.3 to 1.7
- ema_gain_attn_sub: float32 [2048], P(('dp', 'seq')), may hold values from 0.3 to 1.7
- ema_gain_ffn: float32 [2048], P(('dp', 'seq')), may hold values from 0.3 to 1.7
- ema_gain_ffn_sub: float32 [8192], P(('dp', 'seq')), may hold values from 0.3 to 1.7
- out_grad: bfloat16 [4, 1024, 2048], P('dp', 'seq'), may hold values from -6 to 6
Outputs:
- output: bfloat16 [4, 1024, 2048], P('dp', 'seq')
- input_grad: bfloat16 [4, 1024, 2048], P('dp', 'seq')
- grad_w_qkv: float32 [2048, 6144], P(('dp', 'seq'))
- grad_w_out: float32 [2048, 2048], P(('dp', 'seq'))
- grad_w_up: float32 [2048, 8192], P(None, ('dp', 'seq'))
- grad_w_down: float32 [8192, 2048], P(('dp', 'seq'))
- grad_gain_attn: float32 [2048], P(('dp', 'seq'))
- grad_gain_attn_sub: float32 [2048], P(('dp', 'seq'))
- grad_gain_ffn: float32 [2048], P(('dp', 'seq'))
- grad_gain_ffn_sub: float32 [8192], P(('dp', 'seq'))
- new_ema_qkv: float32 [2048, 6144], P(('dp', 'seq'))
- new_ema_out: float32 [2048, 2048], P(('dp', 'seq'))
- new_ema_up: float32 [2048, 8192], P(None, ('dp', 'seq'))
- new_ema_down: float32 [8192, 2048], P(('dp', 'seq'))
- new_ema_gain_attn: float32 [2048], P(('dp', 'seq'))
- new_ema_gain_attn_sub: float32 [2048], P(('dp', 'seq'))
- new_ema_gain_ffn: float32 [2048], P(('dp', 'seq'))
- new_ema_gain_ffn_sub: float32 [8192], P(('dp', 'seq'))
Inputs may be any that keep to these rules, and one draw needn't show every extreme that they name: Along each row segment_ids start at 0 and rise by 0 or 1 from one token to the next, so that every document is a run of consecutive tokens. The first row is one document; every other row holds 8 documents. position_ids is each token's offset from the first token of its document (0 at the row's first token and wherever segment_ids rises).
All inputs are finite; a program needn't handle non-finite values.
Results may differ from a plain program's by a relative error of at most 0.02.
Values may be sent and summed in bfloat16 or wider, within the bound.
A program may use at most 256 MiB of HBM per device.

v0:
```python
import math

import jax
import jax.numpy as jnp
from jax import lax
from jax.sharding import PartitionSpec as P

HEADS = 32
HD = 64


NEG_FILL = -1000000000.0
NORM_EPS = 1e-05
EMA_DECAY = 0.7


def normalize(values):
    centered = values - jnp.mean(values, axis=-1, keepdims=True)
    scaler = lax.rsqrt(jnp.mean(centered * centered, axis=-1, keepdims=True) + NORM_EPS)
    return (centered * scaler, scaler)


def norm_back(scaled_grad, normed, scaler):
    first_mean = jnp.mean(scaled_grad, axis=-1, keepdims=True)
    second_mean = jnp.mean(scaled_grad * normed, axis=-1, keepdims=True)
    return scaler * (scaled_grad - first_mean - normed * second_mean)


def exact_gelu(values):
    return jax.nn.gelu(values, approximate=False)


def swap_pairs(values):
    dims_of = values.shape
    return values.reshape(dims_of[:-1] + (dims_of[-1] // 2, 2))[..., ::-1].reshape(dims_of)


def rotate(values, cosine, sine_table, factor):
    return (values * cosine + swap_pairs(values) * sine_table) * factor


def unrotate(grads, cosine, sine_table, factor):
    scaled = grads * factor
    return scaled * cosine + swap_pairs(scaled * sine_table)


def xpos_tables(positions):
    half_count = HD // 2
    index_half = jnp.arange(half_count).astype(jnp.float32)
    inverse = jnp.exp(-(2.0 * index_half / HD) * math.log(10000.0))
    decay_base = (2.0 * index_half + 0.4 * HD) / (1.4 * HD)
    where_at = positions.astype(jnp.float32)[:, None]
    angles = where_at * inverse[None, :]
    factor = jnp.exp(where_at / 512.0 * jnp.log(decay_base)[None, :])
    sign_row = jnp.where(jnp.arange(HD) % 2 == 0, -1.0, 1.0).astype(jnp.float32)
    cosine = jnp.tile(jnp.repeat(jnp.cos(angles), 2, axis=1), (1, HEADS))
    sine_table = jnp.tile(jnp.repeat(jnp.sin(angles), 2, axis=1) * sign_row[None, :], (1, HEADS))
    factor_table = jnp.tile(jnp.repeat(factor, 2, axis=1), (1, HEADS))
    return (cosine, sine_table, factor_table)


def rows_product(operand, weight_rows):
    return lax.dot_general(
        operand, weight_rows, (((1,), (1,)), ((), ())), preferred_element_type=jnp.float32
    )


def token_product(left_op, right_op):
    return lax.dot_general(
        left_op, right_op, (((0,), (0,)), ((), ())), preferred_element_type=jnp.float32
    )


def block_allowed(seg_block, offset, seg_row, block_rows):
    query_pos = offset + jnp.arange(block_rows)
    key_pos = jnp.arange(seg_row.shape[0])
    return ((key_pos[None, :] <= query_pos[:, None]) & (seg_row[None, :] == seg_block[:, None]))[
        None
    ]


def attend_row(query_row, key_row, value_row, seg_row, block_rows):
    length = query_row.shape[0]
    block_count = length // block_rows
    query_blocks = query_row.reshape((block_count, block_rows) + query_row.shape[1:])
    seg_blocks = seg_row.reshape(block_count, block_rows)
    offsets = jnp.arange(block_count) * block_rows

    def one_block(inputs):
        query_block, seg_block, offset = inputs
        allowed = block_allowed(seg_block, offset, seg_row, block_rows)
        scores = jnp.einsum(
            "qhd,khd->hqk", query_block, key_row, preferred_element_type=jnp.float32
        )
        scores = jnp.where(allowed, scores, NEG_FILL)
        top_score = jnp.max(scores, axis=-1, keepdims=True)
        shifted = jnp.exp(scores - top_score)
        total = jnp.sum(shifted, axis=-1, keepdims=True)
        probs = (shifted / total).astype(jnp.bfloat16)
        attended = jnp.einsum("hqk,khd->qhd", probs, value_row, preferred_element_type=jnp.float32)
        return (attended, top_score + jnp.log(total))

    attended, log_total = lax.map(one_block, (query_blocks, seg_blocks, offsets))
    return (attended.reshape(query_row.shape), log_total)


def attend_back_row(query_row, key_row, value_row, seg_row, grad_row, log_total, block_rows):
    length = query_row.shape[0]
    block_count = length // block_rows
    query_blocks = query_row.reshape((block_count, block_rows) + query_row.shape[1:])
    grad_blocks = grad_row.reshape((block_count, block_rows) + grad_row.shape[1:])
    seg_blocks = seg_row.reshape(block_count, block_rows)
    offsets = jnp.arange(block_count) * block_rows

    def one_block(totals, inputs):
        key_total, value_total = totals
        query_block, grad_block, seg_block, offset, block_total = inputs
        allowed = block_allowed(seg_block, offset, seg_row, block_rows)
        scores = jnp.einsum(
            "qhd,khd->hqk", query_block, key_row, preferred_element_type=jnp.float32
        )
        scores = jnp.where(allowed, scores, NEG_FILL)
        probs = jnp.exp(scores - block_total)
        grad_probs = jnp.einsum(
            "qhd,khd->hqk", grad_block, value_row, preferred_element_type=jnp.float32
        )
        delta = jnp.sum(probs * grad_probs, axis=-1, keepdims=True)
        grad_scores = jnp.where(allowed, probs * (grad_probs - delta), 0.0).astype(jnp.bfloat16)
        grad_query = jnp.einsum(
            "hqk,khd->qhd", grad_scores, key_row, preferred_element_type=jnp.float32
        )
        key_total = key_total + jnp.einsum(
            "hqk,qhd->khd", grad_scores, query_block, preferred_element_type=jnp.float32
        )
        value_total = value_total + jnp.einsum(
            "hqk,qhd->khd",
            probs.astype(jnp.bfloat16),
            grad_block,
            preferred_element_type=jnp.float32,
        )
        return ((key_total, value_total), grad_query)

    zeros = jnp.zeros(key_row.shape, jnp.float32)
    (key_grad, value_grad), query_grad = lax.scan(
        one_block, (zeros, zeros), (query_blocks, grad_blocks, seg_blocks, offsets, log_total)
    )
    return (query_grad.reshape(query_row.shape), key_grad, value_grad)


def body(
    hidden_in,
    segment_ids,
    position_ids,
    w_qkv,
    w_out,
    w_up,
    w_down,
    gain_attn,
    gain_attn_sub,
    gain_ffn,
    gain_ffn_sub,
    ema_qkv,
    ema_out,
    ema_up,
    ema_down,
    ema_gain_attn,
    ema_gain_attn_sub,
    ema_gain_ffn,
    ema_gain_ffn_sub,
    out_grad,
):
    row_count, local_count, model_width = hidden_in.shape
    groups = lax.axis_size("seq")
    dp_count = lax.axis_size("dp")
    head_span = HEADS // groups * HD
    heads_dev = HEADS // groups
    length = local_count * groups
    tokens = row_count * local_count
    block_rows = min(512, length)
    scale = HD ** (-0.5)
    full_qkv, full_out, gain_one, gain_two, gain_three, gain_four = (
        lax.all_gather(w_qkv, ("dp", "seq"), axis=0, tiled=True),
        lax.all_gather(w_out, ("dp", "seq"), axis=0, tiled=True),
        lax.all_gather(gain_attn, ("dp", "seq"), axis=0, tiled=True),
        lax.all_gather(gain_attn_sub, ("dp", "seq"), axis=0, tiled=True),
        lax.all_gather(gain_ffn, ("dp", "seq"), axis=0, tiled=True),
        lax.all_gather(gain_ffn_sub, ("dp", "seq"), axis=0, tiled=True),
    )
    gain_one = gain_one.astype(jnp.float32)
    gain_two = gain_two.astype(jnp.float32)
    gain_three = gain_three.astype(jnp.float32)
    gain_four = gain_four.astype(jnp.float32)
    x_in = hidden_in.reshape(tokens, model_width).astype(jnp.float32)
    cosine, sine_table, factor = xpos_tables(position_ids.reshape(tokens))
    normed_one, scaler_one = normalize(x_in)
    attn_in = (normed_one * gain_one).astype(jnp.bfloat16)
    qkv_raw = jnp.dot(attn_in, full_qkv, preferred_element_type=jnp.float32)
    query_turned = rotate(qkv_raw[:, :model_width], cosine, sine_table, factor) * scale
    key_turned = rotate(qkv_raw[:, model_width : 2 * model_width], cosine, sine_table, 1.0 / factor)
    packed = jnp.stack([query_turned, key_turned, qkv_raw[:, 2 * model_width :]], axis=1).astype(
        jnp.bfloat16
    )
    packed = packed.reshape(row_count, local_count, 3, groups, head_span)
    seg_send = jnp.broadcast_to(
        segment_ids.astype(jnp.bfloat16)[:, :, None, None, None],
        (row_count, local_count, 1, groups, 1),
    )
    by_heads, seg_recv = (
        lax.all_to_all(packed, "seq", split_axis=3, concat_axis=1, tiled=True),
        lax.all_to_all(seg_send, "seq", split_axis=3, concat_axis=1, tiled=True),
    )
    head_queries = by_heads[:, :, 0, 0].reshape(row_count, length, heads_dev, HD)
    head_keys = by_heads[:, :, 1, 0].reshape(row_count, length, heads_dev, HD)
    head_values = by_heads[:, :, 2, 0].reshape(row_count, length, heads_dev, HD)
    seg_rows = seg_recv.reshape(row_count, length).astype(jnp.int32)
    attended, log_total = lax.map(
        lambda inputs: attend_row(inputs[0], inputs[1], inputs[2], inputs[3], block_rows),
        (head_queries, head_keys, head_values, seg_rows),
    )
    attended_send = attended.astype(jnp.bfloat16).reshape(row_count, length, 1, head_span)
    attended_tok = (
        lax.all_to_all(attended_send, "seq", split_axis=1, concat_axis=2, tiled=True)
        .reshape(tokens, model_width)
        .astype(jnp.float32)
    )
    normed_two, scaler_two = normalize(attended_tok)
    attn_sub = (normed_two * gain_two).astype(jnp.bfloat16)
    hmid = x_in + jnp.dot(attn_sub, full_out, preferred_element_type=jnp.float32)
    normed_three, scaler_three = normalize(hmid)
    ffn_in = (normed_three * gain_three).astype(jnp.bfloat16)
    grad_low = out_grad.reshape(tokens, model_width)
    grad_top = grad_low.astype(jnp.float32)
    seq_index = lax.axis_index("seq")
    width_ff = gain_four.shape[0]
    unit_block = width_ff // (dp_count * groups)
    row_tokens = row_count * length
    ffn_rows, grad_rows = (
        lax.all_gather(
            ffn_in.reshape(row_count, local_count, model_width), "seq", axis=1, tiled=True
        ),
        lax.all_gather(out_grad, "seq", axis=1, tiled=True),
    )
    ffn_flat = ffn_rows.reshape(row_tokens, model_width)
    grad_flat = grad_rows.reshape(row_tokens, model_width)
    up_part, down_part = (
        lax.all_gather(w_up, "dp", axis=1, tiled=True),
        lax.all_gather(w_down, "dp", axis=0, tiled=True),
    )
    gain_slice = lax.dynamic_index_in_dim(
        gain_four.reshape(dp_count, groups, unit_block), seq_index, axis=1, keepdims=False
    ).reshape(dp_count * unit_block)
    up_slice = jnp.dot(ffn_flat, up_part, preferred_element_type=jnp.float32)
    activated, gelu_pull = jax.vjp(exact_gelu, up_slice)
    d_sub = rows_product(grad_flat, down_part)
    weighted = d_sub * gain_slice
    sum_act, sum_square, sum_cross, sum_weighted = (
        lax.psum(jnp.sum(activated, axis=1).astype(jnp.bfloat16), "seq").astype(jnp.float32),
        lax.psum(jnp.sum(activated * activated, axis=1).astype(jnp.bfloat16), "seq").astype(
            jnp.float32
        ),
        lax.psum(jnp.sum(weighted * activated, axis=1).astype(jnp.bfloat16), "seq").astype(
            jnp.float32
        ),
        lax.psum(jnp.sum(weighted, axis=1).astype(jnp.bfloat16), "seq").astype(jnp.float32),
    )
    act_mean = sum_act / width_ff
    variance = sum_square / width_ff - act_mean * act_mean
    scaler_row = lax.rsqrt(variance + NORM_EPS)
    normed_four = (activated - act_mean[:, None]) * scaler_row[:, None]
    ffn_sub = (normed_four * gain_slice).astype(jnp.bfloat16)
    partial_out = jnp.dot(ffn_sub, down_part, preferred_element_type=jnp.float32).reshape(
        row_count, length, model_width
    )
    ffn_out = (
        lax.psum_scatter(partial_out.astype(jnp.bfloat16), "seq", scatter_dimension=1, tiled=True)
        .astype(jnp.float32)
        .reshape(tokens, model_width)
    )
    final = hmid + ffn_out
    first_mean = (sum_weighted / width_ff)[:, None]
    second_mean = (scaler_row * (sum_cross - act_mean * sum_weighted) / width_ff)[:, None]
    d_act = scaler_row[:, None] * (weighted - first_mean - normed_four * second_mean)
    slice_gain = jnp.sum(d_sub * normed_four, axis=0)
    gain_holder = jnp.zeros((dp_count, groups, unit_block), jnp.float32)
    grad_gain_four = lax.dynamic_update_slice_in_dim(
        gain_holder, slice_gain.reshape(dp_count, 1, unit_block), seq_index, axis=1
    ).reshape(width_ff)
    (d_up,) = gelu_pull(d_act)
    d_up_low = d_up.astype(jnp.bfloat16)
    grad_up = token_product(ffn_flat, d_up_low)
    grad_down = token_product(ffn_sub, grad_flat)
    partial_in = rows_product(d_up_low, up_part).reshape(row_count, length, model_width)
    d_ffn_in = (
        lax.psum_scatter(partial_in.astype(jnp.bfloat16), "seq", scatter_dimension=1, tiled=True)
        .astype(jnp.float32)
        .reshape(tokens, model_width)
    )
    sum_up, sum_down = (
        lax.psum_scatter(
            grad_up.astype(jnp.bfloat16), "dp", scatter_dimension=1, tiled=True
        ).astype(jnp.float32),
        lax.psum_scatter(
            grad_down.astype(jnp.bfloat16), "dp", scatter_dimension=0, tiled=True
        ).astype(jnp.float32),
    )
    output = final.astype(jnp.bfloat16).reshape(row_count, local_count, model_width)
    grad_gain_three = jnp.sum(d_ffn_in * normed_three, axis=0)
    d_hmid = grad_top + norm_back(d_ffn_in * gain_three, normed_three, scaler_three)
    d_hmid_low = d_hmid.astype(jnp.bfloat16)
    grad_out = token_product(attn_sub, d_hmid_low)
    d_attn_sub = rows_product(d_hmid_low, full_out)
    grad_gain_two = jnp.sum(d_attn_sub * normed_two, axis=0)
    d_attended = norm_back(d_attn_sub * gain_two, normed_two, scaler_two).astype(jnp.bfloat16)
    grad_send = d_attended.reshape(row_count, local_count, groups, head_span)
    grad_heads = lax.all_to_all(grad_send, "seq", split_axis=2, concat_axis=1, tiled=True).reshape(
        row_count, length, heads_dev, HD
    )
    query_grad, key_grad, value_grad = lax.map(
        lambda inputs: attend_back_row(
            inputs[0], inputs[1], inputs[2], inputs[3], inputs[4], inputs[5], block_rows
        ),
        (head_queries, head_keys, head_values, seg_rows, grad_heads, log_total),
    )
    grad_stack = (
        jnp.stack([query_grad, key_grad, value_grad], axis=2)
        .astype(jnp.bfloat16)
        .reshape(row_count, length, 3, 1, head_span)
    )
    grad_tok = (
        lax.all_to_all(grad_stack, "seq", split_axis=1, concat_axis=3, tiled=True)
        .reshape(tokens, 3, model_width)
        .astype(jnp.float32)
    )
    d_query_raw = unrotate(grad_tok[:, 0], cosine, sine_table, factor) * scale
    d_key_raw = unrotate(grad_tok[:, 1], cosine, sine_table, 1.0 / factor)
    d_qkv = jnp.concatenate([d_query_raw, d_key_raw, grad_tok[:, 2]], axis=1).astype(jnp.bfloat16)
    grad_qkv = token_product(attn_in, d_qkv)
    d_attn_in = rows_product(d_qkv, full_qkv)
    grad_gain_one = jnp.sum(d_attn_in * normed_one, axis=0)
    d_input = d_hmid + norm_back(d_attn_in * gain_one, normed_one, scaler_one)
    input_grad = d_input.astype(jnp.bfloat16).reshape(row_count, local_count, model_width)
    sum_qkv, sum_out, sum_gain_one, sum_gain_two, sum_gain_three, sum_gain_four = (
        lax.psum_scatter(grad_qkv, ("dp", "seq"), scatter_dimension=0, tiled=True),
        lax.psum_scatter(grad_out, ("dp", "seq"), scatter_dimension=0, tiled=True),
        lax.psum_scatter(grad_gain_one, ("dp", "seq"), scatter_dimension=0, tiled=True),
        lax.psum_scatter(grad_gain_two, ("dp", "seq"), scatter_dimension=0, tiled=True),
        lax.psum_scatter(grad_gain_three, ("dp", "seq"), scatter_dimension=0, tiled=True),
        lax.psum_scatter(grad_gain_four, ("dp", "seq"), scatter_dimension=0, tiled=True),
    )

    def averaged(average, weight):
        return EMA_DECAY * average + (1.0 - EMA_DECAY) * weight.astype(jnp.float32)

    return (
        output,
        input_grad,
        sum_qkv,
        sum_out,
        sum_up,
        sum_down,
        sum_gain_one,
        sum_gain_two,
        sum_gain_three,
        sum_gain_four,
        averaged(ema_qkv, w_qkv),
        averaged(ema_out, w_out),
        averaged(ema_up, w_up),
        averaged(ema_down, w_down),
        averaged(ema_gain_attn, gain_attn),
        averaged(ema_gain_attn_sub, gain_attn_sub),
        averaged(ema_gain_ffn, gain_ffn),
        averaged(ema_gain_ffn_sub, gain_ffn_sub),
    )


def solution(mesh):
    placed = (
        P("dp", "seq", None),
        P("dp", "seq"),
        P("dp", "seq"),
        P(("dp", "seq"), None),
        P(("dp", "seq"), None),
        P(None, ("dp", "seq")),
        P(("dp", "seq"), None),
        P(("dp", "seq")),
        P(("dp", "seq")),
        P(("dp", "seq")),
        P(("dp", "seq")),
        P(("dp", "seq"), None),
        P(("dp", "seq"), None),
        P(None, ("dp", "seq")),
        P(("dp", "seq"), None),
        P(("dp", "seq")),
        P(("dp", "seq")),
        P(("dp", "seq")),
        P(("dp", "seq")),
        P("dp", "seq", None),
    )
    return jax.shard_map(
        body,
        mesh=mesh,
        in_specs=placed,
        out_specs=(
            P("dp", "seq", None),
            P("dp", "seq", None),
            P(("dp", "seq"), None),
            P(("dp", "seq"), None),
            P(None, ("dp", "seq")),
            P(("dp", "seq"), None),
            P(("dp", "seq")),
            P(("dp", "seq")),
            P(("dp", "seq")),
            P(("dp", "seq")),
            P(("dp", "seq"), None),
            P(("dp", "seq"), None),
            P(None, ("dp", "seq")),
            P(("dp", "seq"), None),
            P(("dp", "seq")),
            P(("dp", "seq")),
            P(("dp", "seq")),
            P(("dp", "seq")),
        ),
        check_vma=False,
    )
```

profile of v0, /device:TPU:9, one launch (start us, length us, event | category | flops | bytes accessed | tf_op | source)
XLA Modules:
  0.0 1446.1 jit_solution(10931215322774067301)
XLA Ops:
  16.9 41.6 %all-reduce.8 = (bf16[2048]{0:T(1024)(128)(2,1)S(1)}, bf16[2048]{0:T(1024)(128)(2,1)S(1)}, bf16[2048]{0:T(1024)(128)(2,1)S(1)}) all-reduce(bf16[2048]{0:T(1024)(128)(2,1)S(1)} %dynamic-update-slice, bf16[2048]{0:T(1024)(128)(2,1)S(1)} %dynamic-update-slice.1, ...), channel_id=1, replica_groups=mesh['dp'=4,'seq'=8] {'dp','seq'}, use_global_device_ids=true, to_apply=%add | all-reduce | flops 6144 | bytes 24576
  64.3 102.3 %all-gather.9.cloned.1.call-done = bf16[2048,6144]{1,0:T(8,128)(2,1)} async-done(((bf16[64,6144]{1,0:T(8,128)(2,1)}), bf16[2048,6144]{1,0:T(8,128)(2,1)}) %all-gather.9.cloned.1.call-update) | async-done | bytes 25165840 | tf_op jit(solution)/shard_map/all_gather | solution.py:182
  166.6 10.1 fusion.140
  208.5 24.5 %all-to-all-done.1 = bf16[1,128,3,8,256]{4,1,2,0,3:T(8,128)(2,1)S(1)} async-done(((bf16[1,128,3,8,256]{4,1,2,0,3:T(8,128)(2,1)}), bf16[1,128,3,8,256]{4,1,2,0,3:T(8,128)(2,1)S(1)}, u32[]{:S(2)}, u32[]{:S(2)}) %all-to-all-start.1) | async-done | bytes 1572896 | tf_op jit(solution)/shard_map/all_to_all | solution.py:209
  236.6 15.9 %while.47 = (s32[]{:T(128)}, bf16[2,512,4,64]{1,3,2,0:T(8,128)(2,1)S(1)}, f32[2,4,512,1]{2,1,3,0:T(4,128)S(1)}, s32[2]{0:T(128)S(1)}, s32[1024]{0:T(1024)S(1)}, ...) while((s32[]{:T(128)}, ...), condition=%wide.region_5.6_spmd, body=%wide.region_2.5_spmd.sunk | while | flops 557316608 | bytes 29177988 | solution.py:103
  265.0 7.9 all-to-all-start.2
  291.0 39.2 %all-gather.1 = bf16[32,1,256]{2,1,0:T(2,128)(2,1)S(1)} all-gather(bf16[1,1,256]{2,1,0:T(2,128)(2,1)S(1)} %reshape.631), channel_id=1, replica_groups=mesh['dp'=4,'seq'=8] {'dp','seq'}, dimensions={0}, use_global_device_ids=true | all-gather | bytes 16896 | tf_op jit(solution)/shard_map/all_gather | solution.py:187
  333.6 40.5 %all-gather.19.cloned.1.call-done = bf16[1024,2048]{1,0:T(8,128)(2,1)} async-done(((bf16[128,2048]{1,0:T(8,128)(2,1)}), bf16[1024,2048]{1,0:T(8,128)(2,1)}) %all-gather.19.cloned.1.call-update) | async-done | bytes 4194320 | tf_op jit(solution)/shard_map/all_gather | solution.py:238
  374.1 19.0 %fusion.142 = (bf16[1024]{0:T(1024)(128)(2,1)S(1)}, bf16[1024]{0:T(1024)(128)(2,1)S(1)}, f32[1024,1024]{0,1:T(8,128)}, f32[1024,1024]{0,1:T(8,128)}, f32[1024,1024]{0,1:T(8,128)}) fusion(bf16[1024,2048]{1,0:T(8,128)(2,1)} %all-gather.19.cloned.1.call-done, bf16[2048,1024]{1,0:T(8,128)(2,1)} %all-gather.13.cloned.1.call-done), kind=kOutput, calls=%fused_computation.215 | convolution fusion | flops 4365219840 | bytes 20975616 | tf_op jit(solution)/shard_map/dot_general | solution.py:252
  393.1 12.0 all-reduce.10
  405.1 48.3 %all-gather.15.cloned.1.call-done = bf16[1024,2048]{1,0:T(8,128)(2,1)} async-done(((bf16[256,2048]{1,0:T(8,128)(2,1)}), bf16[1024,2048]{1,0:T(8,128)(2,1)}) %all-gather.15.cloned.1.call-update) | async-done | bytes 4194320 | tf_op jit(solution)/shard_map/all_gather | solution.py:247
  453.4 40.0 %all-gather.17.cloned.1.call-done = bf16[1,1024,2048]{2,1,0:T(8,128)(2,1)} async-done(((bf16[1,128,2048]{2,1,0:T(8,128)(2,1)}), bf16[1,1024,2048]{2,1,0:T(8,128)(2,1)}) %all-gather.17.cloned.1.call-update) | async-done | bytes 4194320 | tf_op jit(solution)/shard_map/all_gather | solution.py:241
  493.3 12.0 multiply_reduce_fusion.1
  505.4 11.4 all-reduce.9
  516.8 7.5 add_convert_fusion
  532.0 10.2 convert_bitcast_fusion.1
  542.3 10.8 fusion.90
  553.6 9.6 convolution_convert_fusion
  563.2 21.3 %reduce-scatter.9.cloned.1.call-done = bf16[1,128,2048]{2,1,0:T(8,128)(2,1)} async-done(((bf16[1,1024,2048]{2,1,0:T(8,128)(2,1)}), bf16[1,128,2048]{2,1,0:T(8,128)(2,1)}) %reduce-scatter.9.cloned.1.call-update) | async-done | bytes 524304 | tf_op jit(solution)/shard_map/reduce_scatter | solution.py:294
  586.6 53.0 %reduce-scatter.7.cloned.1.call-done = bf16[1,128,2048]{2,1,0:T(8,128)(2,1)} async-done(((bf16[1,1024,2048]{2,1,0:T(8,128)(2,1)}), bf16[1,128,2048]{2,1,0:T(8,128)(2,1)}) %reduce-scatter.7.cloned.1.call-update) | async-done | bytes 524304 | tf_op jit(solution)/shard_map/reduce_scatter | solution.py:275
  643.1 8.8 fusion.129
  676.7 108.0 %while.48 = (s32[]{:T(128)}, f32[1024,4,64]{0,2,1:T(8,128)}, f32[1024,4,64]{0,2,1:T(8,128)S(1)}, bf16[2,512,4,64]{1,3,2,0:T(8,128)(2,1)}, bf16[2,512,4,64]{1,3,2...) while((s32[]{:T(128)}, f32[1024,4,64]{0,2,1:T(8,128)}, ...), condition=%wide.region_27.28_spmd.clone, body=%wide.region_25.27_spmd.clone.sunk | while | flops 1388845568 | bytes 104931016 | solution.py:144
  687.5 19.2 %fusion.204 = f32[1024,4,64]{0,2,1:T(8,128)} fusion(f32[4,512,1024]{2,1,0:T(8,128)} %fusion.201, f32[4,512,1024]{2,1,0:T(8,128)} %fusion.202, f32[4,512]{1,0:T(4,128)S(1)} %dynamic-slice_bitcast_fusion.2, pred[512,1024]{1,0:T(8,128)(4,1)S(1)} %fusion.203, f32[1024,4,64]{0,2,1:T(8,128)} %get-tuple-element.609, pred[]{:T(512)S(6)} %compare.4, ...), kind=kOutput, calls=%fused_computation.41.clone.1 | convolution fusion | flops 287837184 | bytes 36979200 | tf_op jit(solution)/shard_map/while/body/eval_jaxpr/while/body/eval_jaxpr/hqk,qhd->khd/dot_general | solution.py:132
  706.7 18.0 %fusion.206 = bf16[2,512,4,64]{1,3,2,0:T(8,128)(2,1)} fusion(bf16[2,512,4,64]{1,3,2,0:T(8,128)(2,1)} %get-tuple-element.611, s32[]{:T(128)} %get-tuple-element.608, bf16[1024,4,64]{0,2,1:T(8,128)(2,1)S(1)} %get-tuple-element.630, f32[4,512,1024]{2,1,0:T(8,128)} %fusion.201, f32[4,512,1024]{2,1,0:T(8,128)} %fusion.202, ...), kind=kOutput, calls=%fused_computation.44.clone.1 | convolution fusion | flops 287312896 | bytes 35668480 | tf_op jit(solution)/shard_map/while/body/eval_jaxpr/while/body/eval_jaxpr/hqk,khd->qhd/dot_general | solution.py:129
  741.2 19.4 %fusion.204 = f32[1024,4,64]{0,2,1:T(8,128)} fusion(f32[4,512,1024]{2,1,0:T(8,128)} %fusion.201, f32[4,512,1024]{2,1,0:T(8,128)} %fusion.202, f32[4,512]{1,0:T(4,128)S(1)} %dynamic-slice_bitcast_fusion.2, pred[512,1024]{1,0:T(8,128)(4,1)S(1)} %fusion.203, f32[1024,4,64]{0,2,1:T(8,128)} %get-tuple-element.609, pred[]{:T(512)S(6)} %compare.4, ...), kind=kOutput, calls=%fused_computation.41.clone.1 | convolution fusion | flops 287837184 | bytes 36979200 | tf_op jit(solution)/shard_map/while/body/eval_jaxpr/while/body/eval_jaxpr/hqk,qhd->khd/dot_general | solution.py:132
  760.6 18.1 %fusion.206 = bf16[2,512,4,64]{1,3,2,0:T(8,128)(2,1)} fusion(bf16[2,512,4,64]{1,3,2,0:T(8,128)(2,1)} %get-tuple-element.611, s32[]{:T(128)} %get-tuple-element.608, bf16[1024,4,64]{0,2,1:T(8,128)(2,1)S(1)} %get-tuple-element.630, f32[4,512,1024]{2,1,0:T(8,128)} %fusion.201, f32[4,512,1024]{2,1,0:T(8,128)} %fusion.202, ...), kind=kOutput, calls=%fused_computation.44.clone.1 | convolution fusion | flops 287312896 | bytes 35668480 | tf_op jit(solution)/shard_map/while/body/eval_jaxpr/while/body/eval_jaxpr/hqk,khd->qhd/dot_general | solution.py:129
  792.3 48.7 %all_to_all.60 = bf16[1,1024,3,1,256]{4,2,3,0,1:T(4,128)(2,1)S(1)} all-to-all(bf16[1,1024,3,1,256]{4,2,3,0,1:T(4,128)(2,1)S(1)} %copy.207), channel_id=1, replica_groups=mesh['dp'=4,'seq'=8] {'seq'}, dimensions={1} | all-to-all | bytes 3145728 | tf_op jit(solution)/shard_map/all_to_all | solution.py:330
  880.2 20.2 %fusion.125 = f32[2048,6144]{1,0:T(8,128)} fusion(bf16[128,2048]{1,0:T(8,128)(2,1)S(1)} %copy-done.24, bf16[128,2048]{1,0:T(8,128)(2,1)S(1)} %get-tuple-element.404, bf16[128,2048]{1,0:T(8,128)(2,1)S(1)} %get-tuple-element.403, bf16[1,128,2048]{2,1,0:T(8,128)(2,1)S(1)} %copy-done.1, f32[2048]{0:T(1024)S(1)} %copy-done.32, f32[128]{0:T(128)S(1)} %copy-done.38, ...), kind=kOutput, calls=%fused_computation.160 | convolution fusion | flops 3227254784 | bytes 52438016 | tf_op jit(solution)/shard_map/dot_general | solution.py:69
  911.4 14.0 fusion.110
  925.4 45.0 %all-reduce.7 = (f32[2048]{0:T(1024)S(1)}, f32[2048]{0:T(1024)S(1)}, f32[2048]{0:T(1024)S(1)}, f32[8192]{0:T(1024)S(1)}) all-reduce(f32[2048]{0:T(1024)S(1)} %get-tuple-element.339, f32[2048]{0:T(1024)S(1)} %copy-done.36, f32[2048]{0:T(1024)S(1)} %copy-done.35, ...), channel_id=9, replica_groups=mesh['dp'=4,'seq'=8] {'dp','seq'}, use_global_device_ids=true, to_apply=%region_35.36.clone | all-reduce | flops 14336 | bytes 114688
  979.6 20.3 %reduce-scatter.13.cloned.1.call-done = f32[64,2048]{1,0:T(8,128)} async-done(((f32[2048,2048]{1,0:T(8,128)}), f32[64,2048]{1,0:T(8,128)}) %reduce-scatter.13.cloned.1.call-update) | async-done | bytes 524304 | tf_op jit(solution)/shard_map/reduce_scatter | solution.py:344
  1000.0 438.8 %reduce-scatter.11.cloned.1.call-done = f32[64,6144]{1,0:T(8,128)} async-done(((f32[2048,6144]{1,0:T(8,128)}), f32[64,6144]{1,0:T(8,128)}) %reduce-scatter.11.cloned.1.call-update) | async-done | bytes 1572880 | tf_op jit(solution)/shard_map/reduce_scatter | solution.py:343
  (306 shorter events, 238.4 us)
Async XLA Ops:
  7.2 55.1 %copy-start.48 = (s32[1,128]{1,0:T(1,128)S(1)}, s32[1,128]{1,0:T(1,128)}, u32[]{:S(2)}) copy-start(s32[1,128]{1,0:T(1,128)} %param.26) | copy-start | bytes 1540
  7.2 159.4 %all-gather.9.cloned.1.call-start = ((), (), s32[]{:S(2)}) async-start(), calls=%async_computation.11 | async-start | bytes 25952256 | tf_op jit(solution)/shard_map/all_gather | solution.py:182
  7.9 275.7 %all-gather.11.cloned.1.call-start = ((), (), s32[]{:S(2)}) async-start(), calls=%async_computation.12 | async-start | bytes 8650752 | tf_op jit(solution)/shard_map/all_gather | solution.py:183
  9.9 194.1 %all-to-all-start = ((bf16[1,128,1,8,1]{1,4,2,0,3:T(2,128)(2,1)}), bf16[1,128,1,8,1]{1,4,2,0,3:T(2,128)(2,1)S(1)}, u32[]{:S(2)}, u32[]{:S(2)}) async-start(bf16[1,128,1,8,1]{1,4,2,0,3:T(2,128)(2,1)} %broadcast_in_dim.81), calls=%async_computation | async-start | bytes 8192 | tf_op jit(solution)/shard_map/all_to_all | solution.py:210
  58.5 108.2 %copy-start.31 = (f32[2048]{0:T(1024)}, f32[2048]{0:T(1024)S(1)}, u32[]{:S(2)}) copy-start(f32[2048]{0:T(1024)S(1)} %convert_element_type.258) | copy-start | bytes 24580
  62.5 114.2 %copy-start.14 = (f32[128,32,64]{0,2,1:T(8,128)}, f32[128,32,64]{0,2,1:T(8,128)S(1)}, u32[]{:S(2)}) copy-start(f32[128,32,64]{0,2,1:T(8,128)S(1)} %tile.39) | copy-start | bytes 3145732
  64.0 112.8 %copy-start.33 = (f32[128]{0:T(128)}, f32[128]{0:T(128)S(1)}, u32[]{:S(2)}) copy-start(f32[128]{0:T(128)S(1)} %broadcast_multiply_fusion.10) | copy-start | bytes 1540
  64.3 112.5 %copy-start.37 = (f32[128]{0:T(128)}, f32[128]{0:T(128)S(1)}, u32[]{:S(2)}) copy-start(f32[128]{0:T(128)S(1)} %add_rsqrt_fusion.3) | copy-start | bytes 1540
  184.2 14.0 copy-start.17
  204.1 28.9 %all-to-all-start.1 = ((bf16[1,128,3,8,256]{4,1,2,0,3:T(8,128)(2,1)}), bf16[1,128,3,8,256]{4,1,2,0,3:T(8,128)(2,1)S(1)}, u32[]{:S(2)}, u32[]{:S(2)}) async-start(bf16[1,128,3,8,256]{4,1,2,0,3:T(8,128)(2,1)} %pad_maximum_fusion), calls=%async_computation.1 | async-start | bytes 3145728 | tf_op jit(solution)/shard_map/all_to_all | solution.py:209
  207.7 125.9 %all-gather.13.cloned.1.call-start = ((), (), s32[]{:S(2)}) async-start(), calls=%async_computation.13 | async-start | bytes 5242880 | tf_op jit(solution)/shard_map/all_gather | solution.py:246
  252.5 29.0 %copy-start.3 = (bf16[2,512,4,64]{1,3,2,0:T(8,128)(2,1)}, bf16[2,512,4,64]{1,3,2,0:T(8,128)(2,1)S(1)}, u32[]{:S(2)}) copy-start(bf16[2,512,4,64]{1,3,2,0:T(8,128)(2,1)S(1)} %get-tuple-element.655) | copy-start | bytes 1572868
  252.5 29.0 %copy-start.5 = (bf16[1024,4,64]{0,2,1:T(8,128)(2,1)}, bf16[1024,4,64]{0,2,1:T(8,128)(2,1)S(1)}, u32[]{:S(2)}) copy-start(bf16[1024,4,64]{0,2,1:T(8,128)(2,1)S(1)} %get-tuple-element.656) | copy-start | bytes 1572868
  265.0 14.7 %all-to-all-start.2 = ((bf16[8,2,16384]{2,1,0:T(2,128)(2,1)}), bf16[8,2,16384]{2,1,0:T(2,128)(2,1)S(1)}, u32[]{:S(2)}, u32[]{:S(2)}) async-start(bf16[8,2,16384]{2,1,0:T(2,128)(2,1)} %reshape.638), calls=%async_computation.2 | async-start | bytes 1048576 | tf_op jit(solution)/shard_map/all_to_all | solution.py:222
  272.9 101.2 %all-gather.19.cloned.1.call-start = ((), (), s32[]{:S(2)}) async-start(), calls=%async_computation.22 | async-start | bytes 4718592 | tf_op jit(solution)/shard_map/all_gather | solution.py:238
  289.8 163.6 %all-gather.15.cloned.1.call-start = ((), (), s32[]{:S(2)}) async-start(), calls=%async_computation.14 | async-start | bytes 5242880 | tf_op jit(solution)/shard_map/all_gather | solution.py:247
  290.4 203.0 %all-gather.17.cloned.1.call-start = ((), (), s32[]{:S(2)}) async-start(), calls=%async_computation.16 | async-start | bytes 4718592 | tf_op jit(solution)/shard_map/all_gather | solution.py:241
  290.9 293.6 %reduce-scatter.9.cloned.1.call-start = ((), (), s32[]{:S(2)}) async-start(), calls=%async_computation.17 | async-start | bytes 4718592 | tf_op jit(solution)/shard_map/reduce_scatter | solution.py:294
  531.8 107.8 %reduce-scatter.7.cloned.1.call-start = ((), (), s32[]{:S(2)}) async-start(), calls=%async_computation.15 | async-start | bytes 4718592 | tf_op jit(solution)/shard_map/reduce_scatter | solution.py:275
  542.2 431.9 %reduce-scatter.17.cloned.1.call-start = ((), (), s32[]{:S(2)}) async-start(), calls=%async_computation.21 | async-start | bytes 5242880 | tf_op jit(solution)/shard_map/reduce_scatter | solution.py:302
  553.1 423.8 %reduce-scatter.15.cloned.1.call-start = ((), (), s32[]{:S(2)}) async-start(), calls=%async_computation.20 | async-start | bytes 5242880 | tf_op jit(solution)/shard_map/reduce_scatter | solution.py:299
  563.2 76.4 %copy-start.28 = (bf16[1,128,2048]{2,1,0:T(8,128)(2,1)S(1)}, bf16[1,128,2048]{2,1,0:T(8,128)(2,1)}, u32[]{:S(2)}) copy-start(bf16[1,128,2048]{2,1,0:T(8,128)(2,1)} %param.43) | copy-start | bytes 1572868
  563.2 436.8 %reduce-scatter.13.cloned.1.call-start = ((), (), s32[]{:S(2)}) async-start(), calls=%async_computation.19 | async-start | bytes 17301504 | tf_op jit(solution)/shard_map/reduce_scatter | solution.py:344
  660.2 16.4 %copy-start.4 = (bf16[2,512,4,64]{1,3,2,0:T(8,128)(2,1)S(1)}, bf16[2,512,4,64]{1,3,2,0:T(8,128)(2,1)}, u32[]{:S(2)}) copy-start(bf16[2,512,4,64]{1,3,2,0:T(8,128)(2,1)} %copy-done.3) | copy-start | bytes 1572868
  660.2 16.4 %copy-start.6 = (bf16[1024,4,64]{0,2,1:T(8,128)(2,1)S(1)}, bf16[1024,4,64]{0,2,1:T(8,128)(2,1)}, u32[]{:S(2)}) copy-start(bf16[1024,4,64]{0,2,1:T(8,128)(2,1)} %copy-done.5) | copy-start | bytes 1572868
  661.7 10.9 all-to-all-start.3
  665.8 773.0 %reduce-scatter.11.cloned.1.call-start = ((), (), s32[]{:S(2)}) async-start(), calls=%async_computation.18 | async-start | bytes 51904512 | tf_op jit(solution)/shard_map/reduce_scatter | solution.py:343
  880.2 20.3 %copy-start.21 = (bf16[128,2048]{1,0:T(8,128)(2,1)}, bf16[128,2048]{1,0:T(8,128)(2,1)S(1)}, u32[]{:S(2)}) copy-start(bf16[128,2048]{1,0:T(8,128)(2,1)S(1)} %get-tuple-element.403) | copy-start | bytes 1572868
  880.2 20.2 %copy-start.23 = (bf16[128,2048]{1,0:T(8,128)(2,1)}, bf16[128,2048]{1,0:T(8,128)(2,1)S(1)}, u32[]{:S(2)}) copy-start(bf16[128,2048]{1,0:T(8,128)(2,1)S(1)} %get-tuple-element.404) | copy-start | bytes 1572868
  911.4 14.1 copy-start.35
  911.4 14.1 copy-start.36
  911.4 61.5 %copy-start.10 = (f32[128,2048]{1,0:T(8,128)S(1)}, f32[128,2048]{1,0:T(8,128)}, u32[]{:S(2)}) copy-start(f32[128,2048]{1,0:T(8,128)} %copy-done.8) | copy-start | bytes 3145732
  (36 other events, 137.9 us)
Sparse Core Ops, SparseCore 0:
  10.9 155.6 all-gather.8
  169.5 86.3 all-gather.10
  257.5 76.0 all-gather.12
  335.9 38.1 all-gather.18
  375.5 77.8 all-gather.14
  455.1 38.1 all-gather.16
  531.9 52.5 reduce-scatter.8
  588.2 51.3 reduce-scatter.6
  641.9 76.7 reduce-scatter.16
  721.0 77.3 reduce-scatter.14
  801.2 198.7 reduce-scatter.12
  1006.8 431.9 reduce-scatter.10
where the time goes:
time: 1460 us; the launch traced here: 1450 us
  waiting for transfers between devices  808 us (55%)
  matrix products  245 us (17%)
  blocking collectives  198 us (14%)
  local copies, waits for them, and re-layouts  91.9 us (6%)
  other arithmetic  65.2 us (4%)
  starting transfers between devices  21.8 us (1%)
  between operations  15.5 us (1%)
    reduce_scatter x1, waiting for transfers between devices, body(): lax.psum_scatter(grad_qkv, ('dp', 'seq'), scatter_dimension=0, tiled=True)  439 us
    all_gather x1, waiting for transfers between devices, body(): lax.all_gather(w_qkv, ('dp', 'seq'), axis=0, tiled=True)  102 us
    unnamed x2, blocking collectives  86.6 us
    reduce_scatter x1, waiting for transfers between devices, body(): lax.psum_scatter(partial_out.astype(jnp.bfloat16), 'seq', scatter_dimensi...  53 us
    dot_general x4, matrix products, token_product(): lax.dot_general(left_op, right_op, (((0,), (0,)), ((), ())), preferred_el...  49.4 us
    all_to_all x1, blocking collectives, body(): lax.all_to_all(grad_stack, 'seq', split_axis=1, concat_axis=3, tiled=True)  48.7 us
    all_gather x1, waiting for transfers between devices, body(): lax.all_gather(w_down, 'dp', axis=0, tiled=True)  48.3 us
    all_gather x1, waiting for transfers between devices, body(): lax.all_gather(ffn_in.reshape(row_count, local_count, model_width), 'seq'...  40.5 us
  transfers between devices with their start and end apart: 16, of which 12 were waited for; matrix products, arithmetic and copies ran while one was open for 26% of the time, Pallas kernels for 0%

commit v1 on v0

v1 whole, which is shorter than its diff:
```python
import math

import jax
import jax.numpy as jnp
from jax import lax
from jax.sharding import Mesh
from jax.sharding import PartitionSpec as P

HEADS = 32
HD = 64

NEG_FILL = -1000000000.0
NORM_EPS = 1e-05
EMA_DECAY = 0.7
LOW = jnp.bfloat16
F32 = jnp.float32
SEQ = ("chip", "core")
TP = ("dp", "core")
ALL = ("dp", "chip", "core")


def moments(values):
    mean = jnp.mean(values, axis=-1, keepdims=True)
    centered = values - mean
    scaler = lax.rsqrt(jnp.mean(centered * centered, axis=-1, keepdims=True) + NORM_EPS)
    return (centered * scaler, scaler)


def norm_back(scaled_grad, normed, scaler):
    first_mean = jnp.mean(scaled_grad, axis=-1, keepdims=True)
    second_mean = jnp.mean(scaled_grad * normed, axis=-1, keepdims=True)
    return scaler * (scaled_grad - first_mean - normed * second_mean)


def exact_gelu(values):
    return jax.nn.gelu(values, approximate=False)


def swap_pairs(values):
    dims_of = values.shape
    return values.reshape(dims_of[:-1] + (dims_of[-1] // 2, 2))[..., ::-1].reshape(dims_of)


def rotate(values, cosine, sine_table, factor):
    return (values * cosine + swap_pairs(values) * sine_table) * factor


def unrotate(grads, cosine, sine_table, factor):
    scaled = grads * factor
    return scaled * cosine + swap_pairs(scaled * sine_table)


def xpos_tables(positions, heads):
    half_count = HD // 2
    index_half = jnp.arange(half_count).astype(F32)
    inverse = jnp.exp(-(2.0 * index_half / HD) * math.log(10000.0))
    decay_base = (2.0 * index_half + 0.4 * HD) / (1.4 * HD)
    where_at = positions.astype(F32)[:, None]
    angles = where_at * inverse[None, :]
    factor = jnp.exp(where_at / 512.0 * jnp.log(decay_base)[None, :])
    sign_row = jnp.where(jnp.arange(HD) % 2 == 0, -1.0, 1.0).astype(F32)
    cosine = jnp.tile(jnp.repeat(jnp.cos(angles), 2, axis=1), (1, heads))
    sine_table = jnp.tile(jnp.repeat(jnp.sin(angles), 2, axis=1) * sign_row[None, :], (1, heads))
    factor_table = jnp.tile(jnp.repeat(factor, 2, axis=1), (1, heads))
    return (cosine, sine_table, factor_table)


def dot(left_op, right_op):
    return jnp.dot(left_op, right_op, preferred_element_type=F32)


def rows_product(operand, weight_rows):
    return lax.dot_general(
        operand, weight_rows, (((1,), (1,)), ((), ())), preferred_element_type=F32
    )


def token_product(left_op, right_op):
    return lax.dot_general(left_op, right_op, (((0,), (0,)), ((), ())), preferred_element_type=F32)


def block_allowed(seg_block, offset, seg_row, block_rows):
    query_pos = offset + jnp.arange(block_rows)
    key_pos = jnp.arange(seg_row.shape[0])
    return ((key_pos[None, :] <= query_pos[:, None]) & (seg_row[None, :] == seg_block[:, None]))[
        None
    ]


def attend_row(query_row, key_row, value_row, seg_row, block_rows):
    length = query_row.shape[0]
    block_count = length // block_rows
    query_blocks = query_row.reshape((block_count, block_rows) + query_row.shape[1:])
    seg_blocks = seg_row.reshape(block_count, block_rows)
    offsets = jnp.arange(block_count) * block_rows

    def one_block(inputs):
        query_block, seg_block, offset = inputs
        allowed = block_allowed(seg_block, offset, seg_row, block_rows)
        scores = jnp.einsum(
            "qhd,khd->hqk", query_block, key_row, preferred_element_type=jnp.float32
        )
        scores = jnp.where(allowed, scores, NEG_FILL)
        top_score = jnp.max(scores, axis=-1, keepdims=True)
        shifted = jnp.exp(scores - top_score)
        total = jnp.sum(shifted, axis=-1, keepdims=True)
        probs = (shifted / total).astype(jnp.bfloat16)
        attended = jnp.einsum("hqk,khd->qhd", probs, value_row, preferred_element_type=jnp.float32)
        return (attended, top_score + jnp.log(total))

    attended, log_total = lax.map(one_block, (query_blocks, seg_blocks, offsets))
    return (attended.reshape(query_row.shape), log_total)


def attend_back_row(query_row, key_row, value_row, seg_row, grad_row, log_total, block_rows):
    length = query_row.shape[0]
    block_count = length // block_rows
    query_blocks = query_row.reshape((block_count, block_rows) + query_row.shape[1:])
    grad_blocks = grad_row.reshape((block_count, block_rows) + grad_row.shape[1:])
    seg_blocks = seg_row.reshape(block_count, block_rows)
    offsets = jnp.arange(block_count) * block_rows

    def one_block(totals, inputs):
        key_total, value_total = totals
        query_block, grad_block, seg_block, offset, block_total = inputs
        allowed = block_allowed(seg_block, offset, seg_row, block_rows)
        scores = jnp.einsum(
            "qhd,khd->hqk", query_block, key_row, preferred_element_type=jnp.float32
        )
        scores = jnp.where(allowed, scores, NEG_FILL)
        probs = jnp.exp(scores - block_total)
        grad_probs = jnp.einsum(
            "qhd,khd->hqk", grad_block, value_row, preferred_element_type=jnp.float32
        )
        delta = jnp.sum(probs * grad_probs, axis=-1, keepdims=True)
        grad_scores = jnp.where(allowed, probs * (grad_probs - delta), 0.0).astype(jnp.bfloat16)
        grad_query = jnp.einsum(
            "hqk,khd->qhd", grad_scores, key_row, preferred_element_type=jnp.float32
        )
        key_total = key_total + jnp.einsum(
            "hqk,qhd->khd", grad_scores, query_block, preferred_element_type=jnp.float32
        )
        value_total = value_total + jnp.einsum(
            "hqk,qhd->khd",
            probs.astype(jnp.bfloat16),
            grad_block,
            preferred_element_type=jnp.float32,
        )
        return ((key_total, value_total), grad_query)

    zeros = jnp.zeros(key_row.shape, jnp.float32)
    (key_grad, value_grad), query_grad = lax.scan(
        one_block, (zeros, zeros), (query_blocks, grad_blocks, seg_blocks, offsets, log_total)
    )
    return (query_grad.reshape(query_row.shape), key_grad, value_grad)


def body(
    hidden_in,
    segment_ids,
    position_ids,
    w_qkv,
    w_out,
    w_up,
    w_down,
    gain_attn,
    gain_attn_sub,
    gain_ffn,
    gain_ffn_sub,
    ema_qkv,
    ema_out,
    ema_up,
    ema_down,
    ema_gain_attn,
    ema_gain_attn_sub,
    ema_gain_ffn,
    ema_gain_ffn_sub,
    out_grad,
):
    _, tokens, width = hidden_in.shape
    planes, chips = lax.axis_size("dp"), lax.axis_size("chip")
    seqs = 2 * chips
    length = tokens * seqs
    heads = HEADS // seqs
    span = heads * HD
    part = w_qkv.shape[0]
    strided = part % HD == 0
    group_tokens = planes * 2 * tokens
    width_ff = w_down.shape[0] * planes * seqs
    block_rows = min(512, length)
    scale = HD ** (-0.5)
    seq_index = lax.axis_index(SEQ)

    def gain_rows(weight, gain):
        return (weight.astype(F32) * gain.astype(F32)[:, None]).astype(LOW)

    qkv_scaled = gain_rows(w_qkv, gain_attn)
    out_scaled = gain_rows(w_out, gain_attn_sub)
    down_scaled = gain_rows(w_down, gain_ffn_sub)
    if strided:
        qkv_send = qkv_scaled.reshape(part, 3, planes, seqs, HD).transpose(3, 0, 1, 2, 4)
    else:
        qkv_send = qkv_scaled.reshape(part, 3, seqs, span).transpose(2, 0, 1, 3)
    qkv_send = qkv_send.reshape(seqs, part, 3 * span)
    qkv_plane = lax.all_to_all(qkv_send, SEQ, split_axis=0, concat_axis=0, tiled=True)
    qkv_mine = lax.all_gather(
        qkv_plane.reshape(seqs * part, 3 * span), "dp", axis=0, tiled=True
    )
    if strided:
        out_mine = lax.all_gather(out_scaled, "dp", axis=0, tiled=True)
    else:
        out_all = lax.all_gather(out_scaled, ALL, axis=0, tiled=True)
        out_mine = lax.dynamic_slice_in_dim(out_all, seq_index * span, span, axis=0)
    gain_three = lax.all_gather(gain_ffn, ALL, axis=0, tiled=True).astype(F32)

    x_in = hidden_in[0].astype(F32)
    normed_one, scaler_one = moments(x_in)
    normed_low = normed_one.astype(LOW)
    row_in = lax.all_gather(normed_low, SEQ, axis=0, tiled=True)
    row_positions = lax.all_gather(position_ids[0], SEQ, axis=0, tiled=True)
    row_segments = lax.all_gather(segment_ids[0], SEQ, axis=0, tiled=True)
    cosine, sine_table, factor = xpos_tables(row_positions, heads)
    qkv_raw = dot(row_in, qkv_mine)
    queries = (rotate(qkv_raw[:, :span], cosine, sine_table, factor) * scale).astype(LOW)
    keys = rotate(qkv_raw[:, span : 2 * span], cosine, sine_table, 1.0 / factor).astype(LOW)
    values = qkv_raw[:, 2 * span :].astype(LOW)

    def by_head(whole):
        return whole.reshape(length, heads, HD)

    attended, log_total = attend_row(
        by_head(queries), by_head(keys), by_head(values), row_segments, block_rows
    )
    attended = attended.reshape(length, span).astype(LOW)
    attended_wide = attended.astype(F32)
    out_part = dot(attended, out_mine)
    column_part = jnp.sum(out_mine.astype(F32), axis=0)
    out_sum = lax.psum_scatter(
        out_part.astype(LOW), SEQ, scatter_dimension=0, tiled=True
    ).astype(F32)
    column_sum = lax.psum(column_part, SEQ)
    sums = lax.psum_scatter(
        jnp.stack([jnp.sum(attended_wide, axis=1), jnp.sum(attended_wide**2, axis=1)], axis=1),
        SEQ,
        scatter_dimension=0,
        tiled=True,
    )
    mean_two = sums[:, :1] / width
    scaler_two = lax.rsqrt(sums[:, 1:] / width - mean_two * mean_two + NORM_EPS)
    projected = scaler_two * (out_sum - mean_two * column_sum[None, :])
    hmid = x_in + projected
    normed_three, scaler_three = moments(hmid)
    ffn_in = (normed_three * gain_three).astype(LOW)

    grad_low = out_grad[0]
    grad_top = grad_low.astype(F32)
    up_mine = lax.all_gather(w_up, "chip", axis=1, tiled=True)
    down_mine = lax.all_gather(down_scaled, "chip", axis=0, tiled=True)
    grad_flat = lax.all_gather(grad_low, TP, axis=0, tiled=True)
    ffn_flat = lax.all_gather(ffn_in, TP, axis=0, tiled=True)
    weighted = rows_product(grad_flat, down_mine)
    up_slice = dot(ffn_flat, up_mine)
    activated, gelu_pull = jax.vjp(exact_gelu, up_slice)
    stats = lax.psum(
        jnp.stack(
            [
                jnp.sum(activated, axis=1),
                jnp.sum(activated * activated, axis=1),
                jnp.sum(weighted * activated, axis=1),
                jnp.sum(weighted, axis=1),
            ]
        ),
        TP,
    )[:, :, None]
    act_mean = stats[0] / width_ff
    scaler_four = lax.rsqrt(stats[1] / width_ff - act_mean * act_mean + NORM_EPS)
    normed_four = (activated - act_mean) * scaler_four
    normed_four_low = normed_four.astype(LOW)
    first_mean = stats[3] / width_ff
    second_mean = scaler_four * (stats[2] - act_mean * stats[3]) / width_ff
    d_act = scaler_four * (weighted - first_mean - normed_four * second_mean)
    (d_up,) = gelu_pull(d_act)
    d_up_low = d_up.astype(LOW)
    d_ffn_in = lax.psum_scatter(
        rows_product(d_up_low, up_mine).astype(LOW), TP, scatter_dimension=0, tiled=True
    ).astype(F32)
    ffn_out = lax.psum_scatter(
        dot(normed_four_low, down_mine).astype(LOW), TP, scatter_dimension=0, tiled=True
    ).astype(F32)
    grad_up = token_product(ffn_flat, d_up_low)
    grad_down = token_product(normed_four_low, grad_flat)
    sum_up = lax.psum_scatter(
        grad_up.astype(LOW), "chip", scatter_dimension=1, tiled=True
    ).astype(F32)
    sum_down = lax.psum_scatter(
        grad_down.astype(LOW), "chip", scatter_dimension=0, tiled=True
    ).astype(F32)
    output = (hmid + ffn_out).astype(LOW)[None]

    grad_gain_three = lax.psum_scatter(
        jnp.sum(d_ffn_in * normed_three, axis=0), ALL, scatter_dimension=0, tiled=True
    )
    d_hmid = grad_top + norm_back(d_ffn_in * gain_three, normed_three, scaler_three)
    d_hmid_low = d_hmid.astype(LOW)
    d_hmid_wide = d_hmid_low.astype(F32)
    first_two = jnp.sum(d_hmid_wide * column_sum[None, :], axis=1, keepdims=True) / width
    second_two = jnp.sum(d_hmid_wide * projected, axis=1, keepdims=True) / width
    row_grad = lax.all_gather(d_hmid_low, SEQ, axis=0, tiled=True)
    row_stats = lax.all_gather(
        jnp.concatenate([mean_two, scaler_two, first_two, second_two], axis=1),
        SEQ,
        axis=0,
        tiled=True,
    )
    mean_row, scaler_row, first_row, second_row = (row_stats[:, i : i + 1] for i in range(4))
    normed_two = (attended_wide - mean_row) * scaler_row
    d_sub = rows_product(row_grad, out_mine)
    d_attended = (scaler_row * (d_sub - first_row - normed_two * second_row)).astype(LOW)
    grad_out = token_product(normed_two.astype(LOW), row_grad)
    query_grad, key_grad, value_grad = attend_back_row(
        by_head(queries),
        by_head(keys),
        by_head(values),
        row_segments,
        by_head(d_attended),
        log_total,
        block_rows,
    )

    def flat(whole):
        return whole.reshape(length, span).astype(LOW).astype(F32)

    d_query_raw = unrotate(flat(query_grad), cosine, sine_table, factor) * scale
    d_key_raw = unrotate(flat(key_grad), cosine, sine_table, 1.0 / factor)
    d_qkv = jnp.concatenate([d_query_raw, d_key_raw, flat(value_grad)], axis=1).astype(LOW)
    grad_qkv = token_product(row_in, d_qkv)
    d_in = lax.psum_scatter(
        rows_product(d_qkv, qkv_mine).astype(LOW), SEQ, scatter_dimension=0, tiled=True
    ).astype(F32)
    input_grad = (d_hmid + norm_back(d_in, normed_one, scaler_one)).astype(LOW)[None]

    plane_qkv = lax.psum_scatter(grad_qkv.astype(LOW), "dp", scatter_dimension=0, tiled=True)
    part_qkv = lax.all_to_all(
        plane_qkv.reshape(seqs, part, 3 * span), SEQ, split_axis=0, concat_axis=0, tiled=True
    )
    if strided:
        sum_qkv = part_qkv.reshape(seqs, part, 3, planes, HD).transpose(1, 2, 3, 0, 4)
        sum_out = lax.psum_scatter(grad_out.astype(LOW), "dp", scatter_dimension=0, tiled=True)
    else:
        sum_qkv = part_qkv.reshape(seqs, part, 3, span).transpose(1, 2, 0, 3)
        spread = lax.dynamic_update_slice_in_dim(
            jnp.zeros((width, width), LOW), grad_out.astype(LOW), seq_index * span, axis=0
        )
        sum_out = lax.psum_scatter(spread, ALL, scatter_dimension=0, tiled=True)
    sum_qkv = sum_qkv.reshape(part, 3 * width).astype(F32)
    sum_out = sum_out.astype(F32)

    def finish(total, weight, gain):
        wide = weight.astype(F32)
        return (total * gain.astype(F32)[:, None], jnp.sum(total * wide, axis=1))

    sum_qkv, grad_gain_one = finish(sum_qkv, w_qkv, gain_attn)
    sum_out, grad_gain_two = finish(sum_out, w_out, gain_attn_sub)
    sum_down, grad_gain_four = finish(sum_down, w_down, gain_ffn_sub)

    def averaged(average, weight):
        return EMA_DECAY * average + (1.0 - EMA_DECAY) * weight.astype(F32)

    return (
        output,
        input_grad,
        sum_qkv,
        sum_out,
        sum_up,
        sum_down,
        grad_gain_one,
        grad_gain_two,
        grad_gain_three,
        grad_gain_four,
        averaged(ema_qkv, w_qkv),
        averaged(ema_out, w_out),
        averaged(ema_up, w_up),
        averaged(ema_down, w_down),
        averaged(ema_gain_attn, gain_attn),
        averaged(ema_gain_attn_sub, gain_attn_sub),
        averaged(ema_gain_ffn, gain_ffn),
        averaged(ema_gain_ffn_sub, gain_ffn_sub),
    )


def solution(mesh):
    split = Mesh(
        mesh.devices.reshape(mesh.shape["dp"], mesh.shape["seq"] // 2, 2), ("dp", "chip", "core")
    )
    tokens = P("dp", SEQ, None)
    ids = P("dp", SEQ)
    rows = P(ALL, None)
    columns = P(None, ALL)
    vector = P(ALL)
    weights = (rows, rows, columns, rows)
    gains = (vector,) * 4
    return jax.shard_map(
        body,
        mesh=split,
        in_specs=(tokens, ids, ids, *weights, *gains, *weights, *gains, tokens),
        out_specs=(tokens, tokens, *weights, *gains, *weights, *gains),
        check_vma=False,
    )
```

time: 1460 us -> 963 us (0.66)
  waiting for transfers between devices: 808 us -> 383 us
  blocking collectives: 198 us -> 160 us
  matrix products: 245 us -> 208 us
    reduce_scatter x6 -> x8, waiting for transfers between devices: 533 us -> 161 us  [the longest x1 47.9 us: body(): lax.psum_scatter(dot(normed_four_low, down_mine).astype(LOW), TP, scatter...]
    all_to_all x4 -> x1, waiting for transfers between devices: 37.5 us -> 0.01 us  [body(): lax.all_to_all(plane_qkv.reshape(seqs, part, 3 * span), SEQ, split_axis=0...]
    all_to_all x1, blocking collectives: 48.7 us -> 15.5 us  [body(): lax.all_to_all(qkv_send, SEQ, split_axis=0, concat_axis=0, tiled=True)]
    dot_general x4, matrix products: 49.4 us -> 29.1 us  [token_product(): lax.dot_general(left_op, right_op, (((0,), (0,)), ((), ())), preferred_el...]
    reduce_sum x7 -> x11, other arithmetic: 3.25 us -> 18.8 us  [the longest x1 4.11 us: finish(): return (total * gain.astype(F32)[:, None], jnp.sum(total * wide, axis=1))]
    all_to_all x4 -> x1, starting transfers between devices: 20 us -> 5.36 us  [body(): lax.all_to_all(plane_qkv.reshape(seqs, part, 3 * span), SEQ, split_axis=0...]
    all_gather x6 -> x8, waiting for transfers between devices: 234 us -> 220 us  [the longest x1 47.7 us: body(): grad_flat = lax.all_gather(grad_low, TP, axis=0, tiled=True)]
    all_gather x1 -> x3, blocking collectives: 39.2 us -> 26.6 us  [the longest x1 9.08 us: body(): row_segments = lax.all_gather(segment_ids[0], SEQ, axis=0, tiled=True)]
  transfers between devices with their start and end apart: 16 -> 18, of which waited for: 12 -> 10; matrix products, arithmetic and copies ran while one was open for 26% -> 32% of each run, Pallas kernels for 0% -> 0%
where the time goes in v1:
time: 963 us; the launch traced here: 945 us
  waiting for transfers between devices  383 us (40%)
  matrix products  208 us (22%)
  blocking collectives  160 us (17%)
  local copies, waits for them, and re-layouts  86.8 us (9%)
  other arithmetic  72.9 us (8%)
  between operations  16.9 us (2%)
  starting transfers between devices  16.5 us (2%)
    unnamed x2, blocking collectives  82.8 us
    reduce_scatter x1, waiting for transfers between devices, body(): lax.psum_scatter(dot(normed_four_low, down_mine).astype(LOW), TP, scatter...  47.9 us
    all_gather x1, waiting for transfers between devices, body(): grad_flat = lax.all_gather(grad_low, TP, axis=0, tiled=True)  47.7 us
    all_gather x1, waiting for transfers between devices, body(): down_mine = lax.all_gather(down_scaled, 'chip', axis=0, tiled=True)  44.4 us
    all_gather x1, waiting for transfers between devices, body(): ffn_flat = lax.all_gather(ffn_in, TP, axis=0, tiled=True)  43.9 us
    reduce_scatter x1, waiting for transfers between devices, body(): lax.psum_scatter(rows_product(d_qkv, qkv_mine).astype(LOW), SEQ, scatter_...  43.7 us
    reduce_scatter x1, waiting for transfers between devices, body(): lax.psum_scatter(rows_product(d_up_low, up_mine).astype(LOW), TP, scatter...  43.1 us
    all_gather x1, waiting for transfers between devices, body(): row_in = lax.all_gather(normed_low, SEQ, axis=0, tiled=True)  40.7 us
  transfers between devices with their start and end apart: 18, of which 10 were waited for; matrix products, arithmetic and copies ran while one was open for 32% of the time, Pallas kernels for 0%

profile of v1, /device:TPU:9, one launch (start us, length us, event | category | flops | bytes accessed | tf_op | source)
XLA Modules:
  0.0 945.0 jit_solution(18151649288521080120)
XLA Ops:
  16.9 15.5 %all_to_all.10 = bf16[8,64,768]{2,1,0:T(8,128)(2,1)} all-to-all(bf16[8,64,768]{2,1,0:T(8,128)(2,1)S(1)} %reshape.447), channel_id=1, replica_groups=mesh['dp'=4,'chip'=4,'core'=2] {'chip','core'}, dimensions={0} | all-to-all | bytes 1572864 | tf_op jit(solution)/shard_map/all_to_all | solution.py:205
  35.2 8.9 all-gather.1
  45.7 9.1 all-gather
  56.1 37.5 %all-gather.14.cloned.1.call-done = bf16[2048,768]{1,0:T(8,128)(2,1)} async-done(((bf16[512,768]{1,0:T(8,128)(2,1)}), bf16[2048,768]{1,0:T(8,128)(2,1)}) %all-gather.14.cloned.1.call-update) | async-done | bytes 3145744 | tf_op jit(solution)/shard_map/all_gather | solution.py:206
  93.6 40.7 %all-gather.12.cloned.1.call-done = bf16[1024,2048]{1,0:T(8,128)(2,1)} async-done(((bf16[128,2048]{1,0:T(8,128)(2,1)}), bf16[1024,2048]{1,0:T(8,128)(2,1)}) %all-gather.12.cloned.1.call-update) | async-done | bytes 4194320 | tf_op jit(solution)/shard_map/all_gather | solution.py:219
  134.3 6.2 fusion.163
  164.6 15.9 %while.27 = (s32[]{:T(128)}, bf16[2,512,4,64]{1,3,2,0:T(8,128)(2,1)S(1)}, f32[2,4,512,1]{2,1,3,0:T(4,128)S(1)}, s32[2]{0:T(128)S(1)}, s32[1024]{0:T(1024)S(1)}, ...) while((s32[]{:T(128)}, ...), condition=%wide.region_5.6_spmd, body=%wide.region_2.5_spmd.sunk | while | flops 557316608 | bytes 29177988 | solution.py:111
  182.4 10.0 %reduce-scatter.12.cloned.1.call-start = ((), (), s32[]{:S(2)}) async-start(), calls=%async_computation.14 | async-start | bytes 4718592 | tf_op jit(solution)/shard_map/reduce_scatter | solution.py:238
  197.9 39.4 %all-reduce = bf16[2048]{0:T(1024)(128)(2,1)S(1)} all-reduce(bf16[2048]{0:T(1024)(128)(2,1)S(1)} %dynamic-update-slice), channel_id=1, replica_groups=mesh['dp'=4,'chip'=4,'core'=2] {'dp','chip','core'}, use_global_device_ids=true, to_apply=%add | all-reduce | flops 2048 | bytes 8192
  238.8 13.2 %psum.14 = f32[2048]{0:T(1024)S(1)} all-reduce(f32[2048]{0:T(1024)S(1)} %convert_reduce_fusion), channel_id=1, replica_groups=mesh['dp'=4,'chip'=4,'core'=2] {'chip','core'}, use_global_device_ids=true, to_apply=%region_11.12 | all-reduce | flops 2048 | bytes 16384 | tf_op jit(solution)/shard_map/psum | solution.py:241
  253.2 26.4 %reduce-scatter.12.cloned.1.call-done = bf16[128,2048]{1,0:T(8,128)(2,1)} async-done(((bf16[1024,2048]{1,0:T(8,128)(2,1)}), bf16[128,2048]{1,0:T(8,128)(2,1)}) %reduce-scatter.12.cloned.1.call-update) | async-done | bytes 524304 | tf_op jit(solution)/shard_map/reduce_scatter | solution.py:238
  287.0 43.9 %all-gather.18.cloned.1.call-done = bf16[1024,2048]{1,0:T(8,128)(2,1)} async-done(((bf16[128,2048]{1,0:T(8,128)(2,1)}), bf16[1024,2048]{1,0:T(8,128)(2,1)}) %all-gather.18.cloned.1.call-update) | async-done | bytes 4194320 | tf_op jit(solution)/shard_map/all_gather | solution.py:260
  330.9 10.0 %fusion.164 = f32[1024,1024]{0,1:T(8,128)} fusion(bf16[1024,2048]{1,0:T(8,128)(2,1)} %all-gather.18.cloned.1.call-done, bf16[2048,1024]{1,0:T(8,128)(2,1)} %all-gather.20.cloned.1.call-done), kind=kOutput, calls=%fused_computation.250 | convolution fusion | flops 4294967296 | bytes 12582912 | tf_op jit(solution)/shard_map/dot_general | solution.py:69
  340.9 44.4 %all-gather.22.cloned.1.call-done = bf16[1024,2048]{1,0:T(8,128)(2,1)} async-done(((bf16[256,2048]{1,0:T(8,128)(2,1)}), bf16[1024,2048]{1,0:T(8,128)(2,1)}) %all-gather.22.cloned.1.call-update) | async-done | bytes 4194320 | tf_op jit(solution)/shard_map/all_gather | solution.py:258
  385.3 47.7 %all-gather.26.cloned.1.call-done = bf16[1,1024,2048]{2,1,0:T(8,128)(2,1)} async-done(((bf16[1,128,2048]{2,1,0:T(8,128)(2,1)}), bf16[1,1024,2048]{2,1,0:T(8,128)(2,1)}) %all-gather.26.cloned.1.call-update) | async-done | bytes 4194320 | tf_op jit(solution)/shard_map/all_gather | solution.py:259
  433.0 18.8 %fusion.156 = (f32[1024]{0:T(1024)S(1)}, f32[1024]{0:T(1024)S(1)}, f32[1024]{0:T(1024)S(1)}, f32[1024,1024]{0,1:T(8,128)}, f32[1024,1024]{0,1:T(8,128)}, /*index=5*/f32[1024,1024]{1,0:T(8,128)}) fusion(f32[1024,1024]{0,1:T(8,128)} %fusion.164, bf16[1024,2048]{1,0:T(8,128)(2,1)} %all-gather.22.cloned.1.call-done, ...), kind=kOutput, calls=%fused_computation.244 | convolution fusion | flops 4367315968 | bytes 25178112 | tf_op jit(solution)/shard_map/dot_general | solution.py:73
  454.3 21.9 %psum.15 = f32[4,1024]{1,0:T(4,128)S(1)} all-reduce(f32[4,1024]{1,0:T(4,128)S(1)} %pad_maximum_fusion.3), channel_id=1, replica_groups=mesh['dp'=4,'chip'=4,'core'=2] {'dp','core'}, use_global_device_ids=true, to_apply=%region_18.19 | all-reduce | flops 4096 | bytes 32768 | tf_op jit(solution)/shard_map/psum | solution.py:264
  476.2 7.3 add_convert_fusion
  491.1 10.0 %convolution_convert_fusion.4 = bf16[1024,2048]{1,0:T(8,128)(2,1)} fusion(bf16[1024,2048]{1,0:T(8,128)(2,1)} %all-gather.22.cloned.1.call-done, f32[1024,1024]{0,1:T(8,128)} %get-tuple-element.293, f32[1024]{0:T(1024)S(1)} %get-tuple-element.326, f32[1024]{0:T(1024)S(1)} %bitcast.339), kind=kOutput, calls=%fused_computation.100 | convolution fusion | flops 4300210176 | bytes 12591104 | tf_op jit(solution)/shard_map/dot_general | solution.py:69
  501.2 43.1 %reduce-scatter.16.cloned.1.call-done = bf16[128,2048]{1,0:T(8,128)(2,1)} async-done(((bf16[1024,2048]{1,0:T(8,128)(2,1)}), bf16[128,2048]{1,0:T(8,128)(2,1)}) %reduce-scatter.16.cloned.1.call-update) | async-done | bytes 524304 | tf_op jit(solution)/shard_map/reduce_scatter | solution.py:284
  546.6 47.9 %reduce-scatter.14.cloned.1.call-done = bf16[128,2048]{1,0:T(8,128)(2,1)} async-done(((bf16[1024,2048]{1,0:T(8,128)(2,1)}), bf16[128,2048]{1,0:T(8,128)(2,1)}) %reduce-scatter.14.cloned.1.call-update) | async-done | bytes 524304 | tf_op jit(solution)/shard_map/reduce_scatter | solution.py:287
  598.2 9.4 convolution_convert_fusion.2
  607.7 9.9 %fusion.93 = bf16[1024,2048]{1,0:T(8,128)(2,1)} fusion(bf16[1,1024,2048]{2,1,0:T(8,128)(2,1)} %all-gather.26.cloned.1.call-done, f32[1024,1024]{0,1:T(8,128)} %get-tuple-element.293, f32[1024]{0:T(1024)S(1)} %get-tuple-element.326, f32[1024]{0:T(1024)S(1)} %bitcast.340), kind=kOutput, calls=%fused_computation.97 | convolution fusion | flops 4300210176 | bytes 12591104 | tf_op jit(solution)/shard_map/dot_general | solution.py:79
  627.9 8.6 all_gather.46
  656.1 108.7 %while.28 = (s32[]{:T(128)}, f32[1024,4,64]{0,2,1:T(8,128)}, f32[1024,4,64]{0,2,1:T(8,128)S(1)}, bf16[2,512,4,64]{1,3,2,0:T(8,128)(2,1)}, bf16[2,512,4,64]{1,3,2...) while((s32[]{:T(128)}, f32[1024,4,64]{0,2,1:T(8,128)}, ...), condition=%wide.region_27.28_spmd.clone, body=%wide.region_25.27_spmd.clone.sunk | while | flops 1388845568 | bytes 104931016 | solution.py:152
  667.0 19.2 %fusion.226 = f32[1024,4,64]{0,2,1:T(8,128)} fusion(f32[4,512,1024]{2,1,0:T(8,128)} %fusion.223, f32[4,512,1024]{2,1,0:T(8,128)} %fusion.224, f32[4,512]{1,0:T(4,128)S(1)} %dynamic-slice_bitcast_fusion.2, pred[512,1024]{1,0:T(8,128)(4,1)S(1)} %fusion.225, f32[1024,4,64]{0,2,1:T(8,128)} %get-tuple-element.515, pred[]{:T(512)S(6)} %compare.4, ...), kind=kOutput, calls=%fused_computation.41.clone.1 | convolution fusion | flops 287837184 | bytes 36979200 | tf_op jit(solution)/shard_map/while/body/eval_jaxpr/hqk,qhd->khd/dot_general | solution.py:140
  686.2 18.4 %fusion.228 = bf16[2,512,4,64]{1,3,2,0:T(8,128)(2,1)} fusion(bf16[2,512,4,64]{1,3,2,0:T(8,128)(2,1)} %get-tuple-element.517, s32[]{:T(128)} %get-tuple-element.514, bf16[1024,4,64]{0,2,1:T(8,128)(2,1)S(1)} %get-tuple-element.536, f32[4,512,1024]{2,1,0:T(8,128)} %fusion.223, f32[4,512,1024]{2,1,0:T(8,128)} %fusion.224, ...), kind=kOutput, calls=%fused_computation.44.clone.1 | convolution fusion | flops 287312896 | bytes 35668480 | tf_op jit(solution)/shard_map/while/body/eval_jaxpr/hqk,khd->qhd/dot_general | solution.py:137
  721.3 19.5 %fusion.226 = f32[1024,4,64]{0,2,1:T(8,128)} fusion(f32[4,512,1024]{2,1,0:T(8,128)} %fusion.223, f32[4,512,1024]{2,1,0:T(8,128)} %fusion.224, f32[4,512]{1,0:T(4,128)S(1)} %dynamic-slice_bitcast_fusion.2, pred[512,1024]{1,0:T(8,128)(4,1)S(1)} %fusion.225, f32[1024,4,64]{0,2,1:T(8,128)} %get-tuple-element.515, pred[]{:T(512)S(6)} %compare.4, ...), kind=kOutput, calls=%fused_computation.41.clone.1 | convolution fusion | flops 287837184 | bytes 36979200 | tf_op jit(solution)/shard_map/while/body/eval_jaxpr/hqk,qhd->khd/dot_general | solution.py:140
  740.7 18.1 %fusion.228 = bf16[2,512,4,64]{1,3,2,0:T(8,128)(2,1)} fusion(bf16[2,512,4,64]{1,3,2,0:T(8,128)(2,1)} %get-tuple-element.517, s32[]{:T(128)} %get-tuple-element.514, bf16[1024,4,64]{0,2,1:T(8,128)(2,1)S(1)} %get-tuple-element.536, f32[4,512,1024]{2,1,0:T(8,128)} %fusion.223, f32[4,512,1024]{2,1,0:T(8,128)} %fusion.224, ...), kind=kOutput, calls=%fused_computation.44.clone.1 | convolution fusion | flops 287312896 | bytes 35668480 | tf_op jit(solution)/shard_map/while/body/eval_jaxpr/hqk,khd->qhd/dot_general | solution.py:137
  802.5 6.9 convolution_convert_fusion.1
  815.1 43.4 %all-reduce.1 = f32[2048]{0:T(1024)S(1)} all-reduce(f32[2048]{0:T(1024)S(1)} %copy-done.23), channel_id=14, replica_groups=mesh['dp'=4,'chip'=4,'core'=2] {'dp','chip','core'}, use_global_device_ids=true, to_apply=%region_38.39.clone | all-reduce | flops 2048 | bytes 16384
  875.1 43.7 %reduce-scatter.18.cloned.1.call-done = bf16[128,2048]{1,0:T(8,128)(2,1)} async-done(((bf16[1024,2048]{1,0:T(8,128)(2,1)}), bf16[128,2048]{1,0:T(8,128)(2,1)}) %reduce-scatter.18.cloned.1.call-update) | async-done | bytes 524304 | tf_op jit(solution)/shard_map/reduce_scatter | solution.py:337
  (294 shorter events, 228.4 us)
Async XLA Ops:
  8.0 85.6 %all-gather.14.cloned.1.call-start = ((), (), s32[]{:S(2)}) async-start(), calls=%async_computation.12 | async-start | bytes 3932160 | tf_op jit(solution)/shard_map/all_gather | solution.py:206
  32.5 101.9 %all-gather.12.cloned.1.call-start = ((), (), s32[]{:S(2)}) async-start(), calls=%async_computation.11 | async-start | bytes 4718592 | tf_op jit(solution)/shard_map/all_gather | solution.py:219
  34.1 158.3 %all-gather.16.cloned.1.call-start = ((), (), s32[]{:S(2)}) async-start(), calls=%async_computation.13 | async-start | bytes 1310720 | tf_op jit(solution)/shard_map/all_gather | solution.py:210
  35.1 216.9 %reduce-scatter.28.cloned.1.call-start = ((), (), s32[]{:S(2)}) async-start(), calls=%async_computation.27 | async-start | bytes 589824
  45.2 114.5 %copy-start.17 = (f32[1024,64]{0,1:T(8,128)}, f32[1024,64]{0,1:T(8,128)S(1)}, u32[]{:S(2)}) copy-start(f32[1024,64]{0,1:T(8,128)S(1)} %tile.33) | copy-start | bytes 786436
  45.7 114.1 %copy-start.7 = (f32[1024,64]{0,1:T(8,128)}, f32[1024,64]{0,1:T(8,128)S(1)}, u32[]{:S(2)}) copy-start(f32[1024,64]{0,1:T(8,128)S(1)} %tile.38) | copy-start | bytes 786436
  56.1 103.7 %copy-start.16 = (f32[1024,64]{0,1:T(8,128)}, f32[1024,64]{0,1:T(8,128)S(1)}, u32[]{:S(2)}) copy-start(f32[1024,64]{0,1:T(8,128)S(1)} %broadcast_multiply_fusion.1) | copy-start | bytes 786436
  182.4 97.2 %reduce-scatter.12.cloned.1.call-start = ((), (), s32[]{:S(2)}) async-start(), calls=%async_computation.14 | async-start | bytes 4718592 | tf_op jit(solution)/shard_map/reduce_scatter | solution.py:238
  197.0 88.0 %copy-start.37 = (bf16[256]{0:T(256)(128)(2,1)S(1)}, bf16[256]{0:T(256)(128)(2,1)}, u32[]{:S(2)}) copy-start(bf16[256]{0:T(256)(128)(2,1)} %param.34) | copy-start | bytes 1540
  197.0 88.0 %copy-start.10 = (bf16[256,2048]{1,0:T(8,128)(2,1)S(1)}, bf16[256,2048]{1,0:T(8,128)(2,1)}, u32[]{:S(2)}) copy-start(bf16[256,2048]{1,0:T(8,128)(2,1)} %param.30) | copy-start | bytes 3145732
  197.0 90.0 %all-gather.20.cloned.1.call-start = ((), (), s32[]{:S(2)}) async-start(), calls=%async_computation.16 | async-start | bytes 5242880 | tf_op jit(solution)/shard_map/all_gather | solution.py:257
  197.6 133.3 %all-gather.18.cloned.1.call-start = ((), (), s32[]{:S(2)}) async-start(), calls=%async_computation.15 | async-start | bytes 4718592 | tf_op jit(solution)/shard_map/all_gather | solution.py:260
  284.9 100.4 %all-gather.22.cloned.1.call-start = ((), (), s32[]{:S(2)}) async-start(), calls=%async_computation.17 | async-start | bytes 5242880 | tf_op jit(solution)/shard_map/all_gather | solution.py:258
  284.9 55.9 %copy-start.28 = (f32[256]{0:T(256)}, f32[256]{0:T(256)S(1)}, u32[]{:S(2)}) copy-start(f32[256]{0:T(256)S(1)} %convert_element_type.260) | copy-start | bytes 3076
  286.2 146.8 %all-gather.26.cloned.1.call-start = ((), (), s32[]{:S(2)}) async-start(), calls=%async_computation.26 | async-start | bytes 4718592 | tf_op jit(solution)/shard_map/all_gather | solution.py:259
  286.9 257.3 %reduce-scatter.16.cloned.1.call-start = ((), (), s32[]{:S(2)}) async-start(), calls=%async_computation.19 | async-start | bytes 4718592 | tf_op jit(solution)/shard_map/reduce_scatter | solution.py:284
  491.0 103.5 %reduce-scatter.14.cloned.1.call-start = ((), (), s32[]{:S(2)}) async-start(), calls=%async_computation.18 | async-start | bytes 4718592 | tf_op jit(solution)/shard_map/reduce_scatter | solution.py:287
  501.1 43.1 %copy-start.3 = (bf16[128,2048]{1,0:T(8,128)(2,1)S(1)}, bf16[128,2048]{1,0:T(8,128)(2,1)}, u32[]{:S(2)}) copy-start(bf16[128,2048]{1,0:T(8,128)(2,1)} %reduce-scatter.12.cloned.1.call-done) | copy-start | bytes 1572868
  501.1 93.4 %copy-start.18 = (bf16[1,128,2048]{2,1,0:T(8,128)(2,1)S(1)}, bf16[1,128,2048]{2,1,0:T(8,128)(2,1)}, u32[]{:S(2)}) copy-start(bf16[1,128,2048]{2,1,0:T(8,128)(2,1)} %param.43) | copy-start | bytes 1572868
  501.1 141.5 %all-gather.24.cloned.1.call-start = ((), (), s32[]{:S(2)}) async-start(), calls=%async_computation.20 | async-start | bytes 4718592 | tf_op jit(solution)/shard_map/all_gather | solution.py:308
  597.9 261.2 %reduce-scatter.24.cloned.1.call-start = ((), (), s32[]{:S(2)}) async-start(), calls=%async_computation.24 | async-start | bytes 5242880 | tf_op jit(solution)/shard_map/reduce_scatter | solution.py:292
  607.6 254.3 %reduce-scatter.26.cloned.1.call-start = ((), (), s32[]{:S(2)}) async-start(), calls=%async_computation.25 | async-start | bytes 5242880 | tf_op jit(solution)/shard_map/reduce_scatter | solution.py:295
  617.6 249.3 %reduce-scatter.22.cloned.1.call-start = ((), (), s32[]{:S(2)}) async-start(), calls=%async_computation.23 | async-start | bytes 1310720 | tf_op jit(solution)/shard_map/reduce_scatter | solution.py:348
  655.0 214.8 %reduce-scatter.20.cloned.1.call-start = ((), (), s32[]{:S(2)}) async-start(), calls=%async_computation.22 | async-start | bytes 3932160 | tf_op jit(solution)/shard_map/reduce_scatter | solution.py:342
  802.5 116.4 %reduce-scatter.18.cloned.1.call-start = ((), (), s32[]{:S(2)}) async-start(), calls=%async_computation.21 | async-start | bytes 4718592 | tf_op jit(solution)/shard_map/reduce_scatter | solution.py:337
  811.8 50.1 %copy-start.11 = (bf16[256,2048]{1,0:T(8,128)(2,1)S(1)}, bf16[256,2048]{1,0:T(8,128)(2,1)}, u32[]{:S(2)}) copy-start(bf16[256,2048]{1,0:T(8,128)(2,1)} %param.30) | copy-start | bytes 3145732
  811.8 50.1 %copy-start.29 = (f32[256]{0:T(256)S(1)}, f32[256]{0:T(256)}, u32[]{:S(2)}) copy-start(f32[256]{0:T(256)} %copy-done.28) | copy-start | bytes 3076
  861.8 57.1 %copy-start.1 = (bf16[1,128,2048]{2,1,0:T(8,128)(2,1)S(1)}, bf16[1,128,2048]{2,1,0:T(8,128)(2,1)}, u32[]{:S(2)}) copy-start(bf16[1,128,2048]{2,1,0:T(8,128)(2,1)} %param.24) | copy-start | bytes 1572868
  861.8 57.1 %copy-start.25 = (f32[128]{0:T(128)S(1)}, f32[128]{0:T(128)}, u32[]{:S(2)}) copy-start(f32[128]{0:T(128)} %copy-done.24) | copy-start | bytes 1540
  861.8 57.0 %copy-start.27 = (f32[128]{0:T(128)S(1)}, f32[128]{0:T(128)}, u32[]{:S(2)}) copy-start(f32[128]{0:T(128)} %copy-done.26) | copy-start | bytes 1540
  867.0 53.4 %copy-start.12 = (f32[128,2048]{1,0:T(8,128)S(1)}, f32[128,2048]{1,0:T(8,128)}, u32[]{:S(2)}) copy-start(f32[128,2048]{1,0:T(8,128)} %get-tuple-element.292) | copy-start | bytes 3145732
  869.8 52.9 %all-to-all-start.1 = ((bf16[8,64,768]{2,1,0:T(8,128)(2,1)}), bf16[8,64,768]{2,1,0:T(8,128)(2,1)S(1)}, u32[]{:S(2)}, u32[]{:S(2)}) async-start(bf16[8,64,768]{2,1,0:T(8,128)(2,1)} %bitcast.329), calls=%async_computation.6 | async-start | bytes 1572864 | tf_op jit(solution)/shard_map/all_to_all | solution.py:343
  (36 other events, 254.4 us)
Sparse Core Ops, SparseCore 0:
  32.6 60.9 all-gather.13
  96.1 38.2 all-gather.11
  136.5 27.2 all-gather.15
  182.5 40.4 reduce-scatter.27
  226.6 52.9 reduce-scatter.11
  598.1 44.4 all-gather.23
Sparse Core Ops, SparseCore 1:
  199.3 53.5 all-gather.19
  284.9 45.9 all-gather.17
  333.2 52.1 all-gather.21
  386.9 46.0 all-gather.25
  491.1 53.0 reduce-scatter.15
  546.5 47.9 reduce-scatter.13
  607.7 63.0 reduce-scatter.23
  673.9 52.6 reduce-scatter.25
  728.7 25.0 reduce-scatter.21
  802.5 61.0 reduce-scatter.19
  867.2 51.6 reduce-scatter.17

commit v2 on v1

v2 whole, which is shorter than its diff:
```python
import functools
import math

import jax
import jax.numpy as jnp
from jax import lax
from jax.experimental import pallas as pl
from jax.experimental.pallas import tpu as pltpu
from jax.sharding import Mesh
from jax.sharding import PartitionSpec as P

HEADS = 32
HD = 64

NEG_FILL = -1000000000.0
NORM_EPS = 1e-05
EMA_DECAY = 0.7
LOW = jnp.bfloat16
F32 = jnp.float32
SEQ = ("chip", "core")
TP = ("dp", "core")
ALL = ("dp", "chip", "core")


def moments(values):
    mean = jnp.mean(values, axis=-1, keepdims=True)
    centered = values - mean
    scaler = lax.rsqrt(jnp.mean(centered * centered, axis=-1, keepdims=True) + NORM_EPS)
    return (centered * scaler, scaler)


def norm_back(scaled_grad, normed, scaler):
    first_mean = jnp.mean(scaled_grad, axis=-1, keepdims=True)
    second_mean = jnp.mean(scaled_grad * normed, axis=-1, keepdims=True)
    return scaler * (scaled_grad - first_mean - normed * second_mean)


def exact_gelu(values):
    return jax.nn.gelu(values, approximate=False)


def token_tables(positions):
    half_count = HD // 2
    index_half = jnp.arange(half_count).astype(F32)
    inverse = jnp.exp(-(2.0 * index_half / HD) * math.log(10000.0))
    decay_base = (2.0 * index_half + 0.4 * HD) / (1.4 * HD)
    where_at = positions.astype(F32)[:, None]
    angles = where_at * inverse[None, :]
    factor = jnp.exp(where_at / 512.0 * jnp.log(decay_base)[None, :])
    sign_row = jnp.where(jnp.arange(HD) % 2 == 0, -1.0, 1.0).astype(F32)
    cosine = jnp.repeat(jnp.cos(angles), 2, axis=1)
    sine = jnp.repeat(jnp.sin(angles), 2, axis=1) * sign_row[None, :]
    factor = jnp.repeat(factor, 2, axis=1)
    grow = factor * HD ** (-0.5)
    where_block = jnp.broadcast_to(where_at, (positions.shape[0], HD))
    return jnp.concatenate(
        [cosine * grow, sine * grow, HD**0.5 / (factor * factor), where_block], axis=1
    )


def dot(left_op, right_op):
    return jnp.dot(left_op, right_op, preferred_element_type=F32)


def rows_product(operand, weight_rows):
    return lax.dot_general(
        operand, weight_rows, (((1,), (1,)), ((), ())), preferred_element_type=F32
    )


def token_product(left_op, right_op):
    return lax.dot_general(left_op, right_op, (((0,), (0,)), ((), ())), preferred_element_type=F32)


MESH = pl.DeviceIdType.MESH
HBM = pl.BlockSpec(memory_space=pl.ANY)
VMEM = pl.BlockSpec(memory_space=pltpu.VMEM)
VMEM_BYTES = 56 * 1024 * 1024


def shape(dims, kind):
    return jax.ShapeDtypeStruct(dims, kind)


def pairs_of(*counts):
    return [pltpu.SemaphoreType.DMA((count,)) for count in counts for _ in range(2)]


def call(kernel, name, outs, args, in_specs, out_specs, scratch, collective=None):
    return pl.pallas_call(
        kernel,
        name=name,
        out_shape=outs,
        in_specs=in_specs,
        out_specs=out_specs,
        scratch_shapes=scratch,
        compiler_params=pltpu.CompilerParams(
            collective_id=collective,
            has_side_effects=collective is not None,
            vmem_limit_bytes=VMEM_BYTES,
        ),
    )(*args)


def place():
    return (lax.axis_index("dp"), lax.axis_index("chip"), lax.axis_index("core"))


def remote(source, target, sems, index, device):
    return pltpu.make_async_remote_copy(
        src_ref=source,
        dst_ref=target,
        send_sem=sems[0].at[index],
        recv_sem=sems[1].at[index],
        device_id=device,
        device_id_type=MESH,
    )


def greet(barrier, devices):
    for device in devices:
        pl.semaphore_signal(barrier, inc=1, device_id=device, device_id_type=MESH)


def greet_line(barrier, planes, here):
    z, c, core = here

    @pl.when(z < planes - 1)
    def _():
        greet(barrier, [(z + 1, c, core)])

    @pl.when(z > 0)
    def _():
        greet(barrier, [(z - 1, c, core)])


def line_peers(planes, here):
    z = here[0]
    return (2 * planes - 2 - z) // planes + (z + planes - 1) // planes


def chip_peers(chips, here):
    z, c, core = here
    return [(z, lax.rem(c + k, chips), core) for k in range(1, chips)]


def plane_peers(chips, here):
    z, c, core = here
    seqs = 2 * chips
    me = 2 * c + core
    ids = [lax.rem(me + k, seqs) for k in range(1, seqs)]
    return [(z, index // 2, lax.rem(index, 2)) for index in ids]


def column_block(whole, units, index):
    if len(whole.shape) == 3:
        return whole.at[index]
    return whole.at[:, pl.ds(pl.multiple_of(index * units, 128), units)]


class ChipSwap:
    def __init__(self, chips, here, source, slots, sems):
        z, c, core = here
        self.sends = [
            remote(source(device[1]), slots.at[c], sems, k, device)
            for k, device in enumerate(chip_peers(chips, here), 1)
        ]
        self.waits = [
            remote(source(c), slots.at[lax.rem(c + chips - k, chips)], sems, k, here)
            for k in range(1, chips)
        ]
        self.keep = (source(c), slots.at[c])

    def start(self, local):
        for copy in self.sends:
            copy.start()
        self.held = pltpu.make_async_copy(*self.keep, local)
        self.held.start()

    def finish(self):
        self.held.wait()
        for send, wait in zip(self.sends, self.waits):
            send.wait_send()
            wait.wait_recv()


class PlaneGather:
    def __init__(self, chips, here, block, out, far, near):
        self.chips, self.here, self.block, self.out = chips, here, block, out
        self.far, self.near = far, near
        z, c, core = here
        self.me = 2 * c + core
        self.partner = (z, c, 1 - core)

    def source(self, k, core):
        return 2 * lax.rem(self.here[1] + self.chips - k, self.chips) + core

    def sends(self):
        mine = self.out.at[self.me]
        copies = [
            remote(self.block, mine, self.far, k, device)
            for k, device in enumerate(chip_peers(self.chips, self.here), 1)
        ]
        return [*copies, remote(self.block, mine, self.near, 0, self.partner)]

    def start(self):
        for copy in self.sends():
            copy.start()

    def passed(self, k):
        index = self.source(k, self.here[2])
        return remote(self.out.at[index], self.out.at[index], self.near, k, self.partner)

    def forward(self):
        for k in range(1, self.chips):
            index = self.source(k, self.here[2])
            remote(self.block, self.out.at[index], self.far, k, self.partner).wait_recv()
            self.passed(k).start()

    def finish(self):
        for copy in self.sends():
            copy.wait_send()
        for k in range(1, self.chips):
            self.passed(k).wait_send()
        for k in range(self.chips):
            index = self.source(k, 1 - self.here[2])
            remote(self.block, self.out.at[index], self.near, k, self.partner).wait_recv()


class LineGather:
    def __init__(self, planes, here, block, up, down):
        self.planes, self.here, self.block = planes, here, block
        self.up, self.down = up, down

    def upward(self, d):
        z, c, core = self.here
        block = self.block(z - d)
        return remote(block, block, self.up, d, (z + 1, c, core))

    def downward(self, d):
        z, c, core = self.here
        block = self.block(z + d)
        return remote(block, block, self.down, d, (z - 1, c, core))

    def each(self, d, act_up, act_down):
        z, planes = self.here[0], self.planes
        pl.when((z < planes - 1) & (z - d >= 0))(lambda: act_up(self.upward(d)))
        pl.when((z > 0) & (z + d < planes))(lambda: act_down(self.downward(d)))

    def start(self):
        self.each(0, lambda copy: copy.start(), lambda copy: copy.start())

    def step(self, d, arrived=None):
        z, c, core = self.here
        planes = self.planes

        def below():
            block = self.block(z - d)
            remote(block, block, self.up, d - 1, (z, c, core)).wait_recv()
            if d < planes - 1:
                pl.when(z < planes - 1)(lambda: self.upward(d).start())
            if arrived is not None:
                arrived(z - d)

        def above():
            block = self.block(z + d)
            remote(block, block, self.down, d - 1, (z, c, core)).wait_recv()
            if d < planes - 1:
                pl.when(z > 0)(lambda: self.downward(d).start())
            if arrived is not None:
                arrived(z + d)

        pl.when(z - d >= 0)(below)
        pl.when(z + d < planes)(above)

    def finish(self):
        for d in range(self.planes - 1):
            self.each(d, lambda copy: copy.wait_send(), lambda copy: copy.wait_send())


def attention_gather_kernel(
    planes, chips, x_ref, meta_ref, qkv_ref, out_ref, gain_ref, up_ref,
    row_ref, metas_ref, qkvs_ref, outs_ref, gains_ref, ups_ref,
    *sems,
):
    here = place()
    z, c, core = here
    seqs = 2 * chips
    count = planes * seqs
    me = 2 * c + core
    flat = z * seqs + me
    groups = [sems[2 * i : 2 * i + 2] for i in range(11)]
    swap_sems, x_far, x_near, meta_far, meta_near, up, down, up_two, down_two = groups[:9]
    gain_sems, up_sems = groups[9:]
    local = sems[22]
    barrier = pltpu.get_barrier_semaphore()

    def device_of(k):
        other = lax.rem(flat + k, count)
        return (other // seqs, lax.rem(other, seqs) // 2, lax.rem(other, 2))

    def signal(k, carry):
        greet(barrier, [device_of(k)])
        return carry

    lax.fori_loop(1, count, signal, 0)
    pl.semaphore_wait(barrier, count - 1)

    mine = pltpu.make_async_copy(qkv_ref.at[me], qkvs_ref.at[z, me], local.at[0])
    keeps = [
        pltpu.make_async_copy(x_ref, row_ref.at[me], local.at[1]),
        pltpu.make_async_copy(meta_ref, metas_ref.at[me], local.at[2]),
        pltpu.make_async_copy(gain_ref, gains_ref.at[flat], local.at[3]),
    ]
    own_out = pltpu.make_async_copy(out_ref, outs_ref.at[z], local.at[4])
    units = up_ref.shape[1]
    keeps.append(pltpu.make_async_copy(up_ref, column_block(ups_ref, units, c), local.at[5]))
    ups = [
        remote(up_ref, column_block(ups_ref, units, c), up_sems, k, device)
        for k, device in enumerate(chip_peers(chips, here), 1)
    ]
    swaps = [
        remote(qkv_ref.at[2 * device[1] + device[2]], qkvs_ref.at[z, me], swap_sems, k, device)
        for k, device in enumerate(plane_peers(chips, here), 1)
    ]
    mine.start()
    own_out.start()
    for copy in swaps:
        copy.start()
    rows = PlaneGather(chips, here, x_ref, row_ref, x_far, x_near)
    metas = PlaneGather(chips, here, meta_ref, metas_ref, meta_far, meta_near)
    rows.start()
    metas.start()
    for copy in keeps:
        copy.start()

    def gain_copy(k):
        return remote(gain_ref, gains_ref.at[flat], gain_sems, k, device_of(k))

    def gain_start(k, carry):
        gain_copy(k).start()
        return carry

    lax.fori_loop(1, count, gain_start, 0)

    mine.wait()
    own_out.wait()
    for k in range(1, seqs):
        index = lax.rem(me + seqs - k, seqs)
        remote(qkv_ref.at[0], qkvs_ref.at[z, index], swap_sems, k, here).wait_recv()
    line = LineGather(planes, here, lambda t: qkvs_ref.at[t], up, down)
    line_two = LineGather(planes, here, lambda t: outs_ref.at[t], up_two, down_two)
    line.start()
    line_two.start()
    rows.forward()
    metas.forward()
    for copy in ups:
        copy.start()
    for d in range(1, planes):
        line.step(d)
        line_two.step(d)
    line.finish()
    line_two.finish()
    rows.finish()
    metas.finish()
    for copy in swaps:
        copy.wait_send()
    for copy in keeps:
        copy.wait()
    for k in range(1, chips):
        ups[k - 1].wait_send()
        other = lax.rem(c + chips - k, chips)
        remote(up_ref, column_block(ups_ref, units, other), up_sems, k, here).wait_recv()

    def gain_wait(k, carry):
        gain_copy(k).wait_send()
        other = lax.rem(flat + count - k, count)
        remote(gain_ref, gains_ref.at[other], gain_sems, k, here).wait_recv()
        return carry

    lax.fori_loop(1, count, gain_wait, 0)


def attention_gather(planes, chips, x_block, meta, qkv_blocks, out_rows, gain_tile, up_block):
    seqs = 2 * chips
    part, wide = qkv_blocks.shape[1:]
    width, units = up_block.shape
    return call(
        functools.partial(attention_gather_kernel, planes, chips),
        "attention_gather",
        [
            shape((seqs, *x_block.shape), LOW),
            shape((seqs, *meta.shape), F32),
            shape((planes, seqs, part, wide), LOW),
            shape((planes, *out_rows.shape), LOW),
            shape((planes * seqs, *gain_tile.shape), F32),
            shape(
                (width, chips * units) if units % 128 == 0 else (chips, width, units), LOW
            ),
        ],
        (x_block, meta, qkv_blocks, out_rows, gain_tile, up_block),
        [HBM] * 6,
        [HBM] * 6,
        [
            *pairs_of(seqs, *[chips] * 4, *[planes] * 4, planes * seqs, chips),
            pltpu.SemaphoreType.DMA((6,)),
        ],
        1,
    )


def plane_gather_kernel(
    planes, chips, x_ref, stat_ref, tile_ref, row_ref, stats_ref, tiles_ref, *sems
):
    here = place()
    z, c, core = here
    seqs = 2 * chips
    count = planes * seqs
    me = 2 * c + core
    flat = z * seqs + me
    x_far, x_near, s_far, s_near, tile_sems = [sems[2 * i : 2 * i + 2] for i in range(5)]
    local = sems[10]
    barrier = pltpu.get_barrier_semaphore()

    def device_of(k):
        other = lax.rem(flat + k, count)
        return (other // seqs, lax.rem(other, seqs) // 2, lax.rem(other, 2))

    def signal(k, carry):
        greet(barrier, [device_of(k)])
        return carry

    lax.fori_loop(1, count, signal, 0)
    pl.semaphore_wait(barrier, count - 1)
    rows = PlaneGather(chips, here, x_ref, row_ref, x_far, x_near)
    stats = PlaneGather(chips, here, stat_ref, stats_ref, s_far, s_near)
    rows.start()
    stats.start()
    keeps = [
        pltpu.make_async_copy(x_ref, row_ref.at[me], local.at[0]),
        pltpu.make_async_copy(stat_ref, stats_ref.at[me], local.at[1]),
        pltpu.make_async_copy(tile_ref.at[flat], tiles_ref.at[flat], local.at[2]),
    ]
    for copy in keeps:
        copy.start()

    def tile_copy(k):
        other = lax.rem(flat + k, count)
        return remote(tile_ref.at[other], tiles_ref.at[flat], tile_sems, k, device_of(k))

    def tile_start(k, carry):
        tile_copy(k).start()
        return carry

    lax.fori_loop(1, count, tile_start, 0)
    rows.forward()
    stats.forward()
    rows.finish()
    stats.finish()
    for copy in keeps:
        copy.wait()

    def tile_wait(k, carry):
        tile_copy(k).wait_send()
        other = lax.rem(flat + count - k, count)
        remote(tile_ref.at[0], tiles_ref.at[other], tile_sems, k, here).wait_recv()
        return carry

    lax.fori_loop(1, count, tile_wait, 0)


def plane_gather(planes, chips, x_block, stats, tiles):
    seqs = 2 * chips
    return call(
        functools.partial(plane_gather_kernel, planes, chips),
        "plane_gather",
        [
            shape((seqs, *x_block.shape), x_block.dtype),
            shape((seqs, *stats.shape), stats.dtype),
            shape(tiles.shape, tiles.dtype),
        ],
        (x_block, stats, tiles),
        [HBM] * 3,
        [HBM] * 3,
        [
            *pairs_of(chips, chips, chips, chips, planes * seqs),
            pltpu.SemaphoreType.DMA((3,)),
        ],
        2,
    )


COLUMNS = 512


def product(left, right, columns, turned):
    if turned:
        return lax.dot_general(
            left, right[columns, :], (((1,), (1,)), ((), ())), preferred_element_type=F32
        )
    return jnp.dot(left, right[:, columns], preferred_element_type=F32)


class PlaneScatter:
    def __init__(self, chips, here, left, right, turned, near_out, near_in, far_out, far_in, near, far):
        self.chips, self.here = chips, here
        self.left, self.right, self.turned = left, right, turned
        self.near_out, self.near_in, self.far_out, self.far_in = near_out, near_in, far_out, far_in
        self.near, self.far = near, far
        self.width = near_out.shape[-1]

    def target(self, k):
        return lax.rem(self.here[1] + k, self.chips)

    def near_copy(self, k):
        z, c, core = self.here
        return remote(self.near_out.at[k], self.near_in.at[k], self.near, k, (z, c, 1 - core))

    def far_copy(self, k):
        z, _, core = self.here
        return remote(self.far_out.at[k], self.far_in.at[k], self.far, k, (z, self.target(k), core))

    def tiles(self):
        return [pl.ds(at, COLUMNS) for at in range(0, self.width, COLUMNS)]

    def start(self):
        core = self.here[2]
        order = [*range(1, self.chips), 0]
        for k in order:
            left = self.left[2 * self.target(k) + 1 - core]
            for columns in self.tiles():
                part = product(left, self.right, columns, self.turned)
                self.near_out[k, :, columns] = part.astype(LOW)
            self.near_copy(k).start()
        for k in order:
            left = self.left[2 * self.target(k) + core]
            self.near_copy(k).wait_recv()
            for columns in self.tiles():
                part = product(left, self.right, columns, self.turned)
                self.far_out[k, :, columns] = (
                    part + self.near_in[k, :, columns].astype(F32)
                ).astype(LOW)
            if k:
                self.far_copy(k).start()

    def finish(self, out_ref):
        for k in range(1, self.chips):
            self.far_copy(k).wait_recv()
        for columns in self.tiles():
            total = self.far_out[0, :, columns].astype(F32)
            for k in range(1, self.chips):
                total = total + self.far_in[k, :, columns].astype(F32)
            out_ref[:, columns] = total
        for k in range(self.chips):
            self.near_copy(k).wait_send()
        for k in range(1, self.chips):
            self.far_copy(k).wait_send()


def out_scatter_kernel(
    chips, left_ref, right_ref, tile_ref, out_ref, tiles_ref,
    near_out, near_in, far_out, far_in, *sems,
):
    here = place()
    z, c, core = here
    seqs = 2 * chips
    me = 2 * c + core
    near, far, tile_sems = [sems[2 * i : 2 * i + 2] for i in range(3)]
    barrier = pltpu.get_barrier_semaphore()
    peers = plane_peers(chips, here)
    greet(barrier, peers)
    pl.semaphore_wait(barrier, len(peers))
    swaps = [
        remote(tile_ref.at[2 * device[1] + device[2]], tiles_ref.at[me], tile_sems, k, device)
        for k, device in enumerate(peers, 1)
    ]
    for copy in swaps:
        copy.start()
    keep = pltpu.make_async_copy(tile_ref.at[me], tiles_ref.at[me], sems[6].at[0])
    keep.start()
    work = PlaneScatter(
        chips, here, left_ref, right_ref, False, near_out, near_in, far_out, far_in, near, far
    )
    work.start()
    work.finish(out_ref)
    keep.wait()
    for k in range(1, seqs):
        swaps[k - 1].wait_send()
        index = lax.rem(me + seqs - k, seqs)
        remote(tile_ref.at[0], tiles_ref.at[index], tile_sems, k, here).wait_recv()


def out_scatter(chips, left, right, tiles):
    _, tokens, _ = left.shape
    width = right.shape[1]
    return call(
        functools.partial(out_scatter_kernel, chips),
        "out_scatter",
        [shape((tokens, width), F32), shape(tiles.shape, F32)],
        (left, right, tiles),
        [VMEM, VMEM, VMEM],
        [VMEM, VMEM],
        [
            *[pltpu.VMEM((chips, tokens, width), LOW)] * 4,
            *pairs_of(chips, chips, 2 * chips),
            pltpu.SemaphoreType.DMA((1,)),
        ],
        3,
    )


class LineScatter:
    def __init__(self, planes, here, rows, own, above, below, up, down):
        self.planes, self.here, self.rows, self.own = planes, here, rows, own
        self.above, self.below, self.up, self.down = above, below, up, down

    def upward(self, t):
        z, c, core = self.here
        return remote(self.below.at[t], self.below.at[t], self.up, t, (z + 1, c, core))

    def downward(self, t):
        z, c, core = self.here
        return remote(self.above.at[t], self.above.at[t], self.down, t, (z - 1, c, core))

    def add(self, slot, t, fresh):
        for rows in self.rows:
            total = self.own(t, rows)
            if not fresh:
                total = total + slot[t, rows].astype(F32)
            slot[t, rows] = total.astype(LOW)

    def step(self, i):
        z, planes = self.here[0], self.planes
        top, low = planes - 1 - i, i

        def rise():
            @pl.when(z > 0)
            def _():
                self.upward(top).wait_recv()
                self.add(self.below, top, False)

            @pl.when(z == 0)
            def _():
                self.add(self.below, top, True)

            self.upward(top).start()

        def fall():
            @pl.when(z < planes - 1)
            def _():
                self.downward(low).wait_recv()
                self.add(self.above, low, False)

            @pl.when(z == planes - 1)
            def _():
                self.add(self.above, low, True)

            self.downward(low).start()

        pl.when(z < top)(rise)
        pl.when(z > low)(fall)

    def finish(self, store):
        z, planes = self.here[0], self.planes

        @pl.when(z > 0)
        def _():
            self.upward(z).wait_recv()

        @pl.when(z < planes - 1)
        def _():
            self.downward(z).wait_recv()

        def both():
            for rows in self.rows:
                total = self.own(z, rows) + self.below[z, rows].astype(F32)
                store(rows, total + self.above[z, rows].astype(F32))

        def lowest():
            for rows in self.rows:
                store(rows, self.own(z, rows) + self.above[z, rows].astype(F32))

        def highest():
            for rows in self.rows:
                store(rows, self.own(z, rows) + self.below[z, rows].astype(F32))

        pl.when((z > 0) & (z < planes - 1))(both)
        pl.when(z == 0)(lowest)
        pl.when(z == planes - 1)(highest)
        for i in range(planes - 1):
            pl.when(z < planes - 1 - i)(lambda i=i: self.upward(planes - 1 - i).wait_send())
            pl.when(z > i)(lambda i=i: self.downward(i).wait_send())


def row_tiles(count, size):
    return [pl.ds(at, size) for at in range(0, count, size)]


def in_scatter_kernel(
    planes, chips, left_ref, right_ref, grad_ref, out_ref, parts_ref,
    near_out, near_in, far_out, far_in, above, below, mine, *sems,
):
    here = place()
    z, c, core = here
    seqs = 2 * chips
    me = 2 * c + core
    near, far, up, down, swap_sems = [sems[2 * i : 2 * i + 2] for i in range(5)]
    barrier = pltpu.get_barrier_semaphore()
    peers = plane_peers(chips, here)
    greet(barrier, peers)
    greet_line(barrier, planes, here)
    pl.semaphore_wait(barrier, len(peers) + line_peers(planes, here))
    part = mine.shape[1]
    line = LineScatter(
        planes,
        here,
        row_tiles(seqs, 1),
        lambda t, rows: grad_ref[t, rows].astype(F32),
        above,
        below,
        up,
        down,
    )
    line.step(0)
    work = PlaneScatter(
        chips, here, left_ref, right_ref, True, near_out, near_in, far_out, far_in, near, far
    )
    work.start()
    for i in range(1, planes - 1):
        line.step(i)

    def store(rows, total):
        mine[rows] = total.astype(LOW)

    line.finish(store)
    swaps = [
        remote(mine.at[2 * device[1] + device[2]], parts_ref.at[me], swap_sems, k, device)
        for k, device in enumerate(peers, 1)
    ]
    for copy in swaps:
        copy.start()
    parts_ref[me] = mine[me]
    work.finish(out_ref)
    for k in range(1, seqs):
        swaps[k - 1].wait_send()
        index = lax.rem(me + seqs - k, seqs)
        remote(mine.at[0], parts_ref.at[index], swap_sems, k, here).wait_recv()


def in_scatter(planes, chips, left, right, grads):
    _, tokens, _ = left.shape
    width = right.shape[0]
    seqs = 2 * chips
    part, wide = grads.shape[2:]
    return call(
        functools.partial(in_scatter_kernel, planes, chips),
        "in_scatter",
        [shape((tokens, width), F32), shape((seqs, part, wide), LOW)],
        (left, right, grads),
        [VMEM] * 3,
        [VMEM] * 2,
        [
            *[pltpu.VMEM((chips, tokens, width), LOW)] * 4,
            *[pltpu.VMEM((planes, seqs, part, wide), LOW)] * 2,
            pltpu.VMEM((seqs, part, wide), LOW),
            *pairs_of(chips, chips, planes, planes, seqs),
        ],
        4,
    )


def line_gather_kernel(planes, x_ref, out_ref, *sems):
    here = place()
    z, c, core = here
    up, down, near = [sems[2 * i : 2 * i + 2] for i in range(3)]
    partner = (z, c, 1 - core)
    barrier = pltpu.get_barrier_semaphore()
    greet(barrier, [partner])
    greet_line(barrier, planes, here)
    pl.semaphore_wait(barrier, 1 + line_peers(planes, here))
    keep = pltpu.make_async_copy(x_ref, out_ref.at[z, core], sems[6].at[0])
    keep.start()
    keep.wait()

    def passed(t):
        return remote(out_ref.at[t, core], out_ref.at[t, core], near, t, partner)

    line = LineGather(planes, here, lambda t: out_ref.at[t, core], up, down)
    line.start()
    passed(z).start()
    for d in range(1, planes):
        line.step(d, lambda t: passed(t).start())
    line.finish()
    for t in range(planes):
        passed(t).wait_send()
        remote(x_ref, out_ref.at[t, 1 - core], near, t, partner).wait_recv()


def line_gather(planes, x_block):
    return call(
        functools.partial(line_gather_kernel, planes),
        "line_gather",
        shape((planes, 2, *x_block.shape), x_block.dtype),
        (x_block,),
        [HBM],
        HBM,
        [*pairs_of(planes, planes, planes), pltpu.SemaphoreType.DMA((1,))],
        5,
    )


def sums_kernel(planes, x_ref, out_ref, slots, *sems):
    here = place()
    z, c, core = here
    count = 2 * planes
    me = 2 * z + core
    barrier = pltpu.get_barrier_semaphore()
    ids = [lax.rem(me + k, count) for k in range(1, count)]
    peers = [(index // 2, c, lax.rem(index, 2)) for index in ids]
    greet(barrier, peers)
    pl.semaphore_wait(barrier, len(peers))
    copies = [remote(x_ref, slots.at[k], sems, k, device) for k, device in enumerate(peers, 1)]
    for copy in copies:
        copy.start()
    for copy in copies:
        copy.wait_send()
        copy.wait_recv()
    total = x_ref[...]
    for k in range(1, count):
        total = total + slots[k]
    out_ref[...] = total


def group_sums(planes, stats):
    return call(
        functools.partial(sums_kernel, planes),
        "group_sums",
        shape(stats.shape, F32),
        (stats,),
        [VMEM],
        VMEM,
        [pltpu.VMEM((2 * planes, *stats.shape), F32), *pairs_of(2 * planes)],
        6,
    )


class PairScatter:
    def __init__(self, planes, here, left, right, turned, near_out, near_in, own, line, near):
        self.planes, self.here = planes, here
        self.left, self.right, self.turned = left, right, turned
        self.near_out, self.near_in, self.own, self.near = near_out, near_in, own, near
        tokens, width = near_out.shape[1:]
        self.tiles = [pl.ds(at, COLUMNS) for at in range(0, width, COLUMNS)]
        self.line = LineScatter(
            planes,
            here,
            row_tiles(tokens, 32),
            lambda t, rows: own[t, rows].astype(F32),
            *line,
        )

    def near_copy(self, t):
        z, c, core = self.here
        return remote(self.near_out.at[t], self.near_in.at[t], self.near, t, (z, c, 1 - core))

    def start(self):
        core = self.here[2]
        order = []
        for i in range((self.planes + 1) // 2):
            order += [self.planes - 1 - i, i] if self.planes - 1 - i != i else [i]
        for t in order:
            left = self.left[t, 1 - core]
            for columns in self.tiles:
                part = product(left, self.right, columns, self.turned)
                self.near_out[t, :, columns] = part.astype(LOW)
            self.near_copy(t).start()
        for t in order:
            left = self.left[t, core]
            self.near_copy(t).wait_recv()
            for columns in self.tiles:
                part = product(left, self.right, columns, self.turned)
                self.own[t, :, columns] = (
                    part + self.near_in[t, :, columns].astype(F32)
                ).astype(LOW)
        self.line.step(0)

    def finish(self, out_ref):
        def store(rows, total):
            out_ref[rows] = total

        self.line.finish(store)
        for t in range(self.planes):
            self.near_copy(t).wait_send()

    @staticmethod
    def scratch(planes, tokens, width):
        return [pltpu.VMEM((planes, tokens, width), LOW)] * 5


def line_scatter_kernel(
    planes, chips, left_ref, right_ref, grad_ref, out_ref, slots_ref,
    near_out, near_in, own, above, below, *sems,
):
    here = place()
    z, c, core = here
    near, up, down, swap_sems = [sems[2 * i : 2 * i + 2] for i in range(4)]
    barrier = pltpu.get_barrier_semaphore()
    peers = [(z, c, 1 - core), *chip_peers(chips, here)]
    greet(barrier, peers)
    greet_line(barrier, planes, here)
    pl.semaphore_wait(barrier, len(peers) + line_peers(planes, here))
    swap = ChipSwap(chips, here, lambda index: grad_ref.at[index], slots_ref, swap_sems)
    swap.start(sems[8].at[0])
    work = PairScatter(
        planes, here, left_ref, right_ref, True, near_out, near_in, own,
        (above, below, up, down), near,
    )
    work.start()
    for i in range(1, planes - 1):
        work.line.step(i)
    work.finish(out_ref)
    swap.finish()


def line_scatter(planes, chips, left, right, grads):
    tokens, width = left.shape[2], right.shape[0]
    return call(
        functools.partial(line_scatter_kernel, planes, chips),
        "line_scatter",
        [shape((tokens, width), F32), shape(grads.shape, LOW)],
        (left, right, grads),
        [VMEM, VMEM, HBM],
        [VMEM, HBM],
        [
            *PairScatter.scratch(planes, tokens, width),
            *pairs_of(planes, planes, planes, chips),
            pltpu.SemaphoreType.DMA((1,)),
        ],
        7,
    )


def swap_lanes(values):
    lane = lax.broadcasted_iota(jnp.int32, values.shape, 1)
    return jnp.where(
        lax.rem(lane, 2) == 0,
        pltpu.roll(values, values.shape[1] - 1, 1),
        pltpu.roll(values, 1, 1),
    )


def twice(table):
    return jnp.concatenate([table, table], axis=1)


def turns(meta_ref, rows):
    cosine, sine, shrink = [twice(meta_ref[rows, pl.ds(i * HD, HD)]) for i in range(3)]
    return (cosine, sine, cosine * shrink, sine * shrink)


def allowed_block(meta_ref, rows, size, columns):
    query = rows + lax.broadcasted_iota(jnp.int32, (size, columns), 0)
    key = lax.broadcasted_iota(jnp.int32, (size, columns), 1)
    offset = meta_ref[pl.ds(rows, size), pl.ds(3 * HD, 1)].astype(jnp.int32)
    return (key <= query) & (key >= query - offset)


BLOCK = 256


def attention_kernel(heads, raw_ref, meta_ref, q_ref, k_ref, v_ref, out_ref, log_ref, wide):
    length = raw_ref.shape[0]
    span = heads * HD
    for rows in row_tiles(length, BLOCK):
        tables = turns(meta_ref, rows)
        for pair in range(heads // 2):
            lanes = pl.ds(2 * HD * pair, 2 * HD)
            query = raw_ref[rows, lanes]
            query = (query * tables[0] + swap_lanes(query) * tables[1]).astype(LOW)
            key = raw_ref[rows, pl.ds(span + 2 * HD * pair, 2 * HD)]
            key = (key * tables[2] + swap_lanes(key) * tables[3]).astype(LOW)
            value = raw_ref[rows, pl.ds(2 * span + 2 * HD * pair, 2 * HD)].astype(LOW)
            for half in range(2):
                at = slice(half * HD, (half + 1) * HD)
                q_ref[2 * pair + half, rows] = query[:, at]
                k_ref[2 * pair + half, rows] = key[:, at]
                v_ref[2 * pair + half, rows] = value[:, at]
    log_ref[...] = jnp.zeros(log_ref.shape, F32)

    def one_head(head, carry):
        for start in range(0, length, BLOCK):
            columns = start + BLOCK
            rows = pl.ds(start, BLOCK)
            scores = lax.dot_general(
                q_ref[head, rows],
                k_ref[head, pl.ds(0, columns)],
                (((1,), (1,)), ((), ())),
                preferred_element_type=F32,
            )
            allowed = allowed_block(meta_ref, start, BLOCK, columns)
            scores = jnp.where(allowed, scores, NEG_FILL)
            top = jnp.max(scores, axis=1, keepdims=True)
            shifted = jnp.exp(scores - top)
            total = jnp.sum(shifted, axis=1, keepdims=True)
            probs = (shifted * (1.0 / total)).astype(LOW)
            wide[head, rows] = jnp.dot(
                probs, v_ref[head, pl.ds(0, columns)], preferred_element_type=F32
            )
            lane = lax.broadcasted_iota(jnp.int32, (BLOCK, 128), 1)
            log_ref[rows] = jnp.where(lane == head, top + jnp.log(total), log_ref[rows])
        return carry

    lax.fori_loop(0, heads, one_head, 0)
    for rows in row_tiles(length, BLOCK):
        out_ref[rows] = jnp.concatenate(
            [wide[head, rows] for head in range(heads)], axis=1
        ).astype(LOW)


def attention(heads, raw, meta):
    length = raw.shape[0]
    return call(
        functools.partial(attention_kernel, heads),
        "attention",
        [
            *[shape((heads, length, HD), LOW)] * 3,
            shape((length, heads * HD), LOW),
            shape((length, 128), F32),
        ],
        (raw, meta),
        [VMEM] * 2,
        [VMEM] * 5,
        [pltpu.VMEM((heads, length, HD), F32)],
    )


def attention_back_kernel(
    planes, chips, heads,
    q_ref, k_ref, v_ref, att_ref, sub_ref, stat_ref, log_ref, meta_ref, left_ref, right_ref, up_ref,
    out_ref, normed_ref, ffn_ref, slots_ref,
    grad, dq, dk, dv, near_out, near_in, own, above, below, *sems,
):
    here = place()
    z, c, core = here
    near, up, down, swap_sems = [sems[2 * i : 2 * i + 2] for i in range(4)]
    barrier = pltpu.get_barrier_semaphore()
    peers = [(z, c, 1 - core), *chip_peers(chips, here)]
    greet(barrier, peers)
    greet_line(barrier, planes, here)
    pl.semaphore_wait(barrier, len(peers) + line_peers(planes, here))
    units = slots_ref.shape[2]
    swap = ChipSwap(
        chips, here, lambda index: column_block(up_ref, units, index), slots_ref, swap_sems
    )
    swap.start(sems[8].at[0])
    work = PairScatter(
        planes, here, left_ref, right_ref, False, near_out, near_in, own,
        (above, below, up, down), near,
    )
    work.start()
    length = att_ref.shape[0]
    span = heads * HD
    for rows in row_tiles(length, BLOCK):
        mean, scaler, first, second = (stat_ref[rows, pl.ds(i, 1)] for i in range(4))
        normed = (att_ref[rows].astype(F32) - mean) * scaler
        normed_ref[rows] = normed.astype(LOW)
        d_att = (scaler * (sub_ref[rows] - first - normed * second)).astype(LOW)
        for head in range(heads):
            grad[head, rows] = d_att[:, head * HD : (head + 1) * HD]
    dk[...] = jnp.zeros(dk.shape, F32)
    dv[...] = jnp.zeros(dv.shape, F32)

    def one_head(head, carry):
        for start in range(0, length, BLOCK):
            columns = start + BLOCK
            rows = pl.ds(start, BLOCK)
            keys = pl.ds(0, columns)
            query, key = q_ref[head, rows], k_ref[head, keys]
            out_grad = grad[head, rows]
            scores = lax.dot_general(
                query, key, (((1,), (1,)), ((), ())), preferred_element_type=F32
            )
            allowed = allowed_block(meta_ref, start, BLOCK, columns)
            lane = lax.broadcasted_iota(jnp.int32, (BLOCK, 128), 1)
            log_total = jnp.sum(
                jnp.where(lane == head, log_ref[rows], 0.0), axis=1, keepdims=True
            )
            probs = jnp.where(allowed, jnp.exp(scores - log_total), 0.0)
            d_probs = lax.dot_general(
                out_grad, v_ref[head, keys], (((1,), (1,)), ((), ())), preferred_element_type=F32
            )
            delta = jnp.sum(probs * d_probs, axis=1, keepdims=True)
            d_scores = (probs * (d_probs - delta)).astype(LOW)
            dq[head, rows] = jnp.dot(d_scores, key, preferred_element_type=F32)
            dk[head, keys] += token_product(d_scores, query)
            dv[head, keys] += token_product(probs.astype(LOW), out_grad)
        return carry

    first = 0
    for i in range(1, planes - 1):
        last = -(-heads * i // (planes - 1))
        lax.fori_loop(first, last, one_head, 0)
        first = last
        work.line.step(i)
    lax.fori_loop(first, heads, one_head, 0)
    for rows in row_tiles(length, BLOCK):
        tables = turns(meta_ref, rows)
        for pair in range(heads // 2):
            both = [
                jnp.concatenate(
                    [whole[2 * pair, rows], whole[2 * pair + 1, rows]], axis=1
                ).astype(LOW)
                for whole in (dq, dk, dv)
            ]
            query, key = both[0].astype(F32), both[1].astype(F32)
            query = query * tables[0] + swap_lanes(query * tables[1])
            key = key * tables[2] + swap_lanes(key * tables[3])
            out_ref[rows, pl.ds(2 * HD * pair, 2 * HD)] = query.astype(LOW)
            out_ref[rows, pl.ds(span + 2 * HD * pair, 2 * HD)] = key.astype(LOW)
            out_ref[rows, pl.ds(2 * span + 2 * HD * pair, 2 * HD)] = both[2]
    work.finish(ffn_ref)
    swap.finish()


def attention_back(planes, chips, heads, units, attention_args, left, right, up_grads):
    length, span = attention_args[3].shape
    tokens, width = left.shape[2], right.shape[1]
    return call(
        functools.partial(attention_back_kernel, planes, chips, heads),
        "attention_back",
        [
            shape((length, 3 * span), LOW),
            shape((length, span), LOW),
            shape((tokens, width), F32),
            shape((chips, width, units), LOW),
        ],
        (*attention_args, left, right, up_grads),
        [*[VMEM] * 10, HBM],
        [*[VMEM] * 3, HBM],
        [
            pltpu.VMEM((heads, length, HD), LOW),
            *[pltpu.VMEM((heads, length, HD), F32)] * 3,
            *PairScatter.scratch(planes, tokens, width),
            *pairs_of(planes, planes, planes, chips),
            pltpu.SemaphoreType.DMA((1,)),
        ],
        8,
    )


def body(
    hidden_in,
    segment_ids,
    position_ids,
    w_qkv,
    w_out,
    w_up,
    w_down,
    gain_attn,
    gain_attn_sub,
    gain_ffn,
    gain_ffn_sub,
    ema_qkv,
    ema_out,
    ema_up,
    ema_down,
    ema_gain_attn,
    ema_gain_attn_sub,
    ema_gain_ffn,
    ema_gain_ffn_sub,
    out_grad,
):
    _, tokens, width = hidden_in.shape
    planes, chips = lax.axis_size("dp"), lax.axis_size("chip")
    seqs = 2 * chips
    length = tokens * seqs
    heads = HEADS // seqs
    span = heads * HD
    part = w_qkv.shape[0]
    strided = part % HD == 0
    group_tokens = planes * 2 * tokens
    width_ff = w_down.shape[0] * planes * seqs
    seq_index = lax.axis_index(SEQ)

    def gain_rows(weight, gain):
        return (weight.astype(F32) * gain.astype(F32)[:, None]).astype(LOW)

    qkv_scaled = gain_rows(w_qkv, gain_attn)
    out_scaled = gain_rows(w_out, gain_attn_sub)
    down_scaled = gain_rows(w_down, gain_ffn_sub)
    if strided:
        qkv_send = qkv_scaled.reshape(part, 3, planes, seqs, HD).transpose(3, 0, 1, 2, 4)
    else:
        qkv_send = qkv_scaled.reshape(part, 3, seqs, span).transpose(2, 0, 1, 3)
    qkv_send = qkv_send.reshape(seqs, part, 3 * span)
    x_in = hidden_in[0].astype(F32)
    normed_one, scaler_one = moments(x_in)
    normed_low = normed_one.astype(LOW)
    gain_tile = jnp.zeros((8, 128), F32).at[0, :part].set(gain_ffn.astype(F32))

    row_in, meta, qkv_mine, out_mine, gain_tiles, up_mine = attention_gather(
        planes,
        chips,
        normed_low,
        token_tables(position_ids[0]),
        qkv_send,
        out_scaled,
        gain_tile,
        w_up,
    )
    if up_mine.ndim == 3:
        up_mine = up_mine.transpose(1, 0, 2).reshape(width, -1)
    row_in = row_in.reshape(length, width)
    meta = meta.reshape(length, -1)
    qkv_mine = qkv_mine.reshape(width, 3 * span)
    if strided:
        out_mine = out_mine.reshape(span, width)
    else:
        out_all = lax.all_gather(out_scaled, ALL, axis=0, tiled=True)
        out_mine = lax.dynamic_slice_in_dim(out_all, seq_index * span, span, axis=0)
    grad_low, gain_tiles = lax.optimization_barrier((out_grad[0], gain_tiles))
    grad_flat = lax.all_gather(grad_low, TP, axis=0, tiled=True)
    queries, keys, values, attended, log_total = attention(heads, dot(row_in, qkv_mine), meta)
    down_scaled, attended = lax.optimization_barrier((down_scaled, attended))
    down_mine = lax.all_gather(down_scaled, "chip", axis=0, tiled=True)
    attended_wide = attended.astype(F32)
    column_part = jnp.sum(out_mine.astype(F32), axis=0)
    token_sums = jnp.stack(
        [jnp.sum(attended_wide, axis=1), jnp.sum(attended_wide * attended_wide, axis=1)]
    ).reshape(2, seqs, tokens)
    tiles = jnp.concatenate(
        [
            jnp.swapaxes(token_sums, 0, 1),
            jnp.zeros((seqs, 6, tokens), F32),
            jnp.broadcast_to(column_part.reshape(1, -1, tokens), (seqs, width // tokens, tokens)),
        ],
        axis=1,
    )
    out_sum, tiles = out_scatter(chips, attended.reshape(seqs, tokens, span), out_mine, tiles)
    tiles = jnp.sum(tiles, axis=0)
    column_sum = tiles[8:].reshape(width)
    sums = tiles[:2].T
    gain_three = gain_tiles[:, 0, :part].reshape(width)
    mean_two = sums[:, :1] / width
    scaler_two = lax.rsqrt(sums[:, 1:] / width - mean_two * mean_two + NORM_EPS)
    projected = scaler_two * (out_sum - mean_two * column_sum[None, :])
    hmid = x_in + projected
    normed_three, scaler_three = moments(hmid)
    ffn_in = (normed_three * gain_three).astype(LOW)

    grad_top = grad_low.astype(F32)
    ffn_flat = line_gather(planes, ffn_in).reshape(group_tokens, width)
    weighted = rows_product(grad_flat, down_mine)
    up_slice = dot(ffn_flat, up_mine)
    activated, gelu_pull = jax.vjp(exact_gelu, up_slice)
    stats = group_sums(
        planes,
        jnp.stack(
            [
                jnp.sum(activated, axis=1),
                jnp.sum(activated * activated, axis=1),
                jnp.sum(weighted * activated, axis=1),
                jnp.sum(weighted, axis=1),
            ]
        ),
    )[:, :, None]
    act_mean = stats[0] / width_ff
    scaler_four = lax.rsqrt(stats[1] / width_ff - act_mean * act_mean + NORM_EPS)
    normed_four = (activated - act_mean) * scaler_four
    normed_four_low = normed_four.astype(LOW)
    first_mean = stats[3] / width_ff
    second_mean = scaler_four * (stats[2] - act_mean * stats[3]) / width_ff
    d_act = scaler_four * (weighted - first_mean - normed_four * second_mean)
    (d_up,) = gelu_pull(d_act)
    d_up_low = d_up.astype(LOW)
    grad_up = token_product(ffn_flat, d_up_low).astype(LOW)
    grad_down = token_product(normed_four_low, grad_flat).astype(LOW)
    units = w_up.shape[1]
    if units % 128:
        grad_up = grad_up.reshape(width, chips, units).transpose(1, 0, 2)
    d_up_low, grad_up = lax.optimization_barrier((d_up_low, grad_up))
    d_ffn_in, down_slots = line_scatter(
        planes,
        chips,
        d_up_low.reshape(planes, 2, tokens, -1),
        up_mine,
        grad_down.reshape(chips, -1, width),
    )

    gain_part = jnp.sum(d_ffn_in * normed_three, axis=0).reshape(planes * seqs, 1, part)
    gain_part = jnp.pad(gain_part, ((0, 0), (0, 7), (0, 128 - part)))
    d_hmid = grad_top + norm_back(d_ffn_in * gain_three, normed_three, scaler_three)
    d_hmid_low = d_hmid.astype(LOW)
    d_hmid_wide = d_hmid_low.astype(F32)
    first_two = jnp.sum(d_hmid_wide * column_sum[None, :], axis=1, keepdims=True) / width
    second_two = jnp.sum(d_hmid_wide * projected, axis=1, keepdims=True) / width
    token_stats = jnp.concatenate([mean_two, scaler_two, first_two, second_two], axis=1)
    row_grad, row_stats, gain_part = plane_gather(
        planes, chips, d_hmid_low, jnp.pad(token_stats, ((0, 0), (0, 124))), gain_part
    )
    row_grad = row_grad.reshape(length, width)
    row_stats = row_stats.reshape(length, 128)
    grad_gain_three = jnp.sum(gain_part, axis=0)[0, :part]
    d_sub = rows_product(row_grad, out_mine)
    d_qkv, normed_two, ffn_out, up_slots = attention_back(
        planes,
        chips,
        heads,
        units,
        (queries, keys, values, attended, d_sub, row_stats, log_total, meta),
        normed_four_low.reshape(planes, 2, tokens, -1),
        down_mine,
        grad_up,
    )
    output = (hmid + ffn_out).astype(LOW)[None]
    sum_up = jnp.sum(up_slots.astype(F32), axis=0)
    sum_down = jnp.sum(down_slots.astype(F32), axis=0)
    grad_out = token_product(normed_two, row_grad)
    grad_qkv = token_product(row_in, d_qkv).astype(LOW)
    d_in, part_qkv = in_scatter(
        planes,
        chips,
        d_qkv.reshape(seqs, tokens, 3 * span),
        qkv_mine,
        grad_qkv.reshape(planes, seqs, part, 3 * span),
    )
    input_grad = (d_hmid + norm_back(d_in, normed_one, scaler_one)).astype(LOW)[None]

    if strided:
        sum_qkv = part_qkv.reshape(seqs, part, 3, planes, HD).transpose(1, 2, 3, 0, 4)
        sum_out = lax.psum_scatter(grad_out.astype(LOW), "dp", scatter_dimension=0, tiled=True)
    else:
        sum_qkv = part_qkv.reshape(seqs, part, 3, span).transpose(1, 2, 0, 3)
        spread = lax.dynamic_update_slice_in_dim(
            jnp.zeros((width, width), LOW), grad_out.astype(LOW), seq_index * span, axis=0
        )
        sum_out = lax.psum_scatter(spread, ALL, scatter_dimension=0, tiled=True)
    sum_qkv = sum_qkv.reshape(part, 3 * width).astype(F32)
    sum_out = sum_out.astype(F32)

    def finish(total, weight, gain):
        wide = weight.astype(F32)
        return (total * gain.astype(F32)[:, None], jnp.sum(total * wide, axis=1))

    sum_qkv, grad_gain_one = finish(sum_qkv, w_qkv, gain_attn)
    sum_out, grad_gain_two = finish(sum_out, w_out, gain_attn_sub)
    sum_down, grad_gain_four = finish(sum_down, w_down, gain_ffn_sub)

    def averaged(average, weight):
        return EMA_DECAY * average + (1.0 - EMA_DECAY) * weight.astype(F32)

    return (
        output,
        input_grad,
        sum_qkv,
        sum_out,
        sum_up,
        sum_down,
        grad_gain_one,
        grad_gain_two,
        grad_gain_three,
        grad_gain_four,
        averaged(ema_qkv, w_qkv),
        averaged(ema_out, w_out),
        averaged(ema_up, w_up),
        averaged(ema_down, w_down),
        averaged(ema_gain_attn, gain_attn),
        averaged(ema_gain_attn_sub, gain_attn_sub),
        averaged(ema_gain_ffn, gain_ffn),
        averaged(ema_gain_ffn_sub, gain_ffn_sub),
    )


def solution(mesh):
    split = Mesh(
        mesh.devices.reshape(mesh.shape["dp"], mesh.shape["seq"] // 2, 2), ("dp", "chip", "core")
    )
    tokens = P("dp", SEQ, None)
    ids = P("dp", SEQ)
    rows = P(ALL, None)
    columns = P(None, ALL)
    vector = P(ALL)
    weights = (rows, rows, columns, rows)
    gains = (vector,) * 4
    return jax.shard_map(
        body,
        mesh=split,
        in_specs=(tokens, ids, ids, *weights, *gains, *weights, *gains, tokens),
        out_specs=(tokens, tokens, *weights, *gains, *weights, *gains),
        check_vma=False,
    )
```

time: 963 us -> 707 us (0.73)
  Pallas kernels: 0 us -> 530 us
  waiting for transfers between devices: 383 us -> 0.73 us
  blocking collectives: 160 us -> 0 us
  matrix products: 208 us -> 66 us
  local copies, waits for them, and re-layouts: 86.8 us -> 26.6 us
  starting transfers between devices: 16.5 us -> 0.58 us
  other arithmetic: 72.9 us -> 58.6 us
    pallas_call x0 -> x9, Pallas kernels: none -> 530 us  [call(): pl.pallas_call(kernel, name=name, out_shape=outs, in_specs=in_specs, out_...]
    reduce_scatter x7 -> x0, waiting for transfers between devices: 161 us -> none  [the longest x1 47.9 us: body(): lax.psum_scatter(dot(normed_four_low, down_mine).astype(LOW), TP, scatter...]
    all_gather x6 -> x0, waiting for transfers between devices: 128 us -> none  [the longest x1 43.9 us: body(): ffn_flat = lax.all_gather(ffn_in, TP, axis=0, tiled=True)]
    dot_general x14 -> x0, matrix products: 113 us -> none  [the longest x2 38.7 us: one_block(): jnp.einsum('hqk,qhd->khd', grad_scores, query_block, preferred_element_ty...]
    unnamed x2 -> x0, blocking collectives: 82.8 us -> none
    all_gather x1, waiting for transfers between devices: 47.7 us -> 0.01 us  [body(): grad_flat = lax.all_gather(grad_low, TP, axis=0, tiled=True)]
    all_gather x1, waiting for transfers between devices: 44.4 us -> 0.01 us  [body(): down_mine = lax.all_gather(down_scaled, 'chip', axis=0, tiled=True)]
    psum x2 -> x0, blocking collectives: 35 us -> none  [the longest x1 21.9 us: body(): lax.psum(jnp.stack([jnp.sum(activated, axis=1), jnp.sum(activated * activ...]
  transfers between devices with their start and end apart: 18 -> 3, of which waited for: 10 -> 0; matrix products, arithmetic and copies ran while one was open for 32% -> 7% of each run, Pallas kernels for 0% -> 35%
where the time goes in v2:
time: 707 us; the launch traced here: 698 us
  Pallas kernels  530 us (75%)
  matrix products  66 us (9%)
  other arithmetic  58.6 us (8%)
  local copies, waits for them, and re-layouts  26.6 us (4%)
  between operations  14.8 us (2%)
    pallas_call x9, Pallas kernels, call(): pl.pallas_call(kernel, name=name, out_shape=outs, in_specs=in_specs, out_...  530 us
    dot_general x2, matrix products, dot(): return jnp.dot(left_op, right_op, preferred_element_type=F32)  28.1 us
    dot_general x4, matrix products, token_product(): lax.dot_general(left_op, right_op, (((0,), (0,)), ((), ())), preferred_el...  23.5 us
    dot_general x2, matrix products, rows_product(): lax.dot_general(operand, weight_rows, (((1,), (1,)), ((), ())), preferred...  14.4 us
  transfers between devices with their start and end apart: 3, of which 0 were waited for; matrix products, arithmetic and copies ran while one was open for 7% of the time, Pallas kernels for 35%

profile of v2, /device:TPU:9, one launch (start us, length us, event | category | flops | bytes accessed | tf_op | source)
XLA Modules:
  0.0 697.5 jit_solution(7623787172455871303)
XLA Ops:
  13.6 2.2 fusion.19.x_ref
  20.0 1.7 reshape.312.qkv_ref
  27.5 93.0 %attention_gather.1 = (bf16[8,128,2048]{2,1,0:T(8,128)(2,1)}, f32[8,128,256]{2,1,0:T(8,128)}, bf16[4,8,64,768]{3,2,1,0:T(8,128)(2,1)}, bf16[4,64,2048]{2,1,0:T(8...) custom-call(bf16[128,2048]{1,0:T(8,128)(2,1)} %fusion.19.x_ref, f32[128,256]{1,0:T(8,128)} %pad_maximum_fusion.meta_ref, ...), custom_call_target="tpu_custom_call" | custom-call | tf_op jit(solution)/shard_map/attention_gather/pallas_call | solution.py:90
  120.5 8.3 %fusion.42.raw_ref = f32[1024,768]{1,0:T(8,128)} fusion(bf16[1024,2048]{1,0:T(8,128)(2,1)} %bitcast.145, bf16[2048,768]{1,0:T(8,128)(2,1)} %bitcast.119), kind=kOutput, calls=%fused_computation.132 | convolution fusion | flops 3221225472 | bytes 10485760 | tf_op jit(solution)/shard_map/dot_general | solution.py:62
  128.7 15.0 %attention.1 = (bf16[4,1024,64]{2,1,0:T(8,128)(2,1)}, bf16[4,1024,64]{2,1,0:T(8,128)(2,1)}, bf16[4,1024,64]{2,1,0:T(8,128)(2,1)}, bf16[1024,256]{1,0:T(8,128)(2,1)}, f32[1024,128]{1,0:T(8,128)}) custom-call(f32[1024,768]{1,0:T(8,128)} %fusion.42.raw_ref, f32[1024,256]{1,0:T(8,128)} %bitcast.115), custom_call_target="tpu_custom_call" | custom-call | tf_op jit(solution)/shard_map/attention/pallas_call | solution.py:90
  148.6 42.1 %out_scatter.1 = (f32[128,2048]{1,0:T(8,128)}, f32[8,24,128]{2,1,0:T(8,128)}) custom-call(bf16[8,128,256]{2,1,0:T(8,128)(2,1)} %bitcast.111, bf16[256,2048]{1,0:T(8,128)(2,1)} %bitcast.117, f32[8,24,128]{2,1,0:T(8,128)} %pad_maximum_fusion.1.tile_ref), custom_call_target="tpu_custom_call" | custom-call | tf_op jit(solution)/shard_map/out_scatter/pallas_call | solution.py:90
  195.7 87.3 %line_gather.1 = bf16[4,2,128,2048]{3,2,1,0:T(8,128)(2,1)} custom-call(bf16[128,2048]{1,0:T(8,128)(2,1)} %multiply_convert_fusion.x_ref), custom_call_target="tpu_custom_call" | custom-call | tf_op jit(solution)/shard_map/line_gather/pallas_call | solution.py:90
  286.3 10.0 %fusion.41 = (f32[1024]{0:T(1024)S(1)}, f32[1024,1024]{0,1:T(8,128)}) fusion(bf16[1024,2048]{1,0:T(8,128)(2,1)} %all-gather.3.cloned.1.call-done, bf16[1024,2048]{1,0:T(8,128)(2,1)} %all-gather.5.cloned.1.call-done.right_ref), kind=kOutput, calls=%fused_computation.131 | convolution fusion | flops 4296014848 | bytes 12587008 | tf_op jit(solution)/shard_map/dot_general | solution.py:66
  296.3 5.5 copy.71
  301.8 19.8 %fusion.36 = (f32[1024]{0:T(1024)S(1)}, f32[1024]{0:T(1024)S(1)}, f32[1024]{0:T(1024)S(1)}, f32[1024,1024]{1,0:T(8,128)}, f32[1024,1024]{1,0:T(8,128)}) fusion(f32[1024,1024]{1,0:T(8,128)} %copy.71, bf16[1024,2048]{1,0:T(8,128)(2,1)} %bitcast.112, bf16[2048,1024]{1,0:T(8,128)(2,1)} %get-tuple-element.74.right_ref), kind=kOutput, calls=%fused_computation.128 | convolution fusion | flops 4367315968 | bytes 20983808 | tf_op jit(solution)/shard_map/dot_general | solution.py:62
  322.3 12.1 %group_sums.1 = f32[4,1024]{1,0:T(4,128)} custom-call(f32[4,1024]{1,0:T(4,128)} %pad_maximum_fusion.2.x_ref), custom_call_target="tpu_custom_call" | custom-call | tf_op jit(solution)/shard_map/group_sums/pallas_call | solution.py:90
  335.4 5.6 fusion.6
  341.0 6.2 convolution_convert_fusion.1.up_ref
  347.2 6.5 convolution_convert_fusion
  353.7 63.7 %line_scatter.1 = (f32[128,2048]{1,0:T(8,128)}, bf16[4,256,2048]{2,1,0:T(8,128)(2,1)}) custom-call(bf16[4,2,128,1024]{3,2,1,0:T(8,128)(2,1)} %bitcast.109, bf16[2048,1024]{1,0:T(8,128)(2,1)} %get-tuple-element.74.right_ref, bf16[4,256,2048]{2,1,0:T(8,128)(2,1)} %bitcast.114), custom_call_target="tpu_custom_call" | custom-call | tf_op jit(solution)/shard_map/line_scatter/pallas_call | solution.py:90
  417.4 1.7 multiply_reduce_fusion.2
  419.1 3.0 fusion.27
  423.6 36.0 %plane_gather.1 = (bf16[8,128,2048]{2,1,0:T(8,128)(2,1)}, f32[8,128,128]{2,1,0:T(8,128)}, f32[32,8,128]{2,1,0:T(8,128)}) custom-call(bf16[128,2048]{1,0:T(8,128)(2,1)} %get-tuple-element.102.x_ref, f32[128,128]{1,0:T(8,128)} %pad.13.stat_ref, f32[32,8,128]{2,1,0:T(8,128)} %pad.14.tile_ref), custom_call_target="tpu_custom_call" | custom-call | tf_op jit(solution)/shard_map/plane_gather/pallas_call | solution.py:90
  459.7 4.5 fusion.43.sub_ref
  464.1 67.2 %attention_back.1 = (bf16[1024,768]{1,0:T(8,128)(2,1)}, bf16[1024,256]{1,0:T(8,128)(2,1)}, f32[128,2048]{1,0:T(8,128)}, bf16[4,2048,256]{2,1,0:T(8,128)(2,1)}) custom-call(bf16[4,1024,64]{2,1,0:T(8,128)(2,1)} %get-tuple-element.68.q_ref, bf16[4,1024,64]{2,1,0:T(8,128)(2,1)} %get-tuple-element.69.k_ref, bf16[4,1024,64]{2,1,0:T(8,128)(2,1)} %get-tuple-element.70.v_ref, ...), custom_call_target="tpu_custom_call" | custom-call | tf_op jit(solution)/shard_map/attention_back/pallas_call | solution.py:90
  531.4 3.4 convolution_convert_fusion.3
  534.8 7.4 %convolution_convert_fusion.2 = bf16[2048,768]{1,0:T(8,128)(2,1)} fusion(bf16[1024,2048]{1,0:T(8,128)(2,1)} %bitcast.146, bf16[1024,768]{1,0:T(8,128)(2,1)S(1)} %copy-done.18), kind=kOutput, calls=%fused_computation.25 | convolution fusion | flops 3222798336 | bytes 8912896 | tf_op jit(solution)/shard_map/dot_general | solution.py:72
  542.2 113.6 %in_scatter.1 = (f32[128,2048]{1,0:T(8,128)}, bf16[8,64,768]{2,1,0:T(8,128)(2,1)}) custom-call(bf16[8,128,768]{2,1,0:T(8,128)(2,1)} %bitcast.124, bf16[2048,768]{1,0:T(8,128)(2,1)} %bitcast.120, bf16[4,8,64,768]{3,2,1,0:T(8,128)(2,1)} %bitcast.121), custom_call_target="tpu_custom_call" | custom-call | tf_op jit(solution)/shard_map/in_scatter/pallas_call | solution.py:90
  655.9 3.7 reshape.329
  659.6 5.4 copy.74
  665.0 2.4 reshape.328
  667.4 2.1 fusion.37
  670.0 4.3 convert_reduce_fusion.1
  674.9 3.3 convert_reduce_fusion
  679.0 3.5 fusion.11
  682.6 3.0 fusion.8
  687.8 2.7 fusion.31
  (155 shorter events, 36.6 us)
Async XLA Ops:
  7.2 279.2 %all-gather.5.cloned.1.call-start = ((), (), s32[]{:S(2)}) async-start(), calls=%async_computation.2 | async-start | bytes 5242880 | tf_op jit(solution)/shard_map/all_gather | solution.py:1225
  16.4 5.3 copy-start.25
  17.8 5.9 copy-start.20
  128.7 15.0 %copy-start.6 = (bf16[256,2048]{1,0:T(8,128)(2,1)S(1)}, bf16[256,2048]{1,0:T(8,128)(2,1)}, u32[]{:S(2)}) copy-start(bf16[256,2048]{1,0:T(8,128)(2,1)} %param.27) | copy-start | bytes 3145732
  128.7 19.0 %copy-start.8 = (bf16[4,64,2048]{2,1,0:T(8,128)(2,1)S(1)}, bf16[4,64,2048]{2,1,0:T(8,128)(2,1)}, u32[]{:S(2)}) copy-start(bf16[4,64,2048]{2,1,0:T(8,128)(2,1)} %get-tuple-element.65) | copy-start | bytes 3145732
  143.7 49.0 %copy-start = (bf16[1,128,2048]{2,1,0:T(8,128)(2,1)S(1)}, bf16[1,128,2048]{2,1,0:T(8,128)(2,1)}, u32[]{:S(2)}) copy-start(bf16[1,128,2048]{2,1,0:T(8,128)(2,1)} %param.22) | copy-start | bytes 1572868
  144.9 141.4 %all-gather.3.cloned.1.call-start = ((), (), s32[]{:S(2)}) async-start(), calls=%async_computation.1 | async-start | bytes 4718592 | tf_op jit(solution)/shard_map/all_gather | solution.py:1222
  145.7 542.1 %reduce-scatter.2.cloned.1.call-start = ((), (), s32[]{:S(2)}) async-start(), calls=%async_computation.3 | async-start | bytes 1310720 | tf_op jit(solution)/shard_map/reduce_scatter | solution.py:1331
  194.3 88.7 %copy-start.35 = (bf16[64]{0:T(256)(128)(2,1)S(1)}, bf16[64]{0:T(256)(128)(2,1)}, u32[]{:S(2)}) copy-start(bf16[64]{0:T(256)(128)(2,1)} %param.28) | copy-start | bytes 388
  194.3 88.7 %copy-start.36 = (f32[64]{0:T(128)S(1)}, f32[64]{0:T(128)}, u32[]{:S(2)}) copy-start(f32[64]{0:T(128)} %param.36) | copy-start | bytes 772
  194.3 89.2 %copy-start.26 = (f32[256]{0:T(256)S(1)}, f32[256]{0:T(256)}, u32[]{:S(2)}) copy-start(f32[256]{0:T(256)} %param.39) | copy-start | bytes 3076
  194.4 89.2 %copy-start.27 = (bf16[256]{0:T(256)(128)(2,1)S(1)}, bf16[256]{0:T(256)(128)(2,1)}, u32[]{:S(2)}) copy-start(bf16[256]{0:T(256)(128)(2,1)} %param.31) | copy-start | bytes 1540
  194.4 89.8 %copy-start.28 = (bf16[64]{0:T(256)(128)(2,1)S(1)}, bf16[64]{0:T(256)(128)(2,1)}, u32[]{:S(2)}) copy-start(bf16[64]{0:T(256)(128)(2,1)} %param.29) | copy-start | bytes 388
  194.4 89.8 %copy-start.29 = (bf16[64]{0:T(256)(128)(2,1)S(1)}, bf16[64]{0:T(256)(128)(2,1)}, u32[]{:S(2)}) copy-start(bf16[64]{0:T(256)(128)(2,1)} %param.30) | copy-start | bytes 388
  194.4 89.8 %copy-start.30 = (f32[64]{0:T(128)S(1)}, f32[64]{0:T(128)}, u32[]{:S(2)}) copy-start(f32[64]{0:T(128)} %param.38) | copy-start | bytes 772
  194.4 89.8 %copy-start.31 = (f32[64]{0:T(128)S(1)}, f32[64]{0:T(128)}, u32[]{:S(2)}) copy-start(f32[64]{0:T(128)} %param.37) | copy-start | bytes 772
  194.4 90.3 %copy-start.4 = (bf16[2048,256]{1,0:T(8,128)(2,1)S(1)}, bf16[2048,256]{1,0:T(8,128)(2,1)}, u32[]{:S(2)}) copy-start(bf16[2048,256]{1,0:T(8,128)(2,1)} %up_ref.1) | copy-start | bytes 3145732
  194.4 90.3 %copy-start.16 = (f32[2048,256]{1,0:T(8,128)S(1)}, f32[2048,256]{1,0:T(8,128)}, u32[]{:S(2)}) copy-start(f32[2048,256]{1,0:T(8,128)} %param.34) | copy-start | bytes 6291460
  301.8 33.5 %copy-start.1 = (f32[1024,1024]{1,0:T(8,128)S(1)}, f32[1024,1024]{1,0:T(8,128)}, u32[]{:S(2)}) copy-start(f32[1024,1024]{1,0:T(8,128)} %copy.71) | copy-start | bytes 12582916
  335.3 5.6 copy-start.5
  340.9 6.3 copy-start.3
  340.9 6.2 copy-start.2
  341.0 6.2 copy-start.33
  353.7 65.4 %copy-start.10 = (f32[128,2048]{1,0:T(8,128)S(1)}, f32[128,2048]{1,0:T(8,128)}, u32[]{:S(2)}) copy-start(f32[128,2048]{1,0:T(8,128)} %get-tuple-element.67) | copy-start | bytes 3145732
  353.7 65.4 %copy-start.15 = (bf16[1,128,2048]{2,1,0:T(8,128)(2,1)S(1)}, bf16[1,128,2048]{2,1,0:T(8,128)(2,1)}, u32[]{:S(2)}) copy-start(bf16[1,128,2048]{2,1,0:T(8,128)(2,1)} %param.40) | copy-start | bytes 1572868
  417.4 42.3 %copy-start.9 = (bf16[4,64,2048]{2,1,0:T(8,128)(2,1)S(1)}, bf16[4,64,2048]{2,1,0:T(8,128)(2,1)}, u32[]{:S(2)}) copy-start(bf16[4,64,2048]{2,1,0:T(8,128)(2,1)} %get-tuple-element.65) | copy-start | bytes 3145732
  464.1 67.3 %copy-start.34 = (bf16[8,128,2048]{2,1,0:T(8,128)(2,1)S(1)}, bf16[8,128,2048]{2,1,0:T(8,128)(2,1)}, u32[]{:S(2)}) copy-start(bf16[8,128,2048]{2,1,0:T(8,128)(2,1)} %get-tuple-element.78) | copy-start | bytes 12582916
  667.4 6.9 copy-start.22
  674.4 4.7 copy-start.13
  674.4 4.7 copy-start.17
  678.2 4.3 copy-start.7
  678.2 4.3 copy-start.14
  (8 other events, 25.0 us)
Sparse Core Ops, SparseCore 0:
  145.1 74.3 all-gather.4
  221.1 56.8 all-gather.2
  534.9 37.7 reduce-scatter.1

commit v3 on v2

--- a/solution.py
+++ b/solution.py
@@ -228,54 +228,100 @@
 
 
 class LineGather:
-    def __init__(self, planes, here, block, up, down):
-        self.planes, self.here, self.block = planes, here, block
+    def __init__(self, planes, here, parts, up, down):
+        self.planes, self.here, self.parts = planes, here, parts
         self.up, self.down = up, down
-
-    def upward(self, d):
+        self.count = len(parts(here[0]))
+
+    def upward(self, d, p):
         z, c, core = self.here
-        block = self.block(z - d)
-        return remote(block, block, self.up, d, (z + 1, c, core))
-
-    def downward(self, d):
+        block = self.parts(z - d)[p]
+        return remote(block, block, self.up, d * self.count + p, (z + 1, c, core))
+
+    def downward(self, d, p):
         z, c, core = self.here
-        block = self.block(z + d)
-        return remote(block, block, self.down, d, (z - 1, c, core))
-
-    def each(self, d, act_up, act_down):
+        block = self.parts(z + d)[p]
+        return remote(block, block, self.down, d * self.count + p, (z - 1, c, core))
+
+    def each(self, d, p, act):
         z, planes = self.here[0], self.planes
-        pl.when((z < planes - 1) & (z - d >= 0))(lambda: act_up(self.upward(d)))
-        pl.when((z > 0) & (z + d < planes))(lambda: act_down(self.downward(d)))
+        pl.when((z < planes - 1) & (z - d >= 0))(lambda: act(self.upward(d, p)))
+        pl.when((z > 0) & (z + d < planes))(lambda: act(self.downward(d, p)))
 
     def start(self):
-        self.each(0, lambda copy: copy.start(), lambda copy: copy.start())
+        for p in range(self.count):
+            self.each(0, p, lambda copy: copy.start())
 
     def step(self, d, arrived=None):
-        z, c, core = self.here
-        planes = self.planes
-
-        def below():
-            block = self.block(z - d)
-            remote(block, block, self.up, d - 1, (z, c, core)).wait_recv()
+        z, planes = self.here[0], self.planes
+
+        def below(p):
+            block = self.parts(z - d)[p]
+            remote(block, block, self.up, (d - 1) * self.count + p, self.here).wait_recv()
             if d < planes - 1:
-                pl.when(z < planes - 1)(lambda: self.upward(d).start())
+                pl.when(z < planes - 1)(lambda: self.upward(d, p).start())
             if arrived is not None:
-                arrived(z - d)
-
-        def above():
-            block = self.block(z + d)
-            remote(block, block, self.down, d - 1, (z, c, core)).wait_recv()
+                arrived(z - d, p)
+
+        def above(p):
+            block = self.parts(z + d)[p]
+            remote(block, block, self.down, (d - 1) * self.count + p, self.here).wait_recv()
             if d < planes - 1:
-                pl.when(z > 0)(lambda: self.downward(d).start())
+                pl.when(z > 0)(lambda: self.downward(d, p).start())
             if arrived is not None:
-                arrived(z + d)
-
-        pl.when(z - d >= 0)(below)
-        pl.when(z + d < planes)(above)
+                arrived(z + d, p)
+
+        for p in range(self.count):
+            pl.when(z - d >= 0)(lambda p=p: below(p))
+            pl.when(z + d < planes)(lambda p=p: above(p))
 
     def finish(self):
         for d in range(self.planes - 1):
-            self.each(d, lambda copy: copy.wait_send(), lambda copy: copy.wait_send())
+            for p in range(self.count):
+                self.each(d, p, lambda copy: copy.wait_send())
+
+
+class GroupGather:
+    PARTS = 2
+
+    def __init__(self, planes, here, block, out, up, down, near):
+        self.planes, self.here, self.block, self.out, self.near = planes, here, block, out, near
+        self.partner = (here[0], here[1], 1 - here[2])
+        size = block.shape[0] // self.PARTS
+        self.slices = [pl.ds(p * size, size) for p in range(self.PARTS)]
+        core = here[2]
+        self.line = LineGather(planes, here, lambda t: self.parts(t, core), up, down)
+
+    def parts(self, t, core):
+        return [self.out.at[t, core, rows] for rows in self.slices]
+
+    def passed(self, t, p):
+        block = self.parts(t, self.here[2])[p]
+        return remote(block, block, self.near, t * self.PARTS + p, self.partner)
+
+    def start(self, local):
+        z, _, core = self.here
+        keep = pltpu.make_async_copy(self.block, self.out.at[z, core], local)
+        keep.start()
+        keep.wait()
+        self.line.start()
+        for p in range(self.PARTS):
+            self.passed(z, p).start()
+
+    def step(self, d):
+        self.line.step(d, lambda t, p: self.passed(t, p).start())
+
+    def finish(self):
+        self.line.finish()
+        for t in range(self.planes):
+            for p in range(self.PARTS):
+                self.passed(t, p).wait_send()
+                block = self.parts(t, 1 - self.here[2])[p]
+                remote(block, block, self.near, t * self.PARTS + p, self.partner).wait_recv()
+
+    @classmethod
+    def sems(cls, planes):
+        return pairs_of(*[planes * cls.PARTS] * 3)
 
 
 def attention_gather_kernel(
@@ -348,8 +394,11 @@
     for k in range(1, seqs):
         index = lax.rem(me + seqs - k, seqs)
         remote(qkv_ref.at[0], qkvs_ref.at[z, index], swap_sems, k, here).wait_recv()
-    line = LineGather(planes, here, lambda t: qkvs_ref.at[t], up, down)
-    line_two = LineGather(planes, here, lambda t: outs_ref.at[t], up_two, down_two)
+    half = seqs // 2
+    line = LineGather(
+        planes, here, lambda t: [qkvs_ref.at[t, pl.ds(i * half, half)] for i in range(2)], up, down
+    )
+    line_two = LineGather(planes, here, lambda t: [outs_ref.at[t]], up_two, down_two)
     line.start()
     line_two.start()
     rows.forward()
@@ -402,91 +451,12 @@
         [HBM] * 6,
         [HBM] * 6,
         [
-            *pairs_of(seqs, *[chips] * 4, *[planes] * 4, planes * seqs, chips),
+            *pairs_of(
+                seqs, *[chips] * 4, *[2 * planes] * 2, *[planes] * 2, planes * seqs, chips
+            ),
             pltpu.SemaphoreType.DMA((6,)),
         ],
         1,
-    )
-
-
-def plane_gather_kernel(
-    planes, chips, x_ref, stat_ref, tile_ref, row_ref, stats_ref, tiles_ref, *sems
-):
-    here = place()
-    z, c, core = here
-    seqs = 2 * chips
-    count = planes * seqs
-    me = 2 * c + core
-    flat = z * seqs + me
-    x_far, x_near, s_far, s_near, tile_sems = [sems[2 * i : 2 * i + 2] for i in range(5)]
-    local = sems[10]
-    barrier = pltpu.get_barrier_semaphore()
-
-    def device_of(k):
-        other = lax.rem(flat + k, count)
-        return (other // seqs, lax.rem(other, seqs) // 2, lax.rem(other, 2))
-
-    def signal(k, carry):
-        greet(barrier, [device_of(k)])
-        return carry
-
-    lax.fori_loop(1, count, signal, 0)
-    pl.semaphore_wait(barrier, count - 1)
-    rows = PlaneGather(chips, here, x_ref, row_ref, x_far, x_near)
-    stats = PlaneGather(chips, here, stat_ref, stats_ref, s_far, s_near)
-    rows.start()
-    stats.start()
-    keeps = [
-        pltpu.make_async_copy(x_ref, row_ref.at[me], local.at[0]),
-        pltpu.make_async_copy(stat_ref, stats_ref.at[me], local.at[1]),
-        pltpu.make_async_copy(tile_ref.at[flat], tiles_ref.at[flat], local.at[2]),
-    ]
-    for copy in keeps:
-        copy.start()
-
-    def tile_copy(k):
-        other = lax.rem(flat + k, count)
-        return remote(tile_ref.at[other], tiles_ref.at[flat], tile_sems, k, device_of(k))
-
-    def tile_start(k, carry):
-        tile_copy(k).start()
-        return carry
-
-    lax.fori_loop(1, count, tile_start, 0)
-    rows.forward()
-    stats.forward()
-    rows.finish()
-    stats.finish()
-    for copy in keeps:
-        copy.wait()
-
-    def tile_wait(k, carry):
-        tile_copy(k).wait_send()
-        other = lax.rem(flat + count - k, count)
-        remote(tile_ref.at[0], tiles_ref.at[other], tile_sems, k, here).wait_recv()
-        return carry
-
-    lax.fori_loop(1, count, tile_wait, 0)
-
-
-def plane_gather(planes, chips, x_block, stats, tiles):
-    seqs = 2 * chips
-    return call(
-        functools.partial(plane_gather_kernel, planes, chips),
-        "plane_gather",
-        [
-            shape((seqs, *x_block.shape), x_block.dtype),
-            shape((seqs, *stats.shape), stats.dtype),
-            shape(tiles.shape, tiles.dtype),
-        ],
-        (x_block, stats, tiles),
-        [HBM] * 3,
-        [HBM] * 3,
-        [
-            *pairs_of(chips, chips, chips, chips, planes * seqs),
-            pltpu.SemaphoreType.DMA((3,)),
-        ],
-        2,
     )
 
 
@@ -502,87 +472,109 @@
 
 
 class PlaneScatter:
-    def __init__(self, chips, here, left, right, turned, near_out, near_in, far_out, far_in, near, far):
+    def __init__(self, chips, here, left, right, turned, buffers, near, far):
         self.chips, self.here = chips, here
         self.left, self.right, self.turned = left, right, turned
-        self.near_out, self.near_in, self.far_out, self.far_in = near_out, near_in, far_out, far_in
+        self.near_out, self.near_in, self.far_out, self.far_in = buffers
         self.near, self.far = near, far
-        self.width = near_out.shape[-1]
+        self.tokens, width = self.near_out.shape[1:]
+        self.tiles = [pl.ds(at, COLUMNS) for at in range(0, width, COLUMNS)]
+        self.order = [*range(1, chips), 0]
 
     def target(self, k):
         return lax.rem(self.here[1] + k, self.chips)
 
-    def near_copy(self, k):
+    def near_copy(self, i):
         z, c, core = self.here
-        return remote(self.near_out.at[k], self.near_in.at[k], self.near, k, (z, c, 1 - core))
-
-    def far_copy(self, k):
+        at = (slice(None), slice(None), self.tiles[i])
+        return remote(self.near_out.at[at], self.near_in.at[at], self.near, i, (z, c, 1 - core))
+
+    def far_copy(self, k, i):
         z, _, core = self.here
-        return remote(self.far_out.at[k], self.far_in.at[k], self.far, k, (z, self.target(k), core))
-
-    def tiles(self):
-        return [pl.ds(at, COLUMNS) for at in range(0, self.width, COLUMNS)]
+        at = (k, slice(None), self.tiles[i])
+        index = k * len(self.tiles) + i
+        return remote(
+            self.far_out.at[at], self.far_in.at[at], self.far, index, (z, self.target(k), core)
+        )
+
+    def rows(self, position):
+        return slice(position * self.tokens, (position + 1) * self.tokens)
 
     def start(self):
         core = self.here[2]
-        order = [*range(1, self.chips), 0]
-        for k in order:
-            left = self.left[2 * self.target(k) + 1 - core]
-            for columns in self.tiles():
-                part = product(left, self.right, columns, self.turned)
-                self.near_out[k, :, columns] = part.astype(LOW)
-            self.near_copy(k).start()
-        for k in order:
-            left = self.left[2 * self.target(k) + core]
-            self.near_copy(k).wait_recv()
-            for columns in self.tiles():
-                part = product(left, self.right, columns, self.turned)
+        blocks = [self.left[2 * self.target(k) + 1 - core] for k in self.order]
+        left = jnp.concatenate(blocks, axis=0)
+        for i, columns in enumerate(self.tiles):
+            part = product(left, self.right, columns, self.turned).astype(LOW)
+            for position, k in enumerate(self.order):
+                self.near_out[k, :, columns] = part[self.rows(position)]
+            self.near_copy(i).start()
+        blocks = [self.left[2 * self.target(k) + core] for k in self.order]
+        left = jnp.concatenate(blocks, axis=0)
+        for i, columns in enumerate(self.tiles):
+            part = product(left, self.right, columns, self.turned)
+            self.near_copy(i).wait_recv()
+            for position, k in enumerate(self.order):
                 self.far_out[k, :, columns] = (
-                    part + self.near_in[k, :, columns].astype(F32)
+                    part[self.rows(position)] + self.near_in[k, :, columns].astype(F32)
                 ).astype(LOW)
-            if k:
-                self.far_copy(k).start()
+                if k:
+                    self.far_copy(k, i).start()
 
     def finish(self, out_ref):
-        for k in range(1, self.chips):
-            self.far_copy(k).wait_recv()
-        for columns in self.tiles():
+        for i, columns in enumerate(self.tiles):
             total = self.far_out[0, :, columns].astype(F32)
             for k in range(1, self.chips):
+                self.far_copy(k, i).wait_recv()
                 total = total + self.far_in[k, :, columns].astype(F32)
             out_ref[:, columns] = total
-        for k in range(self.chips):
-            self.near_copy(k).wait_send()
-        for k in range(1, self.chips):
-            self.far_copy(k).wait_send()
+        for i in range(len(self.tiles)):
+            self.near_copy(i).wait_send()
+            for k in range(1, self.chips):
+                self.far_copy(k, i).wait_send()
+
+    @staticmethod
+    def scratch(chips, tokens, width):
+        return [pltpu.VMEM((chips, tokens, width), LOW)] * 4
+
+    @staticmethod
+    def sems(chips, width):
+        return pairs_of(width // COLUMNS, chips * (width // COLUMNS))
 
 
 def out_scatter_kernel(
-    chips, left_ref, right_ref, tile_ref, out_ref, tiles_ref,
+    planes, chips, left_ref, right_ref, tile_ref, grad_ref, out_ref, tiles_ref, grads_ref,
     near_out, near_in, far_out, far_in, *sems,
 ):
     here = place()
     z, c, core = here
     seqs = 2 * chips
     me = 2 * c + core
-    near, far, tile_sems = [sems[2 * i : 2 * i + 2] for i in range(3)]
+    near, far, tile_sems, up, down, pair = [sems[2 * i : 2 * i + 2] for i in range(6)]
+    local = sems[12]
     barrier = pltpu.get_barrier_semaphore()
     peers = plane_peers(chips, here)
     greet(barrier, peers)
-    pl.semaphore_wait(barrier, len(peers))
+    greet_line(barrier, planes, here)
+    pl.semaphore_wait(barrier, len(peers) + line_peers(planes, here))
+    group = GroupGather(planes, here, grad_ref, grads_ref, up, down, pair)
+    group.start(local.at[0])
     swaps = [
         remote(tile_ref.at[2 * device[1] + device[2]], tiles_ref.at[me], tile_sems, k, device)
         for k, device in enumerate(peers, 1)
     ]
     for copy in swaps:
         copy.start()
-    keep = pltpu.make_async_copy(tile_ref.at[me], tiles_ref.at[me], sems[6].at[0])
+    keep = pltpu.make_async_copy(tile_ref.at[me], tiles_ref.at[me], local.at[1])
     keep.start()
     work = PlaneScatter(
-        chips, here, left_ref, right_ref, False, near_out, near_in, far_out, far_in, near, far
+        chips, here, left_ref, right_ref, False, (near_out, near_in, far_out, far_in), near, far
     )
     work.start()
+    for d in range(1, planes):
+        group.step(d)
     work.finish(out_ref)
+    group.finish()
     keep.wait()
     for k in range(1, seqs):
         swaps[k - 1].wait_send()
@@ -590,106 +582,125 @@
         remote(tile_ref.at[0], tiles_ref.at[index], tile_sems, k, here).wait_recv()
 
 
-def out_scatter(chips, left, right, tiles):
+def out_scatter(planes, chips, left, right, tiles, grad):
     _, tokens, _ = left.shape
     width = right.shape[1]
     return call(
-        functools.partial(out_scatter_kernel, chips),
+        functools.partial(out_scatter_kernel, planes, chips),
         "out_scatter",
-        [shape((tokens, width), F32), shape(tiles.shape, F32)],
-        (left, right, tiles),
-        [VMEM, VMEM, VMEM],
-        [VMEM, VMEM],
         [
-            *[pltpu.VMEM((chips, tokens, width), LOW)] * 4,
-            *pairs_of(chips, chips, 2 * chips),
-            pltpu.SemaphoreType.DMA((1,)),
+            shape((tokens, width), F32),
+            shape(tiles.shape, F32),
+            shape((planes, 2, *grad.shape), LOW),
+        ],
+        (left, right, tiles, grad),
+        [VMEM, VMEM, VMEM, HBM],
+        [VMEM, VMEM, HBM],
+        [
+            *PlaneScatter.scratch(chips, tokens, width),
+            *PlaneScatter.sems(chips, width),
+            *pairs_of(2 * chips),
+            *GroupGather.sems(planes),
+            pltpu.SemaphoreType.DMA((2,)),
         ],
         3,
     )
 
 
 class LineScatter:
-    def __init__(self, planes, here, rows, own, above, below, up, down):
-        self.planes, self.here, self.rows, self.own = planes, here, rows, own
+    def __init__(self, planes, here, parts, own, above, below, up, down):
+        self.planes, self.here, self.parts, self.own = planes, here, parts, own
         self.above, self.below, self.up, self.down = above, below, up, down
 
-    def upward(self, t):
+    def upward(self, t, p):
         z, c, core = self.here
-        return remote(self.below.at[t], self.below.at[t], self.up, t, (z + 1, c, core))
-
-    def downward(self, t):
+        block = self.below.at[(t, *self.parts[p][0])]
+        return remote(block, block, self.up, t * len(self.parts) + p, (z + 1, c, core))
+
+    def downward(self, t, p):
         z, c, core = self.here
-        return remote(self.above.at[t], self.above.at[t], self.down, t, (z - 1, c, core))
-
-    def add(self, slot, t, fresh):
-        for rows in self.rows:
-            total = self.own(t, rows)
+        block = self.above.at[(t, *self.parts[p][0])]
+        return remote(block, block, self.down, t * len(self.parts) + p, (z - 1, c, core))
+
+    def add(self, slot, t, p, fresh):
+        for tile in self.parts[p][1]:
+            total = self.own(t, tile)
             if not fresh:
-                total = total + slot[t, rows].astype(F32)
-            slot[t, rows] = total.astype(LOW)
+                total = total + slot[(t, *tile)].astype(F32)
+            slot[(t, *tile)] = total.astype(LOW)
 
     def step(self, i):
         z, planes = self.here[0], self.planes
         top, low = planes - 1 - i, i
 
-        def rise():
+        def rise(p):
             @pl.when(z > 0)
             def _():
-                self.upward(top).wait_recv()
-                self.add(self.below, top, False)
+                self.upward(top, p).wait_recv()
+                self.add(self.below, top, p, False)
 
             @pl.when(z == 0)
             def _():
-                self.add(self.below, top, True)
-
-            self.upward(top).start()
-
-        def fall():
+                self.add(self.below, top, p, True)
+
+            self.upward(top, p).start()
+
+        def fall(p):
             @pl.when(z < planes - 1)
             def _():
-                self.downward(low).wait_recv()
-                self.add(self.above, low, False)
+                self.downward(low, p).wait_recv()
+                self.add(self.above, low, p, False)
 
             @pl.when(z == planes - 1)
             def _():
-                self.add(self.above, low, True)
-
-            self.downward(low).start()
-
-        pl.when(z < top)(rise)
-        pl.when(z > low)(fall)
+                self.add(self.above, low, p, True)
+
+            self.downward(low, p).start()
+
+        for p in range(len(self.parts)):
+            pl.when(z < top)(lambda p=p: rise(p))
+            pl.when(z > low)(lambda p=p: fall(p))
 
     def finish(self, store):
         z, planes = self.here[0], self.planes
 
-        @pl.when(z > 0)
-        def _():
-            self.upward(z).wait_recv()
-
-        @pl.when(z < planes - 1)
-        def _():
-            self.downward(z).wait_recv()
-
-        def both():
-            for rows in self.rows:
-                total = self.own(z, rows) + self.below[z, rows].astype(F32)
-                store(rows, total + self.above[z, rows].astype(F32))
-
-        def lowest():
-            for rows in self.rows:
-                store(rows, self.own(z, rows) + self.above[z, rows].astype(F32))
-
-        def highest():
-            for rows in self.rows:
-                store(rows, self.own(z, rows) + self.below[z, rows].astype(F32))
-
-        pl.when((z > 0) & (z < planes - 1))(both)
-        pl.when(z == 0)(lowest)
-        pl.when(z == planes - 1)(highest)
+        def total(tile, *slots):
+            value = self.own(z, tile)
+            for slot in slots:
+                value = value + slot[(z, *tile)].astype(F32)
+            store(tile, value)
+
+        for p, (_, tiles) in enumerate(self.parts):
+
+            @pl.when(z > 0)
+            def _(p=p):
+                self.upward(z, p).wait_recv()
+
+            @pl.when(z < planes - 1)
+            def _(p=p):
+                self.downward(z, p).wait_recv()
+
+            @pl.when((z > 0) & (z < planes - 1))
+            def _(tiles=tiles):
+                for tile in tiles:
+                    total(tile, self.below, self.above)
+
+            @pl.when(z == 0)
+            def _(tiles=tiles):
+                for tile in tiles:
+                    total(tile, self.above)
+
+            @pl.when(z == planes - 1)
+            def _(tiles=tiles):
+                for tile in tiles:
+                    total(tile, self.below)
+
         for i in range(planes - 1):
-            pl.when(z < planes - 1 - i)(lambda i=i: self.upward(planes - 1 - i).wait_send())
-            pl.when(z > i)(lambda i=i: self.downward(i).wait_send())
+            for p in range(len(self.parts)):
+                pl.when(z < planes - 1 - i)(
+                    lambda i=i, p=p: self.upward(planes - 1 - i, p).wait_send()
+                )
+                pl.when(z > i)(lambda i=i, p=p: self.downward(i, p).wait_send())
 
 
 def row_tiles(count, size):
@@ -697,25 +708,26 @@
 
 
 def in_scatter_kernel(
-    planes, chips, left_ref, right_ref, grad_ref, out_ref, parts_ref,
-    near_out, near_in, far_out, far_in, above, below, mine, *sems,
+    planes, chips, heads, strided, left_ref, right_ref, grad_ref, up_ref, weight_ref, gain_ref,
+    out_ref, total_ref, gains_ref, slots_ref,
+    near_out, near_in, far_out, far_in, above, below, mine, parts, *sems,
 ):
     here = place()
     z, c, core = here
     seqs = 2 * chips
     me = 2 * c + core
-    near, far, up, down, swap_sems = [sems[2 * i : 2 * i + 2] for i in range(5)]
+    near, far, up, down, swap_sems, chip_sems = [sems[2 * i : 2 * i + 2] for i in range(6)]
     barrier = pltpu.get_barrier_semaphore()
     peers = plane_peers(chips, here)
     greet(barrier, peers)
     greet_line(barrier, planes, here)
     pl.semaphore_wait(barrier, len(peers) + line_peers(planes, here))
-    part = mine.shape[1]
+    half = seqs // 2
     line = LineScatter(
         planes,
         here,
-        row_tiles(seqs, 1),
-        lambda t, rows: grad_ref[t, rows].astype(F32),
+        [((pl.ds(p * half, half),), [(pl.ds(p * half + i, 1),) for i in range(half)]) for p in range(2)],
+        lambda t, tile: grad_ref[(t, *tile)].astype(F32),
         above,
         below,
         up,
@@ -723,47 +735,77 @@
     )
     line.step(0)
     work = PlaneScatter(
-        chips, here, left_ref, right_ref, True, near_out, near_in, far_out, far_in, near, far
+        chips, here, left_ref, right_ref, True, (near_out, near_in, far_out, far_in), near, far
     )
     work.start()
+    units = slots_ref.shape[2]
+    ups = ChipSwap(
+        chips, here, lambda index: column_block(up_ref, units, index), slots_ref, chip_sems
+    )
+    ups.start(sems[12].at[0])
     for i in range(1, planes - 1):
         line.step(i)
 
-    def store(rows, total):
-        mine[rows] = total.astype(LOW)
+    def store(tile, total):
+        mine[tile] = total.astype(LOW)
 
     line.finish(store)
     swaps = [
-        remote(mine.at[2 * device[1] + device[2]], parts_ref.at[me], swap_sems, k, device)
+        remote(mine.at[2 * device[1] + device[2]], parts.at[me], swap_sems, k, device)
         for k, device in enumerate(peers, 1)
     ]
     for copy in swaps:
         copy.start()
-    parts_ref[me] = mine[me]
+    parts[me] = mine[me]
     work.finish(out_ref)
     for k in range(1, seqs):
         swaps[k - 1].wait_send()
         index = lax.rem(me + seqs - k, seqs)
-        remote(mine.at[0], parts_ref.at[index], swap_sems, k, here).wait_recv()
-
-
-def in_scatter(planes, chips, left, right, grads):
+        remote(mine.at[0], parts.at[index], swap_sems, k, here).wait_recv()
+    span = heads * HD
+    width = seqs * span
+    gain = gain_ref[:, pl.ds(0, 1)]
+    summed = jnp.zeros(gain.shape, F32)
+    for i in range(3):
+        step, pieces = (seqs * HD, planes) if strided else (width, 1)
+        size = step // seqs
+        for piece in range(pieces):
+            at = i * span + piece * size
+            columns = pl.ds(i * width + piece * step, step)
+            total = jnp.concatenate(
+                [parts[s, :, pl.ds(at, size)].astype(F32) for s in range(seqs)], axis=1
+            )
+            weight = weight_ref[:, columns].astype(F32)
+            summed = summed + jnp.sum(total * weight, axis=1, keepdims=True)
+            total_ref[:, columns] = total * gain
+    gains_ref[...] = jnp.broadcast_to(summed, gains_ref.shape)
+    ups.finish()
+
+
+def in_scatter(planes, chips, heads, strided, left, right, grads, up_grads, weight, gain, units):
     _, tokens, _ = left.shape
     width = right.shape[0]
     seqs = 2 * chips
     part, wide = grads.shape[2:]
     return call(
-        functools.partial(in_scatter_kernel, planes, chips),
+        functools.partial(in_scatter_kernel, planes, chips, heads, strided),
         "in_scatter",
-        [shape((tokens, width), F32), shape((seqs, part, wide), LOW)],
-        (left, right, grads),
-        [VMEM] * 3,
-        [VMEM] * 2,
         [
-            *[pltpu.VMEM((chips, tokens, width), LOW)] * 4,
+            shape((tokens, width), F32),
+            shape(weight.shape, F32),
+            shape((part, 128), F32),
+            shape((chips, width, units), LOW),
+        ],
+        (left, right, grads, up_grads, weight, gain),
+        [VMEM, VMEM, VMEM, HBM, VMEM, VMEM],
+        [VMEM, VMEM, VMEM, HBM],
+        [
+            *PlaneScatter.scratch(chips, tokens, width),
             *[pltpu.VMEM((planes, seqs, part, wide), LOW)] * 2,
-            pltpu.VMEM((seqs, part, wide), LOW),
-            *pairs_of(chips, chips, planes, planes, seqs),
+            *[pltpu.VMEM((seqs, part, wide), LOW)] * 2,
+            *PlaneScatter.sems(chips, width),
+            *pairs_of(2 * planes, 2 * planes, seqs, chips),
+            pltpu.SemaphoreType.DMA((1,)),
         ],
         4,
     )
@@ -773,27 +815,15 @@
     here = place()
     z, c, core = here
     up, down, near = [sems[2 * i : 2 * i + 2] for i in range(3)]
-    partner = (z, c, 1 - core)
     barrier = pltpu.get_barrier_semaphore()
-    greet(barrier, [partner])
+    greet(barrier, [(z, c, 1 - core)])
     greet_line(barrier, planes, here)
     pl.semaphore_wait(barrier, 1 + line_peers(planes, here))
-    keep = pltpu.make_async_copy(x_ref, out_ref.at[z, core], sems[6].at[0])
-    keep.start()
-    keep.wait()
-
-    def passed(t):
-        return remote(out_ref.at[t, core], out_ref.at[t, core], near, t, partner)
-
-    line = LineGather(planes, here, lambda t: out_ref.at[t, core], up, down)
-    line.start()
-    passed(z).start()
+    group = GroupGather(planes, here, x_ref, out_ref, up, down, near)
+    group.start(sems[6].at[0])
     for d in range(1, planes):
-        line.step(d, lambda t: passed(t).start())
-    line.finish()
-    for t in range(planes):
-        passed(t).wait_send()
-        remote(x_ref, out_ref.at[t, 1 - core], near, t, partner).wait_recv()
+        group.step(d)
+    group.finish()
 
 
 def line_gather(planes, x_block):
@@ -804,7 +834,7 @@
         (x_block,),
         [HBM],
         HBM,
-        [*pairs_of(planes, planes, planes), pltpu.SemaphoreType.DMA((1,))],
+        [*GroupGather.sems(planes), pltpu.SemaphoreType.DMA((1,))],
         5,
     )
 
@@ -845,56 +875,70 @@
 
 
 class PairScatter:
-    def __init__(self, planes, here, left, right, turned, near_out, near_in, own, line, near):
+    PARTS = 2
+
+    def __init__(self, planes, here, left, right, turned, buffers, near, up, down):
         self.planes, self.here = planes, here
         self.left, self.right, self.turned = left, right, turned
-        self.near_out, self.near_in, self.own, self.near = near_out, near_in, own, near
-        tokens, width = near_out.shape[1:]
+        self.near_out, self.near_in, self.own, above, below = buffers
+        self.near = near
+        self.tokens, width = self.near_out.shape[1:]
         self.tiles = [pl.ds(at, COLUMNS) for at in range(0, width, COLUMNS)]
+        size = width // self.PARTS
+        every = slice(None)
+        parts = [
+            ((every, pl.ds(at, size)), [(rows, pl.ds(at, size)) for rows in row_tiles(self.tokens, 32)])
+            for at in range(0, width, size)
+        ]
         self.line = LineScatter(
             planes,
             here,
-            row_tiles(tokens, 32),
-            lambda t, rows: own[t, rows].astype(F32),
-            *line,
+            parts,
+            lambda t, tile: self.own[(t, *tile)].astype(F32),
+            above,
+            below,
+            up,
+            down,
         )
 
-    def near_copy(self, t):
+    def near_copy(self, i):
         z, c, core = self.here
-        return remote(self.near_out.at[t], self.near_in.at[t], self.near, t, (z, c, 1 - core))
+        at = (slice(None), slice(None), self.tiles[i])
+        return remote(self.near_out.at[at], self.near_in.at[at], self.near, i, (z, c, 1 - core))
 
     def start(self):
-        core = self.here[2]
-        order = []
-        for i in range((self.planes + 1) // 2):
-            order += [self.planes - 1 - i, i] if self.planes - 1 - i != i else [i]
-        for t in order:
-            left = self.left[t, 1 - core]
-            for columns in self.tiles:
-                part = product(left, self.right, columns, self.turned)
-                self.near_out[t, :, columns] = part.astype(LOW)
-            self.near_copy(t).start()
-        for t in order:
-            left = self.left[t, core]
-            self.near_copy(t).wait_recv()
-            for columns in self.tiles:
-                part = product(left, self.right, columns, self.turned)
+        core, tokens = self.here[2], self.tokens
+        left = jnp.concatenate([self.left[t, 1 - core] for t in range(self.planes)], axis=0)
+        for i, columns in enumerate(self.tiles):
+            part = product(left, self.right, columns, self.turned).astype(LOW)
+            for t in range(self.planes):
+                self.near_out[t, :, columns] = part[t * tokens : (t + 1) * tokens]
+            self.near_copy(i).start()
+        left = jnp.concatenate([self.left[t, core] for t in range(self.planes)], axis=0)
+        for i, columns in enumerate(self.tiles):
+            part = product(left, self.right, columns, self.turned)
+            self.near_copy(i).wait_recv()
+            for t in range(self.planes):
                 self.own[t, :, columns] = (
-                    part + self.near_in[t, :, columns].astype(F32)
+                    part[t * tokens : (t + 1) * tokens] + self.near_in[t, :, columns].astype(F32)
                 ).astype(LOW)
         self.line.step(0)
 
     def finish(self, out_ref):
-        def store(rows, total):
-            out_ref[rows] = total
+        def store(tile, total):
+            out_ref[tile] = total
 
         self.line.finish(store)
-        for t in range(self.planes):
-            self.near_copy(t).wait_send()
+        for i in range(len(self.tiles)):
+            self.near_copy(i).wait_send()
 
     @staticmethod
     def scratch(planes, tokens, width):
         return [pltpu.VMEM((planes, tokens, width), LOW)] * 5
+
+    @classmethod
+    def sems(cls, planes, width):
+        return pairs_of(width // COLUMNS, cls.PARTS * planes, cls.PARTS * planes)
 
 
 def line_scatter_kernel(
@@ -912,8 +956,8 @@
     swap = ChipSwap(chips, here, lambda index: grad_ref.at[index], slots_ref, swap_sems)
     swap.start(sems[8].at[0])
     work = PairScatter(
-        planes, here, left_ref, right_ref, True, near_out, near_in, own,
-        (above, below, up, down), near,
+        planes, here, left_ref, right_ref, True, (near_out, near_in, own, above, below),
+        near, up, down,
     )
     work.start()
     for i in range(1, planes - 1):
@@ -933,10 +977,109 @@
         [VMEM, HBM],
         [
             *PairScatter.scratch(planes, tokens, width),
-            *pairs_of(planes, planes, planes, chips),
+            *PairScatter.sems(planes, width),
+            *pairs_of(chips),
             pltpu.SemaphoreType.DMA((1,)),
         ],
         7,
+    )
+
+
+def plane_gather_kernel(
+    planes, chips, x_ref, stat_ref, tile_ref, left_ref, right_ref,
+    row_ref, stats_ref, tiles_ref, ffn_ref,
+    near_out, near_in, own, above, below, *sems,
+):
+    here = place()
+    z, c, core = here
+    seqs = 2 * chips
+    count = planes * seqs
+    me = 2 * c + core
+    flat = z * seqs + me
+    x_far, x_near, s_far, s_near, tile_sems, near, up, down = [
+        sems[2 * i : 2 * i + 2] for i in range(8)
+    ]
+    local = sems[16]
+    barrier = pltpu.get_barrier_semaphore()
+
+    def device_of(k):
+        other = lax.rem(flat + k, count)
+        return (other // seqs, lax.rem(other, seqs) // 2, lax.rem(other, 2))
+
+    def signal(k, carry):
+        greet(barrier, [device_of(k)])
+        return carry
+
+    lax.fori_loop(1, count, signal, 0)
+    pl.semaphore_wait(barrier, count - 1)
+    rows = PlaneGather(chips, here, x_ref, row_ref, x_far, x_near)
+    stats = PlaneGather(chips, here, stat_ref, stats_ref, s_far, s_near)
+    rows.start()
+    stats.start()
+    keeps = [
+        pltpu.make_async_copy(x_ref, row_ref.at[me], local.at[0]),
+        pltpu.make_async_copy(stat_ref, stats_ref.at[me], local.at[1]),
+        pltpu.make_async_copy(tile_ref.at[flat], tiles_ref.at[flat], local.at[2]),
+    ]
+    for copy in keeps:
+        copy.start()
+
+    def tile_copy(k):
+        other = lax.rem(flat + k, count)
+        return remote(tile_ref.at[other], tiles_ref.at[flat], tile_sems, k, device_of(k))
+
+    def tile_start(k, carry):
+        tile_copy(k).start()
+        return carry
+
+    lax.fori_loop(1, count, tile_start, 0)
+    work = PairScatter(
+        planes, here, left_ref, right_ref, False, (near_out, near_in, own, above, below),
+        near, up, down,
+    )
+    work.start()
+    for i in range(1, planes - 1):
+        if i == planes - 2:
+            rows.forward()
+            stats.forward()
+        work.line.step(i)
+    rows.finish()
+    stats.finish()
+    work.finish(ffn_ref)
+    for copy in keeps:
+        copy.wait()
+
+    def tile_wait(k, carry):
+        tile_copy(k).wait_send()
+        other = lax.rem(flat + count - k, count)
+        remote(tile_ref.at[0], tiles_ref.at[other], tile_sems, k, here).wait_recv()
+        return carry
+
+    lax.fori_loop(1, count, tile_wait, 0)
+
+
+def plane_gather(planes, chips, x_block, stats, tiles, left, right):
+    seqs = 2 * chips
+    tokens, width = x_block.shape
+    return call(
+        functools.partial(plane_gather_kernel, planes, chips),
+        "plane_gather",
+        [
+            shape((seqs, *x_block.shape), x_block.dtype),
+            shape((seqs, *stats.shape), stats.dtype),
+            shape(tiles.shape, tiles.dtype),
+            shape((tokens, width), F32),
+        ],
+        (x_block, stats, tiles, left, right),
+        [HBM, HBM, HBM, VMEM, VMEM],
+        [HBM, HBM, HBM, VMEM],
+        [
+            *PairScatter.scratch(planes, tokens, width),
+            *pairs_of(chips, chips, chips, chips, planes * seqs),
+            *PairScatter.sems(planes, width),
+            pltpu.SemaphoreType.DMA((3,)),
+        ],
+        2,
     )
 
 
@@ -1035,38 +1178,43 @@
 
 
 def attention_back_kernel(
-    planes, chips, heads,
-    q_ref, k_ref, v_ref, att_ref, sub_ref, stat_ref, log_ref, meta_ref, left_ref, right_ref, up_ref,
-    out_ref, normed_ref, ffn_ref, slots_ref,
-    grad, dq, dk, dv, near_out, near_in, own, above, below, *sems,
+    planes, heads, strided,
+    q_ref, k_ref, v_ref, att_ref, row_ref, right_ref, stat_ref, log_ref, meta_ref,
+    out_ref, total_ref,
+    grad, dq, dk, dv, normed_all, own, above, below, *sems,
 ):
     here = place()
-    z, c, core = here
-    near, up, down, swap_sems = [sems[2 * i : 2 * i + 2] for i in range(4)]
+    up, down = sems[:2], sems[2:]
     barrier = pltpu.get_barrier_semaphore()
-    peers = [(z, c, 1 - core), *chip_peers(chips, here)]
-    greet(barrier, peers)
     greet_line(barrier, planes, here)
-    pl.semaphore_wait(barrier, len(peers) + line_peers(planes, here))
-    units = slots_ref.shape[2]
-    swap = ChipSwap(
-        chips, here, lambda index: column_block(up_ref, units, index), slots_ref, swap_sems
-    )
-    swap.start(sems[8].at[0])
-    work = PairScatter(
-        planes, here, left_ref, right_ref, False, near_out, near_in, own,
-        (above, below, up, down), near,
-    )
-    work.start()
-    length = att_ref.shape[0]
-    span = heads * HD
+    pl.semaphore_wait(barrier, line_peers(planes, here))
+    length, span = att_ref.shape
+    part, width = own.shape[1:]
     for rows in row_tiles(length, BLOCK):
         mean, scaler, first, second = (stat_ref[rows, pl.ds(i, 1)] for i in range(4))
+        d_sub = product(row_ref[rows], right_ref, slice(None), True)
         normed = (att_ref[rows].astype(F32) - mean) * scaler
-        normed_ref[rows] = normed.astype(LOW)
-        d_att = (scaler * (sub_ref[rows] - first - normed * second)).astype(LOW)
+        normed_all[rows] = normed.astype(LOW)
+        d_att = (scaler * (d_sub - first - normed * second)).astype(LOW)
         for head in range(heads):
             grad[head, rows] = d_att[:, head * HD : (head + 1) * HD]
+    for at in range(0, width, COLUMNS):
+        columns = pl.ds(at, COLUMNS)
+        term = token_product(normed_all[...], row_ref[:, columns]).astype(LOW)
+        for t in range(planes):
+            own[t, :, columns] = term[t * part : (t + 1) * part]
+    line = LineScatter(
+        planes,
+        here,
+        [((slice(None),), [(rows,) for rows in row_tiles(part, 16)])],
+        lambda t, tile: own[(t, *tile)].astype(F32),
+        above,
+        below,
+        up,
+        down,
+    )
+    if strided:
+        line.step(0)
     dk[...] = jnp.zeros(dk.shape, F32)
     dv[...] = jnp.zeros(dv.shape, F32)
 
@@ -1101,7 +1249,8 @@
         last = -(-heads * i // (planes - 1))
         lax.fori_loop(first, last, one_head, 0)
         first = last
-        work.line.step(i)
+        if strided:
+            line.step(i)
     lax.fori_loop(first, heads, one_head, 0)
     for rows in row_tiles(length, BLOCK):
         tables = turns(meta_ref, rows)
@@ -1118,31 +1267,33 @@
             out_ref[rows, pl.ds(2 * HD * pair, 2 * HD)] = query.astype(LOW)
             out_ref[rows, pl.ds(span + 2 * HD * pair, 2 * HD)] = key.astype(LOW)
             out_ref[rows, pl.ds(2 * span + 2 * HD * pair, 2 * HD)] = both[2]
-    work.finish(ffn_ref)
-    swap.finish()
-
-
-def attention_back(planes, chips, heads, units, attention_args, left, right, up_grads):
-    length, span = attention_args[3].shape
-    tokens, width = left.shape[2], right.shape[1]
+    if strided:
+
+        def store(tile, total):
+            total_ref[tile] = total
+
+        line.finish(store)
+    else:
+        for t in range(planes):
+            total_ref[pl.ds(t * part, part)] = own[t].astype(F32)
+
+
+def attention_back(planes, heads, strided, part, args):
+    length, span = args[3].shape
+    width = args[4].shape[1]
     return call(
-        functools.partial(attention_back_kernel, planes, chips, heads),
+        functools.partial(attention_back_kernel, planes, heads, strided),
         "attention_back",
-        [
-            shape((length, 3 * span), LOW),
-            shape((length, span), LOW),
-            shape((tokens, width), F32),
-            shape((chips, width, units), LOW),
-        ],
-        (*attention_args, left, right, up_grads),
-        [*[VMEM] * 10, HBM],
-        [*[VMEM] * 3, HBM],
+        [shape((length, 3 * span), LOW), shape((part if strided else span, width), F32)],
+        args,
+        [VMEM] * 9,
+        [VMEM] * 2,
         [
             pltpu.VMEM((heads, length, HD), LOW),
             *[pltpu.VMEM((heads, length, HD), F32)] * 3,
-            *PairScatter.scratch(planes, tokens, width),
-            *pairs_of(planes, planes, planes, chips),
-            pltpu.SemaphoreType.DMA((1,)),
+            pltpu.VMEM((length, span), LOW),
+            *[pltpu.VMEM((planes, part, width), LOW)] * 3,
+            *pairs_of(planes, planes),
         ],
         8,
     )
@@ -1218,8 +1369,6 @@
     else:
         out_all = lax.all_gather(out_scaled, ALL, axis=0, tiled=True)
         out_mine = lax.dynamic_slice_in_dim(out_all, seq_index * span, span, axis=0)
-    grad_low, gain_tiles = lax.optimization_barrier((out_grad[0], gain_tiles))
-    grad_flat = lax.all_gather(grad_low, TP, axis=0, tiled=True)
     queries, keys, values, attended, log_total = attention(heads, dot(row_in, qkv_mine), meta)
     down_scaled, attended = lax.optimization_barrier((down_scaled, attended))
     down_mine = lax.all_gather(down_scaled, "chip", axis=0, tiled=True)
@@ -1236,7 +1385,11 @@
         ],
         axis=1,
     )
-    out_sum, tiles = out_scatter(chips, attended.reshape(seqs, tokens, span), out_mine, tiles)
+    grad_low = out_grad[0]
+    out_sum, tiles, grad_flat = out_scatter(
+        planes, chips, attended.reshape(seqs, tokens, span), out_mine, tiles, grad_low
+    )
+    grad_flat = grad_flat.reshape(group_tokens, width)
     tiles = jnp.sum(tiles, axis=0)
     column_sum = tiles[8:].reshape(width)
     sums = tiles[:2].T
@@ -1295,54 +1448,55 @@
     first_two = jnp.sum(d_hmid_wide * column_sum[None, :], axis=1, keepdims=True) / width
     second_two = jnp.sum(d_hmid_wide * projected, axis=1, keepdims=True) / width
     token_stats = jnp.concatenate([mean_two, scaler_two, first_two, second_two], axis=1)
-    row_grad, row_stats, gain_part = plane_gather(
-        planes, chips, d_hmid_low, jnp.pad(token_stats, ((0, 0), (0, 124))), gain_part
-    )
+    row_grad, row_stats, gain_part, ffn_out = plane_gather(
+        planes,
+        chips,
+        d_hmid_low,
+        jnp.pad(token_stats, ((0, 0), (0, 124))),
+        gain_part,
+        normed_four_low.reshape(planes, 2, tokens, -1),
+        down_mine,
+    )
+    output = (hmid + ffn_out).astype(LOW)[None]
     row_grad = row_grad.reshape(length, width)
     row_stats = row_stats.reshape(length, 128)
     grad_gain_three = jnp.sum(gain_part, axis=0)[0, :part]
-    d_sub = rows_product(row_grad, out_mine)
-    d_qkv, normed_two, ffn_out, up_slots = attention_back(
+    d_qkv, sum_out = attention_back(
+        planes,
+        heads,
+        strided,
+        part,
+        (queries, keys, values, attended, row_grad, out_mine, row_stats, log_total, meta),
+    )
+    grad_qkv = token_product(row_in, d_qkv).astype(LOW)
+    d_in, sum_qkv, grad_gain_one, up_slots = in_scatter(
         planes,
         chips,
         heads,
-        units,
-        (queries, keys, values, attended, d_sub, row_stats, log_total, meta),
-        normed_four_low.reshape(planes, 2, tokens, -1),
-        down_mine,
-        grad_up,
-    )
-    output = (hmid + ffn_out).astype(LOW)[None]
-    sum_up = jnp.sum(up_slots.astype(F32), axis=0)
-    sum_down = jnp.sum(down_slots.astype(F32), axis=0)
-    grad_out = token_product(normed_two, row_grad)
-    grad_qkv = token_product(row_in, d_qkv).astype(LOW)
-    d_in, part_qkv = in_scatter(
-        planes,
-        chips,
+        strided,
         d_qkv.reshape(seqs, tokens, 3 * span),
         qkv_mine,
         grad_qkv.reshape(planes, seqs, part, 3 * span),
-    )
+        grad_up,
+        w_qkv,
+        jnp.broadcast_to(gain_attn.astype(F32)[:, None], (part, 128)),
+        units,
+    )
+    grad_gain_one = grad_gain_one[:, 0]
+    sum_up = jnp.sum(up_slots.astype(F32), axis=0)
+    sum_down = jnp.sum(down_slots.astype(F32), axis=0)
     input_grad = (d_hmid + norm_back(d_in, normed_one, scaler_one)).astype(LOW)[None]
 
-    if strided:
-        sum_qkv = part_qkv.reshape(seqs, part, 3, planes, HD).transpose(1, 2, 3, 0, 4)
-        sum_out = lax.psum_scatter(grad_out.astype(LOW), "dp", scatter_dimension=0, tiled=True)
-    else:
-        sum_qkv = part_qkv.reshape(seqs, part, 3, span).transpose(1, 2, 0, 3)
+    if not strided:
         spread = lax.dynamic_update_slice_in_dim(
-            jnp.zeros((width, width), LOW), grad_out.astype(LOW), seq_index * span, axis=0
+            jnp.zeros((width, width), LOW), sum_out.astype(LOW), seq_index * span, axis=0
         )
-        sum_out = lax.psum_scatter(spread, ALL, scatter_dimension=0, tiled=True)
-    sum_qkv = sum_qkv.reshape(part, 3 * width).astype(F32)
-    sum_out = sum_out.astype(F32)
+        sum_out = lax.psum_scatter(spread, ALL, scatter_dimension=0, tiled=True).astype(F32)
 
     def finish(total, weight, gain):
         wide = weight.astype(F32)
         return (total * gain.astype(F32)[:, None], jnp.sum(total * wide, axis=1))
 
-    sum_qkv, grad_gain_one = finish(sum_qkv, w_qkv, gain_attn)
     sum_out, grad_gain_two = finish(sum_out, w_out, gain_attn_sub)
     sum_down, grad_gain_four = finish(sum_down, w_down, gain_ffn_sub)
 

time: 707 us -> 673 us (0.952)
  other arithmetic: 58.6 us -> 49.2 us
  matrix products: 66 us -> 57.3 us
  Pallas kernels: 530 us -> 522 us
  local copies, waits for them, and re-layouts: 26.6 us -> 19.3 us
    convert_element_type x3 -> x0, local copies, waits for them, and re-layouts: 11.5 us -> none  [body(): sum_qkv = sum_qkv.reshape(part, 3 * width).astype(F32)]
    pallas_call x9, Pallas kernels: 530 us -> 522 us  [call(): pl.pallas_call(kernel, name=name, out_shape=outs, in_specs=in_specs, out_...]
    dot_general x2 -> x1, matrix products: 14.4 us -> 9.96 us  [rows_product(): lax.dot_general(operand, weight_rows, (((1,), (1,)), ((), ())), preferred...]
    dot_general x4 -> x3, matrix products: 23.5 us -> 19.2 us  [token_product(): lax.dot_general(left_op, right_op, (((0,), (0,)), ((), ())), preferred_el...]
  transfers between devices with their start and end apart: 3 -> 1, of which waited for: 0 -> 0; matrix products, arithmetic and copies ran while one was open for 7% -> 2% of each run, Pallas kernels for 35% -> 18%
where the time goes in v3:
time: 673 us; the launch traced here: 663 us
  Pallas kernels  522 us (78%)
  matrix products  57.3 us (9%)
  other arithmetic  49.2 us (7%)
  local copies, waits for them, and re-layouts  19.3 us (3%)
  between operations  15 us (2%)
    pallas_call x9, Pallas kernels, call(): pl.pallas_call(kernel, name=name, out_shape=outs, in_specs=in_specs, out_...  522 us
    dot_general x2, matrix products, dot(): return jnp.dot(left_op, right_op, preferred_element_type=F32)  28.1 us
    dot_general x3, matrix products, token_product(): lax.dot_general(left_op, right_op, (((0,), (0,)), ((), ())), preferred_el...  19.2 us
  transfers between devices with their start and end apart: 1, of which 0 were waited for; matrix products, arithmetic and copies ran while one was open for 2% of the time, Pallas kernels for 18%

profile of v3, /device:TPU:9, one launch (start us, length us, event | category | flops | bytes accessed | tf_op | source)
XLA Modules:
  0.0 663.3 jit_solution(11159476565247148469)
XLA Ops:
  10.5 1.3 fusion.24
  11.9 2.2 fusion.18.x_ref
  14.7 3.1 fusion.11
  17.8 1.6 reshape.308
  19.4 1.8 copy.72
  21.2 3.6 reshape.309.qkv_ref
  27.1 93.2 %attention_gather.1 = (bf16[8,128,2048]{2,1,0:T(8,128)(2,1)}, f32[8,128,256]{2,1,0:T(8,128)}, bf16[4,8,64,768]{3,2,1,0:T(8,128)(2,1)}, bf16[4,64,2048]{2,1,0:T(8...) custom-call(bf16[128,2048]{1,0:T(8,128)(2,1)} %fusion.18.x_ref, f32[128,256]{1,0:T(8,128)} %pad_maximum_fusion.meta_ref, ...), custom_call_target="tpu_custom_call" | custom-call | tf_op jit(solution)/shard_map/attention_gather/pallas_call | solution.py:90
  120.4 8.3 %fusion.41.raw_ref = f32[1024,768]{1,0:T(8,128)} fusion(bf16[1024,2048]{1,0:T(8,128)(2,1)} %bitcast.140, bf16[2048,768]{1,0:T(8,128)(2,1)} %bitcast.115), kind=kOutput, calls=%fused_computation.129 | convolution fusion | flops 3221225472 | bytes 10485760 | tf_op jit(solution)/shard_map/dot_general | solution.py:62
  128.6 15.0 %attention.1 = (bf16[4,1024,64]{2,1,0:T(8,128)(2,1)}, bf16[4,1024,64]{2,1,0:T(8,128)(2,1)}, bf16[4,1024,64]{2,1,0:T(8,128)(2,1)}, bf16[1024,256]{1,0:T(8,128)(2,1)}, f32[1024,128]{1,0:T(8,128)}) custom-call(f32[1024,768]{1,0:T(8,128)} %fusion.41.raw_ref, f32[1024,256]{1,0:T(8,128)} %bitcast.113), custom_call_target="tpu_custom_call" | custom-call | tf_op jit(solution)/shard_map/attention/pallas_call | solution.py:90
  144.9 1.4 convert_reduce_fusion.3
  147.3 70.7 %out_scatter.1 = (f32[128,2048]{1,0:T(8,128)}, f32[8,24,128]{2,1,0:T(8,128)}, bf16[4,2,128,2048]{3,2,1,0:T(8,128)(2,1)}) custom-call(bf16[8,128,256]{2,1,0:T(8,128)(2,1)} %bitcast.108, bf16[256,2048]{1,0:T(8,128)(2,1)} %bitcast.103, f32[8,24,128]{2,1,0:T(8,128)} %pad_maximum_fusion.1.tile_ref, bf16[128,2048]{1,0:T(8,128)(2,1)} %bitcast.118), custom_call_target="tpu_custom_call" | custom-call | tf_op jit(solution)/shard_map/out_scatter/pallas_call | solution.py:90
  220.0 1.6 fusion.38
  222.9 51.1 %line_gather.1 = bf16[4,2,128,2048]{3,2,1,0:T(8,128)(2,1)} custom-call(bf16[128,2048]{1,0:T(8,128)(2,1)} %multiply_convert_fusion.x_ref), custom_call_target="tpu_custom_call" | custom-call | tf_op jit(solution)/shard_map/line_gather/pallas_call | solution.py:90
  275.7 1.6 multiply_add_fusion
  277.3 10.0 %fusion.40 = (f32[1024]{0:T(1024)S(1)}, f32[1024,1024]{0,1:T(8,128)}) fusion(bf16[1024,2048]{1,0:T(8,128)(2,1)} %bitcast.142, bf16[1024,2048]{1,0:T(8,128)(2,1)} %all-gather.2.cloned.1.call-done.right_ref), kind=kOutput, calls=%fused_computation.128 | convolution fusion | flops 4296014848 | bytes 12587008 | tf_op jit(solution)/shard_map/dot_general | solution.py:66
  287.3 5.5 copy.68
  292.8 19.9 %fusion.35 = (f32[1024]{0:T(1024)S(1)}, f32[1024]{0:T(1024)S(1)}, f32[1024]{0:T(1024)S(1)}, f32[1024,1024]{1,0:T(8,128)}, f32[1024,1024]{1,0:T(8,128)}) fusion(f32[1024,1024]{1,0:T(8,128)} %copy.68, bf16[1024,2048]{1,0:T(8,128)(2,1)} %bitcast.109, bf16[2048,1024]{1,0:T(8,128)(2,1)} %get-tuple-element.69.right_ref), kind=kOutput, calls=%fused_computation.125 | convolution fusion | flops 4367315968 | bytes 20983808 | tf_op jit(solution)/shard_map/dot_general | solution.py:62
  313.3 12.2 %group_sums.1 = f32[4,1024]{1,0:T(4,128)} custom-call(f32[4,1024]{1,0:T(4,128)} %pad_maximum_fusion.2.x_ref), custom_call_target="tpu_custom_call" | custom-call | tf_op jit(solution)/shard_map/group_sums/pallas_call | solution.py:90
  326.5 5.6 fusion.6
  332.1 6.3 convolution_convert_fusion
  338.4 6.6 convolution_convert_fusion.1.up_ref
  345.0 53.8 %line_scatter.1 = (f32[128,2048]{1,0:T(8,128)}, bf16[4,256,2048]{2,1,0:T(8,128)(2,1)}) custom-call(bf16[4,2,128,1024]{3,2,1,0:T(8,128)(2,1)} %bitcast.105, bf16[2048,1024]{1,0:T(8,128)(2,1)} %get-tuple-element.69.right_ref, bf16[4,256,2048]{2,1,0:T(8,128)(2,1)} %bitcast.112), custom_call_target="tpu_custom_call" | custom-call | tf_op jit(solution)/shard_map/line_scatter/pallas_call | solution.py:90
  398.8 1.6 multiply_reduce_fusion.2
  400.4 3.0 fusion.26
  405.0 56.4 %plane_gather.1 = (bf16[8,128,2048]{2,1,0:T(8,128)(2,1)}, f32[8,128,128]{2,1,0:T(8,128)}, f32[32,8,128]{2,1,0:T(8,128)}, f32[128,2048]{1,0:T(8,128)}) custom-call(bf16[128,2048]{1,0:T(8,128)(2,1)} %get-tuple-element.102.x_ref, f32[128,128]{1,0:T(8,128)} %pad.13.stat_ref, f32[32,8,128]{2,1,0:T(8,128)} %pad.14.tile_ref, bf16[4,2,128,1024]{3,2,1,0:T(8,128)(2,1)} %bitcast.106, ...), custom_call_target="tpu_custom_call" | custom-call | tf_op jit(solution)/shard_map/plane_gather/pallas_call | solution.py:90
  461.4 38.4 %attention_back.1 = (bf16[1024,768]{1,0:T(8,128)(2,1)}, f32[64,2048]{1,0:T(8,128)}) custom-call(bf16[4,1024,64]{2,1,0:T(8,128)(2,1)} %get-tuple-element.75.q_ref, bf16[4,1024,64]{2,1,0:T(8,128)(2,1)} %get-tuple-element.76.k_ref, bf16[4,1024,64]{2,1,0:T(8,128)(2,1)} %get-tuple-element.77.v_ref, bf16[1024,256]{1,0:T(8,128)(2,1)} %get-tuple-element.64.att_ref, ...), custom_call_target="tpu_custom_call" | custom-call | tf_op jit(solution)/shard_map/attention_back/pallas_call | solution.py:90
  499.8 6.3 convolution_convert_fusion.2
  506.8 131.5 %in_scatter.1 = (f32[128,2048]{1,0:T(8,128)}, f32[64,6144]{1,0:T(8,128)}, f32[64,128]{1,0:T(8,128)}, bf16[4,2048,256]{2,1,0:T(8,128)(2,1)}) custom-call(bf16[8,128,768]{2,1,0:T(8,128)(2,1)} %bitcast.119, bf16[2048,768]{1,0:T(8,128)(2,1)} %bitcast.116, bf16[4,8,64,768]{3,2,1,0:T(8,128)(2,1)} %bitcast.117, ...), custom_call_target="tpu_custom_call" | custom-call | tf_op jit(solution)/shard_map/in_scatter/pallas_call | solution.py:90
  638.4 4.4 convert_reduce_fusion.1
  645.3 3.4 convert_reduce_fusion
  648.7 1.7 fusion.29
  650.4 3.2 fusion.8
  (136 shorter events, 22.0 us)
Async XLA Ops:
  7.2 270.1 %all-gather.2.cloned.1.call-start = ((), (), s32[]{:S(2)}) async-start(), calls=%async_computation | async-start | bytes 5242880 | tf_op jit(solution)/shard_map/all_gather | solution.py:1374
  17.8 7.0 %copy-start.25 = (bf16[64]{0:T(256)(128)(2,1)S(1)}, bf16[64]{0:T(256)(128)(2,1)}, u32[]{:S(2)}) copy-start(bf16[64]{0:T(256)(128)(2,1)} %param.29) | copy-start | bytes 388
  17.8 7.0 %copy-start.26 = (bf16[64]{0:T(256)(128)(2,1)S(1)}, bf16[64]{0:T(256)(128)(2,1)}, u32[]{:S(2)}) copy-start(bf16[64]{0:T(256)(128)(2,1)} %param.30) | copy-start | bytes 388
  17.8 7.0 %copy-start.24 = (bf16[256]{0:T(256)(128)(2,1)S(1)}, bf16[256]{0:T(256)(128)(2,1)}, u32[]{:S(2)}) copy-start(bf16[256]{0:T(256)(128)(2,1)} %param.31) | copy-start | bytes 1540
  17.8 7.0 %copy-start.16 = (bf16[64,2048]{1,0:T(8,128)(2,1)S(1)}, bf16[64,2048]{1,0:T(8,128)(2,1)}, u32[]{:S(2)}) copy-start(bf16[64,2048]{1,0:T(8,128)(2,1)} %param.25) | copy-start | bytes 786436
  128.6 15.0 %copy-start.7 = (bf16[256,2048]{1,0:T(8,128)(2,1)S(1)}, bf16[256,2048]{1,0:T(8,128)(2,1)}, u32[]{:S(2)}) copy-start(bf16[256,2048]{1,0:T(8,128)(2,1)} %param.27) | copy-start | bytes 3145732
  128.6 17.7 %copy-start.2 = (bf16[4,64,2048]{2,1,0:T(8,128)(2,1)S(1)}, bf16[4,64,2048]{2,1,0:T(8,128)(2,1)}, u32[]{:S(2)}) copy-start(bf16[4,64,2048]{2,1,0:T(8,128)(2,1)} %get-tuple-element.65) | copy-start | bytes 3145732
  143.6 76.3 %copy-start = (bf16[1,128,2048]{2,1,0:T(8,128)(2,1)S(1)}, bf16[1,128,2048]{2,1,0:T(8,128)(2,1)}, u32[]{:S(2)}) copy-start(bf16[1,128,2048]{2,1,0:T(8,128)(2,1)} %param.22) | copy-start | bytes 1572868
  221.5 52.5 %copy-start.23 = (bf16[64]{0:T(256)(128)(2,1)S(1)}, bf16[64]{0:T(256)(128)(2,1)}, u32[]{:S(2)}) copy-start(bf16[64]{0:T(256)(128)(2,1)} %param.28) | copy-start | bytes 388
  221.5 52.5 %copy-start.31 = (f32[64]{0:T(128)S(1)}, f32[64]{0:T(128)}, u32[]{:S(2)}) copy-start(f32[64]{0:T(128)} %param.36) | copy-start | bytes 772
  221.6 53.0 %copy-start.22 = (f32[256]{0:T(256)S(1)}, f32[256]{0:T(256)}, u32[]{:S(2)}) copy-start(f32[256]{0:T(256)} %param.39) | copy-start | bytes 3076
  221.6 53.6 %copy-start.27 = (f32[64]{0:T(128)S(1)}, f32[64]{0:T(128)}, u32[]{:S(2)}) copy-start(f32[64]{0:T(128)} %param.38) | copy-start | bytes 772
  221.6 53.6 %copy-start.28 = (f32[64]{0:T(128)S(1)}, f32[64]{0:T(128)}, u32[]{:S(2)}) copy-start(f32[64]{0:T(128)} %param.37) | copy-start | bytes 772
  221.6 54.1 %copy-start.5 = (bf16[2048,256]{1,0:T(8,128)(2,1)S(1)}, bf16[2048,256]{1,0:T(8,128)(2,1)}, u32[]{:S(2)}) copy-start(bf16[2048,256]{1,0:T(8,128)(2,1)} %up_ref.1) | copy-start | bytes 3145732
  221.6 54.1 %copy-start.13 = (f32[2048,256]{1,0:T(8,128)S(1)}, f32[2048,256]{1,0:T(8,128)}, u32[]{:S(2)}) copy-start(f32[2048,256]{1,0:T(8,128)} %param.34) | copy-start | bytes 6291460
  292.8 33.6 %copy-start.1 = (f32[1024,1024]{1,0:T(8,128)S(1)}, f32[1024,1024]{1,0:T(8,128)}, u32[]{:S(2)}) copy-start(f32[1024,1024]{1,0:T(8,128)} %copy.68) | copy-start | bytes 12582916
  326.5 5.6 copy-start.30
  332.0 6.3 copy-start.4
  332.0 6.3 copy-start.3
  332.1 6.3 copy-start.6
  345.0 55.4 %copy-start.8 = (f32[128,2048]{1,0:T(8,128)S(1)}, f32[128,2048]{1,0:T(8,128)}, u32[]{:S(2)}) copy-start(f32[128,2048]{1,0:T(8,128)} %get-tuple-element.67) | copy-start | bytes 3145732
  345.0 55.4 %copy-start.14 = (bf16[1,128,2048]{2,1,0:T(8,128)(2,1)S(1)}, bf16[1,128,2048]{2,1,0:T(8,128)(2,1)}, u32[]{:S(2)}) copy-start(bf16[1,128,2048]{2,1,0:T(8,128)(2,1)} %param.40) | copy-start | bytes 1572868
  461.4 38.4 %copy-start.29 = (bf16[8,128,2048]{2,1,0:T(8,128)(2,1)S(1)}, bf16[8,128,2048]{2,1,0:T(8,128)(2,1)}, u32[]{:S(2)}) copy-start(bf16[8,128,2048]{2,1,0:T(8,128)(2,1)} %get-tuple-element.60) | copy-start | bytes 12582916
  638.3 4.5 copy-start.9
  638.3 4.8 copy-start.21
  638.3 5.5 copy-start.17
  638.3 6.4 copy-start.20
  644.7 3.9 copy-start.18
  644.7 4.0 copy-start.19
  645.3 5.1 copy-start.12
  650.4 3.2 copy-start.11
  650.4 4.4 copy-start.15
  (1 other events, 3.2 us)
Sparse Core Ops, SparseCore 0:
  145.0 72.7 all-gather.1

commit v4 on v3

--- a/solution.py
+++ b/solution.py
@@ -33,10 +33,6 @@
     first_mean = jnp.mean(scaled_grad, axis=-1, keepdims=True)
     second_mean = jnp.mean(scaled_grad * normed, axis=-1, keepdims=True)
     return scaler * (scaled_grad - first_mean - normed * second_mean)
-
-
-def exact_gelu(values):
-    return jax.nn.gelu(values, approximate=False)
 
 
 def token_tables(positions):
@@ -75,7 +71,7 @@
 MESH = pl.DeviceIdType.MESH
 HBM = pl.BlockSpec(memory_space=pl.ANY)
 VMEM = pl.BlockSpec(memory_space=pltpu.VMEM)
-VMEM_BYTES = 56 * 1024 * 1024
+VMEM_BYTES = 60 * 1024 * 1024
 
 
 def shape(dims, kind):
@@ -158,6 +154,14 @@
     return whole.at[:, pl.ds(pl.multiple_of(index * units, 128), units)]
 
 
+def half_block(whole, slots, index, half):
+    rows, units = slots.shape[1:]
+    at = pl.ds(half * rows, rows)
+    if len(whole.shape) == 3:
+        return whole.at[index, at]
+    return whole.at[at, pl.ds(pl.multiple_of(index * units, 128), units)]
+
+
 class ChipSwap:
     def __init__(self, chips, here, source, slots, sems):
         z, c, core = here
@@ -311,13 +315,16 @@
     def step(self, d):
         self.line.step(d, lambda t, p: self.passed(t, p).start())
 
+    def other(self, t):
+        for p in range(self.PARTS):
+            block = self.parts(t, 1 - self.here[2])[p]
+            remote(block, block, self.near, t * self.PARTS + p, self.partner).wait_recv()
+
     def finish(self):
         self.line.finish()
         for t in range(self.planes):
             for p in range(self.PARTS):
                 self.passed(t, p).wait_send()
-                block = self.parts(t, 1 - self.here[2])[p]
-                remote(block, block, self.near, t * self.PARTS + p, self.partner).wait_recv()
 
     @classmethod
     def sems(cls, planes):
@@ -575,6 +582,8 @@
         group.step(d)
     work.finish(out_ref)
     group.finish()
+    for t in range(planes):
+        group.other(t)
     keep.wait()
     for k in range(1, seqs):
         swaps[k - 1].wait_send()
@@ -608,58 +617,64 @@
 
 
 class LineScatter:
-    def __init__(self, planes, here, parts, own, above, below, up, down):
-        self.planes, self.here, self.parts, self.own = planes, here, parts, own
-        self.above, self.below, self.up, self.down = above, below, up, down
+    def __init__(self, planes, here, count, part, tiles, own, slots, up, down):
+        self.planes, self.here, self.count = planes, here, count
+        self.part, self.tiles, self.own, self.slots = part, tiles, own, slots
+        self.up, self.down = up, down
+        self.steps = (planes - 1) * count
 
     def upward(self, t, p):
         z, c, core = self.here
-        block = self.below.at[(t, *self.parts[p][0])]
-        return remote(block, block, self.up, t * len(self.parts) + p, (z + 1, c, core))
-
-    def downward(self, t, p):
+        block = self.slots.at[(t, *self.part(p))]
+        return remote(block, block, self.up, t * self.count + p, (z + 1, c, core))
+
+    def downward(self, t, p, last):
         z, c, core = self.here
-        block = self.above.at[(t, *self.parts[p][0])]
-        return remote(block, block, self.down, t * len(self.parts) + p, (z - 1, c, core))
-
-    def add(self, slot, t, p, fresh):
-        for tile in self.parts[p][1]:
+        block = self.slots.at[(t, *self.part(p))]
+        target = self.slots.at[(self.planes, *self.part(p))] if last else block
+        return remote(block, target, self.down, t * self.count + p, (z - 1, c, core))
+
+    def add(self, t, p, fresh):
+        for tile in self.tiles(p):
             total = self.own(t, tile)
             if not fresh:
-                total = total + slot[(t, *tile)].astype(F32)
-            slot[(t, *tile)] = total.astype(LOW)
+                total = total + self.slots[(t, *tile)].astype(F32)
+            self.slots[(t, *tile)] = total.astype(LOW)
 
     def step(self, i):
-        z, planes = self.here[0], self.planes
-        top, low = planes - 1 - i, i
-
-        def rise(p):
+        z, planes, count = self.here[0], self.planes, self.count
+        rise, fall = i - z, i - (planes - 1 - z)
+
+        @pl.when((rise >= 0) & (rise < (planes - 1 - z) * count))
+        def _():
+            t, p = planes - 1 - rise // count, lax.rem(rise, count)
+
             @pl.when(z > 0)
             def _():
-                self.upward(top, p).wait_recv()
-                self.add(self.below, top, p, False)
+                self.upward(t, p).wait_recv()
+                self.add(t, p, False)
 
             @pl.when(z == 0)
             def _():
-                self.add(self.below, top, p, True)
-
-            self.upward(top, p).start()
-
-        def fall(p):
+                self.add(t, p, True)
+
+            self.upward(t, p).start()
+
+        @pl.when((fall >= 0) & (fall < z * count))
+        def _():
+            t, p = fall // count, lax.rem(fall, count)
+
             @pl.when(z < planes - 1)
             def _():
-                self.downward(low, p).wait_recv()
-                self.add(self.above, low, p, False)
+                self.downward(t, p, False).wait_recv()
+                self.add(t, p, False)
 
             @pl.when(z == planes - 1)
             def _():
-                self.add(self.above, low, p, True)
-
-            self.downward(low, p).start()
-
-        for p in range(len(self.parts)):
-            pl.when(z < top)(lambda p=p: rise(p))
-            pl.when(z > low)(lambda p=p: fall(p))
+                self.add(t, p, True)
+
+            pl.when(t == z - 1)(lambda: self.downward(t, p, True).start())
+            pl.when(t < z - 1)(lambda: self.downward(t, p, False).start())
 
     def finish(self, store):
         z, planes = self.here[0], self.planes
@@ -667,10 +682,11 @@
         def total(tile, *slots):
             value = self.own(z, tile)
             for slot in slots:
-                value = value + slot[(z, *tile)].astype(F32)
+                value = value + self.slots[(slot, *tile)].astype(F32)
             store(tile, value)
 
-        for p, (_, tiles) in enumerate(self.parts):
+        for p in range(self.count):
+            tiles = self.tiles(p)
 
             @pl.when(z > 0)
             def _(p=p):
@@ -678,29 +694,27 @@
 
             @pl.when(z < planes - 1)
             def _(p=p):
-                self.downward(z, p).wait_recv()
+                self.downward(z, p, True).wait_recv()
 
             @pl.when((z > 0) & (z < planes - 1))
             def _(tiles=tiles):
                 for tile in tiles:
-                    total(tile, self.below, self.above)
+                    total(tile, z, planes)
 
             @pl.when(z == 0)
             def _(tiles=tiles):
                 for tile in tiles:
-                    total(tile, self.above)
+                    total(tile, planes)
 
             @pl.when(z == planes - 1)
             def _(tiles=tiles):
                 for tile in tiles:
-                    total(tile, self.below)
-
-        for i in range(planes - 1):
-            for p in range(len(self.parts)):
-                pl.when(z < planes - 1 - i)(
-                    lambda i=i, p=p: self.upward(planes - 1 - i, p).wait_send()
-                )
-                pl.when(z > i)(lambda i=i, p=p: self.downward(i, p).wait_send())
+                    total(tile, z)
+
+        for t in range(planes):
+            for p in range(self.count):
+                pl.when(z < t)(lambda t=t, p=p: self.upward(t, p).wait_send())
+                pl.when(z > t)(lambda t=t, p=p: self.downward(t, p, False).wait_send())
 
 
 def row_tiles(count, size):
@@ -710,7 +724,7 @@
 def in_scatter_kernel(
     planes, chips, heads, strided, left_ref, right_ref, grad_ref, up_ref, weight_ref, gain_ref,
     out_ref, total_ref, gains_ref, slots_ref,
-    near_out, near_in, far_out, far_in, above, below, mine, parts, *sems,
+    near_out, near_in, far_out, far_in, sums, mine, parts, *sems,
 ):
     here = place()
     z, c, core = here
@@ -726,10 +740,11 @@
     line = LineScatter(
         planes,
         here,
-        [((pl.ds(p * half, half),), [(pl.ds(p * half + i, 1),) for i in range(half)]) for p in range(2)],
+        2,
+        lambda p: (pl.ds(p * half, half),),
+        lambda p: [(pl.ds(p * half + i, 1),) for i in range(half)],
         lambda t, tile: grad_ref[(t, *tile)].astype(F32),
-        above,
-        below,
+        sums,
         up,
         down,
     )
@@ -738,12 +753,11 @@
         chips, here, left_ref, right_ref, True, (near_out, near_in, far_out, far_in), near, far
     )
     work.start()
-    units = slots_ref.shape[2]
     ups = ChipSwap(
-        chips, here, lambda index: column_block(up_ref, units, index), slots_ref, chip_sems
+        chips, here, lambda index: half_block(up_ref, slots_ref, index, 1), slots_ref, chip_sems
     )
     ups.start(sems[12].at[0])
-    for i in range(1, planes - 1):
+    for i in range(1, line.steps):
         line.step(i)
 
     def store(tile, total):
@@ -794,14 +808,14 @@
             shape((tokens, width), F32),
             shape(weight.shape, F32),
             shape((part, 128), F32),
-            shape((chips, width, units), LOW),
+            shape((chips, width // 2, units), LOW),
         ],
         (left, right, grads, up_grads, weight, gain),
         [VMEM, VMEM, VMEM, HBM, VMEM, VMEM],
         [VMEM, VMEM, VMEM, HBM],
         [
             *PlaneScatter.scratch(chips, tokens, width),
-            *[pltpu.VMEM((planes, seqs, part, wide), LOW)] * 2,
+            pltpu.VMEM((planes + 1, seqs, part, wide), LOW),
             *[pltpu.VMEM((seqs, part, wide), LOW)] * 2,
             *PlaneScatter.sems(chips, width),
             *pairs_of(2 * planes, 2 * planes, seqs, chips),
@@ -811,92 +825,30 @@
     )
 
 
-def line_gather_kernel(planes, x_ref, out_ref, *sems):
-    here = place()
-    z, c, core = here
-    up, down, near = [sems[2 * i : 2 * i + 2] for i in range(3)]
-    barrier = pltpu.get_barrier_semaphore()
-    greet(barrier, [(z, c, 1 - core)])
-    greet_line(barrier, planes, here)
-    pl.semaphore_wait(barrier, 1 + line_peers(planes, here))
-    group = GroupGather(planes, here, x_ref, out_ref, up, down, near)
-    group.start(sems[6].at[0])
-    for d in range(1, planes):
-        group.step(d)
-    group.finish()
-
-
-def line_gather(planes, x_block):
-    return call(
-        functools.partial(line_gather_kernel, planes),
-        "line_gather",
-        shape((planes, 2, *x_block.shape), x_block.dtype),
-        (x_block,),
-        [HBM],
-        HBM,
-        [*GroupGather.sems(planes), pltpu.SemaphoreType.DMA((1,))],
-        5,
-    )
-
-
-def sums_kernel(planes, x_ref, out_ref, slots, *sems):
-    here = place()
-    z, c, core = here
-    count = 2 * planes
-    me = 2 * z + core
-    barrier = pltpu.get_barrier_semaphore()
-    ids = [lax.rem(me + k, count) for k in range(1, count)]
-    peers = [(index // 2, c, lax.rem(index, 2)) for index in ids]
-    greet(barrier, peers)
-    pl.semaphore_wait(barrier, len(peers))
-    copies = [remote(x_ref, slots.at[k], sems, k, device) for k, device in enumerate(peers, 1)]
-    for copy in copies:
-        copy.start()
-    for copy in copies:
-        copy.wait_send()
-        copy.wait_recv()
-    total = x_ref[...]
-    for k in range(1, count):
-        total = total + slots[k]
-    out_ref[...] = total
-
-
-def group_sums(planes, stats):
-    return call(
-        functools.partial(sums_kernel, planes),
-        "group_sums",
-        shape(stats.shape, F32),
-        (stats,),
-        [VMEM],
-        VMEM,
-        [pltpu.VMEM((2 * planes, *stats.shape), F32), *pairs_of(2 * planes)],
-        6,
-    )
-
-
 class PairScatter:
     PARTS = 2
 
     def __init__(self, planes, here, left, right, turned, buffers, near, up, down):
         self.planes, self.here = planes, here
         self.left, self.right, self.turned = left, right, turned
-        self.near_out, self.near_in, self.own, above, below = buffers
+        self.near_out, self.own, slots = buffers
         self.near = near
         self.tokens, width = self.near_out.shape[1:]
         self.tiles = [pl.ds(at, COLUMNS) for at in range(0, width, COLUMNS)]
         size = width // self.PARTS
-        every = slice(None)
-        parts = [
-            ((every, pl.ds(at, size)), [(rows, pl.ds(at, size)) for rows in row_tiles(self.tokens, 32)])
-            for at in range(0, width, size)
-        ]
+
+        def part(p):
+            at = p * size if isinstance(p, int) else pl.multiple_of(p * size, 128)
+            return (slice(None), pl.ds(at, size))
+
         self.line = LineScatter(
             planes,
             here,
-            parts,
+            self.PARTS,
+            part,
+            lambda p: [(rows, part(p)[1]) for rows in row_tiles(self.tokens, 32)],
             lambda t, tile: self.own[(t, *tile)].astype(F32),
-            above,
-            below,
+            slots,
             up,
             down,
         )
@@ -904,7 +856,7 @@
     def near_copy(self, i):
         z, c, core = self.here
         at = (slice(None), slice(None), self.tiles[i])
-        return remote(self.near_out.at[at], self.near_in.at[at], self.near, i, (z, c, 1 - core))
+        return remote(self.near_out.at[at], self.own.at[at], self.near, i, (z, c, 1 - core))
 
     def start(self):
         core, tokens = self.here[2], self.tokens
@@ -920,7 +872,7 @@
             self.near_copy(i).wait_recv()
             for t in range(self.planes):
                 self.own[t, :, columns] = (
-                    part[t * tokens : (t + 1) * tokens] + self.near_in[t, :, columns].astype(F32)
+                    part[t * tokens : (t + 1) * tokens] + self.own[t, :, columns].astype(F32)
                 ).astype(LOW)
         self.line.step(0)
 
@@ -934,52 +886,255 @@
 
     @staticmethod
     def scratch(planes, tokens, width):
-        return [pltpu.VMEM((planes, tokens, width), LOW)] * 5
+        return [
+            *[pltpu.VMEM((planes, tokens, width), LOW)] * 2,
+            pltpu.VMEM((planes + 1, tokens, width), LOW),
+        ]
 
     @classmethod
     def sems(cls, planes, width):
         return pairs_of(width // COLUMNS, cls.PARTS * planes, cls.PARTS * planes)
 
 
-def line_scatter_kernel(
-    planes, chips, left_ref, right_ref, grad_ref, out_ref, slots_ref,
-    near_out, near_in, own, above, below, *sems,
+def feed_forward_kernel(
+    planes, chips, width_ff, x_ref, up_ref, grads_ref, down_ref,
+    out_ref, normed_ref, downs_ref, gup_ref, slots_ref,
+    rows, ups, grads, downs, back, act, slope, stat, stat_out, stat_in,
+    normed, d_up, near_out, own, sums, gup, gdown, *sems,
 ):
     here = place()
     z, c, core = here
-    near, up, down, swap_sems = [sems[2 * i : 2 * i + 2] for i in range(4)]
+    count = 2 * planes
+    me = 2 * z + core
+    up, down, near, chip_sems, stat_sems, pair, rise, fall, swap_sems = [
+        sems[2 * i : 2 * i + 2] for i in range(9)
+    ]
+    local = sems[18]
+    tokens, width = x_ref.shape
+    units = ups.shape[1]
+    load_up = pltpu.make_async_copy(up_ref, ups, local.at[0])
+    load_grads = pltpu.make_async_copy(grads_ref, grads, local.at[1])
+    load_up.start()
+    load_grads.start()
     barrier = pltpu.get_barrier_semaphore()
-    peers = [(z, c, 1 - core), *chip_peers(chips, here)]
+    ids = [lax.rem(me + k, count) for k in range(1, count)]
+    group_peers = [(index // 2, c, lax.rem(index, 2)) for index in ids]
+    peers = [*group_peers, *chip_peers(chips, here)]
     greet(barrier, peers)
-    greet_line(barrier, planes, here)
-    pl.semaphore_wait(barrier, len(peers) + line_peers(planes, here))
-    swap = ChipSwap(chips, here, lambda index: grad_ref.at[index], slots_ref, swap_sems)
-    swap.start(sems[8].at[0])
+    pl.semaphore_wait(barrier, len(peers))
+
+    group = GroupGather(planes, here, x_ref, rows, up, down, near)
+    group.start(local.at[2])
+    keep = pltpu.make_async_copy(down_ref, downs.at[c], local.at[3])
+    keep.start()
+    sends = [
+        remote(down_ref, downs.at[c], chip_sems, k, device)
+        for k, device in enumerate(chip_peers(chips, here), 1)
+    ]
+    for copy in sends:
+        copy.start()
+    load_up.wait()
+
+    step = 16
+    lane = lax.broadcasted_iota(jnp.int32, (step, 128), 1)
+
+    def forward(t):
+        group.other(t)
+        block = rows[t].reshape(2 * tokens, width)
+        for at in range(0, units, COLUMNS):
+            columns = pl.ds(at, COLUMNS)
+            act[t, :, columns] = jnp.dot(block, ups[:, columns], preferred_element_type=F32)
+
+        def some(i, carry):
+            at = pl.ds(pl.multiple_of(i * step, step), step)
+            value = act[t, at]
+            phi = 0.5 * (1.0 + lax.erf(value * math.sqrt(0.5)))
+            result = value * phi
+            act[t, at] = result
+            slope[t, at] = phi + value * (
+                jnp.exp(value * value * -0.5) * (1.0 / math.sqrt(2.0 * math.pi))
+            )
+            total = jnp.sum(result, axis=1, keepdims=True)
+            square = jnp.sum(result * result, axis=1, keepdims=True)
+            stat[t, at] = jnp.where(lane == 0, total, jnp.where(lane == 1, square, 0.0))
+            return carry
+
+        lax.fori_loop(0, 2 * tokens // step, some, 0)
+
+    forward(z)
+    for d in range(1, planes):
+        group.step(d)
+        if d > 1:
+            pl.when(z - d + 1 >= 0)(lambda d=d: forward(z - d + 1))
+            pl.when(z + d - 1 < planes)(lambda d=d: forward(z + d - 1))
+    pl.when(z - planes + 1 >= 0)(lambda: forward(z - planes + 1))
+    pl.when(z + planes - 1 < planes)(lambda: forward(z + planes - 1))
+    group.finish()
+    keep.wait()
+    load_grads.wait()
+    for k in range(1, chips):
+        sends[k - 1].wait_send()
+        other = lax.rem(c + chips - k, chips)
+        remote(down_ref, downs.at[other], chip_sems, k, here).wait_recv()
+    out_downs = pltpu.make_async_copy(downs, downs_ref, local.at[4])
+    out_downs.start()
+
+    def backward(t, carry):
+        block = grads[t].reshape(2 * tokens, width)
+        size = units // chips
+        for chip in range(chips):
+            columns = pl.ds(chip * size, size)
+            back[t, :, columns] = rows_product(block, downs[chip])
+
+        def some(i, inner):
+            at = pl.ds(pl.multiple_of(i * step, step), step)
+            value = back[t, at]
+            cross = jnp.sum(value * act[t, at], axis=1, keepdims=True)
+            total = jnp.sum(value, axis=1, keepdims=True)
+            stat[t, at] = jnp.where(lane == 2, cross, jnp.where(lane == 3, total, stat[t, at]))
+            return inner
+
+        lax.fori_loop(0, 2 * tokens // step, some, 0)
+        for half in range(2):
+            turned = stat[t, pl.ds(half * tokens, tokens)].T
+            stat_out[2 * t + half] = turned[:8]
+        return carry
+
+    lax.fori_loop(0, planes, backward, 0)
+    copies = [
+        remote(stat_out, stat_in.at[k], stat_sems, k, device)
+        for k, device in enumerate(group_peers, 1)
+    ]
+    for copy in copies:
+        copy.start()
+    for copy in copies:
+        copy.wait_send()
+        copy.wait_recv()
+
+    def finish(t, carry):
+        for half in range(2):
+            total = stat_out[2 * t + half]
+            for k in range(1, count):
+                total = total + stat_in[k, 2 * t + half]
+            padded = jnp.concatenate([total, jnp.zeros((128 - 8, tokens), F32)], axis=0)
+            stat[t, pl.ds(half * tokens, tokens)] = padded.T
+
+        def some(i, inner):
+            at = pl.ds(pl.multiple_of(i * step, step), step)
+            figures = stat[t, at] * (1.0 / width_ff)
+            mean, square, cross, first = (figures[:, j : j + 1] for j in range(4))
+            scaler = lax.rsqrt(square - mean * mean + NORM_EPS)
+            second = scaler * (cross - mean * first)
+            unit = (act[t, at] - mean) * scaler
+            normed[t, at] = unit.astype(LOW)
+            d_act = scaler * (back[t, at] - first - unit * second)
+            d_up[t, at] = (d_act * slope[t, at]).astype(LOW)
+            return inner
+
+        lax.fori_loop(0, 2 * tokens // step, some, 0)
+        return carry
+
+    lax.fori_loop(0, planes, finish, 0)
+    out_normed = pltpu.make_async_copy(normed, normed_ref, local.at[5])
+    out_normed.start()
     work = PairScatter(
-        planes, here, left_ref, right_ref, True, (near_out, near_in, own, above, below),
-        near, up, down,
+        planes, here, Halves(d_up, tokens), ups, True, (near_out, own, sums), pair, rise, fall
     )
     work.start()
-    for i in range(1, planes - 1):
-        work.line.step(i)
+
+    flat_normed, flat_d_up = (
+        whole[...].reshape(planes * 2 * tokens, units) for whole in (normed, d_up)
+    )
+    size = units // chips
+    swap = ChipSwap(chips, here, lambda index: gdown.at[index], slots_ref, swap_sems)
+    turns_left = list(range(1, work.line.steps))
+
+    def turn():
+        if turns_left:
+            work.line.step(turns_left.pop(0))
+
+    together = max(1, 256 // size)
+    for chip in range(0, chips, together):
+        left = flat_normed[:, chip * size : (chip + together) * size]
+        for at in range(0, width, COLUMNS):
+            columns = pl.ds(at, COLUMNS)
+            right = grads[:, :, :, columns].reshape(planes * 2 * tokens, COLUMNS)
+            term = token_product(left, right).astype(LOW)
+            for i in range(together):
+                gdown[chip + i, :, columns] = term[i * size : (i + 1) * size]
+        turn()
+    swap.start(local.at[6])
+    chunk = gup.shape[1]
+    out_gups = [
+        pltpu.make_async_copy(
+            gup.at[i % 2], gup_ref.at[pl.ds(i * chunk, chunk)], local.at[7 + i % 2]
+        )
+        for i in range(width // chunk)
+    ]
+    for i in range(width // chunk):
+        turn()
+        left = rows[:, :, :, pl.ds(i * chunk, chunk)].reshape(planes * 2 * tokens, chunk)
+        term = token_product(left, flat_d_up).astype(LOW)
+        if i > 1:
+            out_gups[i - 2].wait()
+        gup[i % 2] = term
+        out_gups[i].start()
+    while turns_left:
+        turn()
     work.finish(out_ref)
     swap.finish()
-
-
-def line_scatter(planes, chips, left, right, grads):
-    tokens, width = left.shape[2], right.shape[0]
+    out_downs.wait()
+    out_normed.wait()
+    for copy in out_gups[-2:]:
+        copy.wait()
+
+
+class Halves:
+    def __init__(self, whole, tokens):
+        self.whole, self.tokens = whole, tokens
+
+    def __getitem__(self, at):
+        t, core = at
+        rows = pl.ds(pl.multiple_of(core * self.tokens, self.tokens), self.tokens)
+        return self.whole[t, rows]
+
+
+def feed_forward(planes, chips, width_ff, x_block, up_mine, grads, down_block):
+    tokens, width = x_block.shape
+    units = up_mine.shape[1]
+    size = down_block.shape[0]
+    wide = (planes, 2 * tokens, units)
     return call(
-        functools.partial(line_scatter_kernel, planes, chips),
-        "line_scatter",
-        [shape((tokens, width), F32), shape(grads.shape, LOW)],
-        (left, right, grads),
-        [VMEM, VMEM, HBM],
-        [VMEM, HBM],
+        functools.partial(feed_forward_kernel, planes, chips, width_ff),
+        "feed_forward",
         [
+            shape((tokens, width), F32),
+            shape(wide, LOW),
+            shape((chips, size, width), LOW),
+            shape((width, units), LOW),
+            shape((chips, size, width), LOW),
+        ],
+        (x_block, up_mine, grads, down_block),
+        [HBM] * 4,
+        [VMEM, HBM, HBM, HBM, HBM],
+        [
+            pltpu.VMEM((planes, 2, tokens, width), LOW),
+            pltpu.VMEM((width, units), LOW),
+            pltpu.VMEM((planes, 2, tokens, width), LOW),
+            pltpu.VMEM((chips, size, width), LOW),
+            *[pltpu.VMEM(wide, F32)] * 3,
+            pltpu.VMEM((planes, 2 * tokens, 128), F32),
+            pltpu.VMEM((2 * planes, 8, 128), F32),
+            pltpu.VMEM((2 * planes, 2 * planes, 8, 128), F32),
+            *[pltpu.VMEM(wide, LOW)] * 2,
             *PairScatter.scratch(planes, tokens, width),
+            pltpu.VMEM((2, 256, units), LOW),
+            pltpu.VMEM((chips, size, width), LOW),
+            *GroupGather.sems(planes),
+            *pairs_of(chips, 2 * planes),
             *PairScatter.sems(planes, width),
             *pairs_of(chips),
-            pltpu.SemaphoreType.DMA((1,)),
+            pltpu.SemaphoreType.DMA((9,)),
         ],
         7,
     )
@@ -988,7 +1143,7 @@
 def plane_gather_kernel(
     planes, chips, x_ref, stat_ref, tile_ref, left_ref, right_ref,
     row_ref, stats_ref, tiles_ref, ffn_ref,
-    near_out, near_in, own, above, below, *sems,
+    near_out, own, sums, *sems,
 ):
     here = place()
     z, c, core = here
@@ -1034,12 +1189,12 @@
 
     lax.fori_loop(1, count, tile_start, 0)
     work = PairScatter(
-        planes, here, left_ref, right_ref, False, (near_out, near_in, own, above, below),
+        planes, here, Halves(left_ref, x_ref.shape[0]), right_ref, False, (near_out, own, sums),
         near, up, down,
     )
     work.start()
-    for i in range(1, planes - 1):
-        if i == planes - 2:
+    for i in range(1, work.line.steps):
+        if i == work.line.steps // 2:
             rows.forward()
             stats.forward()
         work.line.step(i)
@@ -1178,16 +1333,21 @@
 
 
 def attention_back_kernel(
-    planes, heads, strided,
-    q_ref, k_ref, v_ref, att_ref, row_ref, right_ref, stat_ref, log_ref, meta_ref,
-    out_ref, total_ref,
-    grad, dq, dk, dv, normed_all, own, above, below, *sems,
+    planes, chips, heads, strided,
+    q_ref, k_ref, v_ref, att_ref, row_ref, right_ref, stat_ref, log_ref, meta_ref, up_ref,
+    out_ref, total_ref, slots_ref,
+    grad, dq, dk, dv, normed_all, own, sums, *sems,
 ):
     here = place()
-    up, down = sems[:2], sems[2:]
+    up, down, swap_sems = [sems[2 * i : 2 * i + 2] for i in range(3)]
     barrier = pltpu.get_barrier_semaphore()
+    greet(barrier, chip_peers(chips, here))
     greet_line(barrier, planes, here)
-    pl.semaphore_wait(barrier, line_peers(planes, here))
+    pl.semaphore_wait(barrier, chips - 1 + line_peers(planes, here))
+    swap = ChipSwap(
+        chips, here, lambda index: half_block(up_ref, slots_ref, index, 0), slots_ref, swap_sems
+    )
+    swap.start(sems[6].at[0])
     length, span = att_ref.shape
     part, width = own.shape[1:]
     for rows in row_tiles(length, BLOCK):
@@ -1206,10 +1366,11 @@
     line = LineScatter(
         planes,
         here,
-        [((slice(None),), [(rows,) for rows in row_tiles(part, 16)])],
+        1,
+        lambda p: (slice(None),),
+        lambda p: [(rows,) for rows in row_tiles(part, 16)],
         lambda t, tile: own[(t, *tile)].astype(F32),
-        above,
-        below,
+        sums,
         up,
         down,
     )
@@ -1276,24 +1437,31 @@
     else:
         for t in range(planes):
             total_ref[pl.ds(t * part, part)] = own[t].astype(F32)
-
-
-def attention_back(planes, heads, strided, part, args):
+    swap.finish()
+
+
+def attention_back(planes, chips, heads, strided, part, units, args):
     length, span = args[3].shape
     width = args[4].shape[1]
     return call(
-        functools.partial(attention_back_kernel, planes, heads, strided),
+        functools.partial(attention_back_kernel, planes, chips, heads, strided),
         "attention_back",
-        [shape((length, 3 * span), LOW), shape((part if strided else span, width), F32)],
+        [
+            shape((length, 3 * span), LOW),
+            shape((part if strided else span, width), F32),
+            shape((chips, width // 2, units), LOW),
+        ],
         args,
-        [VMEM] * 9,
-        [VMEM] * 2,
+        [*[VMEM] * 9, HBM],
+        [*[VMEM] * 2, HBM],
         [
             pltpu.VMEM((heads, length, HD), LOW),
             *[pltpu.VMEM((heads, length, HD), F32)] * 3,
             pltpu.VMEM((length, span), LOW),
-            *[pltpu.VMEM((planes, part, width), LOW)] * 3,
-            *pairs_of(planes, planes),
+            pltpu.VMEM((planes, part, width), LOW),
+            pltpu.VMEM((planes + 1, part, width), LOW),
+            *pairs_of(planes, planes, chips),
+            pltpu.SemaphoreType.DMA((1,)),
         ],
         8,
     )
@@ -1329,7 +1497,6 @@
     span = heads * HD
     part = w_qkv.shape[0]
     strided = part % HD == 0
-    group_tokens = planes * 2 * tokens
     width_ff = w_down.shape[0] * planes * seqs
     seq_index = lax.axis_index(SEQ)
 
@@ -1370,8 +1537,6 @@
         out_all = lax.all_gather(out_scaled, ALL, axis=0, tiled=True)
         out_mine = lax.dynamic_slice_in_dim(out_all, seq_index * span, span, axis=0)
     queries, keys, values, attended, log_total = attention(heads, dot(row_in, qkv_mine), meta)
-    down_scaled, attended = lax.optimization_barrier((down_scaled, attended))
-    down_mine = lax.all_gather(down_scaled, "chip", axis=0, tiled=True)
     attended_wide = attended.astype(F32)
     column_part = jnp.sum(out_mine.astype(F32), axis=0)
     token_sums = jnp.stack(
@@ -1389,7 +1554,6 @@
     out_sum, tiles, grad_flat = out_scatter(
         planes, chips, attended.reshape(seqs, tokens, span), out_mine, tiles, grad_low
     )
-    grad_flat = grad_flat.reshape(group_tokens, width)
     tiles = jnp.sum(tiles, axis=0)
     column_sum = tiles[8:].reshape(width)
     sums = tiles[:2].T
@@ -1402,43 +1566,13 @@
     ffn_in = (normed_three * gain_three).astype(LOW)
 
     grad_top = grad_low.astype(F32)
-    ffn_flat = line_gather(planes, ffn_in).reshape(group_tokens, width)
-    weighted = rows_product(grad_flat, down_mine)
-    up_slice = dot(ffn_flat, up_mine)
-    activated, gelu_pull = jax.vjp(exact_gelu, up_slice)
-    stats = group_sums(
-        planes,
-        jnp.stack(
-            [
-                jnp.sum(activated, axis=1),
-                jnp.sum(activated * activated, axis=1),
-                jnp.sum(weighted * activated, axis=1),
-                jnp.sum(weighted, axis=1),
-            ]
-        ),
-    )[:, :, None]
-    act_mean = stats[0] / width_ff
-    scaler_four = lax.rsqrt(stats[1] / width_ff - act_mean * act_mean + NORM_EPS)
-    normed_four = (activated - act_mean) * scaler_four
-    normed_four_low = normed_four.astype(LOW)
-    first_mean = stats[3] / width_ff
-    second_mean = scaler_four * (stats[2] - act_mean * stats[3]) / width_ff
-    d_act = scaler_four * (weighted - first_mean - normed_four * second_mean)
-    (d_up,) = gelu_pull(d_act)
-    d_up_low = d_up.astype(LOW)
-    grad_up = token_product(ffn_flat, d_up_low).astype(LOW)
-    grad_down = token_product(normed_four_low, grad_flat).astype(LOW)
     units = w_up.shape[1]
+    d_ffn_in, normed_four, down_mine, grad_up, down_slots = feed_forward(
+        planes, chips, width_ff, ffn_in, up_mine, grad_flat, down_scaled
+    )
+    down_mine = down_mine.reshape(-1, width)
     if units % 128:
         grad_up = grad_up.reshape(width, chips, units).transpose(1, 0, 2)
-    d_up_low, grad_up = lax.optimization_barrier((d_up_low, grad_up))
-    d_ffn_in, down_slots = line_scatter(
-        planes,
-        chips,
-        d_up_low.reshape(planes, 2, tokens, -1),
-        up_mine,
-        grad_down.reshape(chips, -1, width),
-    )
 
     gain_part = jnp.sum(d_ffn_in * normed_three, axis=0).reshape(planes * seqs, 1, part)
     gain_part = jnp.pad(gain_part, ((0, 0), (0, 7), (0, 128 - part)))
@@ -1454,22 +1588,24 @@
         d_hmid_low,
         jnp.pad(token_stats, ((0, 0), (0, 124))),
         gain_part,
-        normed_four_low.reshape(planes, 2, tokens, -1),
+        normed_four,
         down_mine,
     )
     output = (hmid + ffn_out).astype(LOW)[None]
     row_grad = row_grad.reshape(length, width)
     row_stats = row_stats.reshape(length, 128)
     grad_gain_three = jnp.sum(gain_part, axis=0)[0, :part]
-    d_qkv, sum_out = attention_back(
+    d_qkv, sum_out, upper_slots = attention_back(
         planes,
+        chips,
         heads,
         strided,
         part,
-        (queries, keys, values, attended, row_grad, out_mine, row_stats, log_total, meta),
+        units,
+        (queries, keys, values, attended, row_grad, out_mine, row_stats, log_total, meta, grad_up),
     )
     grad_qkv = token_product(row_in, d_qkv).astype(LOW)
-    d_in, sum_qkv, grad_gain_one, up_slots = in_scatter(
+    d_in, sum_qkv, grad_gain_one, lower_slots = in_scatter(
         planes,
         chips,
         heads,
@@ -1483,7 +1619,9 @@
         units,
     )
     grad_gain_one = grad_gain_one[:, 0]
-    sum_up = jnp.sum(up_slots.astype(F32), axis=0)
+    sum_up = jnp.concatenate(
+        [jnp.sum(slots.astype(F32), axis=0) for slots in (upper_slots, lower_slots)], axis=0
+    )
     sum_down = jnp.sum(down_slots.astype(F32), axis=0)
     input_grad = (d_hmid + norm_back(d_in, normed_one, scaler_one)).astype(LOW)[None]
 

time: 673 us -> 571 us (0.85)
  matrix products: 57.3 us -> 16.1 us
  Pallas kernels: 522 us -> 494 us
  between operations: 15 us -> 1.55 us
  other arithmetic: 49.2 us -> 36.3 us
    pallas_call x9 -> x7, Pallas kernels: 522 us -> 494 us  [call(): pl.pallas_call(kernel, name=name, out_shape=outs, in_specs=in_specs, out_...]
    dot_general x2 -> x1, matrix products: 28.1 us -> 8.24 us  [dot(): return jnp.dot(left_op, right_op, preferred_element_type=F32)]
    dot_general x3 -> x1, matrix products: 19.2 us -> 7.88 us  [token_product(): lax.dot_general(left_op, right_op, (((0,), (0,)), ((), ())), preferred_el...]
    dot_general x1 -> x0, matrix products: 9.96 us -> none  [rows_product(): lax.dot_general(operand, weight_rows, (((1,), (1,)), ((), ())), preferred...]
  transfers between devices with their start and end apart: 1 -> 0, of which waited for: 0 -> 0; matrix products, arithmetic and copies ran while one was open for 2% -> 0% of each run, Pallas kernels for 18% -> 0%
where the time goes in v4:
time: 571 us; the launch traced here: 562 us
  Pallas kernels  494 us (87%)
  other arithmetic  36.3 us (6%)
  matrix products  16.1 us (3%)
  local copies, waits for them, and re-layouts  14.4 us (3%)
    pallas_call x7, Pallas kernels, call(): pl.pallas_call(kernel, name=name, out_shape=outs, in_specs=in_specs, out_...  494 us

profile of v4, /device:TPU:9, one launch (start us, length us, event | category | flops | bytes accessed | tf_op | source)
XLA Modules:
  0.0 562.3 jit_solution(15033696436922834339)
XLA Ops:
  3.8 1.2 convert_reduce_fusion.5
  5.3 1.1 fusion.11.x_ref
  6.4 1.5 fusion.4
  7.9 1.6 reshape.228
  9.5 1.8 copy.64
  11.3 3.6 reshape.229.qkv_ref
  16.3 93.2 %attention_gather.1 = (bf16[8,128,2048]{2,1,0:T(8,128)(2,1)}, f32[8,128,256]{2,1,0:T(8,128)}, bf16[4,8,64,768]{3,2,1,0:T(8,128)(2,1)}, bf16[4,64,2048]{2,1,0:T(8...) custom-call(bf16[128,2048]{1,0:T(8,128)(2,1)} %fusion.11.x_ref, f32[128,256]{1,0:T(8,128)} %pad_maximum_fusion.1.meta_ref, ...), custom_call_target="tpu_custom_call" | custom-call | tf_op jit(solution)/shard_map/attention_gather/pallas_call | solution.py:86
  109.6 8.2 %fusion.31.raw_ref = f32[1024,768]{1,0:T(8,128)} fusion(bf16[1024,2048]{1,0:T(8,128)(2,1)} %bitcast.107, bf16[2048,768]{1,0:T(8,128)(2,1)} %bitcast.91), kind=kOutput, calls=%fused_computation.100 | convolution fusion | flops 3221225472 | bytes 10485760 | tf_op jit(solution)/shard_map/dot_general | solution.py:58
  117.8 14.9 %attention.1 = (bf16[4,1024,64]{2,1,0:T(8,128)(2,1)}, bf16[4,1024,64]{2,1,0:T(8,128)(2,1)}, bf16[4,1024,64]{2,1,0:T(8,128)(2,1)}, bf16[1024,256]{1,0:T(8,128)(2,1)}, f32[1024,128]{1,0:T(8,128)}) custom-call(f32[1024,768]{1,0:T(8,128)} %fusion.31.raw_ref, f32[1024,256]{1,0:T(8,128)} %bitcast.89), custom_call_target="tpu_custom_call" | custom-call | tf_op jit(solution)/shard_map/attention/pallas_call | solution.py:86
  132.7 1.4 convert_reduce_fusion.4
  135.1 56.4 %out_scatter.1 = (f32[128,2048]{1,0:T(8,128)}, f32[8,24,128]{2,1,0:T(8,128)}, bf16[4,2,128,2048]{3,2,1,0:T(8,128)(2,1)}) custom-call(bf16[8,128,256]{2,1,0:T(8,128)(2,1)} %bitcast.86, bf16[256,2048]{1,0:T(8,128)(2,1)} %bitcast.83, f32[8,24,128]{2,1,0:T(8,128)} %pad_maximum_fusion.2.tile_ref, bf16[128,2048]{1,0:T(8,128)(2,1)} %bitcast.94), custom_call_target="tpu_custom_call" | custom-call | tf_op jit(solution)/shard_map/out_scatter/pallas_call | solution.py:86
  191.5 0.9 reduce_sum.194
  192.5 1.7 fusion.29
  194.4 1.0 slice_reduce_fusion.1
  195.4 1.0 multiply_convert_fusion.x_ref
  196.5 1.2 fusion.down_ref
  197.7 169.4 %feed_forward.1 = (f32[128,2048]{1,0:T(8,128)}, bf16[4,256,1024]{2,1,0:T(8,128)(2,1)}, bf16[4,256,2048]{2,1,0:T(8,128)(2,1)}, bf16[2048,1024]{1,0:T(8,128)(2,1)}, bf16[4,256,2048]{2,1,0:T(8,128)(2,1)}) custom-call(bf16[128,2048]{1,0:T(8,128)(2,1)} %multiply_convert_fusion.x_ref, bf16[2048,1024]{1,0:T(8,128)(2,1)} %get-tuple-element.68.up_ref, ...), custom_call_target="tpu_custom_call" | custom-call | tf_op jit(solution)/shard_map/feed_forward/pallas_call | solution.py:86
  367.1 1.7 multiply_reduce_fusion
  368.9 1.8 fusion.19
  372.3 56.1 %plane_gather.1 = (bf16[8,128,2048]{2,1,0:T(8,128)(2,1)}, f32[8,128,128]{2,1,0:T(8,128)}, f32[32,8,128]{2,1,0:T(8,128)}, f32[128,2048]{1,0:T(8,128)}) custom-call(bf16[128,2048]{1,0:T(8,128)(2,1)} %get-tuple-element.99.x_ref, f32[128,128]{1,0:T(8,128)} %pad.13.stat_ref, f32[32,8,128]{2,1,0:T(8,128)} %pad.14.tile_ref, ...), custom_call_target="tpu_custom_call" | custom-call | tf_op jit(solution)/shard_map/plane_gather/pallas_call | solution.py:86
  428.4 31.5 %attention_back.1 = (bf16[1024,768]{1,0:T(8,128)(2,1)}, f32[64,2048]{1,0:T(8,128)}, bf16[4,1024,256]{2,1,0:T(8,128)(2,1)}) custom-call(bf16[4,1024,64]{2,1,0:T(8,128)(2,1)} %get-tuple-element.74.q_ref, bf16[4,1024,64]{2,1,0:T(8,128)(2,1)} %get-tuple-element.75.k_ref, bf16[4,1024,64]{2,1,0:T(8,128)(2,1)} %get-tuple-element.76.v_ref, ...), custom_call_target="tpu_custom_call" | custom-call | tf_op jit(solution)/shard_map/attention_back/pallas_call | solution.py:86
  459.9 7.9 %convolution_convert_fusion = bf16[2048,768]{1,0:T(8,128)(2,1)} fusion(bf16[1024,2048]{1,0:T(8,128)(2,1)} %bitcast.108, bf16[1024,768]{1,0:T(8,128)(2,1)} %get-tuple-element.81), kind=kOutput, calls=%fused_computation.3 | convolution fusion | flops 3222798336 | bytes 8912896 | tf_op jit(solution)/shard_map/dot_general | solution.py:68
  468.5 72.4 %in_scatter.1 = (f32[128,2048]{1,0:T(8,128)}, f32[64,6144]{1,0:T(8,128)}, f32[64,128]{1,0:T(8,128)}, bf16[4,1024,256]{2,1,0:T(8,128)(2,1)}) custom-call(bf16[8,128,768]{2,1,0:T(8,128)(2,1)} %bitcast.95, bf16[2048,768]{1,0:T(8,128)(2,1)} %bitcast.92, bf16[4,8,64,768]{3,2,1,0:T(8,128)(2,1)} %bitcast.93, bf16[2048,1024]{1,0:T(8,128)(2,1)} %get-tuple-element.80.up_ref, ...), custom_call_target="tpu_custom_call" | custom-call | tf_op jit(solution)/shard_map/in_scatter/pallas_call | solution.py:86
  541.0 2.2 convert_reduce_fusion.1
  543.5 1.5 pad_maximum_fusion
  545.8 1.3 fusion.25
  547.7 1.7 fusion.22
  549.4 0.9 fusion.24
  550.9 3.4 convert_reduce_fusion
  554.4 3.1 fusion.1
  558.0 1.6 multiply_add_fusion
  560.7 1.1 copy.66
  (118 shorter events, 12.4 us)
Async XLA Ops:
  0.7 4.3 copy-start
  0.7 5.7 %copy-start.22 = (bf16[64]{0:T(256)(128)(2,1)S(1)}, bf16[64]{0:T(256)(128)(2,1)}, u32[]{:S(2)}) copy-start(bf16[64]{0:T(256)(128)(2,1)} %param.28) | copy-start | bytes 388
  0.7 5.7 %copy-start.8 = (bf16[64,6144]{1,0:T(8,128)(2,1)S(1)}, bf16[64,6144]{1,0:T(8,128)(2,1)}, u32[]{:S(2)}) copy-start(bf16[64,6144]{1,0:T(8,128)(2,1)} %weight_ref.1) | copy-start | bytes 2359300
  2.9 3.5 copy-start.13
  9.5 5.4 copy-start.24
  9.5 5.4 copy-start.15
  11.3 4.4 copy-start.25
  117.8 16.3 %copy-start.1 = (bf16[4,64,2048]{2,1,0:T(8,128)(2,1)S(1)}, bf16[4,64,2048]{2,1,0:T(8,128)(2,1)}, u32[]{:S(2)}) copy-start(bf16[4,64,2048]{2,1,0:T(8,128)(2,1)} %get-tuple-element.64) | copy-start | bytes 3145732
  192.4 4.0 copy-start.23
  192.5 4.0 copy-start.3
  197.7 171.2 %copy-start.12 = (bf16[1,128,2048]{2,1,0:T(8,128)(2,1)S(1)}, bf16[1,128,2048]{2,1,0:T(8,128)(2,1)}, u32[]{:S(2)}) copy-start(bf16[1,128,2048]{2,1,0:T(8,128)(2,1)} %param.40) | copy-start | bytes 1572868
  367.1 1.8 copy-start.4
  367.1 1.8 copy-start.5
  540.9 2.2 copy-start.10
  543.5 1.6 copy-start.6
  543.5 2.3 copy-start.7
  545.1 2.0 copy-start.20
  545.1 2.6 copy-start.17
  545.1 2.6 copy-start.18
  545.8 3.6 copy-start.16
  547.7 2.7 copy-start.19
  550.9 3.4 copy-start.9
  554.3 3.1 copy-start.26
  554.3 3.1 copy-start.27
  554.3 3.6 copy-start.2
  554.4 3.6 copy-start.11
  558.0 1.7 copy-start.21
  558.0 2.2 copy-start.28
  558.0 2.7 copy-start.14

commit v5 on v4

--- a/solution.py
+++ b/solution.py
@@ -329,142 +329,6 @@
     @classmethod
     def sems(cls, planes):
         return pairs_of(*[planes * cls.PARTS] * 3)
-
-
-def attention_gather_kernel(
-    planes, chips, x_ref, meta_ref, qkv_ref, out_ref, gain_ref, up_ref,
-    row_ref, metas_ref, qkvs_ref, outs_ref, gains_ref, ups_ref,
-    *sems,
-):
-    here = place()
-    z, c, core = here
-    seqs = 2 * chips
-    count = planes * seqs
-    me = 2 * c + core
-    flat = z * seqs + me
-    groups = [sems[2 * i : 2 * i + 2] for i in range(11)]
-    swap_sems, x_far, x_near, meta_far, meta_near, up, down, up_two, down_two = groups[:9]
-    gain_sems, up_sems = groups[9:]
-    local = sems[22]
-    barrier = pltpu.get_barrier_semaphore()
-
-    def device_of(k):
-        other = lax.rem(flat + k, count)
-        return (other // seqs, lax.rem(other, seqs) // 2, lax.rem(other, 2))
-
-    def signal(k, carry):
-        greet(barrier, [device_of(k)])
-        return carry
-
-    lax.fori_loop(1, count, signal, 0)
-    pl.semaphore_wait(barrier, count - 1)
-
-    mine = pltpu.make_async_copy(qkv_ref.at[me], qkvs_ref.at[z, me], local.at[0])
-    keeps = [
-        pltpu.make_async_copy(x_ref, row_ref.at[me], local.at[1]),
-        pltpu.make_async_copy(meta_ref, metas_ref.at[me], local.at[2]),
-        pltpu.make_async_copy(gain_ref, gains_ref.at[flat], local.at[3]),
-    ]
-    own_out = pltpu.make_async_copy(out_ref, outs_ref.at[z], local.at[4])
-    units = up_ref.shape[1]
-    keeps.append(pltpu.make_async_copy(up_ref, column_block(ups_ref, units, c), local.at[5]))
-    ups = [
-        remote(up_ref, column_block(ups_ref, units, c), up_sems, k, device)
-        for k, device in enumerate(chip_peers(chips, here), 1)
-    ]
-    swaps = [
-        remote(qkv_ref.at[2 * device[1] + device[2]], qkvs_ref.at[z, me], swap_sems, k, device)
-        for k, device in enumerate(plane_peers(chips, here), 1)
-    ]
-    mine.start()
-    own_out.start()
-    for copy in swaps:
-        copy.start()
-    rows = PlaneGather(chips, here, x_ref, row_ref, x_far, x_near)
-    metas = PlaneGather(chips, here, meta_ref, metas_ref, meta_far, meta_near)
-    rows.start()
-    metas.start()
-    for copy in keeps:
-        copy.start()
-
-    def gain_copy(k):
-        return remote(gain_ref, gains_ref.at[flat], gain_sems, k, device_of(k))
-
-    def gain_start(k, carry):
-        gain_copy(k).start()
-        return carry
-
-    lax.fori_loop(1, count, gain_start, 0)
-
-    mine.wait()
-    own_out.wait()
-    for k in range(1, seqs):
-        index = lax.rem(me + seqs - k, seqs)
-        remote(qkv_ref.at[0], qkvs_ref.at[z, index], swap_sems, k, here).wait_recv()
-    half = seqs // 2
-    line = LineGather(
-        planes, here, lambda t: [qkvs_ref.at[t, pl.ds(i * half, half)] for i in range(2)], up, down
-    )
-    line_two = LineGather(planes, here, lambda t: [outs_ref.at[t]], up_two, down_two)
-    line.start()
-    line_two.start()
-    rows.forward()
-    metas.forward()
-    for copy in ups:
-        copy.start()
-    for d in range(1, planes):
-        line.step(d)
-        line_two.step(d)
-    line.finish()
-    line_two.finish()
-    rows.finish()
-    metas.finish()
-    for copy in swaps:
-        copy.wait_send()
-    for copy in keeps:
-        copy.wait()
-    for k in range(1, chips):
-        ups[k - 1].wait_send()
-        other = lax.rem(c + chips - k, chips)
-        remote(up_ref, column_block(ups_ref, units, other), up_sems, k, here).wait_recv()
-
-    def gain_wait(k, carry):
-        gain_copy(k).wait_send()
-        other = lax.rem(flat + count - k, count)
-        remote(gain_ref, gains_ref.at[other], gain_sems, k, here).wait_recv()
-        return carry
-
-    lax.fori_loop(1, count, gain_wait, 0)
-
-
-def attention_gather(planes, chips, x_block, meta, qkv_blocks, out_rows, gain_tile, up_block):
-    seqs = 2 * chips
-    part, wide = qkv_blocks.shape[1:]
-    width, units = up_block.shape
-    return call(
-        functools.partial(attention_gather_kernel, planes, chips),
-        "attention_gather",
-        [
-            shape((seqs, *x_block.shape), LOW),
-            shape((seqs, *meta.shape), F32),
-            shape((planes, seqs, part, wide), LOW),
-            shape((planes, *out_rows.shape), LOW),
-            shape((planes * seqs, *gain_tile.shape), F32),
-            shape(
-                (width, chips * units) if units % 128 == 0 else (chips, width, units), LOW
-            ),
-        ],
-        (x_block, meta, qkv_blocks, out_rows, gain_tile, up_block),
-        [HBM] * 6,
-        [HBM] * 6,
-        [
-            *pairs_of(
-                seqs, *[chips] * 4, *[2 * planes] * 2, *[planes] * 2, planes * seqs, chips
-            ),
-            pltpu.SemaphoreType.DMA((6,)),
-        ],
-        1,
-    )
 
 
 COLUMNS = 512
@@ -547,73 +411,6 @@
     @staticmethod
     def sems(chips, width):
         return pairs_of(width // COLUMNS, chips * (width // COLUMNS))
-
-
-def out_scatter_kernel(
-    planes, chips, left_ref, right_ref, tile_ref, grad_ref, out_ref, tiles_ref, grads_ref,
-    near_out, near_in, far_out, far_in, *sems,
-):
-    here = place()
-    z, c, core = here
-    seqs = 2 * chips
-    me = 2 * c + core
-    near, far, tile_sems, up, down, pair = [sems[2 * i : 2 * i + 2] for i in range(6)]
-    local = sems[12]
-    barrier = pltpu.get_barrier_semaphore()
-    peers = plane_peers(chips, here)
-    greet(barrier, peers)
-    greet_line(barrier, planes, here)
-    pl.semaphore_wait(barrier, len(peers) + line_peers(planes, here))
-    group = GroupGather(planes, here, grad_ref, grads_ref, up, down, pair)
-    group.start(local.at[0])
-    swaps = [
-        remote(tile_ref.at[2 * device[1] + device[2]], tiles_ref.at[me], tile_sems, k, device)
-        for k, device in enumerate(peers, 1)
-    ]
-    for copy in swaps:
-        copy.start()
-    keep = pltpu.make_async_copy(tile_ref.at[me], tiles_ref.at[me], local.at[1])
-    keep.start()
-    work = PlaneScatter(
-        chips, here, left_ref, right_ref, False, (near_out, near_in, far_out, far_in), near, far
-    )
-    work.start()
-    for d in range(1, planes):
-        group.step(d)
-    work.finish(out_ref)
-    group.finish()
-    for t in range(planes):
-        group.other(t)
-    keep.wait()
-    for k in range(1, seqs):
-        swaps[k - 1].wait_send()
-        index = lax.rem(me + seqs - k, seqs)
-        remote(tile_ref.at[0], tiles_ref.at[index], tile_sems, k, here).wait_recv()
-
-
-def out_scatter(planes, chips, left, right, tiles, grad):
-    _, tokens, _ = left.shape
-    width = right.shape[1]
-    return call(
-        functools.partial(out_scatter_kernel, planes, chips),
-        "out_scatter",
-        [
-            shape((tokens, width), F32),
-            shape(tiles.shape, F32),
-            shape((planes, 2, *grad.shape), LOW),
-        ],
-        (left, right, tiles, grad),
-        [VMEM, VMEM, VMEM, HBM],
-        [VMEM, VMEM, HBM],
-        [
-            *PlaneScatter.scratch(chips, tokens, width),
-            *PlaneScatter.sems(chips, width),
-            *pairs_of(2 * chips),
-            *GroupGather.sems(planes),
-            pltpu.SemaphoreType.DMA((2,)),
-        ],
-        3,
-    )
 
 
 class LineScatter:
@@ -1062,7 +859,8 @@
             term = token_product(left, right).astype(LOW)
             for i in range(together):
                 gdown[chip + i, :, columns] = term[i * size : (i + 1) * size]
-        turn()
+        if chip // together % 2:
+            turn()
     swap.start(local.at[6])
     chunk = gup.shape[1]
     out_gups = [
@@ -1072,7 +870,8 @@
         for i in range(width // chunk)
     ]
     for i in range(width // chunk):
-        turn()
+        if i % 2 == 0:
+            turn()
         left = rows[:, :, :, pl.ds(i * chunk, chunk)].reshape(planes * 2 * tokens, chunk)
         term = token_product(left, flat_d_up).astype(LOW)
         if i > 1:
@@ -1266,69 +1065,304 @@
 BLOCK = 256
 
 
-def attention_kernel(heads, raw_ref, meta_ref, q_ref, k_ref, v_ref, out_ref, log_ref, wide):
-    length = raw_ref.shape[0]
+def attention_forward_kernel(
+    planes, chips, heads, strided,
+    x_ref, meta_ref, qkv_ref, out_ref, gain_ref, up_ref, grad_ref,
+    q_ref, k_ref, v_ref, att_ref, log_ref, sum_ref,
+    rows_ref, metas_ref, qkvs_ref, outs_ref, gains_ref, ups_ref, grads_ref, tiles_ref,
+    rows, metas, qkvs, outs, raw, wide, tile, near_out, near_in, far_out, far_in,
+    *sems,
+):
+    here = place()
+    z, c, core = here
+    seqs = 2 * chips
+    count = planes * seqs
+    me = 2 * c + core
+    flat = z * seqs + me
+    groups = [sems[2 * i : 2 * i + 2] for i in range(17)]
+    swap_sems, x_far, x_near, meta_far, meta_near, up, down, up_two, down_two = groups[:9]
+    gain_sems, up_sems, near, far, tile_sems, grad_up, grad_down, pair = groups[9:]
+    local = sems[34]
+    tokens, width = x_ref.shape
+    part, three = qkv_ref.shape[1:]
+    length = seqs * tokens
     span = heads * HD
-    for rows in row_tiles(length, BLOCK):
-        tables = turns(meta_ref, rows)
-        for pair in range(heads // 2):
-            lanes = pl.ds(2 * HD * pair, 2 * HD)
-            query = raw_ref[rows, lanes]
+    barrier = pltpu.get_barrier_semaphore()
+
+    def device_of(k):
+        other = lax.rem(flat + k, count)
+        return (other // seqs, lax.rem(other, seqs) // 2, lax.rem(other, 2))
+
+    def signal(k, carry):
+        greet(barrier, [device_of(k)])
+        return carry
+
+    lax.fori_loop(1, count, signal, 0)
+    pl.semaphore_wait(barrier, count - 1)
+
+    mine = pltpu.make_async_copy(qkv_ref.at[me], qkvs.at[z, me], local.at[0])
+    own_out = pltpu.make_async_copy(out_ref, outs.at[z] if strided else outs, local.at[1])
+    units = up_ref.shape[1]
+    keeps = [
+        pltpu.make_async_copy(x_ref, rows.at[me], local.at[2]),
+        pltpu.make_async_copy(meta_ref, metas.at[me], local.at[3]),
+        pltpu.make_async_copy(gain_ref, gains_ref.at[flat], local.at[4]),
+        pltpu.make_async_copy(up_ref, column_block(ups_ref, units, c), local.at[5]),
+    ]
+    peers = plane_peers(chips, here)
+    swaps = [
+        remote(qkv_ref.at[2 * device[1] + device[2]], qkvs.at[z, me], swap_sems, k, device)
+        for k, device in enumerate(peers, 1)
+    ]
+    mine.start()
+    own_out.start()
+    for copy in swaps:
+        copy.start()
+    gather = PlaneGather(chips, here, x_ref, rows, x_far, x_near)
+    meta_gather = PlaneGather(chips, here, meta_ref, metas, meta_far, meta_near)
+    gather.start()
+    meta_gather.start()
+    for copy in keeps:
+        copy.start()
+
+    def gain_copy(k):
+        return remote(gain_ref, gains_ref.at[flat], gain_sems, k, device_of(k))
+
+    def gain_start(k, carry):
+        gain_copy(k).start()
+        return carry
+
+    lax.fori_loop(1, count, gain_start, 0)
+    mine.wait()
+    own_out.wait()
+    for k in range(1, seqs):
+        index = lax.rem(me + seqs - k, seqs)
+        remote(qkv_ref.at[0], qkvs.at[z, index], swap_sems, k, here).wait_recv()
+    half = seqs // 2
+    line = LineGather(
+        planes, here, lambda t: [qkvs.at[t, pl.ds(i * half, half)] for i in range(2)], up, down
+    )
+    line_two = LineGather(planes, here, lambda t: [outs.at[t]], up_two, down_two)
+    line.start()
+    gather.forward()
+    meta_gather.forward()
+    ups = [
+        remote(up_ref, column_block(ups_ref, units, c), up_sems, k, device)
+        for k, device in enumerate(chip_peers(chips, here), 1)
+    ]
+    for copy in ups:
+        copy.start()
+    gather.finish()
+    meta_gather.finish()
+    for copy in keeps:
+        copy.wait()
+
+    block = seqs * part
+
+    def add(t, fresh=False):
+        columns = pl.ds(pl.multiple_of(t * block, 128), block)
+        left = rows[:, :, columns].reshape(length, block)
+        for i in range(3):
+            at = pl.ds(i * span, span)
+            term = jnp.dot(left, qkvs[t, :, :, at].reshape(block, span), preferred_element_type=F32)
+            raw[:, at] = term if fresh else raw[:, at] + term
+
+    add(z, True)
+    for d in range(1, planes):
+        line.step(d)
+        if d == planes - 1:
+            if strided:
+                line_two.start()
+            group = GroupGather(planes, here, grad_ref, grads_ref, grad_up, grad_down, pair)
+            group.start(local.at[6])
+        pl.when(z - d >= 0)(lambda d=d: add(z - d))
+        pl.when(z + d < planes)(lambda d=d: add(z + d))
+    outputs = [
+        pltpu.make_async_copy(rows, rows_ref, local.at[7]),
+        pltpu.make_async_copy(metas, metas_ref, local.at[8]),
+        pltpu.make_async_copy(qkvs, qkvs_ref, local.at[9]),
+    ]
+    for copy in outputs:
+        copy.start()
+
+    table = RowBlocks(metas)
+    for at in range(0, length, BLOCK):
+        at = pl.ds(at, BLOCK)
+        tables = turns(table, at)
+        for two in range(heads // 2):
+            query = raw[at, pl.ds(2 * HD * two, 2 * HD)]
             query = (query * tables[0] + swap_lanes(query) * tables[1]).astype(LOW)
-            key = raw_ref[rows, pl.ds(span + 2 * HD * pair, 2 * HD)]
+            key = raw[at, pl.ds(span + 2 * HD * two, 2 * HD)]
             key = (key * tables[2] + swap_lanes(key) * tables[3]).astype(LOW)
-            value = raw_ref[rows, pl.ds(2 * span + 2 * HD * pair, 2 * HD)].astype(LOW)
-            for half in range(2):
-                at = slice(half * HD, (half + 1) * HD)
-                q_ref[2 * pair + half, rows] = query[:, at]
-                k_ref[2 * pair + half, rows] = key[:, at]
-                v_ref[2 * pair + half, rows] = value[:, at]
+            value = raw[at, pl.ds(2 * span + 2 * HD * two, 2 * HD)].astype(LOW)
+            for side in range(2):
+                lanes = slice(side * HD, (side + 1) * HD)
+                q_ref[2 * two + side, at] = query[:, lanes]
+                k_ref[2 * two + side, at] = key[:, lanes]
+                v_ref[2 * two + side, at] = value[:, lanes]
     log_ref[...] = jnp.zeros(log_ref.shape, F32)
 
     def one_head(head, carry):
         for start in range(0, length, BLOCK):
             columns = start + BLOCK
-            rows = pl.ds(start, BLOCK)
+            at = pl.ds(start, BLOCK)
             scores = lax.dot_general(
-                q_ref[head, rows],
+                q_ref[head, at],
                 k_ref[head, pl.ds(0, columns)],
                 (((1,), (1,)), ((), ())),
                 preferred_element_type=F32,
             )
-            allowed = allowed_block(meta_ref, start, BLOCK, columns)
+            allowed = allowed_block(table, start, BLOCK, columns)
             scores = jnp.where(allowed, scores, NEG_FILL)
             top = jnp.max(scores, axis=1, keepdims=True)
             shifted = jnp.exp(scores - top)
             total = jnp.sum(shifted, axis=1, keepdims=True)
             probs = (shifted * (1.0 / total)).astype(LOW)
-            wide[head, rows] = jnp.dot(
+            wide[head, at] = jnp.dot(
                 probs, v_ref[head, pl.ds(0, columns)], preferred_element_type=F32
             )
             lane = lax.broadcasted_iota(jnp.int32, (BLOCK, 128), 1)
-            log_ref[rows] = jnp.where(lane == head, top + jnp.log(total), log_ref[rows])
+            log_ref[at] = jnp.where(lane == head, top + jnp.log(total), log_ref[at])
         return carry
 
-    lax.fori_loop(0, heads, one_head, 0)
-    for rows in row_tiles(length, BLOCK):
-        out_ref[rows] = jnp.concatenate(
-            [wide[head, rows] for head in range(heads)], axis=1
-        ).astype(LOW)
-
-
-def attention(heads, raw, meta):
-    length = raw.shape[0]
+    first = 0
+    for d in range(1, planes):
+        last = -(-heads * d // planes)
+        lax.fori_loop(first, last, one_head, 0)
+        first = last
+        if strided:
+            line_two.step(d)
+        if d == 1:
+            group.step(d)
+    lax.fori_loop(first, heads, one_head, 0)
+    lane = lax.broadcasted_iota(jnp.int32, (tokens, 128), 1)
+    column = jnp.sum(outs[...].astype(F32).reshape(span, width), axis=0, keepdims=True)
+    for s in range(seqs):
+        at = pl.ds(s * tokens, tokens)
+        low = jnp.concatenate([wide[head, at] for head in range(heads)], axis=1).astype(LOW)
+        att_ref[s] = low
+        value = low.astype(F32)
+        total = jnp.sum(value, axis=1, keepdims=True)
+        square = jnp.sum(value * value, axis=1, keepdims=True)
+        both = jnp.where(lane == 0, total, jnp.where(lane == 1, square, 0.0))
+        tile[s, pl.ds(0, 8)] = both.T[:8]
+        for i in range(width // 128):
+            tile[s, pl.ds(8 + i, 1)] = column[:, i * 128 : (i + 1) * 128]
+    out_tiles = [
+        remote(tile.at[2 * device[1] + device[2]], tiles_ref.at[me], tile_sems, k, device)
+        for k, device in enumerate(peers, 1)
+    ]
+    for copy in out_tiles:
+        copy.start()
+    keep = pltpu.make_async_copy(tile.at[me], tiles_ref.at[me], local.at[10])
+    keep.start()
+    out_outs = pltpu.make_async_copy(outs, outs_ref, local.at[11])
+    out_outs.start()
+    work = PlaneScatter(
+        chips, here, att_ref, Flat(outs, span), False, (near_out, near_in, far_out, far_in), near, far
+    )
+    work.start()
+    for d in range(2, planes):
+        group.step(d)
+    work.finish(sum_ref)
+    group.finish()
+    for t in range(planes):
+        group.other(t)
+    line.finish()
+    if strided:
+        line_two.finish()
+    for copy in [*swaps, *ups]:
+        copy.wait_send()
+    for k in range(1, chips):
+        other = lax.rem(c + chips - k, chips)
+        remote(up_ref, column_block(ups_ref, units, other), up_sems, k, here).wait_recv()
+    for copy in [keep, out_outs, *outputs]:
+        copy.wait()
+    for k in range(1, seqs):
+        out_tiles[k - 1].wait_send()
+        index = lax.rem(me + seqs - k, seqs)
+        remote(tile.at[0], tiles_ref.at[index], tile_sems, k, here).wait_recv()
+
+    def gain_wait(k, carry):
+        gain_copy(k).wait_send()
+        other = lax.rem(flat + count - k, count)
+        remote(gain_ref, gains_ref.at[other], gain_sems, k, here).wait_recv()
+        return carry
+
+    lax.fori_loop(1, count, gain_wait, 0)
+
+
+class Flat:
+    def __init__(self, blocks, count):
+        self.blocks, self.count = blocks, count
+
+    def __getitem__(self, at):
+        if len(self.blocks.shape) == 2:
+            return self.blocks[at]
+        _, columns = at
+        return self.blocks[:, :, columns].reshape(self.count, columns.size)
+
+
+class RowBlocks:
+    def __init__(self, blocks):
+        self.blocks = blocks
+
+    def __getitem__(self, at):
+        rows, columns = at
+        size = self.blocks.shape[1]
+        first, count = rows.start // size, rows.size // size
+        return self.blocks[pl.ds(first, count), :, columns].reshape(rows.size, columns.size)
+
+
+def attention_forward(
+    planes, chips, heads, strided, x_block, meta, qkv_blocks, out_rows, gain_tile, up_block, grad
+):
+    seqs = 2 * chips
+    tokens, width = x_block.shape
+    part, wide = qkv_blocks.shape[1:]
+    units = up_block.shape[1]
+    length = seqs * tokens
+    span = heads * HD
+    outs = (planes, *out_rows.shape) if strided else out_rows.shape
+    tile = (seqs, 8 + width // 128, 128)
     return call(
-        functools.partial(attention_kernel, heads),
-        "attention",
+        functools.partial(attention_forward_kernel, planes, chips, heads, strided),
+        "attention_forward",
         [
             *[shape((heads, length, HD), LOW)] * 3,
-            shape((length, heads * HD), LOW),
+            shape((seqs, tokens, span), LOW),
             shape((length, 128), F32),
+            shape((tokens, width), F32),
+            shape((seqs, tokens, width), LOW),
+            shape((seqs, *meta.shape), F32),
+            shape((planes, seqs, part, wide), LOW),
+            shape(outs, LOW),
+            shape((planes * seqs, *gain_tile.shape), F32),
+            shape((width, chips * units) if units % 128 == 0 else (chips, width, units), LOW),
+            shape((planes, 2, *grad.shape), LOW),
+            shape(tile, F32),
         ],
-        (raw, meta),
-        [VMEM] * 2,
-        [VMEM] * 5,
-        [pltpu.VMEM((heads, length, HD), F32)],
+        (x_block, meta, qkv_blocks, out_rows, gain_tile, up_block, grad),
+        [HBM] * 7,
+        [*[VMEM] * 6, *[HBM] * 8],
+        [
+            pltpu.VMEM((seqs, tokens, width), LOW),
+            pltpu.VMEM((seqs, *meta.shape), F32),
+            pltpu.VMEM((planes, seqs, part, wide), LOW),
+            pltpu.VMEM(outs, LOW),
+            pltpu.VMEM((length, 3 * span), F32),
+            pltpu.VMEM((heads, length, HD), F32),
+            pltpu.VMEM(tile, F32),
+            *PlaneScatter.scratch(chips, tokens, width),
+            *pairs_of(
+                seqs, *[chips] * 4, *[2 * planes] * 2, *[planes] * 2, planes * seqs, chips
+            ),
+            *PlaneScatter.sems(chips, width),
+            *pairs_of(seqs),
+            *GroupGather.sems(planes),
+            pltpu.SemaphoreType.DMA((12,)),
+        ],
+        1,
     )
 
 
@@ -1516,44 +1550,34 @@
     normed_low = normed_one.astype(LOW)
     gain_tile = jnp.zeros((8, 128), F32).at[0, :part].set(gain_ffn.astype(F32))
 
-    row_in, meta, qkv_mine, out_mine, gain_tiles, up_mine = attention_gather(
+    if not strided:
+        out_all = lax.all_gather(out_scaled, ALL, axis=0, tiled=True)
+        out_scaled = lax.dynamic_slice_in_dim(out_all, seq_index * span, span, axis=0)
+
+    grad_low = out_grad[0]
+    (
+        queries, keys, values, attended, log_total, out_sum,
+        row_in, meta, qkv_mine, out_mine, gain_tiles, up_mine, grad_flat, tiles,
+    ) = attention_forward(
         planes,
         chips,
+        heads,
+        strided,
         normed_low,
         token_tables(position_ids[0]),
         qkv_send,
         out_scaled,
         gain_tile,
         w_up,
+        grad_low,
     )
     if up_mine.ndim == 3:
         up_mine = up_mine.transpose(1, 0, 2).reshape(width, -1)
     row_in = row_in.reshape(length, width)
     meta = meta.reshape(length, -1)
     qkv_mine = qkv_mine.reshape(width, 3 * span)
-    if strided:
-        out_mine = out_mine.reshape(span, width)
-    else:
-        out_all = lax.all_gather(out_scaled, ALL, axis=0, tiled=True)
-        out_mine = lax.dynamic_slice_in_dim(out_all, seq_index * span, span, axis=0)
-    queries, keys, values, attended, log_total = attention(heads, dot(row_in, qkv_mine), meta)
-    attended_wide = attended.astype(F32)
-    column_part = jnp.sum(out_mine.astype(F32), axis=0)
-    token_sums = jnp.stack(
-        [jnp.sum(attended_wide, axis=1), jnp.sum(attended_wide * attended_wide, axis=1)]
-    ).reshape(2, seqs, tokens)
-    tiles = jnp.concatenate(
-        [
-            jnp.swapaxes(token_sums, 0, 1),
-            jnp.zeros((seqs, 6, tokens), F32),
-            jnp.broadcast_to(column_part.reshape(1, -1, tokens), (seqs, width // tokens, tokens)),
-        ],
-        axis=1,
-    )
-    grad_low = out_grad[0]
-    out_sum, tiles, grad_flat = out_scatter(
-        planes, chips, attended.reshape(seqs, tokens, span), out_mine, tiles, grad_low
-    )
+    out_mine = out_mine.reshape(span, width)
+    attended = attended.reshape(length, span)
     tiles = jnp.sum(tiles, axis=0)
     column_sum = tiles[8:].reshape(width)
     sums = tiles[:2].T

time: 571 us -> 540 us (0.946)
  Pallas kernels: 494 us -> 475 us
  matrix products: 16.1 us -> 7.88 us
    pallas_call x7 -> x5, Pallas kernels: 494 us -> 475 us  [call(): pl.pallas_call(kernel, name=name, out_shape=outs, in_specs=in_specs, out_...]
    dot_general x1 -> x0, matrix products: 8.24 us -> none  [dot(): return jnp.dot(left_op, right_op, preferred_element_type=F32)]
where the time goes in v5:
time: 540 us; the launch traced here: 533 us
  Pallas kernels  475 us (88%)
  other arithmetic  34 us (6%)
  local copies, waits for them, and re-layouts  14.3 us (3%)
  matrix products  7.88 us (1%)
    pallas_call x5, Pallas kernels, call(): pl.pallas_call(kernel, name=name, out_shape=outs, in_specs=in_specs, out_...  475 us

profile of v5, /device:TPU:9, one launch (start us, length us, event | category | flops | bytes accessed | tf_op | source)
XLA Modules:
  0.0 533.0 jit_solution(18090715163392821162)
XLA Ops:
  0.7 0.8 convert_bitcast_fusion.2
  3.0 0.8 pad_maximum_fusion.1.meta_ref
  3.8 1.2 convert_reduce_fusion.3
  5.3 1.1 fusion.11.x_ref
  6.4 1.5 fusion.4
  7.9 1.6 reshape.221
  9.5 1.8 copy.64
  11.3 3.6 reshape.222.qkv_ref
  14.9 0.8 fusion.20.out_ref
  16.3 152.3 %attention_forward.1 = (bf16[4,1024,64]{2,1,0:T(8,128)(2,1)}, bf16[4,1024,64]{2,1,0:T(8,128)(2,1)}, bf16[4,1024,64]{2,1,0:T(8,128)(2,1)}, bf16[8,128,256]{2,1,0:...) custom-call(bf16[128,2048]{1,0:T(8,128)(2,1)} %fusion.11.x_ref, ...), custom_call_target="tpu_custom_call" | custom-call | tf_op jit(solution)/shard_map/attention_forward/pallas_call | solution.py:86
  168.7 0.9 reduce_sum.164
  169.6 1.7 fusion.28
  171.6 1.0 slice_reduce_fusion.1
  172.6 1.0 multiply_convert_fusion.x_ref
  173.6 1.2 fusion.down_ref
  174.8 163.1 %feed_forward.1 = (f32[128,2048]{1,0:T(8,128)}, bf16[4,256,1024]{2,1,0:T(8,128)(2,1)}, bf16[4,256,2048]{2,1,0:T(8,128)(2,1)}, bf16[2048,1024]{1,0:T(8,128)(2,1)}, bf16[4,256,2048]{2,1,0:T(8,128)(2,1)}) custom-call(bf16[128,2048]{1,0:T(8,128)(2,1)} %multiply_convert_fusion.x_ref, bf16[2048,1024]{1,0:T(8,128)(2,1)} %get-tuple-element.63.up_ref, ...), custom_call_target="tpu_custom_call" | custom-call | tf_op jit(solution)/shard_map/feed_forward/pallas_call | solution.py:86
  338.0 1.7 multiply_reduce_fusion
  339.8 1.8 fusion.18
  343.2 56.6 %plane_gather.1 = (bf16[8,128,2048]{2,1,0:T(8,128)(2,1)}, f32[8,128,128]{2,1,0:T(8,128)}, f32[32,8,128]{2,1,0:T(8,128)}, f32[128,2048]{1,0:T(8,128)}) custom-call(bf16[128,2048]{1,0:T(8,128)(2,1)} %get-tuple-element.97.x_ref, f32[128,128]{1,0:T(8,128)} %pad.13.stat_ref, f32[32,8,128]{2,1,0:T(8,128)} %pad.14.tile_ref, ...), custom_call_target="tpu_custom_call" | custom-call | tf_op jit(solution)/shard_map/plane_gather/pallas_call | solution.py:86
  399.8 30.7 %attention_back.1 = (bf16[1024,768]{1,0:T(8,128)(2,1)}, f32[64,2048]{1,0:T(8,128)}, bf16[4,1024,256]{2,1,0:T(8,128)(2,1)}) custom-call(bf16[4,1024,64]{2,1,0:T(8,128)(2,1)} %get-tuple-element.69.q_ref, bf16[4,1024,64]{2,1,0:T(8,128)(2,1)} %get-tuple-element.70.k_ref, bf16[4,1024,64]{2,1,0:T(8,128)(2,1)} %get-tuple-element.71.v_ref, ...), custom_call_target="tpu_custom_call" | custom-call | tf_op jit(solution)/shard_map/attention_back/pallas_call | solution.py:86
  430.5 7.9 %convolution_convert_fusion = bf16[2048,768]{1,0:T(8,128)(2,1)} fusion(bf16[1024,2048]{1,0:T(8,128)(2,1)} %bitcast.94, bf16[1024,768]{1,0:T(8,128)(2,1)} %get-tuple-element.79), kind=kOutput, calls=%fused_computation.3 | convolution fusion | flops 3222798336 | bytes 8912896 | tf_op jit(solution)/shard_map/dot_general | solution.py:68
  438.3 0.7 broadcast_in_dim.32.gain_ref
  439.0 72.6 %in_scatter.1 = (f32[128,2048]{1,0:T(8,128)}, f32[64,6144]{1,0:T(8,128)}, f32[64,128]{1,0:T(8,128)}, bf16[4,1024,256]{2,1,0:T(8,128)(2,1)}) custom-call(bf16[8,128,768]{2,1,0:T(8,128)(2,1)} %bitcast.82, bf16[2048,768]{1,0:T(8,128)(2,1)} %bitcast.79, bf16[4,8,64,768]{3,2,1,0:T(8,128)(2,1)} %bitcast.80, bf16[2048,1024]{1,0:T(8,128)(2,1)} %get-tuple-element.78.up_ref, ...), custom_call_target="tpu_custom_call" | custom-call | tf_op jit(solution)/shard_map/in_scatter/pallas_call | solution.py:86
  511.6 2.2 convert_reduce_fusion.1
  514.2 1.5 pad_maximum_fusion
  516.5 1.3 fusion.24
  518.4 1.7 fusion.21
  520.1 0.9 fusion.23
  521.6 3.4 convert_reduce_fusion
  525.0 3.1 fusion.1
  528.6 1.6 multiply_add_fusion
  531.4 1.1 copy.66
  (106 shorter events, 8.4 us)
Async XLA Ops:
  0.7 4.3 copy-start
  0.7 5.7 %copy-start.21 = (bf16[64]{0:T(256)(128)(2,1)S(1)}, bf16[64]{0:T(256)(128)(2,1)}, u32[]{:S(2)}) copy-start(bf16[64]{0:T(256)(128)(2,1)} %param.28) | copy-start | bytes 388
  0.7 5.7 %copy-start.7 = (bf16[64,6144]{1,0:T(8,128)(2,1)S(1)}, bf16[64,6144]{1,0:T(8,128)(2,1)}, u32[]{:S(2)}) copy-start(bf16[64,6144]{1,0:T(8,128)(2,1)} %weight_ref.1) | copy-start | bytes 2359300
  2.9 3.5 copy-start.12
  9.5 5.4 %copy-start.23 = (bf16[64]{0:T(256)(128)(2,1)S(1)}, bf16[64]{0:T(256)(128)(2,1)}, u32[]{:S(2)}) copy-start(bf16[64]{0:T(256)(128)(2,1)} %param.29) | copy-start | bytes 388
  9.5 5.4 %copy-start.14 = (bf16[64,2048]{1,0:T(8,128)(2,1)S(1)}, bf16[64,2048]{1,0:T(8,128)(2,1)}, u32[]{:S(2)}) copy-start(bf16[64,2048]{1,0:T(8,128)(2,1)} %param.25) | copy-start | bytes 786436
  11.3 4.4 copy-start.24
  169.6 4.0 copy-start.22
  169.6 4.0 copy-start.2
  174.8 164.9 %copy-start.9 = (bf16[1,128,2048]{2,1,0:T(8,128)(2,1)S(1)}, bf16[1,128,2048]{2,1,0:T(8,128)(2,1)}, u32[]{:S(2)}) copy-start(bf16[1,128,2048]{2,1,0:T(8,128)(2,1)} %param.40) | copy-start | bytes 1572868
  338.0 1.8 copy-start.3
  338.0 1.8 copy-start.4
  511.6 2.2 copy-start.10
  514.2 1.6 copy-start.5
  514.2 2.3 copy-start.6
  515.7 2.0 copy-start.19
  515.7 2.6 copy-start.16
  515.7 2.6 copy-start.17
  516.5 3.6 copy-start.15
  518.4 2.7 copy-start.18
  521.6 3.4 copy-start.8
  525.0 3.1 copy-start.25
  525.0 3.1 copy-start.26
  525.0 3.6 copy-start.1
  525.0 3.6 copy-start.11
  528.6 1.7 copy-start.20
  528.6 2.2 copy-start.27
  528.6 2.7 copy-start.13

commit v6 on v5

--- a/solution.py
+++ b/solution.py
@@ -732,7 +732,7 @@
         copy.start()
     load_up.wait()
 
-    step = 16
+    step = tokens
     lane = lax.broadcasted_iota(jnp.int32, (step, 128), 1)
 
     def forward(t):
@@ -813,18 +813,20 @@
             total = stat_out[2 * t + half]
             for k in range(1, count):
                 total = total + stat_in[k, 2 * t + half]
-            padded = jnp.concatenate([total, jnp.zeros((128 - 8, tokens), F32)], axis=0)
+            mean, square, cross, first = (total[i : i + 1] / width_ff for i in range(4))
+            scaler = lax.rsqrt(square - mean * mean + NORM_EPS)
+            second = scaler * (cross - mean * first)
+            figures = [scaler, -mean * scaler, scaler * first, scaler * second]
+            padded = jnp.concatenate([*figures, jnp.zeros((128 - 4, tokens), F32)], axis=0)
             stat[t, pl.ds(half * tokens, tokens)] = padded.T
 
         def some(i, inner):
             at = pl.ds(pl.multiple_of(i * step, step), step)
-            figures = stat[t, at] * (1.0 / width_ff)
-            mean, square, cross, first = (figures[:, j : j + 1] for j in range(4))
-            scaler = lax.rsqrt(square - mean * mean + NORM_EPS)
-            second = scaler * (cross - mean * first)
-            unit = (act[t, at] - mean) * scaler
+            figures = stat[t, at]
+            scaler, shift, first, second = (figures[:, j : j + 1] for j in range(4))
+            unit = act[t, at] * scaler + shift
             normed[t, at] = unit.astype(LOW)
-            d_act = scaler * (back[t, at] - first - unit * second)
+            d_act = back[t, at] * scaler - first - unit * second
             d_up[t, at] = (d_act * slope[t, at]).astype(LOW)
             return inner
 
@@ -939,104 +941,6 @@
     )
 
 
-def plane_gather_kernel(
-    planes, chips, x_ref, stat_ref, tile_ref, left_ref, right_ref,
-    row_ref, stats_ref, tiles_ref, ffn_ref,
-    near_out, own, sums, *sems,
-):
-    here = place()
-    z, c, core = here
-    seqs = 2 * chips
-    count = planes * seqs
-    me = 2 * c + core
-    flat = z * seqs + me
-    x_far, x_near, s_far, s_near, tile_sems, near, up, down = [
-        sems[2 * i : 2 * i + 2] for i in range(8)
-    ]
-    local = sems[16]
-    barrier = pltpu.get_barrier_semaphore()
-
-    def device_of(k):
-        other = lax.rem(flat + k, count)
-        return (other // seqs, lax.rem(other, seqs) // 2, lax.rem(other, 2))
-
-    def signal(k, carry):
-        greet(barrier, [device_of(k)])
-        return carry
-
-    lax.fori_loop(1, count, signal, 0)
-    pl.semaphore_wait(barrier, count - 1)
-    rows = PlaneGather(chips, here, x_ref, row_ref, x_far, x_near)
-    stats = PlaneGather(chips, here, stat_ref, stats_ref, s_far, s_near)
-    rows.start()
-    stats.start()
-    keeps = [
-        pltpu.make_async_copy(x_ref, row_ref.at[me], local.at[0]),
-        pltpu.make_async_copy(stat_ref, stats_ref.at[me], local.at[1]),
-        pltpu.make_async_copy(tile_ref.at[flat], tiles_ref.at[flat], local.at[2]),
-    ]
-    for copy in keeps:
-        copy.start()
-
-    def tile_copy(k):
-        other = lax.rem(flat + k, count)
-        return remote(tile_ref.at[other], tiles_ref.at[flat], tile_sems, k, device_of(k))
-
-    def tile_start(k, carry):
-        tile_copy(k).start()
-        return carry
-
-    lax.fori_loop(1, count, tile_start, 0)
-    work = PairScatter(
-        planes, here, Halves(left_ref, x_ref.shape[0]), right_ref, False, (near_out, own, sums),
-        near, up, down,
-    )
-    work.start()
-    for i in range(1, work.line.steps):
-        if i == work.line.steps // 2:
-            rows.forward()
-            stats.forward()
-        work.line.step(i)
-    rows.finish()
-    stats.finish()
-    work.finish(ffn_ref)
-    for copy in keeps:
-        copy.wait()
-
-    def tile_wait(k, carry):
-        tile_copy(k).wait_send()
-        other = lax.rem(flat + count - k, count)
-        remote(tile_ref.at[0], tiles_ref.at[other], tile_sems, k, here).wait_recv()
-        return carry
-
-    lax.fori_loop(1, count, tile_wait, 0)
-
-
-def plane_gather(planes, chips, x_block, stats, tiles, left, right):
-    seqs = 2 * chips
-    tokens, width = x_block.shape
-    return call(
-        functools.partial(plane_gather_kernel, planes, chips),
-        "plane_gather",
-        [
-            shape((seqs, *x_block.shape), x_block.dtype),
-            shape((seqs, *stats.shape), stats.dtype),
-            shape(tiles.shape, tiles.dtype),
-            shape((tokens, width), F32),
-        ],
-        (x_block, stats, tiles, left, right),
-        [HBM, HBM, HBM, VMEM, VMEM],
-        [HBM, HBM, HBM, VMEM],
-        [
-            *PairScatter.scratch(planes, tokens, width),
-            *pairs_of(chips, chips, chips, chips, planes * seqs),
-            *PairScatter.sems(planes, width),
-            pltpu.SemaphoreType.DMA((3,)),
-        ],
-        2,
-    )
-
-
 def swap_lanes(values):
     lane = lax.broadcasted_iota(jnp.int32, values.shape, 1)
     return jnp.where(
@@ -1120,8 +1024,6 @@
         copy.start()
     gather = PlaneGather(chips, here, x_ref, rows, x_far, x_near)
     meta_gather = PlaneGather(chips, here, meta_ref, metas, meta_far, meta_near)
-    gather.start()
-    meta_gather.start()
     for copy in keeps:
         copy.start()
 
@@ -1132,7 +1034,6 @@
         gain_copy(k).start()
         return carry
 
-    lax.fori_loop(1, count, gain_start, 0)
     mine.wait()
     own_out.wait()
     for k in range(1, seqs):
@@ -1144,6 +1045,9 @@
     )
     line_two = LineGather(planes, here, lambda t: [outs.at[t]], up_two, down_two)
     line.start()
+    gather.start()
+    meta_gather.start()
+    lax.fori_loop(1, count, gain_start, 0)
     gather.forward()
     meta_gather.forward()
     ups = [
@@ -1173,8 +1077,6 @@
         if d == planes - 1:
             if strided:
                 line_two.start()
-            group = GroupGather(planes, here, grad_ref, grads_ref, grad_up, grad_down, pair)
-            group.start(local.at[6])
         pl.when(z - d >= 0)(lambda d=d: add(z - d))
         pl.when(z + d < planes)(lambda d=d: add(z + d))
     outputs = [
@@ -1232,8 +1134,8 @@
         first = last
         if strided:
             line_two.step(d)
-        if d == 1:
-            group.step(d)
+    group = GroupGather(planes, here, grad_ref, grads_ref, grad_up, grad_down, pair)
+    group.start(local.at[6])
     lax.fori_loop(first, heads, one_head, 0)
     lane = lax.broadcasted_iota(jnp.int32, (tokens, 128), 1)
     column = jnp.sum(outs[...].astype(F32).reshape(span, width), axis=0, keepdims=True)
@@ -1262,7 +1164,7 @@
         chips, here, att_ref, Flat(outs, span), False, (near_out, near_in, far_out, far_in), near, far
     )
     work.start()
-    for d in range(2, planes):
+    for d in range(1, planes):
         group.step(d)
     work.finish(sum_ref)
     group.finish()
@@ -1366,35 +1268,109 @@
     )
 
 
-def attention_back_kernel(
+def attention_backward_kernel(
     planes, chips, heads, strided,
-    q_ref, k_ref, v_ref, att_ref, row_ref, right_ref, stat_ref, log_ref, meta_ref, up_ref,
-    out_ref, total_ref, slots_ref,
-    grad, dq, dk, dv, normed_all, own, sums, *sems,
+    x_ref, stat_ref, tile_ref, left_ref, right_ref,
+    q_in, k_in, v_in, att_in, out_in, log_in, meta_in, up_ref,
+    tiles_ref, ffn_ref, out_ref, total_ref, slots_ref,
+    rows, stats, left, right, q_ref, k_ref, v_ref, att_ref, outs, log_ref, meta_ref,
+    near_out, near_own, near_sums, grad, dq, dk, dv, normed_all, own, sums, *sems,
 ):
     here = place()
-    up, down, swap_sems = [sems[2 * i : 2 * i + 2] for i in range(3)]
+    z, c, core = here
+    seqs = 2 * chips
+    count = planes * seqs
+    me = 2 * c + core
+    flat = z * seqs + me
+    x_far, x_near, s_far, s_near, tile_sems, near, up, down, up_two, down_two, swap_sems = [
+        sems[2 * i : 2 * i + 2] for i in range(11)
+    ]
+    local = sems[22]
+    pairs = [
+        (left_ref, left), (right_ref, right), (att_in, att_ref), (out_in, outs), (meta_in, meta_ref),
+        (q_in, q_ref), (k_in, k_ref), (v_in, v_ref), (log_in, log_ref),
+    ]
+    loads = [pltpu.make_async_copy(*pair, local.at[i]) for i, pair in enumerate(pairs)]
+    for copy in loads:
+        copy.start()
     barrier = pltpu.get_barrier_semaphore()
-    greet(barrier, chip_peers(chips, here))
-    greet_line(barrier, planes, here)
-    pl.semaphore_wait(barrier, chips - 1 + line_peers(planes, here))
+
+    def device_of(k):
+        other = lax.rem(flat + k, count)
+        return (other // seqs, lax.rem(other, seqs) // 2, lax.rem(other, 2))
+
+    def signal(k, carry):
+        greet(barrier, [device_of(k)])
+        return carry
+
+    lax.fori_loop(1, count, signal, 0)
+    pl.semaphore_wait(barrier, count - 1)
+    gather = PlaneGather(chips, here, x_ref, rows, x_far, x_near)
+    stat_gather = PlaneGather(chips, here, stat_ref, stats, s_far, s_near)
+    gather.start()
+    stat_gather.start()
+    keeps = [
+        pltpu.make_async_copy(x_ref, rows.at[me], local.at[9]),
+        pltpu.make_async_copy(stat_ref, stats.at[me], local.at[10]),
+        pltpu.make_async_copy(tile_ref.at[flat], tiles_ref.at[flat], local.at[11]),
+    ]
+    for copy in keeps:
+        copy.start()
+
+    def tile_copy(k):
+        other = lax.rem(flat + k, count)
+        return remote(tile_ref.at[other], tiles_ref.at[flat], tile_sems, k, device_of(k))
+
+    def tile_start(k, carry):
+        tile_copy(k).start()
+        return carry
+
+    lax.fori_loop(1, count, tile_start, 0)
+    tokens, width = x_ref.shape
+    for copy in loads[:2]:
+        copy.wait()
+    work = PairScatter(
+        planes, here, Halves(left, tokens), right, False, (near_out, near_own, near_sums),
+        near, up, down,
+    )
+    work.start()
+    left_turns = list(range(1, work.line.steps))
+
+    def turn(until=None):
+        step = left_turns[0] + 1 if until is None and left_turns else until
+        while left_turns and left_turns[0] < step:
+            work.line.step(left_turns.pop(0))
+
+    turn()
+    turn()
+    gather.forward()
+    stat_gather.forward()
+    gather.finish()
+    stat_gather.finish()
     swap = ChipSwap(
         chips, here, lambda index: half_block(up_ref, slots_ref, index, 0), slots_ref, swap_sems
     )
-    swap.start(sems[6].at[0])
+    swap.start(local.at[12])
+    for copy in [*loads[2:], *keeps]:
+        copy.wait()
+    turn()
     length, span = att_ref.shape
-    part, width = own.shape[1:]
-    for rows in row_tiles(length, BLOCK):
-        mean, scaler, first, second = (stat_ref[rows, pl.ds(i, 1)] for i in range(4))
-        d_sub = product(row_ref[rows], right_ref, slice(None), True)
-        normed = (att_ref[rows].astype(F32) - mean) * scaler
-        normed_all[rows] = normed.astype(LOW)
-        d_att = (scaler * (d_sub - first - normed * second)).astype(LOW)
+    part = own.shape[1]
+    per = BLOCK // tokens
+    for first in range(0, seqs, per):
+        at = pl.ds(first * tokens, BLOCK)
+        figures = stats[pl.ds(first, per)].reshape(BLOCK, 128)
+        mean, scaler, one, two = (figures[:, i : i + 1] for i in range(4))
+        block = rows[pl.ds(first, per)].reshape(BLOCK, width)
+        d_sub = product(block, outs, slice(None), True)
+        normed = (att_ref[at].astype(F32) - mean) * scaler
+        normed_all[at] = normed.astype(LOW)
+        d_att = (scaler * (d_sub - one - normed * two)).astype(LOW)
         for head in range(heads):
-            grad[head, rows] = d_att[:, head * HD : (head + 1) * HD]
+            grad[head, at] = d_att[:, head * HD : (head + 1) * HD]
     for at in range(0, width, COLUMNS):
         columns = pl.ds(at, COLUMNS)
-        term = token_product(normed_all[...], row_ref[:, columns]).astype(LOW)
+        term = token_product(normed_all[...], rows[:, :, columns].reshape(length, COLUMNS)).astype(LOW)
         for t in range(planes):
             own[t, :, columns] = term[t * part : (t + 1) * part]
     line = LineScatter(
@@ -1402,11 +1378,11 @@
         here,
         1,
         lambda p: (slice(None),),
-        lambda p: [(rows,) for rows in row_tiles(part, 16)],
+        lambda p: [(row,) for row in row_tiles(part, 16)],
         lambda t, tile: own[(t, *tile)].astype(F32),
         sums,
-        up,
-        down,
+        up_two,
+        down_two,
     )
     if strided:
         line.step(0)
@@ -1416,25 +1392,23 @@
     def one_head(head, carry):
         for start in range(0, length, BLOCK):
             columns = start + BLOCK
-            rows = pl.ds(start, BLOCK)
+            at = pl.ds(start, BLOCK)
             keys = pl.ds(0, columns)
-            query, key = q_ref[head, rows], k_ref[head, keys]
-            out_grad = grad[head, rows]
+            query, key = q_ref[head, at], k_ref[head, keys]
+            out_grad = grad[head, at]
             scores = lax.dot_general(
                 query, key, (((1,), (1,)), ((), ())), preferred_element_type=F32
             )
             allowed = allowed_block(meta_ref, start, BLOCK, columns)
             lane = lax.broadcasted_iota(jnp.int32, (BLOCK, 128), 1)
-            log_total = jnp.sum(
-                jnp.where(lane == head, log_ref[rows], 0.0), axis=1, keepdims=True
-            )
+            log_total = jnp.sum(jnp.where(lane == head, log_ref[at], 0.0), axis=1, keepdims=True)
             probs = jnp.where(allowed, jnp.exp(scores - log_total), 0.0)
             d_probs = lax.dot_general(
                 out_grad, v_ref[head, keys], (((1,), (1,)), ((), ())), preferred_element_type=F32
             )
             delta = jnp.sum(probs * d_probs, axis=1, keepdims=True)
             d_scores = (probs * (d_probs - delta)).astype(LOW)
-            dq[head, rows] = jnp.dot(d_scores, key, preferred_element_type=F32)
+            dq[head, at] = jnp.dot(d_scores, key, preferred_element_type=F32)
             dk[head, keys] += token_product(d_scores, query)
             dv[head, keys] += token_product(probs.astype(LOW), out_grad)
         return carry
@@ -1444,24 +1418,26 @@
         last = -(-heads * i // (planes - 1))
         lax.fori_loop(first, last, one_head, 0)
         first = last
+        turn()
         if strided:
             line.step(i)
     lax.fori_loop(first, heads, one_head, 0)
-    for rows in row_tiles(length, BLOCK):
-        tables = turns(meta_ref, rows)
-        for pair in range(heads // 2):
+    turn(work.line.steps)
+    for start in range(0, length, BLOCK):
+        at = pl.ds(start, BLOCK)
+        tables = turns(meta_ref, at)
+        for two in range(heads // 2):
             both = [
-                jnp.concatenate(
-                    [whole[2 * pair, rows], whole[2 * pair + 1, rows]], axis=1
-                ).astype(LOW)
+                jnp.concatenate([whole[2 * two, at], whole[2 * two + 1, at]], axis=1).astype(LOW)
                 for whole in (dq, dk, dv)
             ]
             query, key = both[0].astype(F32), both[1].astype(F32)
             query = query * tables[0] + swap_lanes(query * tables[1])
             key = key * tables[2] + swap_lanes(key * tables[3])
-            out_ref[rows, pl.ds(2 * HD * pair, 2 * HD)] = query.astype(LOW)
-            out_ref[rows, pl.ds(span + 2 * HD * pair, 2 * HD)] = key.astype(LOW)
-            out_ref[rows, pl.ds(2 * span + 2 * HD * pair, 2 * HD)] = both[2]
+            out_ref[at, pl.ds(2 * HD * two, 2 * HD)] = query.astype(LOW)
+            out_ref[at, pl.ds(span + 2 * HD * two, 2 * HD)] = key.astype(LOW)
+            out_ref[at, pl.ds(2 * span + 2 * HD * two, 2 * HD)] = both[2]
+    work.finish(ffn_ref)
     if strided:
 
         def store(tile, total):
@@ -1473,31 +1449,49 @@
             total_ref[pl.ds(t * part, part)] = own[t].astype(F32)
     swap.finish()
 
-
-def attention_back(planes, chips, heads, strided, part, units, args):
-    length, span = args[3].shape
-    width = args[4].shape[1]
+    def tile_wait(k, carry):
+        tile_copy(k).wait_send()
+        other = lax.rem(flat + count - k, count)
+        remote(tile_ref.at[0], tiles_ref.at[other], tile_sems, k, here).wait_recv()
+        return carry
+
+    lax.fori_loop(1, count, tile_wait, 0)
+
+
+def attention_backward(planes, chips, heads, strided, part, units, args):
+    tokens, width = args[0].shape
+    seqs = 2 * chips
+    length, span = args[8].shape
+    kept = [pltpu.VMEM(args[i].shape, args[i].dtype) for i in (3, 4, 5, 6, 7, 8, 9, 10, 11)]
     return call(
-        functools.partial(attention_back_kernel, planes, chips, heads, strided),
-        "attention_back",
+        functools.partial(attention_backward_kernel, planes, chips, heads, strided),
+        "attention_backward",
         [
+            shape(args[2].shape, F32),
+            shape((tokens, width), F32),
             shape((length, 3 * span), LOW),
             shape((part if strided else span, width), F32),
             shape((chips, width // 2, units), LOW),
         ],
         args,
-        [*[VMEM] * 9, HBM],
-        [*[VMEM] * 2, HBM],
+        [HBM] * 13,
+        [HBM, VMEM, VMEM, VMEM, HBM],
         [
+            pltpu.VMEM((seqs, tokens, width), LOW),
+            pltpu.VMEM((seqs, tokens, 128), F32),
+            *kept,
+            *PairScatter.scratch(planes, tokens, width),
             pltpu.VMEM((heads, length, HD), LOW),
             *[pltpu.VMEM((heads, length, HD), F32)] * 3,
             pltpu.VMEM((length, span), LOW),
             pltpu.VMEM((planes, part, width), LOW),
             pltpu.VMEM((planes + 1, part, width), LOW),
+            *pairs_of(chips, chips, chips, chips, planes * seqs),
+            *PairScatter.sems(planes, width),
             *pairs_of(planes, planes, chips),
-            pltpu.SemaphoreType.DMA((1,)),
+            pltpu.SemaphoreType.DMA((13,)),
         ],
-        8,
+        2,
     )
 
 
@@ -1606,28 +1600,31 @@
     first_two = jnp.sum(d_hmid_wide * column_sum[None, :], axis=1, keepdims=True) / width
     second_two = jnp.sum(d_hmid_wide * projected, axis=1, keepdims=True) / width
     token_stats = jnp.concatenate([mean_two, scaler_two, first_two, second_two], axis=1)
-    row_grad, row_stats, gain_part, ffn_out = plane_gather(
-        planes,
-        chips,
-        d_hmid_low,
-        jnp.pad(token_stats, ((0, 0), (0, 124))),
-        gain_part,
-        normed_four,
-        down_mine,
-    )
-    output = (hmid + ffn_out).astype(LOW)[None]
-    row_grad = row_grad.reshape(length, width)
-    row_stats = row_stats.reshape(length, 128)
-    grad_gain_three = jnp.sum(gain_part, axis=0)[0, :part]
-    d_qkv, sum_out, upper_slots = attention_back(
+    gain_part, ffn_out, d_qkv, sum_out, upper_slots = attention_backward(
         planes,
         chips,
         heads,
         strided,
         part,
         units,
-        (queries, keys, values, attended, row_grad, out_mine, row_stats, log_total, meta, grad_up),
-    )
+        (
+            d_hmid_low,
+            jnp.pad(token_stats, ((0, 0), (0, 124))),
+            gain_part,
+            normed_four,
+            down_mine,
+            queries,
+            keys,
+            values,
+            attended,
+            out_mine,
+            log_total,
+            meta,
+            grad_up,
+        ),
+    )
+    output = (hmid + ffn_out).astype(LOW)[None]
+    grad_gain_three = jnp.sum(gain_part, axis=0)[0, :part]
     grad_qkv = token_product(row_in, d_qkv).astype(LOW)
     d_in, sum_qkv, grad_gain_one, lower_slots = in_scatter(
         planes,

time: 540 us -> 501 us (0.928)
  Pallas kernels: 475 us -> 435 us
    pallas_call x5 -> x4, Pallas kernels: 475 us -> 435 us  [call(): pl.pallas_call(kernel, name=name, out_shape=outs, in_specs=in_specs, out_...]
where the time goes in v6:
time: 501 us; the launch traced here: 493 us
  Pallas kernels  435 us (87%)
  other arithmetic  34.3 us (7%)
  local copies, waits for them, and re-layouts  15.2 us (3%)
  matrix products  7.88 us (2%)
    pallas_call x4, Pallas kernels, call(): pl.pallas_call(kernel, name=name, out_shape=outs, in_specs=in_specs, out_...  435 us

profile of v6, /device:TPU:9, one launch (start us, length us, event | category | flops | bytes accessed | tf_op | source)
XLA Modules:
  0.0 493.4 jit_solution(7623055538743971644)
XLA Ops:
  0.7 0.8 convert_bitcast_fusion.2
  3.0 0.8 pad_maximum_fusion.1.meta_ref
  3.8 1.2 convert_reduce_fusion.3
  5.3 1.1 fusion.11.x_ref
  6.5 1.7 fusion.4
  8.2 2.5 reshape.215
  10.7 1.8 copy.64
  12.5 3.6 reshape.216.qkv_ref
  16.1 0.8 fusion.20.out_ref
  17.5 151.3 %attention_forward.1 = (bf16[4,1024,64]{2,1,0:T(8,128)(2,1)}, bf16[4,1024,64]{2,1,0:T(8,128)(2,1)}, bf16[4,1024,64]{2,1,0:T(8,128)(2,1)}, bf16[8,128,256]{2,1,0:...) custom-call(bf16[128,2048]{1,0:T(8,128)(2,1)} %fusion.11.x_ref, ...), custom_call_target="tpu_custom_call" | custom-call | tf_op jit(solution)/shard_map/attention_forward/pallas_call | solution.py:86
  168.8 0.9 reduce_sum.164
  169.8 1.7 fusion.28
  171.7 1.0 slice_reduce_fusion.1
  172.8 1.0 multiply_convert_fusion.x_ref
  173.8 1.2 fusion.down_ref
  175.0 140.4 %feed_forward.1 = (f32[128,2048]{1,0:T(8,128)}, bf16[4,256,1024]{2,1,0:T(8,128)(2,1)}, bf16[4,256,2048]{2,1,0:T(8,128)(2,1)}, bf16[2048,1024]{1,0:T(8,128)(2,1)}, bf16[4,256,2048]{2,1,0:T(8,128)(2,1)}) custom-call(bf16[128,2048]{1,0:T(8,128)(2,1)} %multiply_convert_fusion.x_ref, bf16[2048,1024]{1,0:T(8,128)(2,1)} %get-tuple-element.61.up_ref, ...), custom_call_target="tpu_custom_call" | custom-call | tf_op jit(solution)/shard_map/feed_forward/pallas_call | solution.py:86
  315.4 1.7 multiply_reduce_fusion
  317.3 1.8 fusion.18
  319.9 0.7 pad.14.tile_ref
  320.6 72.8 %attention_backward.1 = (f32[32,8,128]{2,1,0:T(8,128)}, f32[128,2048]{1,0:T(8,128)}, bf16[1024,768]{1,0:T(8,128)(2,1)}, f32[64,2048]{1,0:T(8,128)}, bf16[4,1024,256]{2,1,0:T(8,128)(2,1)}) custom-call(bf16[128,2048]{1,0:T(8,128)(2,1)} %get-tuple-element.93.x_ref, f32[128,128]{1,0:T(8,128)} %pad.13.stat_ref, f32[32,8,128]{2,1,0:T(8,128)} %pad.14.tile_ref, ...), custom_call_target="tpu_custom_call" | custom-call | tf_op jit(solution)/shard_map/attention_backward/pallas_call | solution.py:86
  393.4 7.9 %convolution_convert_fusion = bf16[2048,768]{1,0:T(8,128)(2,1)} fusion(bf16[1024,2048]{1,0:T(8,128)(2,1)} %bitcast.90, bf16[1024,768]{1,0:T(8,128)(2,1)} %get-tuple-element.75), kind=kOutput, calls=%fused_computation.3 | convolution fusion | flops 3222798336 | bytes 8912896 | tf_op jit(solution)/shard_map/dot_general | solution.py:68
  401.3 0.7 broadcast_in_dim.32.gain_ref
  402.0 70.1 %in_scatter.1 = (f32[128,2048]{1,0:T(8,128)}, f32[64,6144]{1,0:T(8,128)}, f32[64,128]{1,0:T(8,128)}, bf16[4,1024,256]{2,1,0:T(8,128)(2,1)}) custom-call(bf16[8,128,768]{2,1,0:T(8,128)(2,1)} %bitcast.79, bf16[2048,768]{1,0:T(8,128)(2,1)} %bitcast.76, bf16[4,8,64,768]{3,2,1,0:T(8,128)(2,1)} %bitcast.77, bf16[2048,1024]{1,0:T(8,128)(2,1)} %get-tuple-element.73.up_ref, ...), custom_call_target="tpu_custom_call" | custom-call | tf_op jit(solution)/shard_map/in_scatter/pallas_call | solution.py:86
  472.1 2.2 convert_reduce_fusion.1
  474.7 1.5 pad_maximum_fusion
  476.9 1.3 fusion.24
  478.8 1.7 fusion.21
  480.6 0.9 fusion.23
  482.1 3.4 convert_reduce_fusion
  485.5 3.1 fusion.1
  489.1 1.6 multiply_add_fusion
  491.9 1.1 copy.66
  (105 shorter events, 7.7 us)
Async XLA Ops:
  0.7 4.4 copy-start
  0.7 5.8 %copy-start.21 = (bf16[64]{0:T(256)(128)(2,1)S(1)}, bf16[64]{0:T(256)(128)(2,1)}, u32[]{:S(2)}) copy-start(bf16[64]{0:T(256)(128)(2,1)} %param.28) | copy-start | bytes 388
  0.7 5.8 %copy-start.7 = (bf16[64,6144]{1,0:T(8,128)(2,1)S(1)}, bf16[64,6144]{1,0:T(8,128)(2,1)}, u32[]{:S(2)}) copy-start(bf16[64,6144]{1,0:T(8,128)(2,1)} %weight_ref.1) | copy-start | bytes 2359300
  0.7 5.8 %copy-start.12 = (f32[64,6144]{1,0:T(8,128)S(1)}, f32[64,6144]{1,0:T(8,128)}, u32[]{:S(2)}) copy-start(f32[64,6144]{1,0:T(8,128)} %param.32) | copy-start | bytes 4718596
  10.7 5.4 %copy-start.23 = (bf16[64]{0:T(256)(128)(2,1)S(1)}, bf16[64]{0:T(256)(128)(2,1)}, u32[]{:S(2)}) copy-start(bf16[64]{0:T(256)(128)(2,1)} %param.29) | copy-start | bytes 388
  10.7 5.4 %copy-start.14 = (bf16[64,2048]{1,0:T(8,128)(2,1)S(1)}, bf16[64,2048]{1,0:T(8,128)(2,1)}, u32[]{:S(2)}) copy-start(bf16[64,2048]{1,0:T(8,128)(2,1)} %param.25) | copy-start | bytes 786436
  12.5 4.4 copy-start.24
  169.8 4.0 copy-start.22
  169.8 4.0 copy-start.2
  175.0 142.2 %copy-start.9 = (bf16[1,128,2048]{2,1,0:T(8,128)(2,1)S(1)}, bf16[1,128,2048]{2,1,0:T(8,128)(2,1)}, u32[]{:S(2)}) copy-start(bf16[1,128,2048]{2,1,0:T(8,128)(2,1)} %param.40) | copy-start | bytes 1572868
  315.4 1.8 copy-start.3
  315.4 1.8 copy-start.4
  472.1 2.2 copy-start.10
  474.6 1.6 copy-start.5
  474.6 2.3 copy-start.6
  476.2 2.0 copy-start.19
  476.2 2.6 copy-start.16
  476.2 2.6 copy-start.17
  476.9 3.6 copy-start.15
  478.8 2.7 copy-start.18
  482.1 3.4 copy-start.8
  485.5 3.1 copy-start.25
  485.5 3.1 copy-start.26
  485.5 3.6 copy-start.1
  485.5 3.6 copy-start.11
  489.1 1.7 copy-start.20
  489.1 2.2 copy-start.27
  489.1 2.7 copy-start.13

commit v7 on v6

--- a/solution.py
+++ b/solution.py
@@ -188,47 +188,134 @@
             wait.wait_recv()
 
 
+class ChipGather:
+    def __init__(self, chips, here, source, target, sems):
+        z, c, core = here
+        self.here, self.sems, self.relayed = here, sems, chips == 4
+        if not self.relayed:
+            self.sends = [
+                remote(source(None), target(c, None), sems, k, device)
+                for k, device in enumerate(chip_peers(chips, here), 1)
+            ]
+            self.arrivals = [
+                (lax.rem(c + chips - k, chips), None, k) for k in range(1, chips)
+            ]
+        else:
+            beside = c + 1 - 2 * lax.rem(c, 2)
+            above = c + 2 - 4 * (c // 2)
+            to_beside, to_above = (z, beside, core), (z, above, core)
+            self.sends = [
+                remote(source(0), target(c, 0), sems, 0, to_beside),
+                remote(source(1), target(c, 1), sems, 3, to_above),
+                remote(source(1), target(c, 1), sems, 1, to_beside),
+                remote(source(0), target(c, 0), sems, 2, to_above),
+            ]
+            self.relays = [
+                remote(target(beside, 0), target(beside, 0), sems, 4, to_above),
+                remote(target(above, 1), target(above, 1), sems, 5, to_beside),
+            ]
+            self.arrivals = [
+                (beside, 0, 0), (above, 1, 3), (beside, 1, 1), (above, 0, 2),
+                (3 - c, 0, 4), (3 - c, 1, 5),
+            ]
+        self.target = target
+
+    def start(self):
+        for copy in self.sends:
+            copy.start()
+
+    def arrive(self, i):
+        chip, half, index = self.arrivals[i]
+        block = self.target(chip, half)
+        remote(block, block, self.sems, index, self.here).wait_recv()
+        if self.relayed and i < 2:
+            self.relays[i].start()
+
+    def relay(self):
+        for i in range(2 if self.relayed else 0):
+            self.arrive(i)
+
+    def rest(self):
+        return range(2 if self.relayed else 0, len(self.arrivals))
+
+    def finish(self):
+        for i in self.rest():
+            self.arrive(i)
+        self.sent()
+
+    def sent(self):
+        for copy in [*self.sends, *(self.relays if self.relayed else [])]:
+            copy.wait_send()
+
+    @staticmethod
+    def count(chips):
+        return max(chips, 6)
+
+
 class PlaneGather:
     def __init__(self, chips, here, block, out, far, near):
-        self.chips, self.here, self.block, self.out = chips, here, block, out
-        self.far, self.near = far, near
         z, c, core = here
+        self.here, self.block, self.out, self.near = here, block, out, near
         self.me = 2 * c + core
         self.partner = (z, c, 1 - core)
-
-    def source(self, k, core):
-        return 2 * lax.rem(self.here[1] + self.chips - k, self.chips) + core
-
-    def sends(self):
-        mine = self.out.at[self.me]
-        copies = [
-            remote(self.block, mine, self.far, k, device)
-            for k, device in enumerate(chip_peers(self.chips, self.here), 1)
-        ]
-        return [*copies, remote(self.block, mine, self.near, 0, self.partner)]
+        self.size = block.shape[0] // 2
+        self.chips = ChipGather(
+            chips,
+            here,
+            self.piece,
+            lambda chip, half: self.place(2 * chip + core, half),
+            far,
+        )
+        self.own = remote(block, out.at[self.me], near, len(self.chips.arrivals), self.partner)
+
+    def rows(self, half):
+        return pl.ds(half * self.size, self.size)
+
+    def piece(self, half):
+        return self.block if half is None else self.block.at[self.rows(half)]
+
+    def place(self, index, half):
+        return self.out.at[index] if half is None else self.out.at[index, self.rows(half)]
 
     def start(self):
-        for copy in self.sends():
-            copy.start()
-
-    def passed(self, k):
-        index = self.source(k, self.here[2])
-        return remote(self.out.at[index], self.out.at[index], self.near, k, self.partner)
+        self.chips.start()
+        self.own.start()
+
+    def passed(self, i, other=0):
+        chip, half, _ = self.chips.arrivals[i]
+        core = self.here[2]
+        block = self.place(2 * chip + (1 - core if other else core), half)
+        return remote(block, block, self.near, i, self.partner)
+
+    def relay(self):
+        for i in range(2 if self.chips.relayed else 0):
+            self.chips.arrive(i)
+            self.passed(i).start()
 
     def forward(self):
-        for k in range(1, self.chips):
-            index = self.source(k, self.here[2])
-            remote(self.block, self.out.at[index], self.far, k, self.partner).wait_recv()
-            self.passed(k).start()
+        for i in self.chips.rest():
+            self.chips.arrive(i)
+            self.passed(i).start()
 
     def finish(self):
-        for copy in self.sends():
-            copy.wait_send()
-        for k in range(1, self.chips):
-            self.passed(k).wait_send()
-        for k in range(self.chips):
-            index = self.source(k, 1 - self.here[2])
-            remote(self.block, self.out.at[index], self.near, k, self.partner).wait_recv()
+        self.chips.sent()
+        self.own.wait_send()
+        mine = self.out.at[2 * self.here[1] + 1 - self.here[2]]
+        remote(mine, mine, self.near, len(self.chips.arrivals), self.partner).wait_recv()
+        for i in range(len(self.chips.arrivals)):
+            self.passed(i).wait_send()
+            self.passed(i, 1).wait_recv()
+
+    @staticmethod
+    def sems(chips):
+        return pairs_of(ChipGather.count(chips), ChipGather.count(chips) + 1)
+
+
+def row_half(ref, half):
+    if half is None:
+        return ref
+    size = ref.shape[0] // 2
+    return ref.at[pl.ds(half * size, size)]
 
 
 class LineGather:
@@ -724,12 +811,14 @@
     group.start(local.at[2])
     keep = pltpu.make_async_copy(down_ref, downs.at[c], local.at[3])
     keep.start()
-    sends = [
-        remote(down_ref, downs.at[c], chip_sems, k, device)
-        for k, device in enumerate(chip_peers(chips, here), 1)
-    ]
-    for copy in sends:
-        copy.start()
+    weights = ChipGather(
+        chips,
+        here,
+        lambda half: row_half(down_ref, half),
+        lambda chip, half: row_half(downs.at[chip], half),
+        chip_sems,
+    )
+    weights.start()
     load_up.wait()
 
     step = tokens
@@ -761,6 +850,8 @@
     forward(z)
     for d in range(1, planes):
         group.step(d)
+        if d == 2:
+            weights.relay()
         if d > 1:
             pl.when(z - d + 1 >= 0)(lambda d=d: forward(z - d + 1))
             pl.when(z + d - 1 < planes)(lambda d=d: forward(z + d - 1))
@@ -769,10 +860,7 @@
     group.finish()
     keep.wait()
     load_grads.wait()
-    for k in range(1, chips):
-        sends[k - 1].wait_send()
-        other = lax.rem(c + chips - k, chips)
-        remote(down_ref, downs.at[other], chip_sems, k, here).wait_recv()
+    weights.finish()
     out_downs = pltpu.make_async_copy(downs, downs_ref, local.at[4])
     out_downs.start()
 
@@ -932,7 +1020,7 @@
             pltpu.VMEM((2, 256, units), LOW),
             pltpu.VMEM((chips, size, width), LOW),
             *GroupGather.sems(planes),
-            *pairs_of(chips, 2 * planes),
+            *pairs_of(ChipGather.count(chips), 2 * planes),
             *PairScatter.sems(planes, width),
             *pairs_of(chips),
             pltpu.SemaphoreType.DMA((9,)),
@@ -1048,14 +1136,20 @@
     gather.start()
     meta_gather.start()
     lax.fori_loop(1, count, gain_start, 0)
+    gather.relay()
+    meta_gather.relay()
+    line.step(1)
     gather.forward()
     meta_gather.forward()
-    ups = [
-        remote(up_ref, column_block(ups_ref, units, c), up_sems, k, device)
-        for k, device in enumerate(chip_peers(chips, here), 1)
-    ]
-    for copy in ups:
-        copy.start()
+    ups = ChipGather(
+        chips,
+        here,
+        lambda part: row_half(up_ref, part),
+        lambda chip, part: row_half(column_block(ups_ref, units, chip), part),
+        up_sems,
+    )
+    ups.start()
+    line.step(2)
     gather.finish()
     meta_gather.finish()
     for copy in keeps:
@@ -1073,10 +1167,15 @@
 
     add(z, True)
     for d in range(1, planes):
-        line.step(d)
+        if d == 3:
+            ups.relay()
+        if d > 2:
+            line.step(d)
         if d == planes - 1:
             if strided:
                 line_two.start()
+            group = GroupGather(planes, here, grad_ref, grads_ref, grad_up, grad_down, pair)
+            group.start(local.at[6])
         pl.when(z - d >= 0)(lambda d=d: add(z - d))
         pl.when(z + d < planes)(lambda d=d: add(z + d))
     outputs = [
@@ -1134,8 +1233,8 @@
         first = last
         if strided:
             line_two.step(d)
-    group = GroupGather(planes, here, grad_ref, grads_ref, grad_up, grad_down, pair)
-    group.start(local.at[6])
+        if d == 2:
+            group.step(1)
     lax.fori_loop(first, heads, one_head, 0)
     lane = lax.broadcasted_iota(jnp.int32, (tokens, 128), 1)
     column = jnp.sum(outs[...].astype(F32).reshape(span, width), axis=0, keepdims=True)
@@ -1164,7 +1263,7 @@
         chips, here, att_ref, Flat(outs, span), False, (near_out, near_in, far_out, far_in), near, far
     )
     work.start()
-    for d in range(1, planes):
+    for d in range(2, planes):
         group.step(d)
     work.finish(sum_ref)
     group.finish()
@@ -1173,11 +1272,9 @@
     line.finish()
     if strided:
         line_two.finish()
-    for copy in [*swaps, *ups]:
+    for copy in swaps:
         copy.wait_send()
-    for k in range(1, chips):
-        other = lax.rem(c + chips - k, chips)
-        remote(up_ref, column_block(ups_ref, units, other), up_sems, k, here).wait_recv()
+    ups.finish()
     for copy in [keep, out_outs, *outputs]:
         copy.wait()
     for k in range(1, seqs):
@@ -1256,9 +1353,10 @@
             pltpu.VMEM((heads, length, HD), F32),
             pltpu.VMEM(tile, F32),
             *PlaneScatter.scratch(chips, tokens, width),
-            *pairs_of(
-                seqs, *[chips] * 4, *[2 * planes] * 2, *[planes] * 2, planes * seqs, chips
-            ),
+            *pairs_of(seqs),
+            *PlaneGather.sems(chips),
+            *PlaneGather.sems(chips),
+            *pairs_of(*[2 * planes] * 2, *[planes] * 2, planes * seqs, ChipGather.count(chips)),
             *PlaneScatter.sems(chips, width),
             *pairs_of(seqs),
             *GroupGather.sems(planes),
@@ -1342,6 +1440,8 @@
             work.line.step(left_turns.pop(0))
 
     turn()
+    gather.relay()
+    stat_gather.relay()
     turn()
     gather.forward()
     stat_gather.forward()
@@ -1486,7 +1586,9 @@
             pltpu.VMEM((length, span), LOW),
             pltpu.VMEM((planes, part, width), LOW),
             pltpu.VMEM((planes + 1, part, width), LOW),
-            *pairs_of(chips, chips, chips, chips, planes * seqs),
+            *PlaneGather.sems(chips),
+            *PlaneGather.sems(chips),
+            *pairs_of(planes * seqs),
             *PairScatter.sems(planes, width),
             *pairs_of(planes, planes, chips),
             pltpu.SemaphoreType.DMA((13,)),

time: 501 us -> 465 us (0.928)
  Pallas kernels: 435 us -> 399 us
    pallas_call x4, Pallas kernels: 435 us -> 399 us  [call(): pl.pallas_call(kernel, name=name, out_shape=outs, in_specs=in_specs, out_...]
where the time goes in v7:
time: 465 us; the launch traced here: 458 us
  Pallas kernels  399 us (86%)
  other arithmetic  34.3 us (7%)
  local copies, waits for them, and re-layouts  15.2 us (3%)
  matrix products  7.87 us (2%)
    pallas_call x4, Pallas kernels, call(): pl.pallas_call(kernel, name=name, out_shape=outs, in_specs=in_specs, out_...  399 us

profile of v7, /device:TPU:9, one launch (start us, length us, event | category | flops | bytes accessed | tf_op | source)
XLA Modules:
  0.0 457.9 jit_solution(7308093231613856982)
XLA Ops:
  0.7 0.8 convert_bitcast_fusion.2
  3.0 0.8 pad_maximum_fusion.1.meta_ref
  3.8 1.2 convert_reduce_fusion.3
  5.3 1.1 fusion.11.x_ref
  6.5 1.7 fusion.4
  8.2 2.5 reshape.215
  10.7 1.8 copy.64
  12.5 3.6 reshape.216.qkv_ref
  16.1 0.8 fusion.20.out_ref
  17.5 135.2 %attention_forward.1 = (bf16[4,1024,64]{2,1,0:T(8,128)(2,1)}, bf16[4,1024,64]{2,1,0:T(8,128)(2,1)}, bf16[4,1024,64]{2,1,0:T(8,128)(2,1)}, bf16[8,128,256]{2,1,0:...) custom-call(bf16[128,2048]{1,0:T(8,128)(2,1)} %fusion.11.x_ref, ...), custom_call_target="tpu_custom_call" | custom-call | tf_op jit(solution)/shard_map/attention_forward/pallas_call | solution.py:86
  152.8 0.9 reduce_sum.164
  153.7 1.7 fusion.28
  155.7 1.0 slice_reduce_fusion.1
  156.7 1.0 multiply_convert_fusion.x_ref
  157.7 1.2 fusion.down_ref
  158.9 128.2 %feed_forward.1 = (f32[128,2048]{1,0:T(8,128)}, bf16[4,256,1024]{2,1,0:T(8,128)(2,1)}, bf16[4,256,2048]{2,1,0:T(8,128)(2,1)}, bf16[2048,1024]{1,0:T(8,128)(2,1)}, bf16[4,256,2048]{2,1,0:T(8,128)(2,1)}) custom-call(bf16[128,2048]{1,0:T(8,128)(2,1)} %multiply_convert_fusion.x_ref, bf16[2048,1024]{1,0:T(8,128)(2,1)} %get-tuple-element.61.up_ref, ...), custom_call_target="tpu_custom_call" | custom-call | tf_op jit(solution)/shard_map/feed_forward/pallas_call | solution.py:86
  287.1 1.7 multiply_reduce_fusion
  288.9 1.8 fusion.18
  291.6 0.7 pad.14.tile_ref
  292.3 66.4 %attention_backward.1 = (f32[32,8,128]{2,1,0:T(8,128)}, f32[128,2048]{1,0:T(8,128)}, bf16[1024,768]{1,0:T(8,128)(2,1)}, f32[64,2048]{1,0:T(8,128)}, bf16[4,1024,256]{2,1,0:T(8,128)(2,1)}) custom-call(bf16[128,2048]{1,0:T(8,128)(2,1)} %get-tuple-element.93.x_ref, f32[128,128]{1,0:T(8,128)} %pad.13.stat_ref, f32[32,8,128]{2,1,0:T(8,128)} %pad.14.tile_ref, ...), custom_call_target="tpu_custom_call" | custom-call | tf_op jit(solution)/shard_map/attention_backward/pallas_call | solution.py:86
  358.7 7.9 %convolution_convert_fusion = bf16[2048,768]{1,0:T(8,128)(2,1)} fusion(bf16[1024,2048]{1,0:T(8,128)(2,1)} %bitcast.90, bf16[1024,768]{1,0:T(8,128)(2,1)} %get-tuple-element.75), kind=kOutput, calls=%fused_computation.3 | convolution fusion | flops 3222798336 | bytes 8912896 | tf_op jit(solution)/shard_map/dot_general | solution.py:68
  366.6 0.7 broadcast_in_dim.32.gain_ref
  367.3 69.3 %in_scatter.1 = (f32[128,2048]{1,0:T(8,128)}, f32[64,6144]{1,0:T(8,128)}, f32[64,128]{1,0:T(8,128)}, bf16[4,1024,256]{2,1,0:T(8,128)(2,1)}) custom-call(bf16[8,128,768]{2,1,0:T(8,128)(2,1)} %bitcast.79, bf16[2048,768]{1,0:T(8,128)(2,1)} %bitcast.76, bf16[4,8,64,768]{3,2,1,0:T(8,128)(2,1)} %bitcast.77, bf16[2048,1024]{1,0:T(8,128)(2,1)} %get-tuple-element.73.up_ref, ...), custom_call_target="tpu_custom_call" | custom-call | tf_op jit(solution)/shard_map/in_scatter/pallas_call | solution.py:86
  436.6 2.2 convert_reduce_fusion.1
  439.2 1.5 pad_maximum_fusion
  441.5 1.3 fusion.24
  443.3 1.7 fusion.21
  445.1 0.9 fusion.23
  446.6 3.4 convert_reduce_fusion
  450.0 3.1 fusion.1
  453.6 1.6 multiply_add_fusion
  456.4 1.1 copy.66
  (105 shorter events, 7.7 us)
Async XLA Ops:
  0.7 4.4 copy-start
  0.7 5.8 %copy-start.21 = (bf16[64]{0:T(256)(128)(2,1)S(1)}, bf16[64]{0:T(256)(128)(2,1)}, u32[]{:S(2)}) copy-start(bf16[64]{0:T(256)(128)(2,1)} %param.28) | copy-start | bytes 388
  0.7 5.8 %copy-start.7 = (bf16[64,6144]{1,0:T(8,128)(2,1)S(1)}, bf16[64,6144]{1,0:T(8,128)(2,1)}, u32[]{:S(2)}) copy-start(bf16[64,6144]{1,0:T(8,128)(2,1)} %weight_ref.1) | copy-start | bytes 2359300
  0.7 5.8 %copy-start.12 = (f32[64,6144]{1,0:T(8,128)S(1)}, f32[64,6144]{1,0:T(8,128)}, u32[]{:S(2)}) copy-start(f32[64,6144]{1,0:T(8,128)} %param.32) | copy-start | bytes 4718596
  10.7 5.4 %copy-start.23 = (bf16[64]{0:T(256)(128)(2,1)S(1)}, bf16[64]{0:T(256)(128)(2,1)}, u32[]{:S(2)}) copy-start(bf16[64]{0:T(256)(128)(2,1)} %param.29) | copy-start | bytes 388
  10.7 5.4 %copy-start.14 = (bf16[64,2048]{1,0:T(8,128)(2,1)S(1)}, bf16[64,2048]{1,0:T(8,128)(2,1)}, u32[]{:S(2)}) copy-start(bf16[64,2048]{1,0:T(8,128)(2,1)} %param.25) | copy-start | bytes 786436
  12.5 4.4 copy-start.24
  153.7 4.0 copy-start.22
  153.7 4.0 copy-start.2
  158.9 129.9 %copy-start.9 = (bf16[1,128,2048]{2,1,0:T(8,128)(2,1)S(1)}, bf16[1,128,2048]{2,1,0:T(8,128)(2,1)}, u32[]{:S(2)}) copy-start(bf16[1,128,2048]{2,1,0:T(8,128)(2,1)} %param.40) | copy-start | bytes 1572868
  287.1 1.8 copy-start.3
  287.1 1.8 copy-start.4
  436.6 2.2 copy-start.10
  439.1 1.6 copy-start.5
  439.2 2.3 copy-start.6
  440.7 2.0 copy-start.19
  440.7 2.6 copy-start.16
  440.7 2.6 copy-start.17
  441.4 3.6 copy-start.15
  443.3 2.7 copy-start.18
  446.6 3.4 copy-start.8
  450.0 3.1 copy-start.25
  450.0 3.1 copy-start.26
  450.0 3.6 copy-start.1
  450.0 3.6 copy-start.11
  453.6 1.7 copy-start.20
  453.6 2.2 copy-start.27
  453.6 2.7 copy-start.13

commit v8 on v7

--- a/solution.py
+++ b/solution.py
@@ -82,9 +82,10 @@
     return [pltpu.SemaphoreType.DMA((count,)) for count in counts for _ in range(2)]
 
 
-def call(kernel, name, outs, args, in_specs, out_specs, scratch, collective=None):
+def call(kernel, name, outs, args, in_specs, out_specs, scratch, collective=None, aliases=None):
     return pl.pallas_call(
         kernel,
+        input_output_aliases=aliases or {},
         name=name,
         out_shape=outs,
         in_specs=in_specs,
@@ -154,26 +155,30 @@
     return whole.at[:, pl.ds(pl.multiple_of(index * units, 128), units)]
 
 
-def half_block(whole, slots, index, half):
-    rows, units = slots.shape[1:]
-    at = pl.ds(half * rows, rows)
+def half_rows(rows, half):
+    size = rows // 2
+    return pl.ds(half * size, size)
+
+
+def half_block(whole, units, index, half):
+    at = half_rows(whole.shape[-2], half)
     if len(whole.shape) == 3:
         return whole.at[index, at]
     return whole.at[at, pl.ds(pl.multiple_of(index * units, 128), units)]
 
 
 class ChipSwap:
-    def __init__(self, chips, here, source, slots, sems):
+    def __init__(self, chips, here, source, slot, sems):
         z, c, core = here
         self.sends = [
-            remote(source(device[1]), slots.at[c], sems, k, device)
+            remote(source(device[1]), slot(c), sems, k, device)
             for k, device in enumerate(chip_peers(chips, here), 1)
         ]
         self.waits = [
-            remote(source(c), slots.at[lax.rem(c + chips - k, chips)], sems, k, here)
+            remote(source(c), slot(lax.rem(c + chips - k, chips)), sems, k, here)
             for k in range(1, chips)
         ]
-        self.keep = (source(c), slots.at[c])
+        self.keep = (source(c), slot(c))
 
     def start(self, local):
         for copy in self.sends:
@@ -606,8 +611,9 @@
 
 
 def in_scatter_kernel(
-    planes, chips, heads, strided, left_ref, right_ref, grad_ref, up_ref, weight_ref, gain_ref,
+    planes, chips, heads, strided, left_in, right_in, rows_in, up_ref, weight_ref, gain_ref, _,
     out_ref, total_ref, gains_ref, slots_ref,
+    left_ref, right_ref, rows_ref, grad_ref,
     near_out, near_in, far_out, far_in, sums, mine, parts, *sems,
 ):
     here = place()
@@ -615,6 +621,14 @@
     seqs = 2 * chips
     me = 2 * c + core
     near, far, up, down, swap_sems, chip_sems = [sems[2 * i : 2 * i + 2] for i in range(6)]
+    local = sems[12]
+    loads = [
+        pltpu.make_async_copy(rows_in, rows_ref, local.at[1]),
+        pltpu.make_async_copy(left_in, left_ref, local.at[2]),
+        pltpu.make_async_copy(right_in, right_ref, local.at[3]),
+    ]
+    for copy in loads:
+        copy.start()
     barrier = pltpu.get_barrier_semaphore()
     peers = plane_peers(chips, here)
     greet(barrier, peers)
@@ -632,15 +646,42 @@
         up,
         down,
     )
+    part = grad_ref.shape[2]
+    span = heads * HD
+    block = seqs * part
+    length = rows_ref.shape[0]
+    for copy in loads:
+        copy.wait()
+
+    def grads(t):
+        left = rows_ref[:, t * block : (t + 1) * block]
+        for i in range(3):
+            at = pl.ds(i * span, span)
+            term = token_product(left, left_ref[:, :, at].reshape(length, span))
+            grad_ref[t, :, :, at] = term.astype(LOW).reshape(seqs, part, span)
+
+    order = []
+    for i in range((planes + 1) // 2):
+        order += [planes - 1 - i, i] if planes - 1 - i != i else [i]
+    for t in order[:2]:
+        grads(t)
     line.step(0)
+    for t in order[2:]:
+        grads(t)
     work = PlaneScatter(
         chips, here, left_ref, right_ref, True, (near_out, near_in, far_out, far_in), near, far
     )
     work.start()
+    units = slots_ref.shape[2]
+    lower = half_rows(slots_ref.shape[1], 1)
     ups = ChipSwap(
-        chips, here, lambda index: half_block(up_ref, slots_ref, index, 1), slots_ref, chip_sems
-    )
-    ups.start(sems[12].at[0])
+        chips,
+        here,
+        lambda index: half_block(up_ref, units, index, 1),
+        lambda index: slots_ref.at[index, lower],
+        chip_sems,
+    )
+    ups.start(local.at[0])
     for i in range(1, line.steps):
         line.step(i)
 
@@ -660,7 +701,6 @@
         swaps[k - 1].wait_send()
         index = lax.rem(me + seqs - k, seqs)
         remote(mine.at[0], parts.at[index], swap_sems, k, here).wait_recv()
-    span = heads * HD
     width = seqs * span
     gain = gain_ref[:, pl.ds(0, 1)]
     summed = jnp.zeros(gain.shape, F32)
@@ -680,11 +720,11 @@
     ups.finish()
 
 
-def in_scatter(planes, chips, heads, strided, left, right, grads, up_grads, weight, gain, units):
+def in_scatter(planes, chips, heads, strided, left, right, rows, up_grads, weight, gain, slots):
     _, tokens, _ = left.shape
     width = right.shape[0]
     seqs = 2 * chips
-    part, wide = grads.shape[2:]
+    part, wide = weight.shape[0], left.shape[2]
     return call(
         functools.partial(in_scatter_kernel, planes, chips, heads, strided),
         "in_scatter",
@@ -692,20 +732,23 @@
             shape((tokens, width), F32),
             shape(weight.shape, F32),
             shape((part, 128), F32),
-            shape((chips, width // 2, units), LOW),
+            shape(slots.shape, LOW),
         ],
-        (left, right, grads, up_grads, weight, gain),
-        [VMEM, VMEM, VMEM, HBM, VMEM, VMEM],
+        (left, right, rows, up_grads, weight, gain, slots),
+        [HBM, HBM, HBM, HBM, VMEM, VMEM, HBM],
         [VMEM, VMEM, VMEM, HBM],
         [
+            *[pltpu.VMEM(whole.shape, LOW) for whole in (left, right, rows)],
+            pltpu.VMEM((planes, seqs, part, wide), LOW),
             *PlaneScatter.scratch(chips, tokens, width),
             pltpu.VMEM((planes + 1, seqs, part, wide), LOW),
             *[pltpu.VMEM((seqs, part, wide), LOW)] * 2,
             *PlaneScatter.sems(chips, width),
             *pairs_of(2 * planes, 2 * planes, seqs, chips),
-            pltpu.SemaphoreType.DMA((1,)),
+            pltpu.SemaphoreType.DMA((4,)),
         ],
         4,
+        {6: 3},
     )
 
 
@@ -782,7 +825,7 @@
 
 def feed_forward_kernel(
     planes, chips, width_ff, x_ref, up_ref, grads_ref, down_ref,
-    out_ref, normed_ref, downs_ref, gup_ref, slots_ref,
+    out_ref, normed_ref, downs_ref, gup_ref, gdown_ref, slots_ref,
     rows, ups, grads, downs, back, act, slope, stat, stat_out, stat_in,
     normed, d_up, near_out, own, sums, gup, gdown, *sems,
 ):
@@ -933,7 +976,14 @@
         whole[...].reshape(planes * 2 * tokens, units) for whole in (normed, d_up)
     )
     size = units // chips
-    swap = ChipSwap(chips, here, lambda index: gdown.at[index], slots_ref, swap_sems)
+    upper = half_rows(size, 0)
+    swap = ChipSwap(
+        chips,
+        here,
+        lambda index: gdown.at[index, upper],
+        lambda index: slots_ref.at[index, upper],
+        swap_sems,
+    )
     turns_left = list(range(1, work.line.steps))
 
     def turn():
@@ -952,6 +1002,8 @@
         if chip // together % 2:
             turn()
     swap.start(local.at[6])
+    out_gdown = pltpu.make_async_copy(gdown, gdown_ref, local.at[9])
+    out_gdown.start()
     chunk = gup.shape[1]
     out_gups = [
         pltpu.make_async_copy(
@@ -974,6 +1026,7 @@
     swap.finish()
     out_downs.wait()
     out_normed.wait()
+    out_gdown.wait()
     for copy in out_gups[-2:]:
         copy.wait()
 
@@ -1001,11 +1054,11 @@
             shape(wide, LOW),
             shape((chips, size, width), LOW),
             shape((width, units), LOW),
-            shape((chips, size, width), LOW),
+            *[shape((chips, size, width), LOW)] * 2,
         ],
         (x_block, up_mine, grads, down_block),
         [HBM] * 4,
-        [VMEM, HBM, HBM, HBM, HBM],
+        [VMEM, *[HBM] * 5],
         [
             pltpu.VMEM((planes, 2, tokens, width), LOW),
             pltpu.VMEM((width, units), LOW),
@@ -1023,7 +1076,7 @@
             *pairs_of(ChipGather.count(chips), 2 * planes),
             *PairScatter.sems(planes, width),
             *pairs_of(chips),
-            pltpu.SemaphoreType.DMA((9,)),
+            pltpu.SemaphoreType.DMA((10,)),
         ],
         7,
     )
@@ -1059,10 +1112,10 @@
 
 def attention_forward_kernel(
     planes, chips, heads, strided,
-    x_ref, meta_ref, qkv_ref, out_ref, gain_ref, up_ref, grad_ref,
+    x_ref, meta_ref, weight_ref, scale_ref, out_ref, gain_ref, up_ref, grad_ref,
     q_ref, k_ref, v_ref, att_ref, log_ref, sum_ref,
     rows_ref, metas_ref, qkvs_ref, outs_ref, gains_ref, ups_ref, grads_ref, tiles_ref,
-    rows, metas, qkvs, outs, raw, wide, tile, near_out, near_in, far_out, far_in,
+    qkv_ref, rows, metas, qkvs, outs, raw, wide, tile, near_out, near_in, far_out, far_in,
     *sems,
 ):
     here = place()
@@ -1076,7 +1129,7 @@
     gain_sems, up_sems, near, far, tile_sems, grad_up, grad_down, pair = groups[9:]
     local = sems[34]
     tokens, width = x_ref.shape
-    part, three = qkv_ref.shape[1:]
+    part = qkv_ref.shape[1]
     length = seqs * tokens
     span = heads * HD
     barrier = pltpu.get_barrier_semaphore()
@@ -1090,6 +1143,16 @@
         return carry
 
     lax.fori_loop(1, count, signal, 0)
+    scale = scale_ref[:, pl.ds(0, 1)]
+    for s in range(seqs):
+        for i in range(3):
+            if strided:
+                starts = [i * width + (t * seqs + s) * HD for t in range(planes)]
+                size = span // planes
+            else:
+                starts, size = [i * width + s * span], span
+            piece = jnp.concatenate([weight_ref[:, pl.ds(at, size)] for at in starts], axis=1)
+            qkv_ref[s, :, pl.ds(i * span, span)] = (piece.astype(F32) * scale).astype(LOW)
     pl.semaphore_wait(barrier, count - 1)
 
     mine = pltpu.make_async_copy(qkv_ref.at[me], qkvs.at[z, me], local.at[0])
@@ -1314,11 +1377,11 @@
 
 
 def attention_forward(
-    planes, chips, heads, strided, x_block, meta, qkv_blocks, out_rows, gain_tile, up_block, grad
+    planes, chips, heads, strided, x_block, meta, weight, scale, out_rows, gain_tile, up_block, grad
 ):
     seqs = 2 * chips
     tokens, width = x_block.shape
-    part, wide = qkv_blocks.shape[1:]
+    part, wide = weight.shape[0], 3 * heads * HD
     units = up_block.shape[1]
     length = seqs * tokens
     span = heads * HD
@@ -1341,10 +1404,11 @@
             shape((planes, 2, *grad.shape), LOW),
             shape(tile, F32),
         ],
-        (x_block, meta, qkv_blocks, out_rows, gain_tile, up_block, grad),
-        [HBM] * 7,
+        (x_block, meta, weight, scale, out_rows, gain_tile, up_block, grad),
+        [HBM, HBM, VMEM, VMEM, HBM, HBM, HBM, HBM],
         [*[VMEM] * 6, *[HBM] * 8],
         [
+            pltpu.VMEM((seqs, part, wide), LOW),
             pltpu.VMEM((seqs, tokens, width), LOW),
             pltpu.VMEM((seqs, *meta.shape), F32),
             pltpu.VMEM((planes, seqs, part, wide), LOW),
@@ -1369,8 +1433,8 @@
 def attention_backward_kernel(
     planes, chips, heads, strided,
     x_ref, stat_ref, tile_ref, left_ref, right_ref,
-    q_in, k_in, v_in, att_in, out_in, log_in, meta_in, up_ref,
-    tiles_ref, ffn_ref, out_ref, total_ref, slots_ref,
+    q_in, k_in, v_in, att_in, out_in, log_in, meta_in, up_ref, down_ref, _,
+    tiles_ref, ffn_ref, out_ref, total_ref, slots_ref, down_slots_ref,
     rows, stats, left, right, q_ref, k_ref, v_ref, att_ref, outs, log_ref, meta_ref,
     near_out, near_own, near_sums, grad, dq, dk, dv, normed_all, own, sums, *sems,
 ):
@@ -1383,7 +1447,8 @@
     x_far, x_near, s_far, s_near, tile_sems, near, up, down, up_two, down_two, swap_sems = [
         sems[2 * i : 2 * i + 2] for i in range(11)
     ]
-    local = sems[22]
+    down_sems = sems[22:24]
+    local = sems[24]
     pairs = [
         (left_ref, left), (right_ref, right), (att_in, att_ref), (out_in, outs), (meta_in, meta_ref),
         (q_in, q_ref), (k_in, k_ref), (v_in, v_ref), (log_in, log_ref),
@@ -1447,10 +1512,26 @@
     stat_gather.forward()
     gather.finish()
     stat_gather.finish()
-    swap = ChipSwap(
-        chips, here, lambda index: half_block(up_ref, slots_ref, index, 0), slots_ref, swap_sems
-    )
-    swap.start(local.at[12])
+    units = slots_ref.shape[2]
+    upper, lower = half_rows(width, 0), half_rows(down_ref.shape[1], 1)
+    swaps = [
+        ChipSwap(
+            chips,
+            here,
+            lambda index: half_block(up_ref, units, index, 0),
+            lambda index: slots_ref.at[index, upper],
+            swap_sems,
+        ),
+        ChipSwap(
+            chips,
+            here,
+            lambda index: down_ref.at[index, lower],
+            lambda index: down_slots_ref.at[index, lower],
+            down_sems,
+        ),
+    ]
+    for i, swap in enumerate(swaps):
+        swap.start(local.at[12 + i])
     for copy in [*loads[2:], *keeps]:
         copy.wait()
     turn()
@@ -1547,7 +1628,8 @@
     else:
         for t in range(planes):
             total_ref[pl.ds(t * part, part)] = own[t].astype(F32)
-    swap.finish()
+    for swap in swaps:
+        swap.finish()
 
     def tile_wait(k, carry):
         tile_copy(k).wait_send()
@@ -1571,11 +1653,12 @@
             shape((tokens, width), F32),
             shape((length, 3 * span), LOW),
             shape((part if strided else span, width), F32),
-            shape((chips, width // 2, units), LOW),
+            shape((chips, width, units), LOW),
+            shape(args[14].shape, LOW),
         ],
         args,
-        [HBM] * 13,
-        [HBM, VMEM, VMEM, VMEM, HBM],
+        [HBM] * 15,
+        [HBM, VMEM, VMEM, VMEM, HBM, HBM],
         [
             pltpu.VMEM((seqs, tokens, width), LOW),
             pltpu.VMEM((seqs, tokens, 128), F32),
@@ -1590,10 +1673,11 @@
             *PlaneGather.sems(chips),
             *pairs_of(planes * seqs),
             *PairScatter.sems(planes, width),
-            *pairs_of(planes, planes, chips),
-            pltpu.SemaphoreType.DMA((13,)),
+            *pairs_of(planes, planes, chips, chips),
+            pltpu.SemaphoreType.DMA((14,)),
         ],
         2,
+        {14: 5},
     )
 
 
@@ -1633,17 +1717,12 @@
     def gain_rows(weight, gain):
         return (weight.astype(F32) * gain.astype(F32)[:, None]).astype(LOW)
 
-    qkv_scaled = gain_rows(w_qkv, gain_attn)
     out_scaled = gain_rows(w_out, gain_attn_sub)
     down_scaled = gain_rows(w_down, gain_ffn_sub)
-    if strided:
-        qkv_send = qkv_scaled.reshape(part, 3, planes, seqs, HD).transpose(3, 0, 1, 2, 4)
-    else:
-        qkv_send = qkv_scaled.reshape(part, 3, seqs, span).transpose(2, 0, 1, 3)
-    qkv_send = qkv_send.reshape(seqs, part, 3 * span)
     x_in = hidden_in[0].astype(F32)
     normed_one, scaler_one = moments(x_in)
     normed_low = normed_one.astype(LOW)
+    qkv_gain = jnp.broadcast_to(gain_attn.astype(F32)[:, None], (part, 128))
     gain_tile = jnp.zeros((8, 128), F32).at[0, :part].set(gain_ffn.astype(F32))
 
     if not strided:
@@ -1661,7 +1740,8 @@
         strided,
         normed_low,
         token_tables(position_ids[0]),
-        qkv_send,
+        w_qkv,
+        qkv_gain,
         out_scaled,
         gain_tile,
         w_up,
@@ -1687,7 +1767,7 @@
 
     grad_top = grad_low.astype(F32)
     units = w_up.shape[1]
-    d_ffn_in, normed_four, down_mine, grad_up, down_slots = feed_forward(
+    d_ffn_in, normed_four, down_mine, grad_up, grad_down, down_slots = feed_forward(
         planes, chips, width_ff, ffn_in, up_mine, grad_flat, down_scaled
     )
     down_mine = down_mine.reshape(-1, width)
@@ -1702,7 +1782,7 @@
     first_two = jnp.sum(d_hmid_wide * column_sum[None, :], axis=1, keepdims=True) / width
     second_two = jnp.sum(d_hmid_wide * projected, axis=1, keepdims=True) / width
     token_stats = jnp.concatenate([mean_two, scaler_two, first_two, second_two], axis=1)
-    gain_part, ffn_out, d_qkv, sum_out, upper_slots = attention_backward(
+    gain_part, ffn_out, d_qkv, sum_out, up_slots, down_slots = attention_backward(
         planes,
         chips,
         heads,
@@ -1723,28 +1803,27 @@
             log_total,
             meta,
             grad_up,
+            grad_down,
+            down_slots,
         ),
     )
     output = (hmid + ffn_out).astype(LOW)[None]
     grad_gain_three = jnp.sum(gain_part, axis=0)[0, :part]
-    grad_qkv = token_product(row_in, d_qkv).astype(LOW)
-    d_in, sum_qkv, grad_gain_one, lower_slots = in_scatter(
+    d_in, sum_qkv, grad_gain_one, up_slots = in_scatter(
         planes,
         chips,
         heads,
         strided,
         d_qkv.reshape(seqs, tokens, 3 * span),
         qkv_mine,
-        grad_qkv.reshape(planes, seqs, part, 3 * span),
+        row_in,
         grad_up,
         w_qkv,
-        jnp.broadcast_to(gain_attn.astype(F32)[:, None], (part, 128)),
-        units,
+        qkv_gain,
+        up_slots,
     )
     grad_gain_one = grad_gain_one[:, 0]
-    sum_up = jnp.concatenate(
-        [jnp.sum(slots.astype(F32), axis=0) for slots in (upper_slots, lower_slots)], axis=0
-    )
+    sum_up = jnp.sum(up_slots.astype(F32), axis=0)
     sum_down = jnp.sum(down_slots.astype(F32), axis=0)
     input_grad = (d_hmid + norm_back(d_in, normed_one, scaler_one)).astype(LOW)[None]
 

time: 465 us -> 441 us (0.948)
  matrix products: 7.87 us -> 0 us
  local copies, waits for them, and re-layouts: 15.2 us -> 7.71 us
  Pallas kernels: 399 us -> 392 us
    dot_general x1 -> x0, matrix products: 7.87 us -> none  [token_product(): lax.dot_general(left_op, right_op, (((0,), (0,)), ((), ())), preferred_el...]
    reshape x3 -> x0, local copies, waits for them, and re-layouts: 7.86 us -> none  [the longest x2 4.25 us: body(): qkv_scaled.reshape(part, 3, planes, seqs, HD).transpose(3, 0, 1, 2, 4)]
    pallas_call x4, Pallas kernels: 399 us -> 392 us  [call(): pl.pallas_call(kernel, input_output_aliases=aliases or {}, name=name, out...]
where the time goes in v8:
time: 441 us; the launch traced here: 435 us
  Pallas kernels  392 us (89%)
  other arithmetic  33.5 us (8%)
  local copies, waits for them, and re-layouts  7.71 us (2%)
    pallas_call x4, Pallas kernels, call(): pl.pallas_call(kernel, input_output_aliases=aliases or {}, name=name, out...  392 us

profile of v8, /device:TPU:9, one launch (start us, length us, event | category | flops | bytes accessed | tf_op | source)
XLA Modules:
  0.0 434.8 jit_solution(15125518534789912822)
XLA Ops:
  0.7 0.7 convert_bitcast_fusion.2
  1.7 0.7 broadcast_multiply_fusion.2
  2.9 0.8 pad_maximum_fusion.meta_ref
  3.7 1.2 convert_reduce_fusion.2
  5.2 1.1 fusion.9.x_ref
  6.4 0.8 fusion.18.out_ref
  7.2 0.7 broadcast_in_dim.31.scale_ref.gain_ref
  7.9 0.6 scatter.4.gain_ref
  8.5 136.2 %attention_forward.1 = (bf16[4,1024,64]{2,1,0:T(8,128)(2,1)}, bf16[4,1024,64]{2,1,0:T(8,128)(2,1)}, bf16[4,1024,64]{2,1,0:T(8,128)(2,1)}, bf16[8,128,256]{2,1,0:...) custom-call(bf16[128,2048]{1,0:T(8,128)(2,1)} %fusion.9.x_ref, ...), custom_call_target="tpu_custom_call" | custom-call | tf_op jit(solution)/shard_map/attention_forward/pallas_call | solution.py:86
  144.7 0.9 reduce_sum.155
  145.7 1.7 fusion.26
  147.6 1.0 slice_reduce_fusion.1
  148.6 1.0 multiply_convert_fusion.x_ref
  149.6 1.2 fusion.down_ref
  150.9 105.6 %feed_forward.1 = (f32[128,2048]{1,0:T(8,128)}, bf16[4,256,1024]{2,1,0:T(8,128)(2,1)}, bf16[4,256,2048]{2,1,0:T(8,128)(2,1)}, bf16[2048,1024]{1,0:T(8,128)(2,1)}...) custom-call(bf16[128,2048]{1,0:T(8,128)(2,1)} %multiply_convert_fusion.x_ref, ...), custom_call_target="tpu_custom_call" | custom-call | tf_op jit(solution)/shard_map/feed_forward/pallas_call | solution.py:86
  256.5 1.7 multiply_reduce_fusion
  258.4 1.8 fusion.16
  260.3 0.6 pad.13.stat_ref
  261.0 0.7 pad.14.tile_ref
  261.7 78.6 %attention_backward.1 = (f32[32,8,128]{2,1,0:T(8,128)}, f32[128,2048]{1,0:T(8,128)}, bf16[1024,768]{1,0:T(8,128)(2,1)}, f32[64,2048]{1,0:T(8,128)}, bf16[4,2048,...) custom-call(bf16[128,2048]{1,0:T(8,128)(2,1)} %get-tuple-element.97.x_ref, ...), custom_call_target="tpu_custom_call", output_to_operand_aliasing={{5}: (14, {})} | custom-call | tf_op jit(solution)/shard_map/attention_backward/pallas_call | solution.py:86
  340.3 71.8 %in_scatter.1 = (f32[128,2048]{1,0:T(8,128)}, f32[64,6144]{1,0:T(8,128)}, f32[64,128]{1,0:T(8,128)}, bf16[4,2048,256]{2,1,0:T(8,128)(2,1)}) custom-call(bf16[8,128,768]{2,1,0:T(8,128)(2,1)} %bitcast.72, bf16[2048,768]{1,0:T(8,128)(2,1)} %bitcast.70, bf16[1024,2048]{1,0:T(8,128)(2,1)} %bitcast.68, ...), custom_call_target="tpu_custom_call", output_to_operand_aliasing={{3}: (6, {})} | custom-call | tf_op jit(solution)/shard_map/in_scatter/pallas_call | solution.py:86
  412.1 4.4 %convert_reduce_fusion.1 = f32[2048,256]{1,0:T(8,128)} fusion(bf16[4,2048,256]{2,1,0:T(8,128)(2,1)} %get-tuple-element.86), kind=kLoop, calls=%fused_computation.1 | loop fusion | flops 3670016 | bytes 6291456 | tf_op jit(solution)/shard_map/reduce_sum | solution.py:1826
  416.9 1.3 fusion.22
  418.2 0.6 slice_reduce_fusion
  418.9 0.8 convert_reduce_fusion
  419.7 0.8 copy-done.9
  420.5 3.1 fusion.1
  423.6 1.7 fusion.19
  425.4 0.9 fusion.21
  427.4 3.4 multiply_add_fusion
  430.8 1.4 multiply_add_fusion.1
  433.3 1.1 copy.64
  (96 shorter events, 4.5 us)
Async XLA Ops:
  0.7 4.3 copy-start
  0.7 5.7 %copy-start.22 = (bf16[64]{0:T(256)(128)(2,1)S(1)}, bf16[64]{0:T(256)(128)(2,1)}, u32[]{:S(2)}) copy-start(bf16[64]{0:T(256)(128)(2,1)} %param.29) | copy-start | bytes 388
  0.7 5.7 %copy-start.13 = (bf16[64,2048]{1,0:T(8,128)(2,1)S(1)}, bf16[64,2048]{1,0:T(8,128)(2,1)}, u32[]{:S(2)}) copy-start(bf16[64,2048]{1,0:T(8,128)(2,1)} %param.25) | copy-start | bytes 786436
  0.7 6.5 %copy-start.20 = (bf16[64]{0:T(256)(128)(2,1)S(1)}, bf16[64]{0:T(256)(128)(2,1)}, u32[]{:S(2)}) copy-start(bf16[64]{0:T(256)(128)(2,1)} %param.28) | copy-start | bytes 388
  0.7 7.2 %copy-start.23 = (bf16[64]{0:T(256)(128)(2,1)S(1)}, bf16[64]{0:T(256)(128)(2,1)}, u32[]{:S(2)}) copy-start(bf16[64]{0:T(256)(128)(2,1)} %param.30) | copy-start | bytes 388
  145.6 4.0 copy-start.21
  145.6 4.0 copy-start.4
  150.9 107.4 %copy-start.10 = (bf16[1,128,2048]{2,1,0:T(8,128)(2,1)S(1)}, bf16[1,128,2048]{2,1,0:T(8,128)(2,1)}, u32[]{:S(2)}) copy-start(bf16[1,128,2048]{2,1,0:T(8,128)(2,1)} %param.40) | copy-start | bytes 1572868
  256.5 1.8 copy-start.5
  256.5 1.8 copy-start.6
  412.1 4.5 %copy-start.7 = (f32[128,2048]{1,0:T(8,128)S(1)}, f32[128,2048]{1,0:T(8,128)}, u32[]{:S(2)}) copy-start(f32[128,2048]{1,0:T(8,128)} %get-tuple-element.83) | copy-start | bytes 3145732
  412.1 4.8 %copy-start.8 = (f32[128,2048]{1,0:T(8,128)S(1)}, f32[128,2048]{1,0:T(8,128)}, u32[]{:S(2)}) copy-start(f32[128,2048]{1,0:T(8,128)} %get-tuple-element.98) | copy-start | bytes 3145732
  416.5 1.6 copy-start.18
  416.5 2.4 copy-start.1
  418.9 1.6 copy-start.9
  420.5 3.1 copy-start.15
  420.5 3.1 copy-start.16
  423.6 1.8 copy-start.14
  423.6 2.7 copy-start.17
  423.6 3.2 copy-start.24
  423.6 3.2 copy-start.25
  423.6 3.7 copy-start.3
  427.4 3.4 copy-start.2
  427.4 3.4 copy-start.12
  430.8 1.4 copy-start.19
  430.8 2.0 copy-start.26
  430.8 2.5 copy-start.11

commit v9 on v8

--- a/solution.py
+++ b/solution.py
@@ -155,13 +155,17 @@
     return whole.at[:, pl.ds(pl.multiple_of(index * units, 128), units)]
 
 
-def half_rows(rows, half):
-    size = rows // 2
-    return pl.ds(half * size, size)
-
-
-def half_block(whole, units, index, half):
-    at = half_rows(whole.shape[-2], half)
+UP_FIRST = 3
+DOWN_FIRST = 5
+
+
+def share(rows, second, eighths):
+    first = rows * eighths // 128 * 16
+    return pl.ds(first, rows - first) if second else pl.ds(0, first)
+
+
+def half_block(whole, units, index, second):
+    at = share(whole.shape[-2], second, UP_FIRST)
     if len(whole.shape) == 3:
         return whole.at[index, at]
     return whole.at[at, pl.ds(pl.multiple_of(index * units, 128), units)]
@@ -565,7 +569,7 @@
             pl.when(t == z - 1)(lambda: self.downward(t, p, True).start())
             pl.when(t < z - 1)(lambda: self.downward(t, p, False).start())
 
-    def finish(self, store):
+    def finish(self, store, after=None):
         z, planes = self.here[0], self.planes
 
         def total(tile, *slots):
@@ -599,6 +603,9 @@
             def _(tiles=tiles):
                 for tile in tiles:
                     total(tile, z)
+
+            if after is not None:
+                after(p)
 
         for t in range(planes):
             for p in range(self.count):
@@ -634,6 +641,16 @@
     greet(barrier, peers)
     greet_line(barrier, planes, here)
     pl.semaphore_wait(barrier, len(peers) + line_peers(planes, here))
+    units = slots_ref.shape[2]
+    lower = share(slots_ref.shape[1], 1, UP_FIRST)
+    ups = ChipSwap(
+        chips,
+        here,
+        lambda index: half_block(up_ref, units, index, 1),
+        lambda index: slots_ref.at[index, lower],
+        chip_sems,
+    )
+    ups.start(local.at[0])
     half = seqs // 2
     line = LineScatter(
         planes,
@@ -672,29 +689,23 @@
         chips, here, left_ref, right_ref, True, (near_out, near_in, far_out, far_in), near, far
     )
     work.start()
-    units = slots_ref.shape[2]
-    lower = half_rows(slots_ref.shape[1], 1)
-    ups = ChipSwap(
-        chips,
-        here,
-        lambda index: half_block(up_ref, units, index, 1),
-        lambda index: slots_ref.at[index, lower],
-        chip_sems,
-    )
-    ups.start(local.at[0])
     for i in range(1, line.steps):
         line.step(i)
 
     def store(tile, total):
         mine[tile] = total.astype(LOW)
 
-    line.finish(store)
+    owners = [2 * device[1] + device[2] for device in peers]
     swaps = [
-        remote(mine.at[2 * device[1] + device[2]], parts.at[me], swap_sems, k, device)
-        for k, device in enumerate(peers, 1)
+        remote(mine.at[owner], parts.at[me], swap_sems, k, device)
+        for k, (owner, device) in enumerate(zip(owners, peers), 1)
     ]
-    for copy in swaps:
-        copy.start()
+
+    def send(p):
+        for owner, copy in zip(owners, swaps):
+            pl.when(owner // half == p)(copy.start)
+
+    line.finish(store, send)
     parts[me] = mine[me]
     work.finish(out_ref)
     for k in range(1, seqs):
@@ -976,7 +987,7 @@
         whole[...].reshape(planes * 2 * tokens, units) for whole in (normed, d_up)
     )
     size = units // chips
-    upper = half_rows(size, 0)
+    upper = share(size, 0, DOWN_FIRST)
     swap = ChipSwap(
         chips,
         here,
@@ -999,8 +1010,6 @@
             term = token_product(left, right).astype(LOW)
             for i in range(together):
                 gdown[chip + i, :, columns] = term[i * size : (i + 1) * size]
-        if chip // together % 2:
-            turn()
     swap.start(local.at[6])
     out_gdown = pltpu.make_async_copy(gdown, gdown_ref, local.at[9])
     out_gdown.start()
@@ -1012,7 +1021,7 @@
         for i in range(width // chunk)
     ]
     for i in range(width // chunk):
-        if i % 2 == 0:
+        if i == 0 or i % 2:
             turn()
         left = rows[:, :, :, pl.ds(i * chunk, chunk)].reshape(planes * 2 * tokens, chunk)
         term = token_product(left, flat_d_up).astype(LOW)
@@ -1513,7 +1522,7 @@
     gather.finish()
     stat_gather.finish()
     units = slots_ref.shape[2]
-    upper, lower = half_rows(width, 0), half_rows(down_ref.shape[1], 1)
+    upper, lower = share(width, 0, UP_FIRST), share(down_ref.shape[1], 1, DOWN_FIRST)
     swaps = [
         ChipSwap(
             chips,

time: 441 us -> 426 us (0.966)
  Pallas kernels: 392 us -> 376 us
    pallas_call x4, Pallas kernels: 392 us -> 376 us  [call(): pl.pallas_call(kernel, input_output_aliases=aliases or {}, name=name, out...]
where the time goes in v9:
time: 426 us; the launch traced here: 419 us
  Pallas kernels  376 us (88%)
  other arithmetic  33.5 us (8%)
  local copies, waits for them, and re-layouts  7.71 us (2%)
    pallas_call x4, Pallas kernels, call(): pl.pallas_call(kernel, input_output_aliases=aliases or {}, name=name, out...  376 us

profile of v9, /device:TPU:9, one launch (start us, length us, event | category | flops | bytes accessed | tf_op | source)
XLA Modules:
  0.0 418.9 jit_solution(14465652156160647846)
XLA Ops:
  0.7 0.7 convert_bitcast_fusion.2
  1.7 0.7 broadcast_multiply_fusion.2
  2.9 0.8 pad_maximum_fusion.meta_ref
  3.7 1.2 convert_reduce_fusion.2
  5.2 1.1 fusion.9.x_ref
  6.4 0.8 fusion.18.out_ref
  7.2 0.7 broadcast_in_dim.31.scale_ref.gain_ref
  7.9 0.6 scatter.4.gain_ref
  8.5 136.2 %attention_forward.1 = (bf16[4,1024,64]{2,1,0:T(8,128)(2,1)}, bf16[4,1024,64]{2,1,0:T(8,128)(2,1)}, bf16[4,1024,64]{2,1,0:T(8,128)(2,1)}, bf16[8,128,256]{2,1,0:...) custom-call(bf16[128,2048]{1,0:T(8,128)(2,1)} %fusion.9.x_ref, ...), custom_call_target="tpu_custom_call" | custom-call | tf_op jit(solution)/shard_map/attention_forward/pallas_call | solution.py:86
  144.7 0.9 reduce_sum.155
  145.7 1.7 fusion.26
  147.6 1.0 slice_reduce_fusion.1
  148.6 1.0 multiply_convert_fusion.x_ref
  149.6 1.2 fusion.down_ref
  150.9 101.1 %feed_forward.1 = (f32[128,2048]{1,0:T(8,128)}, bf16[4,256,1024]{2,1,0:T(8,128)(2,1)}, bf16[4,256,2048]{2,1,0:T(8,128)(2,1)}, bf16[2048,1024]{1,0:T(8,128)(2,1)}...) custom-call(bf16[128,2048]{1,0:T(8,128)(2,1)} %multiply_convert_fusion.x_ref, ...), custom_call_target="tpu_custom_call" | custom-call | tf_op jit(solution)/shard_map/feed_forward/pallas_call | solution.py:86
  252.0 1.7 multiply_reduce_fusion
  253.9 1.8 fusion.16
  255.8 0.6 pad.13.stat_ref
  256.5 0.7 pad.14.tile_ref
  257.2 68.9 %attention_backward.1 = (f32[32,8,128]{2,1,0:T(8,128)}, f32[128,2048]{1,0:T(8,128)}, bf16[1024,768]{1,0:T(8,128)(2,1)}, f32[64,2048]{1,0:T(8,128)}, bf16[4,2048,...) custom-call(bf16[128,2048]{1,0:T(8,128)(2,1)} %get-tuple-element.97.x_ref, ...), custom_call_target="tpu_custom_call", output_to_operand_aliasing={{5}: (14, {})} | custom-call | tf_op jit(solution)/shard_map/attention_backward/pallas_call | solution.py:86
  326.1 70.1 %in_scatter.1 = (f32[128,2048]{1,0:T(8,128)}, f32[64,6144]{1,0:T(8,128)}, f32[64,128]{1,0:T(8,128)}, bf16[4,2048,256]{2,1,0:T(8,128)(2,1)}) custom-call(bf16[8,128,768]{2,1,0:T(8,128)(2,1)} %bitcast.72, bf16[2048,768]{1,0:T(8,128)(2,1)} %bitcast.70, bf16[1024,2048]{1,0:T(8,128)(2,1)} %bitcast.68, ...), custom_call_target="tpu_custom_call", output_to_operand_aliasing={{3}: (6, {})} | custom-call | tf_op jit(solution)/shard_map/in_scatter/pallas_call | solution.py:86
  396.2 4.4 %convert_reduce_fusion.1 = f32[2048,256]{1,0:T(8,128)} fusion(bf16[4,2048,256]{2,1,0:T(8,128)(2,1)} %get-tuple-element.86), kind=kLoop, calls=%fused_computation.1 | loop fusion | flops 3670016 | bytes 6291456 | tf_op jit(solution)/shard_map/reduce_sum | solution.py:1835
  401.0 1.3 fusion.22
  402.2 0.6 slice_reduce_fusion
  403.0 0.8 convert_reduce_fusion
  403.8 0.8 copy-done.9
  404.6 3.1 fusion.1
  407.7 1.7 fusion.19
  409.5 0.9 fusion.21
  411.4 3.4 multiply_add_fusion
  414.8 1.4 multiply_add_fusion.1
  417.3 1.1 copy.64
  (96 shorter events, 4.5 us)
Async XLA Ops:
  0.7 4.3 %copy-start = (bf16[1,128,2048]{2,1,0:T(8,128)(2,1)S(1)}, bf16[1,128,2048]{2,1,0:T(8,128)(2,1)}, u32[]{:S(2)}) copy-start(bf16[1,128,2048]{2,1,0:T(8,128)(2,1)} %param.22) | copy-start | bytes 1572868
  0.7 5.7 %copy-start.22 = (bf16[64]{0:T(256)(128)(2,1)S(1)}, bf16[64]{0:T(256)(128)(2,1)}, u32[]{:S(2)}) copy-start(bf16[64]{0:T(256)(128)(2,1)} %param.29) | copy-start | bytes 388
  0.7 5.7 %copy-start.13 = (bf16[64,2048]{1,0:T(8,128)(2,1)S(1)}, bf16[64,2048]{1,0:T(8,128)(2,1)}, u32[]{:S(2)}) copy-start(bf16[64,2048]{1,0:T(8,128)(2,1)} %param.25) | copy-start | bytes 786436
  0.7 6.5 %copy-start.20 = (bf16[64]{0:T(256)(128)(2,1)S(1)}, bf16[64]{0:T(256)(128)(2,1)}, u32[]{:S(2)}) copy-start(bf16[64]{0:T(256)(128)(2,1)} %param.28) | copy-start | bytes 388
  0.7 7.2 %copy-start.23 = (bf16[64]{0:T(256)(128)(2,1)S(1)}, bf16[64]{0:T(256)(128)(2,1)}, u32[]{:S(2)}) copy-start(bf16[64]{0:T(256)(128)(2,1)} %param.30) | copy-start | bytes 388
  145.6 4.0 copy-start.21
  145.6 4.0 copy-start.4
  150.9 102.9 %copy-start.10 = (bf16[1,128,2048]{2,1,0:T(8,128)(2,1)S(1)}, bf16[1,128,2048]{2,1,0:T(8,128)(2,1)}, u32[]{:S(2)}) copy-start(bf16[1,128,2048]{2,1,0:T(8,128)(2,1)} %param.40) | copy-start | bytes 1572868
  252.0 1.8 copy-start.5
  252.0 1.8 copy-start.6
  396.1 4.5 %copy-start.7 = (f32[128,2048]{1,0:T(8,128)S(1)}, f32[128,2048]{1,0:T(8,128)}, u32[]{:S(2)}) copy-start(f32[128,2048]{1,0:T(8,128)} %get-tuple-element.83) | copy-start | bytes 3145732
  396.2 4.8 %copy-start.8 = (f32[128,2048]{1,0:T(8,128)S(1)}, f32[128,2048]{1,0:T(8,128)}, u32[]{:S(2)}) copy-start(f32[128,2048]{1,0:T(8,128)} %get-tuple-element.98) | copy-start | bytes 3145732
  400.6 1.6 copy-start.18
  400.6 2.4 copy-start.1
  403.0 1.6 copy-start.9
  404.6 3.1 copy-start.15
  404.6 3.1 copy-start.16
  407.7 1.8 copy-start.14
  407.7 2.7 copy-start.17
  407.7 3.2 copy-start.24
  407.7 3.2 copy-start.25
  407.7 3.7 copy-start.3
  411.4 3.4 copy-start.2
  411.4 3.4 copy-start.12
  414.8 1.4 copy-start.19
  414.8 2.0 copy-start.26
  414.8 2.5 copy-start.11

commit v10 on v9

--- a/solution.py
+++ b/solution.py
@@ -835,8 +835,8 @@
 
 
 def feed_forward_kernel(
-    planes, chips, width_ff, x_ref, up_ref, grads_ref, down_ref,
-    out_ref, normed_ref, downs_ref, gup_ref, gdown_ref, slots_ref,
+    planes, chips, width_ff, x_ref, up_ref, grads_ref, downs_ref,
+    out_ref, normed_ref, gup_ref, gdown_ref, slots_ref,
     rows, ups, grads, downs, back, act, slope, stat, stat_out, stat_in,
     normed, d_up, near_out, own, sums, gup, gdown, *sems,
 ):
@@ -844,16 +844,18 @@
     z, c, core = here
     count = 2 * planes
     me = 2 * z + core
-    up, down, near, chip_sems, stat_sems, pair, rise, fall, swap_sems = [
-        sems[2 * i : 2 * i + 2] for i in range(9)
+    up, down, near, stat_sems, pair, rise, fall, swap_sems = [
+        sems[2 * i : 2 * i + 2] for i in range(8)
     ]
-    local = sems[18]
+    local = sems[16]
     tokens, width = x_ref.shape
     units = ups.shape[1]
     load_up = pltpu.make_async_copy(up_ref, ups, local.at[0])
     load_grads = pltpu.make_async_copy(grads_ref, grads, local.at[1])
     load_up.start()
     load_grads.start()
+    load_downs = pltpu.make_async_copy(downs_ref, downs, local.at[3])
+    load_downs.start()
     barrier = pltpu.get_barrier_semaphore()
     ids = [lax.rem(me + k, count) for k in range(1, count)]
     group_peers = [(index // 2, c, lax.rem(index, 2)) for index in ids]
@@ -863,16 +865,6 @@
 
     group = GroupGather(planes, here, x_ref, rows, up, down, near)
     group.start(local.at[2])
-    keep = pltpu.make_async_copy(down_ref, downs.at[c], local.at[3])
-    keep.start()
-    weights = ChipGather(
-        chips,
-        here,
-        lambda half: row_half(down_ref, half),
-        lambda chip, half: row_half(downs.at[chip], half),
-        chip_sems,
-    )
-    weights.start()
     load_up.wait()
 
     step = tokens
@@ -901,30 +893,27 @@
 
         lax.fori_loop(0, 2 * tokens // step, some, 0)
 
+    def project(t):
+        block = grads[t].reshape(2 * tokens, width)
+        size = units // chips
+        for chip in range(chips):
+            back[t, :, pl.ds(chip * size, size)] = rows_product(block, downs[chip])
+
     forward(z)
+    load_grads.wait()
+    load_downs.wait()
+    project(0)
     for d in range(1, planes):
         group.step(d)
-        if d == 2:
-            weights.relay()
+        project(d)
         if d > 1:
             pl.when(z - d + 1 >= 0)(lambda d=d: forward(z - d + 1))
             pl.when(z + d - 1 < planes)(lambda d=d: forward(z + d - 1))
     pl.when(z - planes + 1 >= 0)(lambda: forward(z - planes + 1))
     pl.when(z + planes - 1 < planes)(lambda: forward(z + planes - 1))
     group.finish()
-    keep.wait()
-    load_grads.wait()
-    weights.finish()
-    out_downs = pltpu.make_async_copy(downs, downs_ref, local.at[4])
-    out_downs.start()
 
     def backward(t, carry):
-        block = grads[t].reshape(2 * tokens, width)
-        size = units // chips
-        for chip in range(chips):
-            columns = pl.ds(chip * size, size)
-            back[t, :, columns] = rows_product(block, downs[chip])
-
         def some(i, inner):
             at = pl.ds(pl.multiple_of(i * step, step), step)
             value = back[t, at]
@@ -1033,7 +1022,6 @@
         turn()
     work.finish(out_ref)
     swap.finish()
-    out_downs.wait()
     out_normed.wait()
     out_gdown.wait()
     for copy in out_gups[-2:]:
@@ -1050,10 +1038,10 @@
         return self.whole[t, rows]
 
 
-def feed_forward(planes, chips, width_ff, x_block, up_mine, grads, down_block):
+def feed_forward(planes, chips, width_ff, x_block, up_mine, grads, downs):
     tokens, width = x_block.shape
     units = up_mine.shape[1]
-    size = down_block.shape[0]
+    size = downs.shape[1]
     wide = (planes, 2 * tokens, units)
     return call(
         functools.partial(feed_forward_kernel, planes, chips, width_ff),
@@ -1061,13 +1049,12 @@
         [
             shape((tokens, width), F32),
             shape(wide, LOW),
-            shape((chips, size, width), LOW),
             shape((width, units), LOW),
             *[shape((chips, size, width), LOW)] * 2,
         ],
-        (x_block, up_mine, grads, down_block),
+        (x_block, up_mine, grads, downs),
         [HBM] * 4,
-        [VMEM, *[HBM] * 5],
+        [VMEM, *[HBM] * 4],
         [
             pltpu.VMEM((planes, 2, tokens, width), LOW),
             pltpu.VMEM((width, units), LOW),
@@ -1082,7 +1069,7 @@
             pltpu.VMEM((2, 256, units), LOW),
             pltpu.VMEM((chips, size, width), LOW),
             *GroupGather.sems(planes),
-            *pairs_of(ChipGather.count(chips), 2 * planes),
+            *pairs_of(2 * planes),
             *PairScatter.sems(planes, width),
             *pairs_of(chips),
             pltpu.SemaphoreType.DMA((10,)),
@@ -1121,9 +1108,9 @@
 
 def attention_forward_kernel(
     planes, chips, heads, strided,
-    x_ref, meta_ref, weight_ref, scale_ref, out_ref, gain_ref, up_ref, grad_ref,
+    x_ref, meta_ref, weight_ref, scale_ref, out_ref, gain_ref, up_ref, down_ref, grad_ref,
     q_ref, k_ref, v_ref, att_ref, log_ref, sum_ref,
-    rows_ref, metas_ref, qkvs_ref, outs_ref, gains_ref, ups_ref, grads_ref, tiles_ref,
+    rows_ref, metas_ref, qkvs_ref, outs_ref, gains_ref, ups_ref, downs_ref, grads_ref, tiles_ref,
     qkv_ref, rows, metas, qkvs, outs, raw, wide, tile, near_out, near_in, far_out, far_in,
     *sems,
 ):
@@ -1133,10 +1120,10 @@
     count = planes * seqs
     me = 2 * c + core
     flat = z * seqs + me
-    groups = [sems[2 * i : 2 * i + 2] for i in range(17)]
+    groups = [sems[2 * i : 2 * i + 2] for i in range(18)]
     swap_sems, x_far, x_near, meta_far, meta_near, up, down, up_two, down_two = groups[:9]
-    gain_sems, up_sems, near, far, tile_sems, grad_up, grad_down, pair = groups[9:]
-    local = sems[34]
+    gain_sems, up_sems, near, far, tile_sems, grad_up, grad_down, pair, weight_sems = groups[9:]
+    local = sems[36]
     tokens, width = x_ref.shape
     part = qkv_ref.shape[1]
     length = seqs * tokens
@@ -1172,6 +1159,7 @@
         pltpu.make_async_copy(meta_ref, metas.at[me], local.at[3]),
         pltpu.make_async_copy(gain_ref, gains_ref.at[flat], local.at[4]),
         pltpu.make_async_copy(up_ref, column_block(ups_ref, units, c), local.at[5]),
+        pltpu.make_async_copy(down_ref, downs_ref.at[c], local.at[12]),
     ]
     peers = plane_peers(chips, here)
     swaps = [
@@ -1221,6 +1209,13 @@
         up_sems,
     )
     ups.start()
+    weights = ChipGather(
+        chips,
+        here,
+        lambda half: row_half(down_ref, half),
+        lambda chip, half: row_half(downs_ref.at[chip], half),
+        weight_sems,
+    )
     line.step(2)
     gather.finish()
     meta_gather.finish()
@@ -1239,8 +1234,9 @@
 
     add(z, True)
     for d in range(1, planes):
-        if d == 3:
+        if d == planes - 1:
             ups.relay()
+            weights.start()
         if d > 2:
             line.step(d)
         if d == planes - 1:
@@ -1331,6 +1327,7 @@
     keep.start()
     out_outs = pltpu.make_async_copy(outs, outs_ref, local.at[11])
     out_outs.start()
+    weights.relay()
     work = PlaneScatter(
         chips, here, att_ref, Flat(outs, span), False, (near_out, near_in, far_out, far_in), near, far
     )
@@ -1347,6 +1344,7 @@
     for copy in swaps:
         copy.wait_send()
     ups.finish()
+    weights.finish()
     for copy in [keep, out_outs, *outputs]:
         copy.wait()
     for k in range(1, seqs):
@@ -1386,7 +1384,8 @@
 
 
 def attention_forward(
-    planes, chips, heads, strided, x_block, meta, weight, scale, out_rows, gain_tile, up_block, grad
+    planes, chips, heads, strided,
+    x_block, meta, weight, scale, out_rows, gain_tile, up_block, down_block, grad,
 ):
     seqs = 2 * chips
     tokens, width = x_block.shape
@@ -1410,12 +1409,13 @@
             shape(outs, LOW),
             shape((planes * seqs, *gain_tile.shape), F32),
             shape((width, chips * units) if units % 128 == 0 else (chips, width, units), LOW),
+            shape((chips, *down_block.shape), LOW),
             shape((planes, 2, *grad.shape), LOW),
             shape(tile, F32),
         ],
-        (x_block, meta, weight, scale, out_rows, gain_tile, up_block, grad),
-        [HBM, HBM, VMEM, VMEM, HBM, HBM, HBM, HBM],
-        [*[VMEM] * 6, *[HBM] * 8],
+        (x_block, meta, weight, scale, out_rows, gain_tile, up_block, down_block, grad),
+        [HBM, HBM, VMEM, VMEM, HBM, HBM, HBM, HBM, HBM],
+        [*[VMEM] * 6, *[HBM] * 9],
         [
             pltpu.VMEM((seqs, part, wide), LOW),
             pltpu.VMEM((seqs, tokens, width), LOW),
@@ -1433,7 +1433,8 @@
             *PlaneScatter.sems(chips, width),
             *pairs_of(seqs),
             *GroupGather.sems(planes),
-            pltpu.SemaphoreType.DMA((12,)),
+            *pairs_of(ChipGather.count(chips)),
+            pltpu.SemaphoreType.DMA((13,)),
         ],
         1,
     )
@@ -1741,7 +1742,7 @@
     grad_low = out_grad[0]
     (
         queries, keys, values, attended, log_total, out_sum,
-        row_in, meta, qkv_mine, out_mine, gain_tiles, up_mine, grad_flat, tiles,
+        row_in, meta, qkv_mine, out_mine, gain_tiles, up_mine, down_mine, grad_flat, tiles,
     ) = attention_forward(
         planes,
         chips,
@@ -1754,6 +1755,7 @@
         out_scaled,
         gain_tile,
         w_up,
+        down_scaled,
         grad_low,
     )
     if up_mine.ndim == 3:
@@ -1776,8 +1778,8 @@
 
     grad_top = grad_low.astype(F32)
     units = w_up.shape[1]
-    d_ffn_in, normed_four, down_mine, grad_up, grad_down, down_slots = feed_forward(
-        planes, chips, width_ff, ffn_in, up_mine, grad_flat, down_scaled
+    d_ffn_in, normed_four, grad_up, grad_down, down_slots = feed_forward(
+        planes, chips, width_ff, ffn_in, up_mine, grad_flat, down_mine
     )
     down_mine = down_mine.reshape(-1, width)
     if units % 128:

time: 426 us -> 448 us (1.052)
  Pallas kernels: 376 us -> 398 us
    pallas_call x4, Pallas kernels: 376 us -> 398 us  [call(): pl.pallas_call(kernel, input_output_aliases=aliases or {}, name=name, out...]
where the time goes in v10:
time: 448 us; the launch traced here: 441 us
  Pallas kernels  398 us (89%)
  other arithmetic  33.5 us (7%)
  local copies, waits for them, and re-layouts  7.71 us (2%)
    pallas_call x4, Pallas kernels, call(): pl.pallas_call(kernel, input_output_aliases=aliases or {}, name=name, out...  398 us

profile of v10, /device:TPU:9, one launch (start us, length us, event | category | flops | bytes accessed | tf_op | source)
XLA Modules:
  0.0 440.9 jit_solution(15797678428407851313)
XLA Ops:
  0.7 0.8 convert_bitcast_fusion.2
  1.7 0.7 broadcast_multiply_fusion.2
  3.0 0.8 pad_maximum_fusion.meta_ref
  3.8 1.2 convert_reduce_fusion.2
  5.3 1.1 fusion.9.x_ref
  6.5 1.2 fusion.down_ref
  7.7 0.8 fusion.18.out_ref
  8.5 0.7 broadcast_in_dim.31.scale_ref.gain_ref
  9.2 0.6 scatter.4.gain_ref
  9.8 157.1 %attention_forward.1 = (bf16[4,1024,64]{2,1,0:T(8,128)(2,1)}, bf16[4,1024,64]{2,1,0:T(8,128)(2,1)}, bf16[4,1024,64]{2,1,0:T(8,128)(2,1)}, bf16[8,128,256]{2,1,0:...) custom-call(bf16[128,2048]{1,0:T(8,128)(2,1)} %fusion.9.x_ref, ...), custom_call_target="tpu_custom_call" | custom-call | tf_op jit(solution)/shard_map/attention_forward/pallas_call | solution.py:86
  167.0 0.9 reduce_sum.155
  167.9 1.6 fusion.26
  169.8 1.0 slice_reduce_fusion.1
  170.8 1.0 multiply_convert_fusion.x_ref
  171.8 101.3 %feed_forward.1 = (f32[128,2048]{1,0:T(8,128)}, bf16[4,256,1024]{2,1,0:T(8,128)(2,1)}, bf16[2048,1024]{1,0:T(8,128)(2,1)}, bf16[4,256,2048]{2,1,0:T(8,128)(2,1)}, bf16[4,256,2048]{2,1,0:T(8,128)(2,1)}) custom-call(bf16[128,2048]{1,0:T(8,128)(2,1)} %multiply_convert_fusion.x_ref, bf16[2048,1024]{1,0:T(8,128)(2,1)} %get-tuple-element.63.up_ref, ...), custom_call_target="tpu_custom_call" | custom-call | tf_op jit(solution)/shard_map/feed_forward/pallas_call | solution.py:86
  273.1 1.7 multiply_reduce_fusion
  274.9 1.8 fusion.16
  276.9 0.6 pad.13.stat_ref
  277.6 0.7 pad.14.tile_ref
  278.3 69.0 %attention_backward.1 = (f32[32,8,128]{2,1,0:T(8,128)}, f32[128,2048]{1,0:T(8,128)}, bf16[1024,768]{1,0:T(8,128)(2,1)}, f32[64,2048]{1,0:T(8,128)}, bf16[4,2048,...) custom-call(bf16[128,2048]{1,0:T(8,128)(2,1)} %get-tuple-element.97.x_ref, ...), custom_call_target="tpu_custom_call", output_to_operand_aliasing={{5}: (14, {})} | custom-call | tf_op jit(solution)/shard_map/attention_backward/pallas_call | solution.py:86
  347.2 70.9 %in_scatter.1 = (f32[128,2048]{1,0:T(8,128)}, f32[64,6144]{1,0:T(8,128)}, f32[64,128]{1,0:T(8,128)}, bf16[4,2048,256]{2,1,0:T(8,128)(2,1)}) custom-call(bf16[8,128,768]{2,1,0:T(8,128)(2,1)} %bitcast.72, bf16[2048,768]{1,0:T(8,128)(2,1)} %bitcast.70, bf16[1024,2048]{1,0:T(8,128)(2,1)} %bitcast.69, ...), custom_call_target="tpu_custom_call", output_to_operand_aliasing={{3}: (6, {})} | custom-call | tf_op jit(solution)/shard_map/in_scatter/pallas_call | solution.py:86
  418.1 4.4 %convert_reduce_fusion.1 = f32[2048,256]{1,0:T(8,128)} fusion(bf16[4,2048,256]{2,1,0:T(8,128)(2,1)} %get-tuple-element.86), kind=kLoop, calls=%fused_computation.1 | loop fusion | flops 3670016 | bytes 6291456 | tf_op jit(solution)/shard_map/reduce_sum | solution.py:1837
  422.9 1.3 fusion.22
  424.2 0.6 slice_reduce_fusion
  425.0 0.8 convert_reduce_fusion
  425.8 0.8 copy-done.9
  426.6 3.1 fusion.1
  429.7 1.7 fusion.19
  431.4 0.9 fusion.21
  433.4 3.4 multiply_add_fusion
  436.8 1.4 multiply_add_fusion.1
  439.3 1.1 copy.64
  (96 shorter events, 4.5 us)
Async XLA Ops:
  0.7 4.4 copy-start
  0.7 5.8 %copy-start.21 = (bf16[256]{0:T(256)(128)(2,1)S(1)}, bf16[256]{0:T(256)(128)(2,1)}, u32[]{:S(2)}) copy-start(bf16[256]{0:T(256)(128)(2,1)} %param.31) | copy-start | bytes 1540
  0.7 5.8 %copy-start.4 = (bf16[256,2048]{1,0:T(8,128)(2,1)S(1)}, bf16[256,2048]{1,0:T(8,128)(2,1)}, u32[]{:S(2)}) copy-start(bf16[256,2048]{1,0:T(8,128)(2,1)} %param.27) | copy-start | bytes 3145732
  3.8 3.9 copy-start.22
  3.8 3.9 copy-start.13
  5.0 3.5 copy-start.20
  5.0 4.2 copy-start.23
  171.8 103.0 %copy-start.10 = (bf16[1,128,2048]{2,1,0:T(8,128)(2,1)S(1)}, bf16[1,128,2048]{2,1,0:T(8,128)(2,1)}, u32[]{:S(2)}) copy-start(bf16[1,128,2048]{2,1,0:T(8,128)(2,1)} %param.40) | copy-start | bytes 1572868
  273.1 1.8 copy-start.5
  273.1 1.8 copy-start.6
  418.1 4.5 %copy-start.7 = (f32[128,2048]{1,0:T(8,128)S(1)}, f32[128,2048]{1,0:T(8,128)}, u32[]{:S(2)}) copy-start(f32[128,2048]{1,0:T(8,128)} %get-tuple-element.83) | copy-start | bytes 3145732
  418.1 4.8 %copy-start.8 = (f32[128,2048]{1,0:T(8,128)S(1)}, f32[128,2048]{1,0:T(8,128)}, u32[]{:S(2)}) copy-start(f32[128,2048]{1,0:T(8,128)} %get-tuple-element.98) | copy-start | bytes 3145732
  422.6 1.6 copy-start.18
  422.6 2.4 copy-start.1
  425.0 1.6 copy-start.9
  426.5 3.1 copy-start.15
  426.6 3.1 copy-start.16
  429.6 1.8 copy-start.14
  429.6 2.7 copy-start.17
  429.6 3.2 copy-start.24
  429.6 3.2 copy-start.25
  429.7 3.7 copy-start.3
  433.4 3.4 copy-start.2
  433.4 3.4 copy-start.12
  436.8 1.4 copy-start.19
  436.8 2.0 copy-start.26
  436.8 2.5 copy-start.11

commit v11 on v9

--- a/solution.py
+++ b/solution.py
@@ -1519,8 +1519,6 @@
     turn()
     gather.forward()
     stat_gather.forward()
-    gather.finish()
-    stat_gather.finish()
     units = slots_ref.shape[2]
     upper, lower = share(width, 0, UP_FIRST), share(down_ref.shape[1], 1, DOWN_FIRST)
     swaps = [
@@ -1541,6 +1539,8 @@
     ]
     for i, swap in enumerate(swaps):
         swap.start(local.at[12 + i])
+    gather.finish()
+    stat_gather.finish()
     for copy in [*loads[2:], *keeps]:
         copy.wait()
     turn()

time: 426 us -> 425 us (level)
  no operation moved by 1% of the time
where the time goes in v11:
time: 425 us; the launch traced here: 417 us
  Pallas kernels  374 us (88%)
  other arithmetic  33.5 us (8%)
  local copies, waits for them, and re-layouts  7.71 us (2%)
    pallas_call x4, Pallas kernels, call(): pl.pallas_call(kernel, input_output_aliases=aliases or {}, name=name, out...  374 us

profile of v11, /device:TPU:9, one launch (start us, length us, event | category | flops | bytes accessed | tf_op | source)
XLA Modules:
  0.0 417.0 jit_solution(4891961418922702827)
XLA Ops:
  0.7 0.7 convert_bitcast_fusion.2
  1.7 0.7 broadcast_multiply_fusion.2
  2.9 0.8 pad_maximum_fusion.meta_ref
  3.7 1.2 convert_reduce_fusion.2
  5.2 1.1 fusion.9.x_ref
  6.4 0.8 fusion.18.out_ref
  7.2 0.7 broadcast_in_dim.31.scale_ref.gain_ref
  7.9 0.6 scatter.4.gain_ref
  8.5 136.2 %attention_forward.1 = (bf16[4,1024,64]{2,1,0:T(8,128)(2,1)}, bf16[4,1024,64]{2,1,0:T(8,128)(2,1)}, bf16[4,1024,64]{2,1,0:T(8,128)(2,1)}, bf16[8,128,256]{2,1,0:...) custom-call(bf16[128,2048]{1,0:T(8,128)(2,1)} %fusion.9.x_ref, ...), custom_call_target="tpu_custom_call" | custom-call | tf_op jit(solution)/shard_map/attention_forward/pallas_call | solution.py:86
  144.7 0.9 reduce_sum.155
  145.7 1.7 fusion.26
  147.6 1.0 slice_reduce_fusion.1
  148.6 1.0 multiply_convert_fusion.x_ref
  149.6 1.2 fusion.down_ref
  150.9 101.1 %feed_forward.1 = (f32[128,2048]{1,0:T(8,128)}, bf16[4,256,1024]{2,1,0:T(8,128)(2,1)}, bf16[4,256,2048]{2,1,0:T(8,128)(2,1)}, bf16[2048,1024]{1,0:T(8,128)(2,1)}...) custom-call(bf16[128,2048]{1,0:T(8,128)(2,1)} %multiply_convert_fusion.x_ref, ...), custom_call_target="tpu_custom_call" | custom-call | tf_op jit(solution)/shard_map/feed_forward/pallas_call | solution.py:86
  252.0 1.7 multiply_reduce_fusion
  253.9 1.8 fusion.16
  255.8 0.6 pad.13.stat_ref
  256.5 0.7 pad.14.tile_ref
  257.2 68.8 %attention_backward.1 = (f32[32,8,128]{2,1,0:T(8,128)}, f32[128,2048]{1,0:T(8,128)}, bf16[1024,768]{1,0:T(8,128)(2,1)}, f32[64,2048]{1,0:T(8,128)}, bf16[4,2048,...) custom-call(bf16[128,2048]{1,0:T(8,128)(2,1)} %get-tuple-element.97.x_ref, ...), custom_call_target="tpu_custom_call", output_to_operand_aliasing={{5}: (14, {})} | custom-call | tf_op jit(solution)/shard_map/attention_backward/pallas_call | solution.py:86
  326.0 68.3 %in_scatter.1 = (f32[128,2048]{1,0:T(8,128)}, f32[64,6144]{1,0:T(8,128)}, f32[64,128]{1,0:T(8,128)}, bf16[4,2048,256]{2,1,0:T(8,128)(2,1)}) custom-call(bf16[8,128,768]{2,1,0:T(8,128)(2,1)} %bitcast.72, bf16[2048,768]{1,0:T(8,128)(2,1)} %bitcast.70, bf16[1024,2048]{1,0:T(8,128)(2,1)} %bitcast.68, ...), custom_call_target="tpu_custom_call", output_to_operand_aliasing={{3}: (6, {})} | custom-call | tf_op jit(solution)/shard_map/in_scatter/pallas_call | solution.py:86
  394.3 4.4 %convert_reduce_fusion.1 = f32[2048,256]{1,0:T(8,128)} fusion(bf16[4,2048,256]{2,1,0:T(8,128)(2,1)} %get-tuple-element.86), kind=kLoop, calls=%fused_computation.1 | loop fusion | flops 3670016 | bytes 6291456 | tf_op jit(solution)/shard_map/reduce_sum | solution.py:1835
  399.1 1.3 fusion.22
  400.3 0.6 slice_reduce_fusion
  401.1 0.8 convert_reduce_fusion
  401.9 0.8 copy-done.9
  402.7 3.1 fusion.1
  405.8 1.7 fusion.19
  407.5 0.9 fusion.21
  409.5 3.4 multiply_add_fusion
  412.9 1.4 multiply_add_fusion.1
  415.4 1.1 copy.64
  (96 shorter events, 4.5 us)
Async XLA Ops:
  0.7 4.3 %copy-start = (bf16[1,128,2048]{2,1,0:T(8,128)(2,1)S(1)}, bf16[1,128,2048]{2,1,0:T(8,128)(2,1)}, u32[]{:S(2)}) copy-start(bf16[1,128,2048]{2,1,0:T(8,128)(2,1)} %param.22) | copy-start | bytes 1572868
  0.7 5.7 %copy-start.22 = (bf16[64]{0:T(256)(128)(2,1)S(1)}, bf16[64]{0:T(256)(128)(2,1)}, u32[]{:S(2)}) copy-start(bf16[64]{0:T(256)(128)(2,1)} %param.29) | copy-start | bytes 388
  0.7 5.7 %copy-start.13 = (bf16[64,2048]{1,0:T(8,128)(2,1)S(1)}, bf16[64,2048]{1,0:T(8,128)(2,1)}, u32[]{:S(2)}) copy-start(bf16[64,2048]{1,0:T(8,128)(2,1)} %param.25) | copy-start | bytes 786436
  0.7 6.5 %copy-start.20 = (bf16[64]{0:T(256)(128)(2,1)S(1)}, bf16[64]{0:T(256)(128)(2,1)}, u32[]{:S(2)}) copy-start(bf16[64]{0:T(256)(128)(2,1)} %param.28) | copy-start | bytes 388
  0.7 7.2 %copy-start.23 = (bf16[64]{0:T(256)(128)(2,1)S(1)}, bf16[64]{0:T(256)(128)(2,1)}, u32[]{:S(2)}) copy-start(bf16[64]{0:T(256)(128)(2,1)} %param.30) | copy-start | bytes 388
  145.6 4.0 copy-start.21
  145.6 4.0 copy-start.4
  150.9 102.9 %copy-start.10 = (bf16[1,128,2048]{2,1,0:T(8,128)(2,1)S(1)}, bf16[1,128,2048]{2,1,0:T(8,128)(2,1)}, u32[]{:S(2)}) copy-start(bf16[1,128,2048]{2,1,0:T(8,128)(2,1)} %param.40) | copy-start | bytes 1572868
  252.0 1.8 copy-start.5
  252.0 1.8 copy-start.6
  394.2 4.5 %copy-start.7 = (f32[128,2048]{1,0:T(8,128)S(1)}, f32[128,2048]{1,0:T(8,128)}, u32[]{:S(2)}) copy-start(f32[128,2048]{1,0:T(8,128)} %get-tuple-element.83) | copy-start | bytes 3145732
  394.2 4.8 %copy-start.8 = (f32[128,2048]{1,0:T(8,128)S(1)}, f32[128,2048]{1,0:T(8,128)}, u32[]{:S(2)}) copy-start(f32[128,2048]{1,0:T(8,128)} %get-tuple-element.98) | copy-start | bytes 3145732
  398.7 1.6 copy-start.18
  398.7 2.4 copy-start.1
  401.1 1.6 copy-start.9
  402.7 3.1 copy-start.15
  402.7 3.1 copy-start.16
  405.7 1.8 copy-start.14
  405.8 2.7 copy-start.17
  405.8 3.2 copy-start.24
  405.8 3.2 copy-start.25
  405.8 3.7 copy-start.3
  409.5 3.4 copy-start.2
  409.5 3.4 copy-start.12
  412.9 1.4 copy-start.19
  412.9 2.0 copy-start.26
  412.9 2.5 copy-start.11
